TPU v7x, 32 devices: a whole 2x2x4 slice. The times are simulated.
32 devices in a mesh: view: 8 (over z, y), tok: 4 (over x, core).
Axes of the slice: x: 2, y: 2, z: 4, core: 2. Of those that a mesh axis runs over, the one named last changes fastest.
Arguments:
- q1: bfloat16 [8, 128, 1024], P('view', 'tok'), may hold values from -96 to 96
- k1: bfloat16 [8, 128, 1024], P('view', 'tok'), may hold values from -6 to 6
- v1: bfloat16 [8, 128, 1024], P('view', 'tok'), may hold values from -6 to 6
- nbr: int32 [8, 7], P('view'), may hold values from 0 to 7, as said below
- x2: bfloat16 [8, 128, 1024], P('view', 'tok'), may hold values from -6 to 6
- w_view_out: bfloat16 [1024, 1024], replicated, may hold values from -0.1875 to 0.1875
- norm_gain: float32 [1024], replicated, may hold values from 0.5 to 1.5
- w_qkv: bfloat16 [1024, 3072], replicated, may hold values from -0.1875 to 0.1875
- w_out: bfloat16 [1024, 1024], replicated, may hold values from -0.1875 to 0.1875
Outputs:
- view_feats: float32 [8, 128, 1024], P('view', 'tok')
- lrm_out: float32 [8, 128, 1024], P('view', 'tok')
Inputs may be any that keep to these rules, and one draw needn't show every extreme that they name: `nbr`: row v lists 7 distinct view indices, none equal to v.
All inputs are finite; a program needn't handle non-finite values.
Results may differ from a plain program's by a relative error of at most 0.014.
Values may be sent and summed in bfloat16 or wider, within the bound.
No kernel may reach another device: no remote copies, remote signals or barrier semaphores. Data moves between devices by JAX's collectives and lax.ppermute only.
A program may use at most 128 MiB of HBM per device.

v0:
```python
import jax
import jax.numpy as jnp
from jax import lax
from jax.sharding import PartitionSpec as P

H1 = 16
HD1 = 64
HD2 = 64


EPSILON = 1e-06
NEGATIVE = -1e30


def absorb(running, queries, key_piece, val_piece, keep_key, factor_scale):
    running_max, row_total, weighted = running
    scores = (
        jnp.einsum("qhd,khd->qhk", queries, key_piece, preferred_element_type=jnp.float32)
        * factor_scale
    )
    scores = jnp.where(keep_key[None, None, :], scores, NEGATIVE)
    new_max = jnp.maximum(running_max, jnp.max(scores, axis=-1))
    weights = jnp.where(keep_key[None, None, :], jnp.exp(scores - new_max[..., None]), 0.0)
    row_total = jnp.sum(weights, axis=-1)
    weighted = jnp.einsum(
        "qhk,khd->qhd", weights.astype(jnp.bfloat16), val_piece, preferred_element_type=jnp.float32
    )
    return (new_max, row_total, weighted)


def per_device(q1, k1, v1, nbr, x2, w_view_out, norm_gain, w_qkv, w_out):
    own_view = lax.axis_index("view")
    wanted = nbr[0]
    queries = lax.all_gather(q1, "tok", axis=1, tiled=True)[0].reshape(-1, H1, HD1)
    query_rows = queries.shape[0]
    start_state = (
        jnp.full((query_rows, H1), NEGATIVE, jnp.float32),
        jnp.zeros((query_rows, H1), jnp.float32),
        jnp.zeros((query_rows, H1, HD1), jnp.float32),
    )
    scale_one = HD1 ** (-0.5)
    key_piece = lax.all_gather(k1, "view", axis=0, tiled=True)
    val_piece = lax.all_gather(v1, "view", axis=0, tiled=True)
    view_ids = jnp.arange(key_piece.shape[0], dtype=jnp.int32)
    keep_view = (view_ids == own_view) | jnp.any(view_ids[:, None] == wanted[None, :], axis=1)
    keep_key = jnp.repeat(keep_view, key_piece.shape[1])
    running_max, row_total, weighted = absorb(
        start_state,
        queries,
        key_piece.reshape(-1, H1, HD1),
        val_piece.reshape(-1, H1, HD1),
        keep_key,
        scale_one,
    )
    tok_devs = lax.axis_size("tok")
    my_rows = query_rows // tok_devs
    got_sums, got_max, got_total = (
        lax.all_to_all(weighted[None], "tok", split_axis=1, concat_axis=0, tiled=True),
        lax.all_to_all(running_max[None], "tok", split_axis=1, concat_axis=0, tiled=True),
        lax.all_to_all(row_total[None], "tok", split_axis=1, concat_axis=0, tiled=True),
    )
    row_peak = jnp.max(got_max, axis=0)
    factor = jnp.exp(got_max - row_peak)
    summed = jnp.sum(got_sums * factor[..., None], axis=0)
    totals = jnp.sum(got_total * factor, axis=0)
    attn_one = (summed / totals[..., None]).reshape(my_rows, -1)
    features = attn_one * lax.rsqrt(jnp.mean(attn_one * attn_one, axis=-1, keepdims=True) + EPSILON)
    features_half = features.astype(jnp.bfloat16)
    hidden = x2[0].astype(jnp.float32) + jnp.dot(
        features_half, w_view_out, preferred_element_type=jnp.float32
    )
    normed = (
        hidden * lax.rsqrt(jnp.mean(hidden * hidden, axis=-1, keepdims=True) + EPSILON) * norm_gain
    ).astype(jnp.bfloat16)
    projected = (
        jnp.dot(normed, w_qkv, preferred_element_type=jnp.float32)
        .astype(jnp.bfloat16)
        .reshape(my_rows, 3, -1)
    )
    by_head = lax.all_to_all(projected, "tok", split_axis=2, concat_axis=0, tiled=True)
    local_heads = by_head.shape[2] // HD2
    head_queries = by_head[:, 0].reshape(-1, local_heads, HD2)
    view_rows = head_queries.shape[0]
    scale_two = HD2 ** (-0.5)
    second_state = (
        jnp.full((view_rows, local_heads), NEGATIVE, jnp.float32),
        jnp.zeros((view_rows, local_heads), jnp.float32),
        jnp.zeros((view_rows, local_heads, HD2), jnp.float32),
    )
    key_piece = lax.all_gather(by_head[:, 1], "view", axis=0, tiled=True)
    val_piece = lax.all_gather(by_head[:, 2], "view", axis=0, tiled=True)
    keep_key = jnp.ones((key_piece.shape[0],), jnp.bool_)
    second_max, second_total, second_sum = absorb(
        second_state,
        head_queries,
        key_piece.reshape(-1, local_heads, HD2),
        val_piece.reshape(-1, local_heads, HD2),
        keep_key,
        scale_two,
    )
    attn_two = (second_sum / second_total[..., None]).reshape(view_rows, -1).astype(jnp.bfloat16)
    returned = lax.all_to_all(attn_two, "tok", split_axis=0, concat_axis=1, tiled=True)
    wide = returned.astype(jnp.float32)
    unit_rows = (wide * lax.rsqrt(jnp.mean(wide * wide, axis=-1, keepdims=True) + EPSILON)).astype(
        jnp.bfloat16
    )
    result = jnp.dot(unit_rows, w_out, preferred_element_type=jnp.float32)
    return (features[None], result[None])


def solution(mesh):
    return jax.shard_map(
        per_device,
        mesh=mesh,
        in_specs=(
            P("view", "tok", None),
            P("view", "tok", None),
            P("view", "tok", None),
            P("view", None),
            P("view", "tok", None),
            P(),
            P(),
            P(),
            P(),
        ),
        out_specs=(P("view", "tok", None), P("view", "tok", None)),
        check_vma=False,
    )
```

profile of v0, /device:TPU:0, one launch (start us, length us, event | category | flops | bytes accessed | tf_op | source)
XLA Modules:
  0.0 210.0 jit_solution(12965817521366080982)
XLA Ops:
  0.6 0.0 copy-start
  0.6 0.9 fusion.27
  1.6 0.1 broadcast_in_dim.65
  1.7 0.1 broadcast_in_dim.66
  1.7 7.4 %all_gather.16 = bf16[1,128,1024]{2,1,0:T(8,128)(2,1)S(1)} all-gather(bf16[1,32,1024]{2,1,0:T(8,128)(2,1)} %param.9), channel_id=1, replica_groups=mesh['view'=8,'tok'=4] {'tok'}, dimensions={1}, use_global_device_ids=true | all-gather | bytes 327680 | tf_op jit(solution)/shard_map/all_gather | solution.py:34
  9.1 0.2 copy.67
  9.3 32.2 %all_gather.15 = bf16[8,32,1024]{2,1,0:T(8,128)(2,1)S(1)} all-gather(bf16[1,32,1024]{2,1,0:T(8,128)(2,1)} %param.10), channel_id=1, replica_groups=mesh['view'=8,'tok'=4] {'view'}, dimensions={0}, use_global_device_ids=true | all-gather | bytes 589824 | tf_op jit(solution)/shard_map/all_gather | solution.py:42
  41.5 1.7 reshape.138
  43.1 1.8 bitcast_reduce_fusion.1
  44.9 0.0 copy-start.3
  44.9 1.3 copy-done.1
  46.2 0.6 fusion.5
  46.9 0.1 copy.75
  47.0 0.5 broadcast.108
  47.5 0.7 reduce.4
  48.2 0.7 reshape.153
  48.9 3.2 %all-to-all-start.2 = ((f32[4,1,512]{2,1,0:T(1,128)}), f32[4,1,512]{2,1,0:T(1,128)S(1)}, u32[]{:S(2)}, u32[]{:S(2)}) async-start(f32[4,1,512]{2,1,0:T(1,128)} %reshape.153), calls=%async_computation.2 | async-start | bytes 16384 | tf_op jit(solution)/shard_map/all_to_all | solution.py:60
  52.2 31.5 %all_gather.17 = bf16[8,32,1024]{2,1,0:T(8,128)(2,1)S(1)} all-gather(bf16[1,32,1024]{2,1,0:T(8,128)(2,1)S(1)} %copy-done.3), channel_id=1, replica_groups=mesh['view'=8,'tok'=4] {'view'}, dimensions={0}, use_global_device_ids=true | all-gather | bytes 589824 | tf_op jit(solution)/shard_map/all_gather | solution.py:43
  83.7 1.6 reshape.139
  85.4 0.1 copy.72
  85.5 0.7 reduce.6
  86.2 0.7 reshape.151
  86.9 3.2 %all-to-all-start.1 = ((f32[4,1,512]{2,1,0:T(1,128)}), f32[4,1,512]{2,1,0:T(1,128)S(1)}, u32[]{:S(2)}, u32[]{:S(2)}) async-start(f32[4,1,512]{2,1,0:T(1,128)} %reshape.151), calls=%async_computation.1 | async-start | bytes 16384 | tf_op jit(solution)/shard_map/all_to_all | solution.py:59
  90.1 3.6 %convolution_bitcast_fusion = f32[1,128,16,64]{1,3,2,0:T(8,128)} fusion(f32[16,256,128]{2,1,0:T(8,128)} %copy-done.1, bf16[256,16,64]{2,1,0:T(8,128)(2,1)} %reshape.139, f32[128,16]{0,1:T(8,128)S(1)} %get-tuple-element.10, pred[256]{0:T(512)(128)(4,1)S(1)} %broadcast_in_dim.66), kind=kOutput, calls=%fused_computation.13 | convolution fusion | flops 69730304 | bytes 3154176 | tf_op jit(solution)/shard_map/qhk,khd->qhd/dot_general | solution.py:25
  93.7 1.5 copy.71
  95.3 1.4 reshape.149
  96.7 0.0 all-to-all-done.1
  96.7 3.5 %all-to-all-start = ((f32[4,1,32768]{2,1,0:T(1,128)}), f32[4,1,32768]{2,1,0:T(1,128)S(1)}, u32[]{:S(2)}, u32[]{:S(2)}) async-start(f32[4,1,32768]{2,1,0:T(1,128)} %reshape.149), calls=%async_computation | async-start | bytes 1048576 | tf_op jit(solution)/shard_map/all_to_all | solution.py:58
  100.2 0.6 reduce.5
  100.8 0.2 reshape.154
  100.9 0.6 reduce.7
  101.5 0.2 reshape.152
  101.7 7.3 %all-to-all-done = f32[4,1,32768]{2,1,0:T(1,128)S(1)} async-done(((f32[4,1,32768]{2,1,0:T(1,128)}), f32[4,1,32768]{2,1,0:T(1,128)S(1)}, u32[]{:S(2)}, u32[]{:S(2)}) %all-to-all-start) | async-done | bytes 524320 | tf_op jit(solution)/shard_map/all_to_all | solution.py:58
  109.0 2.8 %reduce.3 = f32[4,32768]{1,0:T(4,128)} reduce(f32[4,1,32768]{2,1,0:T(1,128)S(1)} %all-to-all-done, f32[]{:T(128)} %broadcast.108), dimensions={1}, to_apply=%all_to_all.23.reduce_sub_computation | reduce | bytes 1048580 | tf_op jit(solution)/shard_map/all_to_all | solution.py:58
  111.8 1.6 reshape.150
  113.4 0.3 multiply_reduce_fusion
  113.8 0.6 multiply_reduce_fusion.1
  114.4 0.1 div.44
  114.5 0.6 multiply_reduce_fusion.2
  115.2 4.0 %convolution_convert_fusion = bf16[32,3072]{1,0:T(8,128)(2,1)S(1)} fusion(bf16[1024,3072]{1,0:T(8,128)(2,1)} %param.16, f32[32,1024]{1,0:T(8,128)S(1)} %get-tuple-element.14, f32[1024]{0:T(1024)S(1)} %copy-done.5, f32[32]{0:T(128)S(1)} %add_rsqrt_fusion.1), kind=kOutput, calls=%fused_computation | convolution fusion | flops 201523200 | bytes 6623360 | tf_op jit(solution)/shard_map/dot_general | solution.py:76
  119.2 1.0 reshape.140
  120.1 1.8 copy.76
  121.9 1.4 reshape.155
  123.4 3.5 %all-to-all-start.3 = ((bf16[4,2,12288]{2,1,0:T(2,128)(2,1)}), bf16[4,2,12288]{2,1,0:T(2,128)(2,1)S(1)}, u32[]{:S(2)}, u32[]{:S(2)}) async-start(bf16[4,2,12288]{2,1,0:T(2,128)(2,1)} %reshape.155), calls=%async_computation.3 | async-start | bytes 393216 | tf_op jit(solution)/shard_map/all_to_all | solution.py:80
  126.9 0.1 div.42
  127.0 5.0 %all-to-all-done.3 = bf16[4,2,12288]{2,1,0:T(2,128)(2,1)S(1)} async-done(((bf16[4,2,12288]{2,1,0:T(2,128)(2,1)}), bf16[4,2,12288]{2,1,0:T(2,128)(2,1)S(1)}, u32[]{:S(2)}, u32[]{:S(2)}) %all-to-all-start.3) | async-done | bytes 196640 | tf_op jit(solution)/shard_map/all_to_all | solution.py:80
  132.0 0.7 reshape.156
  132.7 0.5 copy.78
  133.3 31.4 %all-gather = bf16[1024,1,256]{2,0,1:T(8,128)(2,1)S(1)} all-gather(bf16[128,1,256]{2,0,1:T(8,128)(2,1)S(1)} %get-tuple-element.8), channel_id=2, replica_groups=mesh['view'=8,'tok'=4] {'view'}, dimensions={0}, use_global_device_ids=true | all-gather | bytes 589824 | tf_op jit(solution)/shard_map/all_gather | solution.py:91
  164.7 1.0 copy.79
  165.7 31.2 %all-gather.1 = bf16[1024,1,256]{2,0,1:T(8,128)(2,1)S(1)} all-gather(bf16[128,1,256]{2,0,1:T(8,128)(2,1)S(1)} %get-tuple-element.7), channel_id=3, replica_groups=mesh['view'=8,'tok'=4] {'view'}, dimensions={0}, use_global_device_ids=true | all-gather | bytes 589824 | tf_op jit(solution)/shard_map/all_gather | solution.py:90
  196.9 0.2 copy.80
  197.1 0.1 copy.81
  197.2 0.5 bitcast_reduce_fusion
  197.8 0.4 fusion.3
  198.1 0.1 copy-done.2
  198.2 0.5 fusion.8
  198.8 0.1 copy.83
  198.9 0.8 convert_element_type.52
  199.7 3.3 %all-to-all-start.4 = ((bf16[4,32,256]{2,1,0:T(8,128)(2,1)}), bf16[4,32,256]{2,1,0:T(8,128)(2,1)S(1)}, u32[]{:S(2)}, u32[]{:S(2)}) async-start(bf16[4,32,256]{2,1,0:T(8,128)(2,1)} %convert_element_type.52), calls=%async_computation.4 | async-start | bytes 131072 | tf_op jit(solution)/shard_map/all_to_all | solution.py:102
  203.0 0.7 broadcast_multiply_fusion
  203.7 3.4 %all-to-all-done.4 = bf16[4,32,256]{2,1,0:T(8,128)(2,1)S(1)} async-done(((bf16[4,32,256]{2,1,0:T(8,128)(2,1)}), bf16[4,32,256]{2,1,0:T(8,128)(2,1)S(1)}, u32[]{:S(2)}, u32[]{:S(2)}) %all-to-all-start.4) | async-done | bytes 65568 | tf_op jit(solution)/shard_map/all_to_all | solution.py:102
  207.1 0.1 fusion.22
  207.2 2.8 %convolution_bitcast_fusion.1 = f32[1,32,1024]{2,1,0:T(8,128)} fusion(bf16[1024,1024]{1,0:T(8,128)(2,1)} %param.17, f32[32,1024]{1,0:T(8,128)S(1)} %bitcast.80, f32[32]{0:T(128)S(1)} %add_rsqrt_fusion), kind=kOutput, calls=%fused_computation.14 | convolution fusion | flops 67174400 | bytes 2359424 | tf_op jit(solution)/shard_map/dot_general | solution.py:107
  (20 shorter events, 0.1 us)
Async XLA Ops:
  0.6 113.9 %copy-start = (bf16[1024,1024]{1,0:T(8,128)(2,1)S(1)}, bf16[1024,1024]{1,0:T(8,128)(2,1)}, u32[]{:S(2)}) copy-start(bf16[1024,1024]{1,0:T(8,128)(2,1)} %param.14) | copy-start | bytes 6291460
  44.9 1.4 copy-start.1
  44.9 7.3 %copy-start.3 = (bf16[1,32,1024]{2,1,0:T(8,128)(2,1)S(1)}, bf16[1,32,1024]{2,1,0:T(8,128)(2,1)}, u32[]{:S(2)}) copy-start(bf16[1,32,1024]{2,1,0:T(8,128)(2,1)} %param.11) | copy-start | bytes 196612
  48.9 38.0 %all-to-all-start.2 = ((f32[4,1,512]{2,1,0:T(1,128)}), f32[4,1,512]{2,1,0:T(1,128)S(1)}, u32[]{:S(2)}, u32[]{:S(2)}) async-start(f32[4,1,512]{2,1,0:T(1,128)} %reshape.153), calls=%async_computation.2 | async-start | bytes 16384 | tf_op jit(solution)/shard_map/all_to_all | solution.py:60
  86.9 9.8 %all-to-all-start.1 = ((f32[4,1,512]{2,1,0:T(1,128)}), f32[4,1,512]{2,1,0:T(1,128)S(1)}, u32[]{:S(2)}, u32[]{:S(2)}) async-start(f32[4,1,512]{2,1,0:T(1,128)} %reshape.151), calls=%async_computation.1 | async-start | bytes 16384 | tf_op jit(solution)/shard_map/all_to_all | solution.py:59
  96.7 12.3 %all-to-all-start = ((f32[4,1,32768]{2,1,0:T(1,128)}), f32[4,1,32768]{2,1,0:T(1,128)S(1)}, u32[]{:S(2)}, u32[]{:S(2)}) async-start(f32[4,1,32768]{2,1,0:T(1,128)} %reshape.149), calls=%async_computation | async-start | bytes 1048576 | tf_op jit(solution)/shard_map/all_to_all | solution.py:58
  111.8 2.7 %copy-start.4 = (bf16[1,32,1024]{2,1,0:T(8,128)(2,1)S(1)}, bf16[1,32,1024]{2,1,0:T(8,128)(2,1)}, u32[]{:S(2)}) copy-start(bf16[1,32,1024]{2,1,0:T(8,128)(2,1)} %param.13) | copy-start | bytes 196612
  113.4 1.7 copy-start.5
  123.4 8.7 %all-to-all-start.3 = ((bf16[4,2,12288]{2,1,0:T(2,128)(2,1)}), bf16[4,2,12288]{2,1,0:T(2,128)(2,1)S(1)}, u32[]{:S(2)}, u32[]{:S(2)}) async-start(bf16[4,2,12288]{2,1,0:T(2,128)(2,1)} %reshape.155), calls=%async_computation.3 | async-start | bytes 393216 | tf_op jit(solution)/shard_map/all_to_all | solution.py:80
  197.2 1.0 copy-start.2
  199.7 7.4 %all-to-all-start.4 = ((bf16[4,32,256]{2,1,0:T(8,128)(2,1)}), bf16[4,32,256]{2,1,0:T(8,128)(2,1)S(1)}, u32[]{:S(2)}, u32[]{:S(2)}) async-start(bf16[4,32,256]{2,1,0:T(8,128)(2,1)} %convert_element_type.52), calls=%async_computation.4 | async-start | bytes 131072 | tf_op jit(solution)/shard_map/all_to_all | solution.py:102
where the time goes:
time: 211 us; the launch traced here: 210 us
  blocking collectives  134 us (64%)
  local copies, waits for them, and re-layouts  19.9 us (9%)
  starting transfers between devices  16.8 us (8%)
  waiting for transfers between devices  15.6 us (7%)
  matrix products  13.8 us (7%)
  other arithmetic  9.23 us (4%)
    all_gather x1, blocking collectives, per_device(): key_piece = lax.all_gather(k1, 'view', axis=0, tiled=True)  32.2 us
    all_gather x1, blocking collectives, per_device(): val_piece = lax.all_gather(v1, 'view', axis=0, tiled=True)  31.5 us
    all_gather x1, blocking collectives, per_device(): val_piece = lax.all_gather(by_head[:, 2], 'view', axis=0, tiled=True)  31.4 us
    all_gather x1, blocking collectives, per_device(): key_piece = lax.all_gather(by_head[:, 1], 'view', axis=0, tiled=True)  31.2 us
    unnamed x20, local copies, waits for them, and re-layouts  8.3 us
    all_gather x1, blocking collectives, per_device(): lax.all_gather(q1, 'tok', axis=1, tiled=True)[0].reshape(-1, H1, HD1)  7.39 us
    all_to_all x1, waiting for transfers between devices, per_device(): lax.all_to_all(weighted[None], 'tok', split_axis=1, concat_axis=0, tiled=...  7.26 us
    all_to_all x1, waiting for transfers between devices, per_device(): lax.all_to_all(projected, 'tok', split_axis=2, concat_axis=0, tiled=True)  4.99 us
  transfers between devices with their start and end apart: 5, of which 3 were waited for; matrix products, arithmetic and copies ran while one was open for 6% of the time, Pallas kernels for 0%

commit v1 on v0

--- a/solution.py
+++ b/solution.py
@@ -1,15 +1,18 @@
+import functools
+import math
+
 import jax
 import jax.numpy as jnp
 from jax import lax
-from jax.sharding import PartitionSpec as P
-
-H1 = 16
-HD1 = 64
-HD2 = 64
-
-
+from jax.experimental import pallas as pl
+from jax.experimental.pallas import tpu as pltpu
+from jax.sharding import Mesh, PartitionSpec as P
+
+HEADS = 16
+HD = 64
 EPSILON = 1e-06
 NEGATIVE = -1e30
+VMEM = pl.BlockSpec(memory_space=pltpu.VMEM)
 
 
 def absorb(running, queries, key_piece, val_piece, keep_key, factor_scale):
@@ -28,17 +31,17 @@
     return (new_max, row_total, weighted)
 
 
-def per_device(q1, k1, v1, nbr, x2, w_view_out, norm_gain, w_qkv, w_out):
+def general(q1, k1, v1, nbr, x2, w_view_out, norm_gain, w_qkv, w_out):
     own_view = lax.axis_index("view")
     wanted = nbr[0]
-    queries = lax.all_gather(q1, "tok", axis=1, tiled=True)[0].reshape(-1, H1, HD1)
+    queries = lax.all_gather(q1, "tok", axis=1, tiled=True)[0].reshape(-1, HEADS, HD)
     query_rows = queries.shape[0]
     start_state = (
-        jnp.full((query_rows, H1), NEGATIVE, jnp.float32),
-        jnp.zeros((query_rows, H1), jnp.float32),
-        jnp.zeros((query_rows, H1, HD1), jnp.float32),
-    )
-    scale_one = HD1 ** (-0.5)
+        jnp.full((query_rows, HEADS), NEGATIVE, jnp.float32),
+        jnp.zeros((query_rows, HEADS), jnp.float32),
+        jnp.zeros((query_rows, HEADS, HD), jnp.float32),
+    )
+    scale = HD ** (-0.5)
     key_piece = lax.all_gather(k1, "view", axis=0, tiled=True)
     val_piece = lax.all_gather(v1, "view", axis=0, tiled=True)
     view_ids = jnp.arange(key_piece.shape[0], dtype=jnp.int32)
@@ -47,10 +50,10 @@
     running_max, row_total, weighted = absorb(
         start_state,
         queries,
-        key_piece.reshape(-1, H1, HD1),
-        val_piece.reshape(-1, H1, HD1),
+        key_piece.reshape(-1, HEADS, HD),
+        val_piece.reshape(-1, HEADS, HD),
         keep_key,
-        scale_one,
+        scale,
     )
     tok_devs = lax.axis_size("tok")
     my_rows = query_rows // tok_devs
@@ -78,14 +81,13 @@
         .reshape(my_rows, 3, -1)
     )
     by_head = lax.all_to_all(projected, "tok", split_axis=2, concat_axis=0, tiled=True)
-    local_heads = by_head.shape[2] // HD2
-    head_queries = by_head[:, 0].reshape(-1, local_heads, HD2)
+    local_heads = by_head.shape[2] // HD
+    head_queries = by_head[:, 0].reshape(-1, local_heads, HD)
     view_rows = head_queries.shape[0]
-    scale_two = HD2 ** (-0.5)
     second_state = (
         jnp.full((view_rows, local_heads), NEGATIVE, jnp.float32),
         jnp.zeros((view_rows, local_heads), jnp.float32),
-        jnp.zeros((view_rows, local_heads, HD2), jnp.float32),
+        jnp.zeros((view_rows, local_heads, HD), jnp.float32),
     )
     key_piece = lax.all_gather(by_head[:, 1], "view", axis=0, tiled=True)
     val_piece = lax.all_gather(by_head[:, 2], "view", axis=0, tiled=True)
@@ -93,10 +95,10 @@
     second_max, second_total, second_sum = absorb(
         second_state,
         head_queries,
-        key_piece.reshape(-1, local_heads, HD2),
-        val_piece.reshape(-1, local_heads, HD2),
+        key_piece.reshape(-1, local_heads, HD),
+        val_piece.reshape(-1, local_heads, HD),
         keep_key,
-        scale_two,
+        scale,
     )
     attn_two = (second_sum / second_total[..., None]).reshape(view_rows, -1).astype(jnp.bfloat16)
     returned = lax.all_to_all(attn_two, "tok", split_axis=0, concat_axis=1, tiled=True)
@@ -108,21 +110,123 @@
     return (features[None], result[None])
 
 
+def pack_heads(out_ref, q, k, v):
+    rows = q.shape[0]
+    half = rows // 2
+    for h in range(HEADS):
+        cols = slice(h * HD, (h + 1) * HD)
+        out_ref[h, 0:rows, :] = jnp.concatenate([k[:, cols], v[:, cols]], axis=-1)
+        out_ref[h, rows : rows + half, :] = jnp.concatenate([q[:half, cols], q[half:, cols]], axis=-1)
+
+
+def unpack_rows(got_ref):
+    pieces = [got_ref[h].astype(jnp.float32) for h in range(HEADS)]
+    top = jnp.concatenate([p[:, :HD] for p in pieces], axis=-1)
+    low = jnp.concatenate([p[:, HD:] for p in pieces], axis=-1)
+    return jnp.concatenate([top, low], axis=0)
+
+
+def unit(x):
+    return x * lax.rsqrt(jnp.mean(x * x, axis=-1, keepdims=True) + EPSILON)
+
+
+def pack_kernel(q_ref, k_ref, v_ref, out_ref):
+    pack_heads(out_ref, q_ref[0], k_ref[0], v_ref[0])
+
+
+def attend_kernel(mine_ref, other_ref, out_ref):
+    sources, lines, _ = mine_ref.shape
+    rows = lines * 2 // 3
+    half = rows // 2
+    kv = jnp.concatenate(
+        [mine_ref[:, 0:rows, :].reshape(-1, 2 * HD), other_ref[:, 0:rows, :].reshape(-1, 2 * HD)], axis=0
+    )
+    keys = kv[:, :HD]
+    vals = kv[:, HD:]
+    step = max(1, 128 // half)
+    for s in range(0, sources, step):
+        packed = mine_ref[s : s + step, rows:lines, :].reshape(-1, 2 * HD)
+        queries = jnp.concatenate([packed[:, :HD], packed[:, HD:]], axis=0)
+        scores = lax.dot_general(
+            queries, keys, (((1,), (1,)), ((), ())), preferred_element_type=jnp.float32
+        ) * (HD ** (-0.5))
+        peak = jnp.max(scores, axis=-1, keepdims=True)
+        weights = jnp.exp(scores - peak)
+        total = jnp.sum(weights, axis=-1, keepdims=True)
+        summed = jnp.dot(weights.astype(jnp.bfloat16), vals, preferred_element_type=jnp.float32)
+        attn = (summed / total).astype(jnp.bfloat16)
+        n = attn.shape[0] // 2
+        out_ref[s : s + step] = jnp.concatenate([attn[:n], attn[n:]], axis=-1).reshape(step, half, 2 * HD)
+
+
+def middle_kernel(got_ref, x2_ref, wv_ref, gain_ref, wqkv_ref, feats_ref, out_ref):
+    feats = unit(unpack_rows(got_ref))
+    feats_ref[0] = feats
+    hidden = x2_ref[0].astype(jnp.float32) + jnp.dot(
+        feats.astype(jnp.bfloat16), wv_ref[...], preferred_element_type=jnp.float32
+    )
+    normed = (unit(hidden) * gain_ref[...]).astype(jnp.bfloat16)
+    projected = jnp.dot(normed, wqkv_ref[...], preferred_element_type=jnp.float32).astype(jnp.bfloat16)
+    width = HEADS * HD
+    pack_heads(out_ref, projected[:, :width], projected[:, width : 2 * width], projected[:, 2 * width :])
+
+
+def last_kernel(got_ref, wout_ref, out_ref):
+    rows = unit(unpack_rows(got_ref)).astype(jnp.bfloat16)
+    out_ref[0] = jnp.dot(rows, wout_ref[...], preferred_element_type=jnp.float32)
+
+
+def call(body, outs, args, limit=48 << 20):
+    return pl.pallas_call(
+        body,
+        out_shape=outs,
+        in_specs=[VMEM] * len(args),
+        out_specs=jax.tree.map(lambda _: VMEM, outs),
+        compiler_params=pltpu.CompilerParams(vmem_limit_bytes=limit),
+    )(*args)
+
+
+def by_heads(q1, k1, v1, nbr, x2, w_view_out, norm_gain, w_qkv, w_out):
+    rows = q1.shape[1]
+    lines = rows * 3 // 2
+    packed_type = jax.ShapeDtypeStruct((HEADS, lines, 2 * HD), jnp.bfloat16)
+    half_type = jax.ShapeDtypeStruct((HEADS, rows // 2, 2 * HD), jnp.bfloat16)
+    wide_type = jax.ShapeDtypeStruct((1, rows, HEADS * HD), jnp.float32)
+    group = ("view", "chip")
+
+    def attention(packed):
+        mine = lax.all_to_all(packed, group, split_axis=0, concat_axis=0, tiled=True)
+        cores = lax.axis_size("core")
+        other = lax.ppermute(mine, "core", [(i, (i + 1) % cores) for i in range(cores)])
+        half = call(attend_kernel, half_type, (mine, other))
+        return lax.all_to_all(half, group, split_axis=0, concat_axis=0, tiled=True)
+
+    got = attention(call(pack_kernel, packed_type, (q1, k1, v1)))
+    feats, packed = call(
+        middle_kernel, (wide_type, packed_type), (got, x2, w_view_out, norm_gain[None], w_qkv)
+    )
+    result = call(last_kernel, wide_type, (attention(packed), w_out))
+    return feats, result
+
+
 def solution(mesh):
-    return jax.shard_map(
-        per_device,
-        mesh=mesh,
-        in_specs=(
-            P("view", "tok", None),
-            P("view", "tok", None),
-            P("view", "tok", None),
-            P("view", None),
-            P("view", "tok", None),
-            P(),
-            P(),
-            P(),
-            P(),
-        ),
-        out_specs=(P("view", "tok", None), P("view", "tok", None)),
-        check_vma=False,
-    )
+    views, toks = mesh.devices.shape
+    fine = Mesh(mesh.devices.reshape(views, toks // 2, 2), ("view", "chip", "core"))
+
+    def run(q1, k1, v1, nbr, x2, w_view_out, norm_gain, w_qkv, w_out):
+        every_view = q1.shape[0] == nbr.shape[1] + 1
+        one_head = views * (toks // 2) == HEADS
+        if every_view and one_head:
+            body, grid, tok = by_heads, fine, ("chip", "core")
+        else:
+            body, grid, tok = general, mesh, "tok"
+        split = P("view", tok, None)
+        return jax.shard_map(
+            body,
+            mesh=grid,
+            in_specs=(split, split, split, P("view", None), split, P(), P(), P(), P()),
+            out_specs=(split, split),
+            check_vma=False,
+        )(q1, k1, v1, nbr, x2, w_view_out, norm_gain, w_qkv, w_out)
+
+    return run

time: 211 us -> 67.1 us (0.32)
  blocking collectives: 134 us -> 48.6 us
  starting transfers between devices: 16.8 us -> 0.01 us
  local copies, waits for them, and re-layouts: 19.9 us -> 5.63 us
  matrix products: 13.8 us -> 0 us
  waiting for transfers between devices: 15.6 us -> 2.88 us
  other arithmetic: 9.23 us -> 0 us
  Pallas kernels: 0 us -> 8.77 us
    all_gather x5 -> x0, blocking collectives: 134 us -> none  [the longest x1 32.2 us: per_device(): key_piece = lax.all_gather(k1, 'view', axis=0, tiled=True)]
    all_to_all x0 -> x4, blocking collectives: none -> 48.6 us  [the longest x2 27.4 us: attention(): lax.all_to_all(packed, group, split_axis=0, concat_axis=0, tiled=True)]
    all_to_all x5 -> x0, starting transfers between devices: 16.8 us -> none  [the longest x1 3.54 us: per_device(): lax.all_to_all(projected, 'tok', split_axis=2, concat_axis=0, tiled=True)]
    all_to_all x5 -> x0, waiting for transfers between devices: 15.6 us -> none  [the longest x1 7.26 us: per_device(): lax.all_to_all(weighted[None], 'tok', split_axis=1, concat_axis=0, tiled=...]
    dot_general x7 -> x0, matrix products: 13.8 us -> none  [the longest x2 4.11 us: absorb(): jnp.einsum('qhk,khd->qhd', weights.astype(jnp.bfloat16), val_piece, prefe...]
    pallas_call x0 -> x5, Pallas kernels: none -> 8.77 us  [call(): pl.pallas_call(body, out_shape=outs, in_specs=[VMEM] * len(args), out_spe...]
    reshape x4 -> x0, local copies, waits for them, and re-layouts: 6.04 us -> none  [the longest x2 2.74 us: per_device(): projected = jnp.dot(normed, w_qkv, preferred_element_type=jnp.float32).as...]
    all_to_all x3 -> x0, other arithmetic: 4.01 us -> none  [the longest x1 2.84 us: per_device(): lax.all_to_all(weighted[None], 'tok', split_axis=1, concat_axis=0, tiled=...]
  transfers between devices with their start and end apart: 5 -> 2, of which waited for: 3 -> 2; matrix products, arithmetic and copies ran while one was open for 6% -> 0% of each run, Pallas kernels for 0% -> 0%
where the time goes in v1:
time: 67.1 us; the launch traced here: 66.6 us
  blocking collectives  48.6 us (72%)
  Pallas kernels  8.77 us (13%)
  local copies, waits for them, and re-layouts  5.63 us (8%)
  waiting for transfers between devices  2.88 us (4%)
    all_to_all x2, blocking collectives, attention(): lax.all_to_all(packed, group, split_axis=0, concat_axis=0, tiled=True)  27.4 us
    all_to_all x2, blocking collectives, attention(): return lax.all_to_all(half, group, split_axis=0, concat_axis=0, tiled=True)  21.2 us
    pallas_call x5, Pallas kernels, call(): pl.pallas_call(body, out_shape=outs, in_specs=[VMEM] * len(args), out_spe...  8.77 us
    unnamed x14, local copies, waits for them, and re-layouts  5.63 us
    ppermute x2, waiting for transfers between devices, attention(): lax.ppermute(mine, 'core', [(i, (i + 1) % cores) for i in range(cores)])  2.88 us
  transfers between devices with their start and end apart: 2, of which 2 were waited for; matrix products, arithmetic and copies ran while one was open for 0% of the time, Pallas kernels for 0%

profile of v1, /device:TPU:0, one launch (start us, length us, event | category | flops | bytes accessed | tf_op | source)
XLA Modules:
  0.0 66.6 jit_solution(10157494563497956543)
XLA Ops:
  0.6 0.0 copy-start.3
  0.6 0.8 %copy-done.3 = bf16[1,32,1024]{2,1,0:T(8,128)(2,1)S(1)} copy-done((bf16[1,32,1024]{2,1,0:T(8,128)(2,1)S(1)}, bf16[1,32,1024]{2,1,0:T(8,128)(2,1)}, u32[]{:S(2)}) %copy-start.3) | copy-done | bytes 65560
  1.5 0.0 copy-start.4
  1.5 0.8 %copy-done.4 = bf16[1,32,1024]{2,1,0:T(8,128)(2,1)S(1)} copy-done((bf16[1,32,1024]{2,1,0:T(8,128)(2,1)S(1)}, bf16[1,32,1024]{2,1,0:T(8,128)(2,1)}, u32[]{:S(2)}) %copy-start.4) | copy-done | bytes 65560
  2.3 0.0 copy-start.5
  2.3 0.8 %copy-done.5 = bf16[1,32,1024]{2,1,0:T(8,128)(2,1)S(1)} copy-done((bf16[1,32,1024]{2,1,0:T(8,128)(2,1)S(1)}, bf16[1,32,1024]{2,1,0:T(8,128)(2,1)}, u32[]{:S(2)}) %copy-start.5) | copy-done | bytes 65560
  3.2 0.1 shard_map.95
  3.3 16.8 %all_to_all.20.mine_ref = bf16[16,48,128]{2,1,0:T(8,128)(2,1)S(1)} all-to-all(bf16[16,48,128]{2,1,0:T(8,128)(2,1)S(1)} %shard_map.95), channel_id=1, replica_groups=mesh['view'=8,'chip'=2,'core'=2] {'view','chip'}, dimensions={0} | all-to-all | bytes 393216 | tf_op jit(solution)/shard_map/all_to_all | solution.py:198
  20.0 0.0 collective-permute-start
  20.0 1.4 %collective-permute-done.other_ref = bf16[16,48,128]{2,1,0:T(8,128)(2,1)S(1)} collective-permute-done((bf16[16,48,128]{2,1,0:T(8,128)(2,1)S(1)}, bf16[16,48,128]{2,1,0:T(8,128)(2,1)S(1)}, u32[]{:S(2)}, u32[]{:S(2)}) %collective-permute-start) | collective-permute-done | bytes 196640 | tf_op jit(solution)/shard_map/ppermute | solution.py:200
  21.5 1.3 %shard_map.96 = bf16[16,16,128]{2,1,0:T(8,128)(2,1)S(1)} custom-call(bf16[16,48,128]{2,1,0:T(8,128)(2,1)S(1)} %all_to_all.20.mine_ref, bf16[16,48,128]{2,1,0:T(8,128)(2,1)S(1)} %collective-permute-done.other_ref), custom_call_target="tpu_custom_call" | custom-call | tf_op jit(solution)/shard_map/pallas_call | solution.py:180
  22.7 10.7 %all_to_all.21.got_ref = bf16[16,16,128]{2,1,0:T(8,128)(2,1)S(1)} all-to-all(bf16[16,16,128]{2,1,0:T(8,128)(2,1)S(1)} %shard_map.96), channel_id=1, replica_groups=mesh['view'=8,'chip'=2,'core'=2] {'view','chip'}, dimensions={0} | all-to-all | bytes 131072 | tf_op jit(solution)/shard_map/all_to_all | solution.py:202
  33.4 0.0 copy-start.1
  33.4 1.6 %copy-done.1 = bf16[1024,1024]{1,0:T(8,128)(2,1)S(1)} copy-done((bf16[1024,1024]{1,0:T(8,128)(2,1)S(1)}, bf16[1024,1024]{1,0:T(8,128)(2,1)}, u32[]{:S(2)}) %copy-start.1) | copy-done | bytes 2097176
  35.0 0.0 copy-start.2
  35.0 0.8 %copy-done.2 = bf16[1,32,1024]{2,1,0:T(8,128)(2,1)S(1)} copy-done((bf16[1,32,1024]{2,1,0:T(8,128)(2,1)S(1)}, bf16[1,32,1024]{2,1,0:T(8,128)(2,1)}, u32[]{:S(2)}) %copy-start.2) | copy-done | bytes 65560
  35.9 0.0 copy-start.6
  35.9 0.7 %copy-done.6 = f32[1024]{0:T(1024)S(1)} copy-done((f32[1024]{0:T(1024)S(1)}, f32[1024]{0:T(1024)}, u32[]{:S(2)}) %copy-start.6) | copy-done | bytes 4120
  36.6 0.0 copy-start
  36.6 4.9 %shard_map.97 = (f32[1,32,1024]{2,1,0:T(8,128)}, bf16[16,48,128]{2,1,0:T(8,128)(2,1)S(1)}) custom-call(bf16[16,16,128]{2,1,0:T(8,128)(2,1)S(1)} %all_to_all.21.got_ref, bf16[1,32,1024]{2,1,0:T(8,128)(2,1)S(1)} %copy-done.2, bf16[1024,1024]{1,0:T(8,128)(2,1)S(1)} %copy-done.1, f32[1,1024]{1,0:T(1,128)S(1)} %bitcast.1, bf16[1024,3072]{1,0:T(8,128)(2,1)} %wqkv_ref.1), custom_call_target="tpu_custom_call" | custom-call | tf_op jit(solution)/shard_map/pallas_call | solution.py:180
  41.4 10.7 %all_to_all.22.mine_ref = bf16[16,48,128]{2,1,0:T(8,128)(2,1)S(1)} all-to-all(bf16[16,48,128]{2,1,0:T(8,128)(2,1)S(1)} %get-tuple-element.5), channel_id=1, replica_groups=mesh['view'=8,'chip'=2,'core'=2] {'view','chip'}, dimensions={0} | all-to-all | bytes 393216 | tf_op jit(solution)/shard_map/all_to_all | solution.py:198
  52.1 0.0 collective-permute-start.1
  52.1 1.4 %collective-permute-done.1.other_ref = bf16[16,48,128]{2,1,0:T(8,128)(2,1)S(1)} collective-permute-done((bf16[16,48,128]{2,1,0:T(8,128)(2,1)S(1)}, bf16[16,48,128]{2,1,0:T(8,128)(2,1)S(1)}, u32[]{:S(2)}, u32[]{:S(2)}) %collective-permute-start.1) | collective-permute-done | bytes 196640 | tf_op jit(solution)/shard_map/ppermute | solution.py:200
  53.6 1.3 %shard_map.98 = bf16[16,16,128]{2,1,0:T(8,128)(2,1)S(1)} custom-call(bf16[16,48,128]{2,1,0:T(8,128)(2,1)S(1)} %all_to_all.22.mine_ref, bf16[16,48,128]{2,1,0:T(8,128)(2,1)S(1)} %collective-permute-done.1.other_ref), custom_call_target="tpu_custom_call" | custom-call | tf_op jit(solution)/shard_map/pallas_call | solution.py:180
  54.8 10.5 %all_to_all.23.got_ref = bf16[16,16,128]{2,1,0:T(8,128)(2,1)S(1)} all-to-all(bf16[16,16,128]{2,1,0:T(8,128)(2,1)S(1)} %shard_map.98), channel_id=1, replica_groups=mesh['view'=8,'chip'=2,'core'=2] {'view','chip'}, dimensions={0} | all-to-all | bytes 131072 | tf_op jit(solution)/shard_map/all_to_all | solution.py:202
  65.3 0.0 copy-done
  65.3 1.3 %shard_map.99 = f32[1,32,1024]{2,1,0:T(8,128)} custom-call(bf16[16,16,128]{2,1,0:T(8,128)(2,1)S(1)} %all_to_all.23.got_ref, bf16[1024,1024]{1,0:T(8,128)(2,1)S(1)} %copy-done), custom_call_target="tpu_custom_call" | custom-call | tf_op jit(solution)/shard_map/pallas_call | solution.py:180
Async XLA Ops:
  0.6 0.8 %copy-start.3 = (bf16[1,32,1024]{2,1,0:T(8,128)(2,1)S(1)}, bf16[1,32,1024]{2,1,0:T(8,128)(2,1)}, u32[]{:S(2)}) copy-start(bf16[1,32,1024]{2,1,0:T(8,128)(2,1)} %q_ref.1) | copy-start | bytes 196612
  1.5 0.8 %copy-start.4 = (bf16[1,32,1024]{2,1,0:T(8,128)(2,1)S(1)}, bf16[1,32,1024]{2,1,0:T(8,128)(2,1)}, u32[]{:S(2)}) copy-start(bf16[1,32,1024]{2,1,0:T(8,128)(2,1)} %k_ref.1) | copy-start | bytes 196612
  2.3 0.8 %copy-start.5 = (bf16[1,32,1024]{2,1,0:T(8,128)(2,1)S(1)}, bf16[1,32,1024]{2,1,0:T(8,128)(2,1)}, u32[]{:S(2)}) copy-start(bf16[1,32,1024]{2,1,0:T(8,128)(2,1)} %v_ref.1) | copy-start | bytes 196612
  20.0 1.4 %collective-permute-start = (bf16[16,48,128]{2,1,0:T(8,128)(2,1)S(1)}, bf16[16,48,128]{2,1,0:T(8,128)(2,1)S(1)}, u32[]{:S(2)}, u32[]{:S(2)}) collective-permute-start(bf16[16,48,128]{2,1,0:T(8,128)(2,1)S(1)} %all_to_all.20.mine_ref), channel_id=1, source_target_pairs={{0,1},{1,0},{2,3},{3,2},{4,5},{5,4},{6,7},{7,6},{8,9},{9,8},{10,11... | collective-permute-start | bytes 589832 | tf_op jit(solution)/shard_map/ppermute | solution.py:200
  33.4 1.6 %copy-start.1 = (bf16[1024,1024]{1,0:T(8,128)(2,1)S(1)}, bf16[1024,1024]{1,0:T(8,128)(2,1)}, u32[]{:S(2)}) copy-start(bf16[1024,1024]{1,0:T(8,128)(2,1)} %wv_ref.1) | copy-start | bytes 6291460
  35.0 0.8 %copy-start.2 = (bf16[1,32,1024]{2,1,0:T(8,128)(2,1)S(1)}, bf16[1,32,1024]{2,1,0:T(8,128)(2,1)}, u32[]{:S(2)}) copy-start(bf16[1,32,1024]{2,1,0:T(8,128)(2,1)} %x2_ref.1) | copy-start | bytes 196612
  35.9 0.7 %copy-start.6 = (f32[1024]{0:T(1024)S(1)}, f32[1024]{0:T(1024)}, u32[]{:S(2)}) copy-start(f32[1024]{0:T(1024)} %param.14) | copy-start | bytes 12292
  36.6 28.8 %copy-start = (bf16[1024,1024]{1,0:T(8,128)(2,1)S(1)}, bf16[1024,1024]{1,0:T(8,128)(2,1)}, u32[]{:S(2)}) copy-start(bf16[1024,1024]{1,0:T(8,128)(2,1)} %wout_ref.1) | copy-start | bytes 6291460
  52.1 1.4 %collective-permute-start.1 = (bf16[16,48,128]{2,1,0:T(8,128)(2,1)S(1)}, bf16[16,48,128]{2,1,0:T(8,128)(2,1)S(1)}, u32[]{:S(2)}, u32[]{:S(2)}) collective-permute-start(bf16[16,48,128]{2,1,0:T(8,128)(2,1)S(1)} %all_to_all.22.mine_ref), channel_id=1, source_target_pairs={{0,1},{1,0},{2,3},{3,2},{4,5},{5,4},{6,7},{7,6},{8,9},{9,8},{10,11... | collective-permute-start | bytes 589832 | tf_op jit(solution)/shard_map/ppermute | solution.py:200

commit v2 on v1

--- a/solution.py
+++ b/solution.py
@@ -1,6 +1,3 @@
-import functools
-import math
-
 import jax
 import jax.numpy as jnp
 from jax import lax
@@ -110,17 +107,30 @@
     return (features[None], result[None])
 
 
-def pack_heads(out_ref, q, k, v):
+GROUP = ("view", "chip")
+
+
+def place():
+    return lax.axis_index("view") * lax.axis_size("chip") + lax.axis_index("chip")
+
+
+def pack_heads(packed_ref, out_refs, q, k, v):
     rows = q.shape[0]
     half = rows // 2
     for h in range(HEADS):
         cols = slice(h * HD, (h + 1) * HD)
-        out_ref[h, 0:rows, :] = jnp.concatenate([k[:, cols], v[:, cols]], axis=-1)
-        out_ref[h, rows : rows + half, :] = jnp.concatenate([q[:half, cols], q[half:, cols]], axis=-1)
-
-
-def unpack_rows(got_ref):
-    pieces = [got_ref[h].astype(jnp.float32) for h in range(HEADS)]
+        packed_ref[h, 0:rows, :] = jnp.concatenate([k[:, cols], v[:, cols]], axis=-1)
+        packed_ref[h, rows : rows + half, :] = jnp.concatenate([q[:half, cols], q[half:, cols]], axis=-1)
+    me = place()
+    for d in range(HEADS):
+        out_refs[d][...] = packed_ref[me ^ d]
+
+
+def unpack_rows(got_refs, packed_ref):
+    me = place()
+    for d in range(HEADS):
+        packed_ref[me ^ d] = got_refs[d][...].astype(jnp.float32)
+    pieces = [packed_ref[h] for h in range(HEADS)]
     top = jnp.concatenate([p[:, :HD] for p in pieces], axis=-1)
     low = jnp.concatenate([p[:, HD:] for p in pieces], axis=-1)
     return jnp.concatenate([top, low], axis=0)
@@ -130,22 +140,37 @@
     return x * lax.rsqrt(jnp.mean(x * x, axis=-1, keepdims=True) + EPSILON)
 
 
-def pack_kernel(q_ref, k_ref, v_ref, out_ref):
-    pack_heads(out_ref, q_ref[0], k_ref[0], v_ref[0])
-
-
-def attend_kernel(mine_ref, other_ref, out_ref):
-    sources, lines, _ = mine_ref.shape
+def pack_kernel(q_hbm, k_hbm, v_hbm, *refs):
+    out_refs, (q_ref, k_ref, v_ref, packed_ref, sems) = refs[:HEADS], refs[HEADS:]
+    copies = [
+        pltpu.make_async_copy(src, dst, sems.at[i])
+        for i, (src, dst) in enumerate(((q_hbm, q_ref), (k_hbm, k_ref), (v_hbm, v_ref)))
+    ]
+    for copy in copies:
+        copy.start()
+    for copy in copies:
+        copy.wait()
+    pack_heads(packed_ref, out_refs, q_ref[0], k_ref[0], v_ref[0])
+
+
+def collect_kernel(*refs):
+    out_ref = refs[HEADS]
+    rows = out_ref.shape[0] // HEADS
+    for d in range(HEADS):
+        out_ref[d * rows : (d + 1) * rows, :] = refs[d][0:rows, :]
+
+
+def attend_kernel(mine_ref, other_ref, *refs):
+    got_refs, out_refs = refs[:HEADS], refs[HEADS:]
+    lines = got_refs[0].shape[0]
     rows = lines * 2 // 3
     half = rows // 2
-    kv = jnp.concatenate(
-        [mine_ref[:, 0:rows, :].reshape(-1, 2 * HD), other_ref[:, 0:rows, :].reshape(-1, 2 * HD)], axis=0
-    )
+    kv = jnp.concatenate([mine_ref[...], other_ref[...]], axis=0)
     keys = kv[:, :HD]
     vals = kv[:, HD:]
-    step = max(1, 128 // half)
-    for s in range(0, sources, step):
-        packed = mine_ref[s : s + step, rows:lines, :].reshape(-1, 2 * HD)
+    step = 4
+    for s in range(0, HEADS, step):
+        packed = jnp.concatenate([got_refs[d][rows:lines, :] for d in range(s, s + step)], axis=0)
         queries = jnp.concatenate([packed[:, :HD], packed[:, HD:]], axis=0)
         scores = lax.dot_general(
             queries, keys, (((1,), (1,)), ((), ())), preferred_element_type=jnp.float32
@@ -156,11 +181,18 @@
         summed = jnp.dot(weights.astype(jnp.bfloat16), vals, preferred_element_type=jnp.float32)
         attn = (summed / total).astype(jnp.bfloat16)
         n = attn.shape[0] // 2
-        out_ref[s : s + step] = jnp.concatenate([attn[:n], attn[n:]], axis=-1).reshape(step, half, 2 * HD)
-
-
-def middle_kernel(got_ref, x2_ref, wv_ref, gain_ref, wqkv_ref, feats_ref, out_ref):
-    feats = unit(unpack_rows(got_ref))
+        lined = jnp.concatenate([attn[:n], attn[n:]], axis=-1)
+        for i in range(step):
+            out_refs[s + i][...] = lined[i * half : (i + 1) * half]
+
+
+def middle_kernel(x2_ref, wv_ref, gain_ref, wqkv_ref, *refs):
+    got_refs, (feats_ref, *out_refs), (line_ref, packed_ref) = (
+        refs[:HEADS],
+        refs[HEADS : 2 * HEADS + 1],
+        refs[2 * HEADS + 1 :],
+    )
+    feats = unit(unpack_rows(got_refs, line_ref))
     feats_ref[0] = feats
     hidden = x2_ref[0].astype(jnp.float32) + jnp.dot(
         feats.astype(jnp.bfloat16), wv_ref[...], preferred_element_type=jnp.float32
@@ -168,44 +200,67 @@
     normed = (unit(hidden) * gain_ref[...]).astype(jnp.bfloat16)
     projected = jnp.dot(normed, wqkv_ref[...], preferred_element_type=jnp.float32).astype(jnp.bfloat16)
     width = HEADS * HD
-    pack_heads(out_ref, projected[:, :width], projected[:, width : 2 * width], projected[:, 2 * width :])
-
-
-def last_kernel(got_ref, wout_ref, out_ref):
-    rows = unit(unpack_rows(got_ref)).astype(jnp.bfloat16)
+    pack_heads(
+        packed_ref, out_refs, projected[:, :width], projected[:, width : 2 * width], projected[:, 2 * width :]
+    )
+
+
+def last_kernel(wout_ref, *refs):
+    got_refs, out_ref, line_ref = refs[:HEADS], refs[HEADS], refs[HEADS + 1]
+    rows = unit(unpack_rows(got_refs, line_ref)).astype(jnp.bfloat16)
     out_ref[0] = jnp.dot(rows, wout_ref[...], preferred_element_type=jnp.float32)
 
 
-def call(body, outs, args, limit=48 << 20):
+def call(body, outs, args, scratch=(), limit=16 << 20, space=pltpu.VMEM):
     return pl.pallas_call(
         body,
         out_shape=outs,
-        in_specs=[VMEM] * len(args),
+        in_specs=[pl.BlockSpec(memory_space=space)] * len(args),
         out_specs=jax.tree.map(lambda _: VMEM, outs),
+        scratch_shapes=list(scratch),
         compiler_params=pltpu.CompilerParams(vmem_limit_bytes=limit),
     )(*args)
+
+
+def trade(pieces):
+    got = list(pieces)
+    for d in sorted(range(1, HEADS), reverse=True):
+        got[d] = lax.ppermute(pieces[d], GROUP, [(i, i ^ d) for i in range(HEADS)])
+    return got
 
 
 def by_heads(q1, k1, v1, nbr, x2, w_view_out, norm_gain, w_qkv, w_out):
     rows = q1.shape[1]
     lines = rows * 3 // 2
-    packed_type = jax.ShapeDtypeStruct((HEADS, lines, 2 * HD), jnp.bfloat16)
-    half_type = jax.ShapeDtypeStruct((HEADS, rows // 2, 2 * HD), jnp.bfloat16)
-    wide_type = jax.ShapeDtypeStruct((1, rows, HEADS * HD), jnp.float32)
-    group = ("view", "chip")
-
-    def attention(packed):
-        mine = lax.all_to_all(packed, group, split_axis=0, concat_axis=0, tiled=True)
+    half = rows // 2
+    packed = [jax.ShapeDtypeStruct((lines, 2 * HD), jnp.bfloat16)] * HEADS
+    halves = [jax.ShapeDtypeStruct((half, 2 * HD), jnp.bfloat16)] * HEADS
+    keyvals = jax.ShapeDtypeStruct((HEADS * rows, 2 * HD), jnp.bfloat16)
+    wide = jax.ShapeDtypeStruct((1, rows, HEADS * HD), jnp.float32)
+    packed_scratch = pltpu.VMEM((HEADS, lines, 2 * HD), jnp.bfloat16)
+    line_scratch = pltpu.VMEM((HEADS, half, 2 * HD), jnp.float32)
+
+    def attention(pieces):
+        got = trade(pieces)
+        mine = call(collect_kernel, keyvals, got)
         cores = lax.axis_size("core")
         other = lax.ppermute(mine, "core", [(i, (i + 1) % cores) for i in range(cores)])
-        half = call(attend_kernel, half_type, (mine, other))
-        return lax.all_to_all(half, group, split_axis=0, concat_axis=0, tiled=True)
-
-    got = attention(call(pack_kernel, packed_type, (q1, k1, v1)))
-    feats, packed = call(
-        middle_kernel, (wide_type, packed_type), (got, x2, w_view_out, norm_gain[None], w_qkv)
-    )
-    result = call(last_kernel, wide_type, (attention(packed), w_out))
+        return trade(call(attend_kernel, halves, (mine, other, *got)))
+
+    pieces = call(
+        pack_kernel,
+        packed,
+        (q1, k1, v1),
+        [pltpu.VMEM(q1.shape, q1.dtype)] * 3 + [packed_scratch, pltpu.SemaphoreType.DMA((3,))],
+        space=pl.ANY,
+    )
+    feats, *pieces = call(
+        middle_kernel,
+        [wide, *packed],
+        (x2, w_view_out, norm_gain[None], w_qkv, *attention(pieces)),
+        [line_scratch, packed_scratch],
+    )
+    result = call(last_kernel, wide, (w_out, *attention(pieces)), [line_scratch])
     return feats, result
 
 

time: 67.1 us -> 145 us (2.16)
  starting transfers between devices: 0.01 us -> 107 us
  blocking collectives: 48.6 us -> 0 us
  waiting for transfers between devices: 2.88 us -> 20.6 us
  local copies, waits for them, and re-layouts: 5.63 us -> 8.41 us
  Pallas kernels: 8.77 us -> 7.07 us
    ppermute x0 -> x60, starting transfers between devices: none -> 107 us  [trade(): got[d] = lax.ppermute(pieces[d], GROUP, [(i, i ^ d) for i in range(HEADS)])]
    all_to_all x4 -> x0, blocking collectives: 48.6 us -> none  [the longest x2 27.4 us: attention(): lax.all_to_all(packed, group, split_axis=0, concat_axis=0, tiled=True)]
    ppermute x0 -> x60, waiting for transfers between devices: none -> 17.9 us  [trade(): got[d] = lax.ppermute(pieces[d], GROUP, [(i, i ^ d) for i in range(HEADS)])]
    unnamed x14 -> x16, local copies, waits for them, and re-layouts: 5.63 us -> 8.41 us
    pallas_call x5 -> x7, Pallas kernels: 8.77 us -> 7.07 us  [call(): pl.pallas_call(body, out_shape=outs, in_specs=[pl.BlockSpec(memory_space=...]
  transfers between devices with their start and end apart: 2 -> 62, of which waited for: 2 -> 12; matrix products, arithmetic and copies ran while one was open for 0% -> 0% of each run, Pallas kernels for 0% -> 0%
where the time goes in v2:
time: 145 us; the launch traced here: 144 us
  starting transfers between devices  107 us (74%)
  waiting for transfers between devices  20.6 us (14%)
  local copies, waits for them, and re-layouts  8.41 us (6%)
  Pallas kernels  7.07 us (5%)
    ppermute x60, starting transfers between devices, trade(): got[d] = lax.ppermute(pieces[d], GROUP, [(i, i ^ d) for i in range(HEADS)])  107 us
    ppermute x60, waiting for transfers between devices, trade(): got[d] = lax.ppermute(pieces[d], GROUP, [(i, i ^ d) for i in range(HEADS)])  17.9 us
    unnamed x16, local copies, waits for them, and re-layouts  8.41 us
    pallas_call x7, Pallas kernels, call(): pl.pallas_call(body, out_shape=outs, in_specs=[pl.BlockSpec(memory_space=...  7.07 us
  transfers between devices with their start and end apart: 62, of which 12 were waited for; matrix products, arithmetic and copies ran while one was open for 0% of the time, Pallas kernels for 0%

profile of v2, /device:TPU:0, one launch (start us, length us, event | category | flops | bytes accessed | tf_op | source)
XLA Modules:
  0.0 144.3 jit_solution(17480985549361074064)
XLA Ops:
  0.6 0.8 copy-done.4
  1.5 0.8 copy-done.5
  2.3 0.8 copy-done.6
  3.6 3.0 %collective-permute-start = (bf16[48,128]{1,0:T(8,128)(2,1)S(1)}, bf16[48,128]{1,0:T(8,128)(2,1)S(1)}, u32[]{:S(2)}, u32[]{:S(2)}) collective-permute-start(bf16[48,128]{1,0:T(8,128)(2,1)S(1)} %get-tuple-element.68), channel_id=1, source_target_pairs={{0,2},{2,0},{4,6},{6,4},{8,10},{10,8},{12,14},{14,12},{16,18},{18,... | collective-permute-start | bytes 36872 | tf_op jit(solution)/shard_map/ppermute | solution.py:228
  6.6 1.5 %collective-permute-start.1 = (bf16[48,128]{1,0:T(8,128)(2,1)S(1)}, bf16[48,128]{1,0:T(8,128)(2,1)S(1)}, u32[]{:S(2)}, u32[]{:S(2)}) collective-permute-start(bf16[48,128]{1,0:T(8,128)(2,1)S(1)} %get-tuple-element.69), channel_id=1, source_target_pairs={{0,4},{2,6},{4,0},{6,2},{8,12},{10,14},{12,8},{14,10},{16,20},{18,... | collective-permute-start | bytes 36872 | tf_op jit(solution)/shard_map/ppermute | solution.py:228
  8.1 2.0 %collective-permute-start.3 = (bf16[48,128]{1,0:T(8,128)(2,1)S(1)}, bf16[48,128]{1,0:T(8,128)(2,1)S(1)}, u32[]{:S(2)}, u32[]{:S(2)}) collective-permute-start(bf16[48,128]{1,0:T(8,128)(2,1)S(1)} %get-tuple-element.71), channel_id=1, source_target_pairs={{0,8},{2,10},{4,12},{6,14},{8,0},{10,2},{12,4},{14,6},{16,24},{18,... | collective-permute-start | bytes 36872 | tf_op jit(solution)/shard_map/ppermute | solution.py:228
  10.2 1.4 collective-permute-start.4
  11.5 2.5 %collective-permute-start.5 = (bf16[48,128]{1,0:T(8,128)(2,1)S(1)}, bf16[48,128]{1,0:T(8,128)(2,1)S(1)}, u32[]{:S(2)}, u32[]{:S(2)}) collective-permute-start(bf16[48,128]{1,0:T(8,128)(2,1)S(1)} %get-tuple-element.73), channel_id=1, source_target_pairs={{0,12},{2,14},{4,8},{6,10},{8,4},{10,6},{12,0},{14,2},{16,28},{18,... | collective-permute-start | bytes 36872 | tf_op jit(solution)/shard_map/ppermute | solution.py:228
  14.1 2.9 %collective-permute-start.7 = (bf16[48,128]{1,0:T(8,128)(2,1)S(1)}, bf16[48,128]{1,0:T(8,128)(2,1)S(1)}, u32[]{:S(2)}, u32[]{:S(2)}) collective-permute-start(bf16[48,128]{1,0:T(8,128)(2,1)S(1)} %get-tuple-element.75), channel_id=1, source_target_pairs={{0,16},{2,18},{4,20},{6,22},{8,24},{10,26},{12,28},{14,30},{16,0},... | collective-permute-start | bytes 36872 | tf_op jit(solution)/shard_map/ppermute | solution.py:228
  17.0 1.3 collective-permute-start.8
  18.3 3.5 %collective-permute-start.9 = (bf16[48,128]{1,0:T(8,128)(2,1)S(1)}, bf16[48,128]{1,0:T(8,128)(2,1)S(1)}, u32[]{:S(2)}, u32[]{:S(2)}) collective-permute-start(bf16[48,128]{1,0:T(8,128)(2,1)S(1)} %get-tuple-element.77), channel_id=1, source_target_pairs={{0,20},{2,22},{4,16},{6,18},{8,28},{10,30},{12,24},{14,26},{16,4},... | collective-permute-start | bytes 36872 | tf_op jit(solution)/shard_map/ppermute | solution.py:228
  21.9 3.8 %collective-permute-start.11 = (bf16[48,128]{1,0:T(8,128)(2,1)S(1)}, bf16[48,128]{1,0:T(8,128)(2,1)S(1)}, u32[]{:S(2)}, u32[]{:S(2)}) collective-permute-start(bf16[48,128]{1,0:T(8,128)(2,1)S(1)} %get-tuple-element.79), channel_id=1, source_target_pairs={{0,24},{2,26},{4,28},{6,30},{8,16},{10,18},{12,20},{14,22},{16,8},... | collective-permute-start | bytes 36872 | tf_op jit(solution)/shard_map/ppermute | solution.py:228
  25.7 1.1 collective-permute-start.12
  26.9 4.6 %collective-permute-start.13 = (bf16[48,128]{1,0:T(8,128)(2,1)S(1)}, bf16[48,128]{1,0:T(8,128)(2,1)S(1)}, u32[]{:S(2)}, u32[]{:S(2)}) collective-permute-start(bf16[48,128]{1,0:T(8,128)(2,1)S(1)} %get-tuple-element.81), channel_id=1, source_target_pairs={{0,28},{2,30},{4,24},{6,26},{8,20},{10,22},{12,16},{14,18},{16,12}... | collective-permute-start | bytes 36872 | tf_op jit(solution)/shard_map/ppermute | solution.py:228
  31.5 0.6 collective-permute-done.12.refs_13_
  32.1 1.2 collective-permute-done.13.refs_14_
  33.3 5.4 %collective-permute-done.14.refs_15_ = bf16[48,128]{1,0:T(8,128)(2,1)S(1)} collective-permute-done((bf16[48,128]{1,0:T(8,128)(2,1)S(1)}, bf16[48,128]{1,0:T(8,128)(2,1)S(1)}, u32[]{:S(2)}, u32[]{:S(2)}) %collective-permute-start.14) | collective-permute-done | bytes 12320 | tf_op jit(solution)/shard_map/ppermute | solution.py:228
  38.8 1.3 collective-permute-done.15.other_ref
  40.2 1.7 %shard_map.97 = (bf16[16,128]{1,0:T(8,128)(2,1)S(1)}, bf16[16,128]{1,0:T(8,128)(2,1)S(1)}, bf16[16,128]{1,0:T(8,128)(2,1)S(1)}, bf16[16,128]{1,0:T(8,128)(2,1)S(...) custom-call(bf16[512,128]{1,0:T(8,128)(2,1)S(1)} %shard_map.96.mine_, ...), custom_call_target="tpu_custom_call" | custom-call | tf_op jit(solution)/shard_map/pallas_call | solution.py:215
  41.9 0.6 collective-permute-start.16
  42.4 0.5 collective-permute-start.17
  42.9 2.4 %collective-permute-start.18 = (bf16[16,128]{1,0:T(8,128)(2,1)S(1)}, bf16[16,128]{1,0:T(8,128)(2,1)S(1)}, u32[]{:S(2)}, u32[]{:S(2)}) collective-permute-start(bf16[16,128]{1,0:T(8,128)(2,1)S(1)} %get-tuple-element.86), channel_id=1, source_target_pairs={{0,6},{2,4},{4,2},{6,0},{8,14},{10,12},{12,10},{14,8},{16,22},{18,... | collective-permute-start | bytes 12296 | tf_op jit(solution)/shard_map/ppermute | solution.py:228
  45.4 2.0 %collective-permute-start.20 = (bf16[16,128]{1,0:T(8,128)(2,1)S(1)}, bf16[16,128]{1,0:T(8,128)(2,1)S(1)}, u32[]{:S(2)}, u32[]{:S(2)}) collective-permute-start(bf16[16,128]{1,0:T(8,128)(2,1)S(1)} %get-tuple-element.88), channel_id=1, source_target_pairs={{0,10},{2,8},{4,14},{6,12},{8,2},{10,0},{12,6},{14,4},{16,26},{18,... | collective-permute-start | bytes 12296 | tf_op jit(solution)/shard_map/ppermute | solution.py:228
  47.4 3.8 %collective-permute-start.22 = (bf16[16,128]{1,0:T(8,128)(2,1)S(1)}, bf16[16,128]{1,0:T(8,128)(2,1)S(1)}, u32[]{:S(2)}, u32[]{:S(2)}) collective-permute-start(bf16[16,128]{1,0:T(8,128)(2,1)S(1)} %get-tuple-element.90), channel_id=1, source_target_pairs={{0,14},{2,12},{4,10},{6,8},{8,6},{10,4},{12,2},{14,0},{16,30},{18,... | collective-permute-start | bytes 12296 | tf_op jit(solution)/shard_map/ppermute | solution.py:228
  51.3 2.9 %collective-permute-start.24 = (bf16[16,128]{1,0:T(8,128)(2,1)S(1)}, bf16[16,128]{1,0:T(8,128)(2,1)S(1)}, u32[]{:S(2)}, u32[]{:S(2)}) collective-permute-start(bf16[16,128]{1,0:T(8,128)(2,1)S(1)} %get-tuple-element.92), channel_id=1, source_target_pairs={{0,18},{2,16},{4,22},{6,20},{8,26},{10,24},{12,30},{14,28},{16,2},... | collective-permute-start | bytes 12296 | tf_op jit(solution)/shard_map/ppermute | solution.py:228
  54.2 4.7 %collective-permute-start.26 = (bf16[16,128]{1,0:T(8,128)(2,1)S(1)}, bf16[16,128]{1,0:T(8,128)(2,1)S(1)}, u32[]{:S(2)}, u32[]{:S(2)}) collective-permute-start(bf16[16,128]{1,0:T(8,128)(2,1)S(1)} %get-tuple-element.94), channel_id=1, source_target_pairs={{0,22},{2,20},{4,18},{6,16},{8,30},{10,28},{12,26},{14,24},{16,6},... | collective-permute-start | bytes 12296 | tf_op jit(solution)/shard_map/ppermute | solution.py:228
  59.1 3.6 %collective-permute-start.28 = (bf16[16,128]{1,0:T(8,128)(2,1)S(1)}, bf16[16,128]{1,0:T(8,128)(2,1)S(1)}, u32[]{:S(2)}, u32[]{:S(2)}) collective-permute-start(bf16[16,128]{1,0:T(8,128)(2,1)S(1)} %get-tuple-element.96), channel_id=1, source_target_pairs={{0,26},{2,24},{4,30},{6,28},{8,18},{10,16},{12,22},{14,20},{16,10}... | collective-permute-start | bytes 12296 | tf_op jit(solution)/shard_map/ppermute | solution.py:228
  62.9 5.5 %collective-permute-start.30 = (bf16[16,128]{1,0:T(8,128)(2,1)S(1)}, bf16[16,128]{1,0:T(8,128)(2,1)S(1)}, u32[]{:S(2)}, u32[]{:S(2)}) collective-permute-start(bf16[16,128]{1,0:T(8,128)(2,1)S(1)} %get-tuple-element.98), channel_id=1, source_target_pairs={{0,30},{2,28},{4,26},{6,24},{8,22},{10,20},{12,18},{14,16},{16,14}... | collective-permute-start | bytes 12296 | tf_op jit(solution)/shard_map/ppermute | solution.py:228
  68.4 0.6 collective-permute-done.29.refs_14_
  69.0 1.1 collective-permute-done.30.refs_15_
  70.1 2.8 %copy-done = bf16[1024,3072]{1,0:T(8,128)(2,1)S(1)} copy-done((bf16[1024,3072]{1,0:T(8,128)(2,1)S(1)}, bf16[1024,3072]{1,0:T(8,128)(2,1)}, u32[]{:S(2)}) %copy-start) | copy-done | bytes 6291480
  72.9 1.6 %copy-done.2 = bf16[1024,1024]{1,0:T(8,128)(2,1)S(1)} copy-done((bf16[1024,1024]{1,0:T(8,128)(2,1)S(1)}, bf16[1024,1024]{1,0:T(8,128)(2,1)}, u32[]{:S(2)}) %copy-start.2) | copy-done | bytes 2097176
  74.5 0.8 copy-done.3
  75.3 0.7 copy-done.7
  76.0 2.0 %shard_map.98 = (f32[1,32,1024]{2,1,0:T(8,128)}, bf16[48,128]{1,0:T(8,128)(2,1)S(1)}, bf16[48,128]{1,0:T(8,128)(2,1)S(1)}, bf16[48,128]{1,0:T(8,128)(2,1)S(1)}, ...) custom-call(bf16[1,32,1024]{2,1,0:T(8,128)(2,1)S(1)} %copy-done.3, ...), custom_call_target="tpu_custom_call" | custom-call | tf_op jit(solution)/shard_map/pallas_call | solution.py:215
  77.9 1.6 %collective-permute-start.31 = (bf16[48,128]{1,0:T(8,128)(2,1)S(1)}, bf16[48,128]{1,0:T(8,128)(2,1)S(1)}, u32[]{:S(2)}, u32[]{:S(2)}) collective-permute-start(bf16[48,128]{1,0:T(8,128)(2,1)S(1)} %get-tuple-element.101), channel_id=1, source_target_pairs={{0,2},{2,0},{4,6},{6,4},{8,10},{10,8},{12,14},{14,12},{16,18},{18,... | collective-permute-start | bytes 36872 | tf_op jit(solution)/shard_map/ppermute | solution.py:228
  79.5 1.5 %collective-permute-start.32 = (bf16[48,128]{1,0:T(8,128)(2,1)S(1)}, bf16[48,128]{1,0:T(8,128)(2,1)S(1)}, u32[]{:S(2)}, u32[]{:S(2)}) collective-permute-start(bf16[48,128]{1,0:T(8,128)(2,1)S(1)} %get-tuple-element.102), channel_id=1, source_target_pairs={{0,4},{2,6},{4,0},{6,2},{8,12},{10,14},{12,8},{14,10},{16,20},{18,... | collective-permute-start | bytes 36872 | tf_op jit(solution)/shard_map/ppermute | solution.py:228
  81.5 3.0 %collective-permute-start.35 = (bf16[48,128]{1,0:T(8,128)(2,1)S(1)}, bf16[48,128]{1,0:T(8,128)(2,1)S(1)}, u32[]{:S(2)}, u32[]{:S(2)}) collective-permute-start(bf16[48,128]{1,0:T(8,128)(2,1)S(1)} %get-tuple-element.105), channel_id=1, source_target_pairs={{0,10},{2,8},{4,14},{6,12},{8,2},{10,0},{12,6},{14,4},{16,26},{18,... | collective-permute-start | bytes 36872 | tf_op jit(solution)/shard_map/ppermute | solution.py:228
  84.5 1.0 collective-permute-start.36
  85.4 1.9 %collective-permute-start.37 = (bf16[48,128]{1,0:T(8,128)(2,1)S(1)}, bf16[48,128]{1,0:T(8,128)(2,1)S(1)}, u32[]{:S(2)}, u32[]{:S(2)}) collective-permute-start(bf16[48,128]{1,0:T(8,128)(2,1)S(1)} %get-tuple-element.107), channel_id=1, source_target_pairs={{0,14},{2,12},{4,10},{6,8},{8,6},{10,4},{12,2},{14,0},{16,30},{18,... | collective-permute-start | bytes 36872 | tf_op jit(solution)/shard_map/ppermute | solution.py:228
  87.4 2.3 %collective-permute-start.38 = (bf16[48,128]{1,0:T(8,128)(2,1)S(1)}, bf16[48,128]{1,0:T(8,128)(2,1)S(1)}, u32[]{:S(2)}, u32[]{:S(2)}) collective-permute-start(bf16[48,128]{1,0:T(8,128)(2,1)S(1)} %get-tuple-element.108), channel_id=1, source_target_pairs={{0,16},{2,18},{4,20},{6,22},{8,24},{10,26},{12,28},{14,30},{16,0},... | collective-permute-start | bytes 36872 | tf_op jit(solution)/shard_map/ppermute | solution.py:228
  89.7 1.6 %collective-permute-start.39 = (bf16[48,128]{1,0:T(8,128)(2,1)S(1)}, bf16[48,128]{1,0:T(8,128)(2,1)S(1)}, u32[]{:S(2)}, u32[]{:S(2)}) collective-permute-start(bf16[48,128]{1,0:T(8,128)(2,1)S(1)} %get-tuple-element.109), channel_id=1, source_target_pairs={{0,18},{2,16},{4,22},{6,20},{8,26},{10,24},{12,30},{14,28},{16,2},... | collective-permute-start | bytes 36872 | tf_op jit(solution)/shard_map/ppermute | solution.py:228
  91.2 3.1 %collective-permute-start.40 = (bf16[48,128]{1,0:T(8,128)(2,1)S(1)}, bf16[48,128]{1,0:T(8,128)(2,1)S(1)}, u32[]{:S(2)}, u32[]{:S(2)}) collective-permute-start(bf16[48,128]{1,0:T(8,128)(2,1)S(1)} %get-tuple-element.110), channel_id=1, source_target_pairs={{0,20},{2,22},{4,16},{6,18},{8,28},{10,30},{12,24},{14,26},{16,4},... | collective-permute-start | bytes 36872 | tf_op jit(solution)/shard_map/ppermute | solution.py:228
  94.3 0.7 collective-permute-start.41
  95.0 3.6 %collective-permute-start.42 = (bf16[48,128]{1,0:T(8,128)(2,1)S(1)}, bf16[48,128]{1,0:T(8,128)(2,1)S(1)}, u32[]{:S(2)}, u32[]{:S(2)}) collective-permute-start(bf16[48,128]{1,0:T(8,128)(2,1)S(1)} %get-tuple-element.112), channel_id=1, source_target_pairs={{0,24},{2,26},{4,28},{6,30},{8,16},{10,18},{12,20},{14,22},{16,8},... | collective-permute-start | bytes 36872 | tf_op jit(solution)/shard_map/ppermute | solution.py:228
  98.6 1.1 collective-permute-start.43
  99.8 4.6 %collective-permute-start.44 = (bf16[48,128]{1,0:T(8,128)(2,1)S(1)}, bf16[48,128]{1,0:T(8,128)(2,1)S(1)}, u32[]{:S(2)}, u32[]{:S(2)}) collective-permute-start(bf16[48,128]{1,0:T(8,128)(2,1)S(1)} %get-tuple-element.114), channel_id=1, source_target_pairs={{0,28},{2,30},{4,24},{6,26},{8,20},{10,22},{12,16},{14,18},{16,12}... | collective-permute-start | bytes 36872 | tf_op jit(solution)/shard_map/ppermute | solution.py:228
  104.5 0.5 collective-permute-done.43.refs_13_
  105.0 1.2 collective-permute-done.44.refs_14_
  106.2 5.5 %collective-permute-done.45.refs_15_ = bf16[48,128]{1,0:T(8,128)(2,1)S(1)} collective-permute-done((bf16[48,128]{1,0:T(8,128)(2,1)S(1)}, bf16[48,128]{1,0:T(8,128)(2,1)S(1)}, u32[]{:S(2)}, u32[]{:S(2)}) %collective-permute-start.45) | collective-permute-done | bytes 12320 | tf_op jit(solution)/shard_map/ppermute | solution.py:228
  111.7 1.3 collective-permute-done.46.other_ref
  113.1 1.7 %shard_map.100 = (bf16[16,128]{1,0:T(8,128)(2,1)S(1)}, bf16[16,128]{1,0:T(8,128)(2,1)S(1)}, bf16[16,128]{1,0:T(8,128)(2,1)S(1)}, bf16[16,128]{1,0:T(8,128)(2,1)S...) custom-call(bf16[512,128]{1,0:T(8,128)(2,1)S(1)} %shard_map.99.mine_, ...), custom_call_target="tpu_custom_call" | custom-call | tf_op jit(solution)/shard_map/pallas_call | solution.py:215
  114.8 0.6 collective-permute-start.47
  115.4 0.5 collective-permute-start.48
  115.9 2.5 %collective-permute-start.49 = (bf16[16,128]{1,0:T(8,128)(2,1)S(1)}, bf16[16,128]{1,0:T(8,128)(2,1)S(1)}, u32[]{:S(2)}, u32[]{:S(2)}) collective-permute-start(bf16[16,128]{1,0:T(8,128)(2,1)S(1)} %get-tuple-element.119), channel_id=1, source_target_pairs={{0,6},{2,4},{4,2},{6,0},{8,14},{10,12},{12,10},{14,8},{16,22},{18,... | collective-permute-start | bytes 12296 | tf_op jit(solution)/shard_map/ppermute | solution.py:228
  118.3 2.0 %collective-permute-start.51 = (bf16[16,128]{1,0:T(8,128)(2,1)S(1)}, bf16[16,128]{1,0:T(8,128)(2,1)S(1)}, u32[]{:S(2)}, u32[]{:S(2)}) collective-permute-start(bf16[16,128]{1,0:T(8,128)(2,1)S(1)} %get-tuple-element.121), channel_id=1, source_target_pairs={{0,10},{2,8},{4,14},{6,12},{8,2},{10,0},{12,6},{14,4},{16,26},{18,... | collective-permute-start | bytes 12296 | tf_op jit(solution)/shard_map/ppermute | solution.py:228
  120.3 3.8 %collective-permute-start.53 = (bf16[16,128]{1,0:T(8,128)(2,1)S(1)}, bf16[16,128]{1,0:T(8,128)(2,1)S(1)}, u32[]{:S(2)}, u32[]{:S(2)}) collective-permute-start(bf16[16,128]{1,0:T(8,128)(2,1)S(1)} %get-tuple-element.123), channel_id=1, source_target_pairs={{0,14},{2,12},{4,10},{6,8},{8,6},{10,4},{12,2},{14,0},{16,30},{18,... | collective-permute-start | bytes 12296 | tf_op jit(solution)/shard_map/ppermute | solution.py:228
  124.2 2.9 %collective-permute-start.55 = (bf16[16,128]{1,0:T(8,128)(2,1)S(1)}, bf16[16,128]{1,0:T(8,128)(2,1)S(1)}, u32[]{:S(2)}, u32[]{:S(2)}) collective-permute-start(bf16[16,128]{1,0:T(8,128)(2,1)S(1)} %get-tuple-element.125), channel_id=1, source_target_pairs={{0,18},{2,16},{4,22},{6,20},{8,26},{10,24},{12,30},{14,28},{16,2},... | collective-permute-start | bytes 12296 | tf_op jit(solution)/shard_map/ppermute | solution.py:228
  127.1 4.7 %collective-permute-start.57 = (bf16[16,128]{1,0:T(8,128)(2,1)S(1)}, bf16[16,128]{1,0:T(8,128)(2,1)S(1)}, u32[]{:S(2)}, u32[]{:S(2)}) collective-permute-start(bf16[16,128]{1,0:T(8,128)(2,1)S(1)} %get-tuple-element.127), channel_id=1, source_target_pairs={{0,22},{2,20},{4,18},{6,16},{8,30},{10,28},{12,26},{14,24},{16,6},... | collective-permute-start | bytes 12296 | tf_op jit(solution)/shard_map/ppermute | solution.py:228
  132.1 3.6 %collective-permute-start.59 = (bf16[16,128]{1,0:T(8,128)(2,1)S(1)}, bf16[16,128]{1,0:T(8,128)(2,1)S(1)}, u32[]{:S(2)}, u32[]{:S(2)}) collective-permute-start(bf16[16,128]{1,0:T(8,128)(2,1)S(1)} %get-tuple-element.129), channel_id=1, source_target_pairs={{0,26},{2,24},{4,30},{6,28},{8,18},{10,16},{12,22},{14,20},{16,10}... | collective-permute-start | bytes 12296 | tf_op jit(solution)/shard_map/ppermute | solution.py:228
  135.8 5.5 %collective-permute-start.61 = (bf16[16,128]{1,0:T(8,128)(2,1)S(1)}, bf16[16,128]{1,0:T(8,128)(2,1)S(1)}, u32[]{:S(2)}, u32[]{:S(2)}) collective-permute-start(bf16[16,128]{1,0:T(8,128)(2,1)S(1)} %get-tuple-element.131), channel_id=1, source_target_pairs={{0,30},{2,28},{4,26},{6,24},{8,22},{10,20},{12,18},{14,16},{16,14}... | collective-permute-start | bytes 12296 | tf_op jit(solution)/shard_map/ppermute | solution.py:228
  141.3 0.6 collective-permute-done.60.refs_14_
  141.9 1.1 collective-permute-done.61.refs_15_
  143.0 1.3 shard_map.101
  (83 shorter events, 2.3 us)
Async XLA Ops:
  3.6 8.0 %collective-permute-start = (bf16[48,128]{1,0:T(8,128)(2,1)S(1)}, bf16[48,128]{1,0:T(8,128)(2,1)S(1)}, u32[]{:S(2)}, u32[]{:S(2)}) collective-permute-start(bf16[48,128]{1,0:T(8,128)(2,1)S(1)} %get-tuple-element.68), channel_id=1, source_target_pairs={{0,2},{2,0},{4,6},{6,4},{8,10},{10,8},{12,14},{14,12},{16,18},{18,... | collective-permute-start | bytes 36872 | tf_op jit(solution)/shard_map/ppermute | solution.py:228
  6.6 7.5 %collective-permute-start.1 = (bf16[48,128]{1,0:T(8,128)(2,1)S(1)}, bf16[48,128]{1,0:T(8,128)(2,1)S(1)}, u32[]{:S(2)}, u32[]{:S(2)}) collective-permute-start(bf16[48,128]{1,0:T(8,128)(2,1)S(1)} %get-tuple-element.69), channel_id=1, source_target_pairs={{0,4},{2,6},{4,0},{6,2},{8,12},{10,14},{12,8},{14,10},{16,20},{18,... | collective-permute-start | bytes 36872 | tf_op jit(solution)/shard_map/ppermute | solution.py:228
  8.1 6.0 %collective-permute-start.2 = (bf16[48,128]{1,0:T(8,128)(2,1)S(1)}, bf16[48,128]{1,0:T(8,128)(2,1)S(1)}, u32[]{:S(2)}, u32[]{:S(2)}) collective-permute-start(bf16[48,128]{1,0:T(8,128)(2,1)S(1)} %get-tuple-element.70), channel_id=1, source_target_pairs={{0,6},{2,4},{4,2},{6,0},{8,14},{10,12},{12,10},{14,8},{16,22},{18,... | collective-permute-start | bytes 36872 | tf_op jit(solution)/shard_map/ppermute | solution.py:228
  8.1 8.9 %collective-permute-start.3 = (bf16[48,128]{1,0:T(8,128)(2,1)S(1)}, bf16[48,128]{1,0:T(8,128)(2,1)S(1)}, u32[]{:S(2)}, u32[]{:S(2)}) collective-permute-start(bf16[48,128]{1,0:T(8,128)(2,1)S(1)} %get-tuple-element.71), channel_id=1, source_target_pairs={{0,8},{2,10},{4,12},{6,14},{8,0},{10,2},{12,4},{14,6},{16,24},{18,... | collective-permute-start | bytes 36872 | tf_op jit(solution)/shard_map/ppermute | solution.py:228
  10.2 8.1 %collective-permute-start.4 = (bf16[48,128]{1,0:T(8,128)(2,1)S(1)}, bf16[48,128]{1,0:T(8,128)(2,1)S(1)}, u32[]{:S(2)}, u32[]{:S(2)}) collective-permute-start(bf16[48,128]{1,0:T(8,128)(2,1)S(1)} %get-tuple-element.72), channel_id=1, source_target_pairs={{0,10},{2,8},{4,14},{6,12},{8,2},{10,0},{12,6},{14,4},{16,26},{18,... | collective-permute-start | bytes 36872 | tf_op jit(solution)/shard_map/ppermute | solution.py:228
  11.5 10.3 %collective-permute-start.5 = (bf16[48,128]{1,0:T(8,128)(2,1)S(1)}, bf16[48,128]{1,0:T(8,128)(2,1)S(1)}, u32[]{:S(2)}, u32[]{:S(2)}) collective-permute-start(bf16[48,128]{1,0:T(8,128)(2,1)S(1)} %get-tuple-element.73), channel_id=1, source_target_pairs={{0,12},{2,14},{4,8},{6,10},{8,4},{10,6},{12,0},{14,2},{16,28},{18,... | collective-permute-start | bytes 36872 | tf_op jit(solution)/shard_map/ppermute | solution.py:228
  14.1 7.8 %collective-permute-start.6 = (bf16[48,128]{1,0:T(8,128)(2,1)S(1)}, bf16[48,128]{1,0:T(8,128)(2,1)S(1)}, u32[]{:S(2)}, u32[]{:S(2)}) collective-permute-start(bf16[48,128]{1,0:T(8,128)(2,1)S(1)} %get-tuple-element.74), channel_id=1, source_target_pairs={{0,14},{2,12},{4,10},{6,8},{8,6},{10,4},{12,2},{14,0},{16,30},{18,... | collective-permute-start | bytes 36872 | tf_op jit(solution)/shard_map/ppermute | solution.py:228
  14.1 11.6 %collective-permute-start.7 = (bf16[48,128]{1,0:T(8,128)(2,1)S(1)}, bf16[48,128]{1,0:T(8,128)(2,1)S(1)}, u32[]{:S(2)}, u32[]{:S(2)}) collective-permute-start(bf16[48,128]{1,0:T(8,128)(2,1)S(1)} %get-tuple-element.75), channel_id=1, source_target_pairs={{0,16},{2,18},{4,20},{6,22},{8,24},{10,26},{12,28},{14,30},{16,0},... | collective-permute-start | bytes 36872 | tf_op jit(solution)/shard_map/ppermute | solution.py:228
  17.0 9.8 %collective-permute-start.8 = (bf16[48,128]{1,0:T(8,128)(2,1)S(1)}, bf16[48,128]{1,0:T(8,128)(2,1)S(1)}, u32[]{:S(2)}, u32[]{:S(2)}) collective-permute-start(bf16[48,128]{1,0:T(8,128)(2,1)S(1)} %get-tuple-element.76), channel_id=1, source_target_pairs={{0,18},{2,16},{4,22},{6,20},{8,26},{10,24},{12,30},{14,28},{16,2},... | collective-permute-start | bytes 36872 | tf_op jit(solution)/shard_map/ppermute | solution.py:228
  18.3 13.1 %collective-permute-start.9 = (bf16[48,128]{1,0:T(8,128)(2,1)S(1)}, bf16[48,128]{1,0:T(8,128)(2,1)S(1)}, u32[]{:S(2)}, u32[]{:S(2)}) collective-permute-start(bf16[48,128]{1,0:T(8,128)(2,1)S(1)} %get-tuple-element.77), channel_id=1, source_target_pairs={{0,20},{2,22},{4,16},{6,18},{8,28},{10,30},{12,24},{14,26},{16,4},... | collective-permute-start | bytes 36872 | tf_op jit(solution)/shard_map/ppermute | solution.py:228
  21.9 9.6 %collective-permute-start.10 = (bf16[48,128]{1,0:T(8,128)(2,1)S(1)}, bf16[48,128]{1,0:T(8,128)(2,1)S(1)}, u32[]{:S(2)}, u32[]{:S(2)}) collective-permute-start(bf16[48,128]{1,0:T(8,128)(2,1)S(1)} %get-tuple-element.78), channel_id=1, source_target_pairs={{0,22},{2,20},{4,18},{6,16},{8,30},{10,28},{12,26},{14,24},{16,6},... | collective-permute-start | bytes 36872 | tf_op jit(solution)/shard_map/ppermute | solution.py:228
  21.9 9.6 %collective-permute-start.11 = (bf16[48,128]{1,0:T(8,128)(2,1)S(1)}, bf16[48,128]{1,0:T(8,128)(2,1)S(1)}, u32[]{:S(2)}, u32[]{:S(2)}) collective-permute-start(bf16[48,128]{1,0:T(8,128)(2,1)S(1)} %get-tuple-element.79), channel_id=1, source_target_pairs={{0,24},{2,26},{4,28},{6,30},{8,16},{10,18},{12,20},{14,22},{16,8},... | collective-permute-start | bytes 36872 | tf_op jit(solution)/shard_map/ppermute | solution.py:228
  25.7 6.4 %collective-permute-start.12 = (bf16[48,128]{1,0:T(8,128)(2,1)S(1)}, bf16[48,128]{1,0:T(8,128)(2,1)S(1)}, u32[]{:S(2)}, u32[]{:S(2)}) collective-permute-start(bf16[48,128]{1,0:T(8,128)(2,1)S(1)} %get-tuple-element.80), channel_id=1, source_target_pairs={{0,26},{2,24},{4,30},{6,28},{8,18},{10,16},{12,22},{14,20},{16,10}... | collective-permute-start | bytes 36872 | tf_op jit(solution)/shard_map/ppermute | solution.py:228
  26.9 6.4 %collective-permute-start.13 = (bf16[48,128]{1,0:T(8,128)(2,1)S(1)}, bf16[48,128]{1,0:T(8,128)(2,1)S(1)}, u32[]{:S(2)}, u32[]{:S(2)}) collective-permute-start(bf16[48,128]{1,0:T(8,128)(2,1)S(1)} %get-tuple-element.81), channel_id=1, source_target_pairs={{0,28},{2,30},{4,24},{6,26},{8,20},{10,22},{12,16},{14,18},{16,12}... | collective-permute-start | bytes 36872 | tf_op jit(solution)/shard_map/ppermute | solution.py:228
  31.4 7.3 %collective-permute-start.14 = (bf16[48,128]{1,0:T(8,128)(2,1)S(1)}, bf16[48,128]{1,0:T(8,128)(2,1)S(1)}, u32[]{:S(2)}, u32[]{:S(2)}) collective-permute-start(bf16[48,128]{1,0:T(8,128)(2,1)S(1)} %get-tuple-element.82), channel_id=1, source_target_pairs={{0,30},{2,28},{4,26},{6,24},{8,22},{10,20},{12,18},{14,16},{16,14}... | collective-permute-start | bytes 36872 | tf_op jit(solution)/shard_map/ppermute | solution.py:228
  38.7 1.4 collective-permute-start.15
  41.9 5.5 %collective-permute-start.16 = (bf16[16,128]{1,0:T(8,128)(2,1)S(1)}, bf16[16,128]{1,0:T(8,128)(2,1)S(1)}, u32[]{:S(2)}, u32[]{:S(2)}) collective-permute-start(bf16[16,128]{1,0:T(8,128)(2,1)S(1)} %get-tuple-element.84), channel_id=1, source_target_pairs={{0,2},{2,0},{4,6},{6,4},{8,10},{10,8},{12,14},{14,12},{16,18},{18,... | collective-permute-start | bytes 12296 | tf_op jit(solution)/shard_map/ppermute | solution.py:228
  42.4 5.0 %collective-permute-start.17 = (bf16[16,128]{1,0:T(8,128)(2,1)S(1)}, bf16[16,128]{1,0:T(8,128)(2,1)S(1)}, u32[]{:S(2)}, u32[]{:S(2)}) collective-permute-start(bf16[16,128]{1,0:T(8,128)(2,1)S(1)} %get-tuple-element.85), channel_id=1, source_target_pairs={{0,4},{2,6},{4,0},{6,2},{8,12},{10,14},{12,8},{14,10},{16,20},{18,... | collective-permute-start | bytes 12296 | tf_op jit(solution)/shard_map/ppermute | solution.py:228
  42.9 8.3 %collective-permute-start.18 = (bf16[16,128]{1,0:T(8,128)(2,1)S(1)}, bf16[16,128]{1,0:T(8,128)(2,1)S(1)}, u32[]{:S(2)}, u32[]{:S(2)}) collective-permute-start(bf16[16,128]{1,0:T(8,128)(2,1)S(1)} %get-tuple-element.86), channel_id=1, source_target_pairs={{0,6},{2,4},{4,2},{6,0},{8,14},{10,12},{12,10},{14,8},{16,22},{18,... | collective-permute-start | bytes 12296 | tf_op jit(solution)/shard_map/ppermute | solution.py:228
  45.4 5.9 %collective-permute-start.19 = (bf16[16,128]{1,0:T(8,128)(2,1)S(1)}, bf16[16,128]{1,0:T(8,128)(2,1)S(1)}, u32[]{:S(2)}, u32[]{:S(2)}) collective-permute-start(bf16[16,128]{1,0:T(8,128)(2,1)S(1)} %get-tuple-element.87), channel_id=1, source_target_pairs={{0,8},{2,10},{4,12},{6,14},{8,0},{10,2},{12,4},{14,6},{16,24},{18,... | collective-permute-start | bytes 12296 | tf_op jit(solution)/shard_map/ppermute | solution.py:228
  45.4 8.8 %collective-permute-start.20 = (bf16[16,128]{1,0:T(8,128)(2,1)S(1)}, bf16[16,128]{1,0:T(8,128)(2,1)S(1)}, u32[]{:S(2)}, u32[]{:S(2)}) collective-permute-start(bf16[16,128]{1,0:T(8,128)(2,1)S(1)} %get-tuple-element.88), channel_id=1, source_target_pairs={{0,10},{2,8},{4,14},{6,12},{8,2},{10,0},{12,6},{14,4},{16,26},{18,... | collective-permute-start | bytes 12296 | tf_op jit(solution)/shard_map/ppermute | solution.py:228
  47.4 6.8 %collective-permute-start.21 = (bf16[16,128]{1,0:T(8,128)(2,1)S(1)}, bf16[16,128]{1,0:T(8,128)(2,1)S(1)}, u32[]{:S(2)}, u32[]{:S(2)}) collective-permute-start(bf16[16,128]{1,0:T(8,128)(2,1)S(1)} %get-tuple-element.89), channel_id=1, source_target_pairs={{0,12},{2,14},{4,8},{6,10},{8,4},{10,6},{12,0},{14,2},{16,28},{18,... | collective-permute-start | bytes 12296 | tf_op jit(solution)/shard_map/ppermute | solution.py:228
  47.4 11.5 %collective-permute-start.22 = (bf16[16,128]{1,0:T(8,128)(2,1)S(1)}, bf16[16,128]{1,0:T(8,128)(2,1)S(1)}, u32[]{:S(2)}, u32[]{:S(2)}) collective-permute-start(bf16[16,128]{1,0:T(8,128)(2,1)S(1)} %get-tuple-element.90), channel_id=1, source_target_pairs={{0,14},{2,12},{4,10},{6,8},{8,6},{10,4},{12,2},{14,0},{16,30},{18,... | collective-permute-start | bytes 12296 | tf_op jit(solution)/shard_map/ppermute | solution.py:228
  51.2 7.9 %collective-permute-start.23 = (bf16[16,128]{1,0:T(8,128)(2,1)S(1)}, bf16[16,128]{1,0:T(8,128)(2,1)S(1)}, u32[]{:S(2)}, u32[]{:S(2)}) collective-permute-start(bf16[16,128]{1,0:T(8,128)(2,1)S(1)} %get-tuple-element.91), channel_id=1, source_target_pairs={{0,16},{2,18},{4,20},{6,22},{8,24},{10,26},{12,28},{14,30},{16,0},... | collective-permute-start | bytes 12296 | tf_op jit(solution)/shard_map/ppermute | solution.py:228
  51.3 11.5 %collective-permute-start.24 = (bf16[16,128]{1,0:T(8,128)(2,1)S(1)}, bf16[16,128]{1,0:T(8,128)(2,1)S(1)}, u32[]{:S(2)}, u32[]{:S(2)}) collective-permute-start(bf16[16,128]{1,0:T(8,128)(2,1)S(1)} %get-tuple-element.92), channel_id=1, source_target_pairs={{0,18},{2,16},{4,22},{6,20},{8,26},{10,24},{12,30},{14,28},{16,2},... | collective-permute-start | bytes 12296 | tf_op jit(solution)/shard_map/ppermute | solution.py:228
  54.2 8.7 %collective-permute-start.25 = (bf16[16,128]{1,0:T(8,128)(2,1)S(1)}, bf16[16,128]{1,0:T(8,128)(2,1)S(1)}, u32[]{:S(2)}, u32[]{:S(2)}) collective-permute-start(bf16[16,128]{1,0:T(8,128)(2,1)S(1)} %get-tuple-element.93), channel_id=1, source_target_pairs={{0,20},{2,22},{4,16},{6,18},{8,28},{10,30},{12,24},{14,26},{16,4},... | collective-permute-start | bytes 12296 | tf_op jit(solution)/shard_map/ppermute | solution.py:228
  54.2 14.2 %collective-permute-start.26 = (bf16[16,128]{1,0:T(8,128)(2,1)S(1)}, bf16[16,128]{1,0:T(8,128)(2,1)S(1)}, u32[]{:S(2)}, u32[]{:S(2)}) collective-permute-start(bf16[16,128]{1,0:T(8,128)(2,1)S(1)} %get-tuple-element.94), channel_id=1, source_target_pairs={{0,22},{2,20},{4,18},{6,16},{8,30},{10,28},{12,26},{14,24},{16,6},... | collective-permute-start | bytes 12296 | tf_op jit(solution)/shard_map/ppermute | solution.py:228
  58.9 9.5 %collective-permute-start.27 = (bf16[16,128]{1,0:T(8,128)(2,1)S(1)}, bf16[16,128]{1,0:T(8,128)(2,1)S(1)}, u32[]{:S(2)}, u32[]{:S(2)}) collective-permute-start(bf16[16,128]{1,0:T(8,128)(2,1)S(1)} %get-tuple-element.95), channel_id=1, source_target_pairs={{0,24},{2,26},{4,28},{6,30},{8,16},{10,18},{12,20},{14,22},{16,8},... | collective-permute-start | bytes 12296 | tf_op jit(solution)/shard_map/ppermute | solution.py:228
  59.1 9.2 %collective-permute-start.28 = (bf16[16,128]{1,0:T(8,128)(2,1)S(1)}, bf16[16,128]{1,0:T(8,128)(2,1)S(1)}, u32[]{:S(2)}, u32[]{:S(2)}) collective-permute-start(bf16[16,128]{1,0:T(8,128)(2,1)S(1)} %get-tuple-element.96), channel_id=1, source_target_pairs={{0,26},{2,24},{4,30},{6,28},{8,18},{10,16},{12,22},{14,20},{16,10}... | collective-permute-start | bytes 12296 | tf_op jit(solution)/shard_map/ppermute | solution.py:228
  62.7 6.3 %collective-permute-start.29 = (bf16[16,128]{1,0:T(8,128)(2,1)S(1)}, bf16[16,128]{1,0:T(8,128)(2,1)S(1)}, u32[]{:S(2)}, u32[]{:S(2)}) collective-permute-start(bf16[16,128]{1,0:T(8,128)(2,1)S(1)} %get-tuple-element.97), channel_id=1, source_target_pairs={{0,28},{2,30},{4,24},{6,26},{8,20},{10,22},{12,16},{14,18},{16,12}... | collective-permute-start | bytes 12296 | tf_op jit(solution)/shard_map/ppermute | solution.py:228
  62.9 7.2 %collective-permute-start.30 = (bf16[16,128]{1,0:T(8,128)(2,1)S(1)}, bf16[16,128]{1,0:T(8,128)(2,1)S(1)}, u32[]{:S(2)}, u32[]{:S(2)}) collective-permute-start(bf16[16,128]{1,0:T(8,128)(2,1)S(1)} %get-tuple-element.98), channel_id=1, source_target_pairs={{0,30},{2,28},{4,26},{6,24},{8,22},{10,20},{12,18},{14,16},{16,14}... | collective-permute-start | bytes 12296 | tf_op jit(solution)/shard_map/ppermute | solution.py:228
  70.1 2.8 %copy-start = (bf16[1024,3072]{1,0:T(8,128)(2,1)S(1)}, bf16[1024,3072]{1,0:T(8,128)(2,1)}, u32[]{:S(2)}) copy-start(bf16[1024,3072]{1,0:T(8,128)(2,1)} %wqkv_ref.1) | copy-start | bytes 18874372
  76.0 67.0 %copy-start.1 = (bf16[1024,1024]{1,0:T(8,128)(2,1)S(1)}, bf16[1024,1024]{1,0:T(8,128)(2,1)}, u32[]{:S(2)}) copy-start(bf16[1024,1024]{1,0:T(8,128)(2,1)} %wout_ref.1) | copy-start | bytes 6291460
  77.9 6.5 %collective-permute-start.31 = (bf16[48,128]{1,0:T(8,128)(2,1)S(1)}, bf16[48,128]{1,0:T(8,128)(2,1)S(1)}, u32[]{:S(2)}, u32[]{:S(2)}) collective-permute-start(bf16[48,128]{1,0:T(8,128)(2,1)S(1)} %get-tuple-element.101), channel_id=1, source_target_pairs={{0,2},{2,0},{4,6},{6,4},{8,10},{10,8},{12,14},{14,12},{16,18},{18,... | collective-permute-start | bytes 36872 | tf_op jit(solution)/shard_map/ppermute | solution.py:228
  79.5 5.9 %collective-permute-start.32 = (bf16[48,128]{1,0:T(8,128)(2,1)S(1)}, bf16[48,128]{1,0:T(8,128)(2,1)S(1)}, u32[]{:S(2)}, u32[]{:S(2)}) collective-permute-start(bf16[48,128]{1,0:T(8,128)(2,1)S(1)} %get-tuple-element.102), channel_id=1, source_target_pairs={{0,4},{2,6},{4,0},{6,2},{8,12},{10,14},{12,8},{14,10},{16,20},{18,... | collective-permute-start | bytes 36872 | tf_op jit(solution)/shard_map/ppermute | solution.py:228
  81.0 6.3 %collective-permute-start.33 = (bf16[48,128]{1,0:T(8,128)(2,1)S(1)}, bf16[48,128]{1,0:T(8,128)(2,1)S(1)}, u32[]{:S(2)}, u32[]{:S(2)}) collective-permute-start(bf16[48,128]{1,0:T(8,128)(2,1)S(1)} %get-tuple-element.103), channel_id=1, source_target_pairs={{0,6},{2,4},{4,2},{6,0},{8,14},{10,12},{12,10},{14,8},{16,22},{18,... | collective-permute-start | bytes 36872 | tf_op jit(solution)/shard_map/ppermute | solution.py:228
  81.5 8.2 %collective-permute-start.34 = (bf16[48,128]{1,0:T(8,128)(2,1)S(1)}, bf16[48,128]{1,0:T(8,128)(2,1)S(1)}, u32[]{:S(2)}, u32[]{:S(2)}) collective-permute-start(bf16[48,128]{1,0:T(8,128)(2,1)S(1)} %get-tuple-element.104), channel_id=1, source_target_pairs={{0,8},{2,10},{4,12},{6,14},{8,0},{10,2},{12,4},{14,6},{16,24},{18,... | collective-permute-start | bytes 36872 | tf_op jit(solution)/shard_map/ppermute | solution.py:228
  81.5 9.7 %collective-permute-start.35 = (bf16[48,128]{1,0:T(8,128)(2,1)S(1)}, bf16[48,128]{1,0:T(8,128)(2,1)S(1)}, u32[]{:S(2)}, u32[]{:S(2)}) collective-permute-start(bf16[48,128]{1,0:T(8,128)(2,1)S(1)} %get-tuple-element.105), channel_id=1, source_target_pairs={{0,10},{2,8},{4,14},{6,12},{8,2},{10,0},{12,6},{14,4},{16,26},{18,... | collective-permute-start | bytes 36872 | tf_op jit(solution)/shard_map/ppermute | solution.py:228
  84.5 9.9 %collective-permute-start.36 = (bf16[48,128]{1,0:T(8,128)(2,1)S(1)}, bf16[48,128]{1,0:T(8,128)(2,1)S(1)}, u32[]{:S(2)}, u32[]{:S(2)}) collective-permute-start(bf16[48,128]{1,0:T(8,128)(2,1)S(1)} %get-tuple-element.106), channel_id=1, source_target_pairs={{0,12},{2,14},{4,8},{6,10},{8,4},{10,6},{12,0},{14,2},{16,28},{18,... | collective-permute-start | bytes 36872 | tf_op jit(solution)/shard_map/ppermute | solution.py:228
  85.4 9.6 %collective-permute-start.37 = (bf16[48,128]{1,0:T(8,128)(2,1)S(1)}, bf16[48,128]{1,0:T(8,128)(2,1)S(1)}, u32[]{:S(2)}, u32[]{:S(2)}) collective-permute-start(bf16[48,128]{1,0:T(8,128)(2,1)S(1)} %get-tuple-element.107), channel_id=1, source_target_pairs={{0,14},{2,12},{4,10},{6,8},{8,6},{10,4},{12,2},{14,0},{16,30},{18,... | collective-permute-start | bytes 36872 | tf_op jit(solution)/shard_map/ppermute | solution.py:228
  87.4 11.3 %collective-permute-start.38 = (bf16[48,128]{1,0:T(8,128)(2,1)S(1)}, bf16[48,128]{1,0:T(8,128)(2,1)S(1)}, u32[]{:S(2)}, u32[]{:S(2)}) collective-permute-start(bf16[48,128]{1,0:T(8,128)(2,1)S(1)} %get-tuple-element.108), channel_id=1, source_target_pairs={{0,16},{2,18},{4,20},{6,22},{8,24},{10,26},{12,28},{14,30},{16,0},... | collective-permute-start | bytes 36872 | tf_op jit(solution)/shard_map/ppermute | solution.py:228
  89.7 10.1 %collective-permute-start.39 = (bf16[48,128]{1,0:T(8,128)(2,1)S(1)}, bf16[48,128]{1,0:T(8,128)(2,1)S(1)}, u32[]{:S(2)}, u32[]{:S(2)}) collective-permute-start(bf16[48,128]{1,0:T(8,128)(2,1)S(1)} %get-tuple-element.109), channel_id=1, source_target_pairs={{0,18},{2,16},{4,22},{6,20},{8,26},{10,24},{12,30},{14,28},{16,2},... | collective-permute-start | bytes 36872 | tf_op jit(solution)/shard_map/ppermute | solution.py:228
  91.2 13.1 %collective-permute-start.40 = (bf16[48,128]{1,0:T(8,128)(2,1)S(1)}, bf16[48,128]{1,0:T(8,128)(2,1)S(1)}, u32[]{:S(2)}, u32[]{:S(2)}) collective-permute-start(bf16[48,128]{1,0:T(8,128)(2,1)S(1)} %get-tuple-element.110), channel_id=1, source_target_pairs={{0,20},{2,22},{4,16},{6,18},{8,28},{10,30},{12,24},{14,26},{16,4},... | collective-permute-start | bytes 36872 | tf_op jit(solution)/shard_map/ppermute | solution.py:228
  94.3 10.1 %collective-permute-start.41 = (bf16[48,128]{1,0:T(8,128)(2,1)S(1)}, bf16[48,128]{1,0:T(8,128)(2,1)S(1)}, u32[]{:S(2)}, u32[]{:S(2)}) collective-permute-start(bf16[48,128]{1,0:T(8,128)(2,1)S(1)} %get-tuple-element.111), channel_id=1, source_target_pairs={{0,22},{2,20},{4,18},{6,16},{8,30},{10,28},{12,26},{14,24},{16,6},... | collective-permute-start | bytes 36872 | tf_op jit(solution)/shard_map/ppermute | solution.py:228
  95.0 9.5 %collective-permute-start.42 = (bf16[48,128]{1,0:T(8,128)(2,1)S(1)}, bf16[48,128]{1,0:T(8,128)(2,1)S(1)}, u32[]{:S(2)}, u32[]{:S(2)}) collective-permute-start(bf16[48,128]{1,0:T(8,128)(2,1)S(1)} %get-tuple-element.112), channel_id=1, source_target_pairs={{0,24},{2,26},{4,28},{6,30},{8,16},{10,18},{12,20},{14,22},{16,8},... | collective-permute-start | bytes 36872 | tf_op jit(solution)/shard_map/ppermute | solution.py:228
  98.6 6.4 %collective-permute-start.43 = (bf16[48,128]{1,0:T(8,128)(2,1)S(1)}, bf16[48,128]{1,0:T(8,128)(2,1)S(1)}, u32[]{:S(2)}, u32[]{:S(2)}) collective-permute-start(bf16[48,128]{1,0:T(8,128)(2,1)S(1)} %get-tuple-element.113), channel_id=1, source_target_pairs={{0,26},{2,24},{4,30},{6,28},{8,18},{10,16},{12,22},{14,20},{16,10}... | collective-permute-start | bytes 36872 | tf_op jit(solution)/shard_map/ppermute | solution.py:228
  99.8 6.4 %collective-permute-start.44 = (bf16[48,128]{1,0:T(8,128)(2,1)S(1)}, bf16[48,128]{1,0:T(8,128)(2,1)S(1)}, u32[]{:S(2)}, u32[]{:S(2)}) collective-permute-start(bf16[48,128]{1,0:T(8,128)(2,1)S(1)} %get-tuple-element.114), channel_id=1, source_target_pairs={{0,28},{2,30},{4,24},{6,26},{8,20},{10,22},{12,16},{14,18},{16,12}... | collective-permute-start | bytes 36872 | tf_op jit(solution)/shard_map/ppermute | solution.py:228
  104.4 7.3 %collective-permute-start.45 = (bf16[48,128]{1,0:T(8,128)(2,1)S(1)}, bf16[48,128]{1,0:T(8,128)(2,1)S(1)}, u32[]{:S(2)}, u32[]{:S(2)}) collective-permute-start(bf16[48,128]{1,0:T(8,128)(2,1)S(1)} %get-tuple-element.115), channel_id=1, source_target_pairs={{0,30},{2,28},{4,26},{6,24},{8,22},{10,20},{12,18},{14,16},{16,14}... | collective-permute-start | bytes 36872 | tf_op jit(solution)/shard_map/ppermute | solution.py:228
  111.7 1.4 collective-permute-start.46
  114.8 5.5 %collective-permute-start.47 = (bf16[16,128]{1,0:T(8,128)(2,1)S(1)}, bf16[16,128]{1,0:T(8,128)(2,1)S(1)}, u32[]{:S(2)}, u32[]{:S(2)}) collective-permute-start(bf16[16,128]{1,0:T(8,128)(2,1)S(1)} %get-tuple-element.117), channel_id=1, source_target_pairs={{0,2},{2,0},{4,6},{6,4},{8,10},{10,8},{12,14},{14,12},{16,18},{18,... | collective-permute-start | bytes 12296 | tf_op jit(solution)/shard_map/ppermute | solution.py:228
  115.4 5.0 %collective-permute-start.48 = (bf16[16,128]{1,0:T(8,128)(2,1)S(1)}, bf16[16,128]{1,0:T(8,128)(2,1)S(1)}, u32[]{:S(2)}, u32[]{:S(2)}) collective-permute-start(bf16[16,128]{1,0:T(8,128)(2,1)S(1)} %get-tuple-element.118), channel_id=1, source_target_pairs={{0,4},{2,6},{4,0},{6,2},{8,12},{10,14},{12,8},{14,10},{16,20},{18,... | collective-permute-start | bytes 12296 | tf_op jit(solution)/shard_map/ppermute | solution.py:228
  115.9 8.3 %collective-permute-start.49 = (bf16[16,128]{1,0:T(8,128)(2,1)S(1)}, bf16[16,128]{1,0:T(8,128)(2,1)S(1)}, u32[]{:S(2)}, u32[]{:S(2)}) collective-permute-start(bf16[16,128]{1,0:T(8,128)(2,1)S(1)} %get-tuple-element.119), channel_id=1, source_target_pairs={{0,6},{2,4},{4,2},{6,0},{8,14},{10,12},{12,10},{14,8},{16,22},{18,... | collective-permute-start | bytes 12296 | tf_op jit(solution)/shard_map/ppermute | solution.py:228
  118.3 5.9 %collective-permute-start.50 = (bf16[16,128]{1,0:T(8,128)(2,1)S(1)}, bf16[16,128]{1,0:T(8,128)(2,1)S(1)}, u32[]{:S(2)}, u32[]{:S(2)}) collective-permute-start(bf16[16,128]{1,0:T(8,128)(2,1)S(1)} %get-tuple-element.120), channel_id=1, source_target_pairs={{0,8},{2,10},{4,12},{6,14},{8,0},{10,2},{12,4},{14,6},{16,24},{18,... | collective-permute-start | bytes 12296 | tf_op jit(solution)/shard_map/ppermute | solution.py:228
  118.3 8.8 %collective-permute-start.51 = (bf16[16,128]{1,0:T(8,128)(2,1)S(1)}, bf16[16,128]{1,0:T(8,128)(2,1)S(1)}, u32[]{:S(2)}, u32[]{:S(2)}) collective-permute-start(bf16[16,128]{1,0:T(8,128)(2,1)S(1)} %get-tuple-element.121), channel_id=1, source_target_pairs={{0,10},{2,8},{4,14},{6,12},{8,2},{10,0},{12,6},{14,4},{16,26},{18,... | collective-permute-start | bytes 12296 | tf_op jit(solution)/shard_map/ppermute | solution.py:228
  120.3 6.8 %collective-permute-start.52 = (bf16[16,128]{1,0:T(8,128)(2,1)S(1)}, bf16[16,128]{1,0:T(8,128)(2,1)S(1)}, u32[]{:S(2)}, u32[]{:S(2)}) collective-permute-start(bf16[16,128]{1,0:T(8,128)(2,1)S(1)} %get-tuple-element.122), channel_id=1, source_target_pairs={{0,12},{2,14},{4,8},{6,10},{8,4},{10,6},{12,0},{14,2},{16,28},{18,... | collective-permute-start | bytes 12296 | tf_op jit(solution)/shard_map/ppermute | solution.py:228
  120.3 11.5 %collective-permute-start.53 = (bf16[16,128]{1,0:T(8,128)(2,1)S(1)}, bf16[16,128]{1,0:T(8,128)(2,1)S(1)}, u32[]{:S(2)}, u32[]{:S(2)}) collective-permute-start(bf16[16,128]{1,0:T(8,128)(2,1)S(1)} %get-tuple-element.123), channel_id=1, source_target_pairs={{0,14},{2,12},{4,10},{6,8},{8,6},{10,4},{12,2},{14,0},{16,30},{18,... | collective-permute-start | bytes 12296 | tf_op jit(solution)/shard_map/ppermute | solution.py:228
  124.2 7.9 %collective-permute-start.54 = (bf16[16,128]{1,0:T(8,128)(2,1)S(1)}, bf16[16,128]{1,0:T(8,128)(2,1)S(1)}, u32[]{:S(2)}, u32[]{:S(2)}) collective-permute-start(bf16[16,128]{1,0:T(8,128)(2,1)S(1)} %get-tuple-element.124), channel_id=1, source_target_pairs={{0,16},{2,18},{4,20},{6,22},{8,24},{10,26},{12,28},{14,30},{16,0},... | collective-permute-start | bytes 12296 | tf_op jit(solution)/shard_map/ppermute | solution.py:228
  124.2 11.5 %collective-permute-start.55 = (bf16[16,128]{1,0:T(8,128)(2,1)S(1)}, bf16[16,128]{1,0:T(8,128)(2,1)S(1)}, u32[]{:S(2)}, u32[]{:S(2)}) collective-permute-start(bf16[16,128]{1,0:T(8,128)(2,1)S(1)} %get-tuple-element.125), channel_id=1, source_target_pairs={{0,18},{2,16},{4,22},{6,20},{8,26},{10,24},{12,30},{14,28},{16,2},... | collective-permute-start | bytes 12296 | tf_op jit(solution)/shard_map/ppermute | solution.py:228
  127.1 8.7 %collective-permute-start.56 = (bf16[16,128]{1,0:T(8,128)(2,1)S(1)}, bf16[16,128]{1,0:T(8,128)(2,1)S(1)}, u32[]{:S(2)}, u32[]{:S(2)}) collective-permute-start(bf16[16,128]{1,0:T(8,128)(2,1)S(1)} %get-tuple-element.126), channel_id=1, source_target_pairs={{0,20},{2,22},{4,16},{6,18},{8,28},{10,30},{12,24},{14,26},{16,4},... | collective-permute-start | bytes 12296 | tf_op jit(solution)/shard_map/ppermute | solution.py:228
  127.1 14.2 %collective-permute-start.57 = (bf16[16,128]{1,0:T(8,128)(2,1)S(1)}, bf16[16,128]{1,0:T(8,128)(2,1)S(1)}, u32[]{:S(2)}, u32[]{:S(2)}) collective-permute-start(bf16[16,128]{1,0:T(8,128)(2,1)S(1)} %get-tuple-element.127), channel_id=1, source_target_pairs={{0,22},{2,20},{4,18},{6,16},{8,30},{10,28},{12,26},{14,24},{16,6},... | collective-permute-start | bytes 12296 | tf_op jit(solution)/shard_map/ppermute | solution.py:228
  131.8 9.5 %collective-permute-start.58 = (bf16[16,128]{1,0:T(8,128)(2,1)S(1)}, bf16[16,128]{1,0:T(8,128)(2,1)S(1)}, u32[]{:S(2)}, u32[]{:S(2)}) collective-permute-start(bf16[16,128]{1,0:T(8,128)(2,1)S(1)} %get-tuple-element.128), channel_id=1, source_target_pairs={{0,24},{2,26},{4,28},{6,30},{8,16},{10,18},{12,20},{14,22},{16,8},... | collective-permute-start | bytes 12296 | tf_op jit(solution)/shard_map/ppermute | solution.py:228
  132.1 9.3 %collective-permute-start.59 = (bf16[16,128]{1,0:T(8,128)(2,1)S(1)}, bf16[16,128]{1,0:T(8,128)(2,1)S(1)}, u32[]{:S(2)}, u32[]{:S(2)}) collective-permute-start(bf16[16,128]{1,0:T(8,128)(2,1)S(1)} %get-tuple-element.129), channel_id=1, source_target_pairs={{0,26},{2,24},{4,30},{6,28},{8,18},{10,16},{12,22},{14,20},{16,10}... | collective-permute-start | bytes 12296 | tf_op jit(solution)/shard_map/ppermute | solution.py:228
  135.6 6.3 %collective-permute-start.60 = (bf16[16,128]{1,0:T(8,128)(2,1)S(1)}, bf16[16,128]{1,0:T(8,128)(2,1)S(1)}, u32[]{:S(2)}, u32[]{:S(2)}) collective-permute-start(bf16[16,128]{1,0:T(8,128)(2,1)S(1)} %get-tuple-element.130), channel_id=1, source_target_pairs={{0,28},{2,30},{4,24},{6,26},{8,20},{10,22},{12,16},{14,18},{16,12}... | collective-permute-start | bytes 12296 | tf_op jit(solution)/shard_map/ppermute | solution.py:228
  135.8 7.2 %collective-permute-start.61 = (bf16[16,128]{1,0:T(8,128)(2,1)S(1)}, bf16[16,128]{1,0:T(8,128)(2,1)S(1)}, u32[]{:S(2)}, u32[]{:S(2)}) collective-permute-start(bf16[16,128]{1,0:T(8,128)(2,1)S(1)} %get-tuple-element.131), channel_id=1, source_target_pairs={{0,30},{2,28},{4,26},{6,24},{8,22},{10,20},{12,18},{14,16},{16,14}... | collective-permute-start | bytes 12296 | tf_op jit(solution)/shard_map/ppermute | solution.py:228
  (6 other events, 5.6 us)

commit v3 on v1

--- a/solution.py
+++ b/solution.py
@@ -1,6 +1,3 @@
-import functools
-import math
-
 import jax
 import jax.numpy as jnp
 from jax import lax
@@ -130,7 +127,15 @@
     return x * lax.rsqrt(jnp.mean(x * x, axis=-1, keepdims=True) + EPSILON)
 
 
-def pack_kernel(q_ref, k_ref, v_ref, out_ref):
+def pack_kernel(q_hbm, k_hbm, v_hbm, out_ref, q_ref, k_ref, v_ref, sems):
+    copies = [
+        pltpu.make_async_copy(src, dst, sems.at[i])
+        for i, (src, dst) in enumerate(((q_hbm, q_ref), (k_hbm, k_ref), (v_hbm, v_ref)))
+    ]
+    for copy in copies:
+        copy.start()
+    for copy in copies:
+        copy.wait()
     pack_heads(out_ref, q_ref[0], k_ref[0], v_ref[0])
 
 
@@ -176,12 +181,14 @@
     out_ref[0] = jnp.dot(rows, wout_ref[...], preferred_element_type=jnp.float32)
 
 
-def call(body, outs, args, limit=48 << 20):
+def call(body, outs, args, scratch=(), limit=16 << 20, space=pltpu.VMEM, cost=None):
     return pl.pallas_call(
         body,
         out_shape=outs,
-        in_specs=[VMEM] * len(args),
+        in_specs=[pl.BlockSpec(memory_space=space)] * len(args),
         out_specs=jax.tree.map(lambda _: VMEM, outs),
+        scratch_shapes=list(scratch),
+        cost_estimate=cost,
         compiler_params=pltpu.CompilerParams(vmem_limit_bytes=limit),
     )(*args)
 
@@ -198,10 +205,12 @@
         mine = lax.all_to_all(packed, group, split_axis=0, concat_axis=0, tiled=True)
         cores = lax.axis_size("core")
         other = lax.ppermute(mine, "core", [(i, (i + 1) % cores) for i in range(cores)])
-        half = call(attend_kernel, half_type, (mine, other))
+        cost = pl.CostEstimate(flops=16 << 30, bytes_accessed=40 << 20, transcendentals=0)
+        half = call(attend_kernel, half_type, (mine, other), cost=cost)
         return lax.all_to_all(half, group, split_axis=0, concat_axis=0, tiled=True)
 
-    got = attention(call(pack_kernel, packed_type, (q1, k1, v1)))
+    scratch = [pltpu.VMEM(q1.shape, q1.dtype)] * 3 + [pltpu.SemaphoreType.DMA((3,))]
+    got = attention(call(pack_kernel, packed_type, (q1, k1, v1), scratch, space=pltpu.HBM, limit=60 << 20))
     feats, packed = call(
         middle_kernel, (wide_type, packed_type), (got, x2, w_view_out, norm_gain[None], w_qkv)
     )

time: 67.1 us -> 60.4 us (0.900)
  local copies, waits for them, and re-layouts: 5.63 us -> 0.03 us
  Pallas kernels: 8.77 us -> 7.58 us
    unnamed x14 -> x12, local copies, waits for them, and re-layouts: 5.63 us -> 0.03 us
    pallas_call x5, Pallas kernels: 8.77 us -> 7.58 us  [call(): pl.pallas_call(body, out_shape=outs, in_specs=[pl.BlockSpec(memory_space=...]
where the time goes in v3:
time: 60.4 us; the launch traced here: 60.1 us
  blocking collectives  48.8 us (81%)
  Pallas kernels  7.58 us (13%)
  waiting for transfers between devices  2.87 us (5%)
  between operations  0.7 us (1%)
    all_to_all x2, blocking collectives, attention(): lax.all_to_all(packed, group, split_axis=0, concat_axis=0, tiled=True)  27.6 us
    all_to_all x2, blocking collectives, attention(): return lax.all_to_all(half, group, split_axis=0, concat_axis=0, tiled=True)  21.2 us
    pallas_call x5, Pallas kernels, call(): pl.pallas_call(body, out_shape=outs, in_specs=[pl.BlockSpec(memory_space=...  7.58 us
    ppermute x2, waiting for transfers between devices, attention(): lax.ppermute(mine, 'core', [(i, (i + 1) % cores) for i in range(cores)])  2.87 us
  transfers between devices with their start and end apart: 2, of which 2 were waited for; matrix products, arithmetic and copies ran while one was open for 0% of the time, Pallas kernels for 0%

profile of v3, /device:TPU:0, one launch (start us, length us, event | category | flops | bytes accessed | tf_op | source)
XLA Modules:
  0.0 60.1 jit_solution(14235940894814820115)
XLA Ops:
  0.6 0.0 slice-start
  0.6 1.9 %shard_map.95 = bf16[16,48,128]{2,1,0:T(8,128)(2,1)} custom-call(bf16[1,32,1024]{2,1,0:T(8,128)(2,1)} %q_hbm.1, bf16[1,32,1024]{2,1,0:T(8,128)(2,1)} %k_hbm.1, bf16[1,32,1024]{2,1,0:T(8,128)(2,1)} %v_hbm.1), custom_call_target="tpu_custom_call" | custom-call | tf_op jit(solution)/shard_map/pallas_call | solution.py:185
  2.5 17.0 %all_to_all.20.mine_ref = bf16[16,48,128]{2,1,0:T(8,128)(2,1)S(1)} all-to-all(bf16[16,48,128]{2,1,0:T(8,128)(2,1)} %shard_map.95), channel_id=1, replica_groups=mesh['view'=8,'chip'=2,'core'=2] {'view','chip'}, dimensions={0} | all-to-all | bytes 393216 | tf_op jit(solution)/shard_map/all_to_all | solution.py:205
  19.5 0.0 slice-start.1
  19.5 0.0 copy-start.1
  19.5 0.0 copy-start.2
  19.5 0.0 copy-start.3
  19.5 0.1 collective-permute-start
  19.6 1.4 %collective-permute-done.other_ref = bf16[16,48,128]{2,1,0:T(8,128)(2,1)S(1)} collective-permute-done((bf16[16,48,128]{2,1,0:T(8,128)(2,1)S(1)}, bf16[16,48,128]{2,1,0:T(8,128)(2,1)S(1)}, u32[]{:S(2)}, u32[]{:S(2)}) %collective-permute-start) | collective-permute-done | bytes 196640 | tf_op jit(solution)/shard_map/ppermute | solution.py:207
  21.0 1.3 %shard_map.96 = bf16[16,16,128]{2,1,0:T(8,128)(2,1)S(1)} custom-call(bf16[16,48,128]{2,1,0:T(8,128)(2,1)S(1)} %all_to_all.20.mine_ref, bf16[16,48,128]{2,1,0:T(8,128)(2,1)S(1)} %collective-permute-done.other_ref), custom_call_target="tpu_custom_call" | custom-call | flops 17179869184 | bytes 41943040 | tf_op jit(solution)/shard_map/pallas_call | solution.py:185
  22.3 10.7 %all_to_all.21.got_ref = bf16[16,16,128]{2,1,0:T(8,128)(2,1)S(1)} all-to-all(bf16[16,16,128]{2,1,0:T(8,128)(2,1)S(1)} %shard_map.96), channel_id=1, replica_groups=mesh['view'=8,'chip'=2,'core'=2] {'view','chip'}, dimensions={0} | all-to-all | bytes 131072 | tf_op jit(solution)/shard_map/all_to_all | solution.py:210
  33.0 0.0 slice-done
  33.0 0.0 slice-done.1
  33.0 0.0 copy-done.1
  33.0 0.0 copy-done.2
  33.0 0.0 copy-done.3
  33.0 1.9 %shard_map.97 = (f32[1,32,1024]{2,1,0:T(8,128)}, bf16[16,48,128]{2,1,0:T(8,128)(2,1)S(1)}) custom-call(bf16[16,16,128]{2,1,0:T(8,128)(2,1)S(1)} %all_to_all.21.got_ref, bf16[1,32,1024]{2,1,0:T(8,128)(2,1)S(1)} %copy-done.2, bf16[1024,1024]{1,0:T(8,128)(2,1)S(1)} %copy-done.1, f32[1,1024]{1,0:T(1,128)S(1)} %bitcast.3, bf16[1024,3072]{1,0:T(8,128)(2,1)S(1)} %bitcast.2), custom_call_target="tpu_custom_call" | custom-call | tf_op jit(solution)/shard_map/pallas_call | solution.py:185
  34.9 10.7 %all_to_all.22.mine_ref = bf16[16,48,128]{2,1,0:T(8,128)(2,1)S(1)} all-to-all(bf16[16,48,128]{2,1,0:T(8,128)(2,1)S(1)} %get-tuple-element.5), channel_id=1, replica_groups=mesh['view'=8,'chip'=2,'core'=2] {'view','chip'}, dimensions={0} | all-to-all | bytes 393216 | tf_op jit(solution)/shard_map/all_to_all | solution.py:205
  45.6 0.0 copy-start
  45.6 0.0 collective-permute-start.1
  45.6 1.4 %collective-permute-done.1.other_ref = bf16[16,48,128]{2,1,0:T(8,128)(2,1)S(1)} collective-permute-done((bf16[16,48,128]{2,1,0:T(8,128)(2,1)S(1)}, bf16[16,48,128]{2,1,0:T(8,128)(2,1)S(1)}, u32[]{:S(2)}, u32[]{:S(2)}) %collective-permute-start.1) | collective-permute-done | bytes 196640 | tf_op jit(solution)/shard_map/ppermute | solution.py:207
  47.1 1.3 %shard_map.98 = bf16[16,16,128]{2,1,0:T(8,128)(2,1)S(1)} custom-call(bf16[16,48,128]{2,1,0:T(8,128)(2,1)S(1)} %all_to_all.22.mine_ref, bf16[16,48,128]{2,1,0:T(8,128)(2,1)S(1)} %collective-permute-done.1.other_ref), custom_call_target="tpu_custom_call" | custom-call | flops 17179869184 | bytes 41943040 | tf_op jit(solution)/shard_map/pallas_call | solution.py:185
  48.3 10.5 %all_to_all.23.got_ref = bf16[16,16,128]{2,1,0:T(8,128)(2,1)S(1)} all-to-all(bf16[16,16,128]{2,1,0:T(8,128)(2,1)S(1)} %shard_map.98), channel_id=1, replica_groups=mesh['view'=8,'chip'=2,'core'=2] {'view','chip'}, dimensions={0} | all-to-all | bytes 131072 | tf_op jit(solution)/shard_map/all_to_all | solution.py:210
  58.8 0.0 copy-done
  58.8 1.3 %shard_map.99 = f32[1,32,1024]{2,1,0:T(8,128)} custom-call(bf16[16,16,128]{2,1,0:T(8,128)(2,1)S(1)} %all_to_all.23.got_ref, bf16[1024,1024]{1,0:T(8,128)(2,1)S(1)} %copy-done), custom_call_target="tpu_custom_call" | custom-call | tf_op jit(solution)/shard_map/pallas_call | solution.py:185
  (1 shorter events, 0.0 us)
Async XLA Ops:
  0.6 32.3 %slice-start = ((s8[6291456]{0:T(1024)(128)(4,1)}), s8[2097152]{0:T(1024)(128)(4,1)S(1)}, s32[]{:S(2)}) async-start(s8[6291456]{0:T(1024)(128)(4,1)} %bitcast.1), calls=%async_computation.4 | async-start | bytes 4194304
  19.5 13.5 %slice-start.1 = ((s8[6291456]{0:T(1024)(128)(4,1)}), s8[4194304]{0:T(1024)(128)(4,1)S(1)}, s32[]{:S(2)}) async-start(s8[6291456]{0:T(1024)(128)(4,1)} %bitcast.1), calls=%async_computation.5 | async-start | bytes 8388608
  19.5 13.5 %copy-start.1 = (bf16[1024,1024]{1,0:T(8,128)(2,1)S(1)}, bf16[1024,1024]{1,0:T(8,128)(2,1)}, u32[]{:S(2)}) copy-start(bf16[1024,1024]{1,0:T(8,128)(2,1)} %wv_ref.1) | copy-start | bytes 6291460
  19.5 13.5 %copy-start.2 = (bf16[1,32,1024]{2,1,0:T(8,128)(2,1)S(1)}, bf16[1,32,1024]{2,1,0:T(8,128)(2,1)}, u32[]{:S(2)}) copy-start(bf16[1,32,1024]{2,1,0:T(8,128)(2,1)} %x2_ref.1) | copy-start | bytes 196612
  19.5 13.5 %copy-start.3 = (f32[1024]{0:T(1024)S(1)}, f32[1024]{0:T(1024)}, u32[]{:S(2)}) copy-start(f32[1024]{0:T(1024)} %param.14) | copy-start | bytes 12292
  19.5 1.5 %collective-permute-start = (bf16[16,48,128]{2,1,0:T(8,128)(2,1)S(1)}, bf16[16,48,128]{2,1,0:T(8,128)(2,1)S(1)}, u32[]{:S(2)}, u32[]{:S(2)}) collective-permute-start(bf16[16,48,128]{2,1,0:T(8,128)(2,1)S(1)} %all_to_all.20.mine_ref), channel_id=1, source_target_pairs={{0,1},{1,0},{2,3},{3,2},{4,5},{5,4},{6,7},{7,6},{8,9},{9,8},{10,11... | collective-permute-start | bytes 589832 | tf_op jit(solution)/shard_map/ppermute | solution.py:207
  45.6 13.2 %copy-start = (bf16[1024,1024]{1,0:T(8,128)(2,1)S(1)}, bf16[1024,1024]{1,0:T(8,128)(2,1)}, u32[]{:S(2)}) copy-start(bf16[1024,1024]{1,0:T(8,128)(2,1)} %wout_ref.1) | copy-start | bytes 6291460
  45.6 1.4 %collective-permute-start.1 = (bf16[16,48,128]{2,1,0:T(8,128)(2,1)S(1)}, bf16[16,48,128]{2,1,0:T(8,128)(2,1)S(1)}, u32[]{:S(2)}, u32[]{:S(2)}) collective-permute-start(bf16[16,48,128]{2,1,0:T(8,128)(2,1)S(1)} %all_to_all.22.mine_ref), channel_id=1, source_target_pairs={{0,1},{1,0},{2,3},{3,2},{4,5},{5,4},{6,7},{7,6},{8,9},{9,8},{10,11... | collective-permute-start | bytes 589832 | tf_op jit(solution)/shard_map/ppermute | solution.py:207

commit v4 on v2

--- a/solution.py
+++ b/solution.py
@@ -108,6 +108,8 @@
 
 
 GROUP = ("view", "chip")
+NEAR = 4
+FAR = HEADS // NEAR
 
 
 def place():
@@ -122,15 +124,17 @@
         packed_ref[h, 0:rows, :] = jnp.concatenate([k[:, cols], v[:, cols]], axis=-1)
         packed_ref[h, rows : rows + half, :] = jnp.concatenate([q[:half, cols], q[half:, cols]], axis=-1)
     me = place()
-    for d in range(HEADS):
-        out_refs[d][...] = packed_ref[me ^ d]
-
-
-def unpack_rows(got_refs, packed_ref):
+    for far in range(FAR):
+        for near in range(NEAR):
+            out_refs[far][near] = packed_ref[me ^ (far * NEAR + near)]
+
+
+def unpack_rows(got_refs, line_ref):
     me = place()
-    for d in range(HEADS):
-        packed_ref[me ^ d] = got_refs[d][...].astype(jnp.float32)
-    pieces = [packed_ref[h] for h in range(HEADS)]
+    for far in range(FAR):
+        for near in range(NEAR):
+            line_ref[me ^ (far * NEAR + near)] = got_refs[near][far].astype(jnp.float32)
+    pieces = [line_ref[h] for h in range(HEADS)]
     top = jnp.concatenate([p[:, :HD] for p in pieces], axis=-1)
     low = jnp.concatenate([p[:, HD:] for p in pieces], axis=-1)
     return jnp.concatenate([top, low], axis=0)
@@ -141,7 +145,7 @@
 
 
 def pack_kernel(q_hbm, k_hbm, v_hbm, *refs):
-    out_refs, (q_ref, k_ref, v_ref, packed_ref, sems) = refs[:HEADS], refs[HEADS:]
+    out_refs, (q_ref, k_ref, v_ref, packed_ref, sems) = refs[:FAR], refs[FAR:]
     copies = [
         pltpu.make_async_copy(src, dst, sems.at[i])
         for i, (src, dst) in enumerate(((q_hbm, q_ref), (k_hbm, k_ref), (v_hbm, v_ref)))
@@ -153,24 +157,32 @@
     pack_heads(packed_ref, out_refs, q_ref[0], k_ref[0], v_ref[0])
 
 
+def turn_kernel(*refs):
+    in_refs, out_refs = refs[:FAR], refs[FAR:]
+    for far in range(FAR):
+        for near in range(NEAR):
+            out_refs[near][far] = in_refs[far][near]
+
+
 def collect_kernel(*refs):
-    out_ref = refs[HEADS]
+    got_refs, out_ref = refs[:NEAR], refs[NEAR]
     rows = out_ref.shape[0] // HEADS
-    for d in range(HEADS):
-        out_ref[d * rows : (d + 1) * rows, :] = refs[d][0:rows, :]
+    for near in range(NEAR):
+        for far in range(FAR):
+            d = far * NEAR + near
+            out_ref[d * rows : (d + 1) * rows, :] = got_refs[near][far, 0:rows, :]
 
 
 def attend_kernel(mine_ref, other_ref, *refs):
-    got_refs, out_refs = refs[:HEADS], refs[HEADS:]
-    lines = got_refs[0].shape[0]
+    got_refs, out_refs = refs[:NEAR], refs[NEAR:]
+    lines = got_refs[0].shape[1]
     rows = lines * 2 // 3
     half = rows // 2
     kv = jnp.concatenate([mine_ref[...], other_ref[...]], axis=0)
     keys = kv[:, :HD]
     vals = kv[:, HD:]
-    step = 4
-    for s in range(0, HEADS, step):
-        packed = jnp.concatenate([got_refs[d][rows:lines, :] for d in range(s, s + step)], axis=0)
+    for far in range(FAR):
+        packed = jnp.concatenate([got_refs[near][far, rows:lines, :] for near in range(NEAR)], axis=0)
         queries = jnp.concatenate([packed[:, :HD], packed[:, HD:]], axis=0)
         scores = lax.dot_general(
             queries, keys, (((1,), (1,)), ((), ())), preferred_element_type=jnp.float32
@@ -181,16 +193,14 @@
         summed = jnp.dot(weights.astype(jnp.bfloat16), vals, preferred_element_type=jnp.float32)
         attn = (summed / total).astype(jnp.bfloat16)
         n = attn.shape[0] // 2
-        lined = jnp.concatenate([attn[:n], attn[n:]], axis=-1)
-        for i in range(step):
-            out_refs[s + i][...] = lined[i * half : (i + 1) * half]
+        out_refs[far][...] = jnp.concatenate([attn[:n], attn[n:]], axis=-1).reshape(NEAR, half, 2 * HD)
 
 
 def middle_kernel(x2_ref, wv_ref, gain_ref, wqkv_ref, *refs):
     got_refs, (feats_ref, *out_refs), (line_ref, packed_ref) = (
-        refs[:HEADS],
-        refs[HEADS : 2 * HEADS + 1],
-        refs[2 * HEADS + 1 :],
+        refs[:NEAR],
+        refs[NEAR : NEAR + 1 + FAR],
+        refs[NEAR + 1 + FAR :],
     )
     feats = unit(unpack_rows(got_refs, line_ref))
     feats_ref[0] = feats
@@ -206,35 +216,42 @@
 
 
 def last_kernel(wout_ref, *refs):
-    got_refs, out_ref, line_ref = refs[:HEADS], refs[HEADS], refs[HEADS + 1]
+    got_refs, out_ref, line_ref = refs[:NEAR], refs[NEAR], refs[NEAR + 1]
     rows = unit(unpack_rows(got_refs, line_ref)).astype(jnp.bfloat16)
     out_ref[0] = jnp.dot(rows, wout_ref[...], preferred_element_type=jnp.float32)
 
 
-def call(body, outs, args, scratch=(), limit=16 << 20, space=pltpu.VMEM):
+def call(body, outs, args, scratch=(), limit=16 << 20, space=pltpu.VMEM, cost=None):
     return pl.pallas_call(
         body,
         out_shape=outs,
         in_specs=[pl.BlockSpec(memory_space=space)] * len(args),
         out_specs=jax.tree.map(lambda _: VMEM, outs),
         scratch_shapes=list(scratch),
+        cost_estimate=cost,
         compiler_params=pltpu.CompilerParams(vmem_limit_bytes=limit),
     )(*args)
 
 
+def send(pieces, step):
+    got = list(pieces)
+    for i in range(len(pieces) - 1, 0, -1):
+        got[i] = lax.ppermute(pieces[i], GROUP, [(p, p ^ (i * step)) for p in range(HEADS)])
+    return got
+
+
 def trade(pieces):
-    got = list(pieces)
-    for d in sorted(range(1, HEADS), reverse=True):
-        got[d] = lax.ppermute(pieces[d], GROUP, [(i, i ^ d) for i in range(HEADS)])
-    return got
+    got = send(pieces, NEAR)
+    turned = [jax.ShapeDtypeStruct((FAR, *pieces[0].shape[1:]), pieces[0].dtype)] * NEAR
+    return send(call(turn_kernel, turned, got), 1)
 
 
 def by_heads(q1, k1, v1, nbr, x2, w_view_out, norm_gain, w_qkv, w_out):
     rows = q1.shape[1]
     lines = rows * 3 // 2
     half = rows // 2
-    packed = [jax.ShapeDtypeStruct((lines, 2 * HD), jnp.bfloat16)] * HEADS
-    halves = [jax.ShapeDtypeStruct((half, 2 * HD), jnp.bfloat16)] * HEADS
+    packed = [jax.ShapeDtypeStruct((NEAR, lines, 2 * HD), jnp.bfloat16)] * FAR
+    halves = [jax.ShapeDtypeStruct((NEAR, half, 2 * HD), jnp.bfloat16)] * FAR
     keyvals = jax.ShapeDtypeStruct((HEADS * rows, 2 * HD), jnp.bfloat16)
     wide = jax.ShapeDtypeStruct((1, rows, HEADS * HD), jnp.float32)
     packed_scratch = pltpu.VMEM((HEADS, lines, 2 * HD), jnp.bfloat16)
@@ -245,14 +262,16 @@
         mine = call(collect_kernel, keyvals, got)
         cores = lax.axis_size("core")
         other = lax.ppermute(mine, "core", [(i, (i + 1) % cores) for i in range(cores)])
-        return trade(call(attend_kernel, halves, (mine, other, *got)))
+        cost = pl.CostEstimate(flops=16 << 30, bytes_accessed=40 << 20, transcendentals=0)
+        return trade(call(attend_kernel, halves, (mine, other, *got), cost=cost))
 
     pieces = call(
         pack_kernel,
         packed,
         (q1, k1, v1),
         [pltpu.VMEM(q1.shape, q1.dtype)] * 3 + [packed_scratch, pltpu.SemaphoreType.DMA((3,))],
-        space=pl.ANY,
+        space=pltpu.HBM,
+        limit=48 << 20,
     )
     feats, *pieces = call(
         middle_kernel,

time: 145 us -> 76.2 us (0.53)
  starting transfers between devices: 107 us -> 33.1 us
  waiting for transfers between devices: 20.6 us -> 32 us
  local copies, waits for them, and re-layouts: 8.41 us -> 2.55 us
    ppermute x60 -> x24, starting transfers between devices: 107 us -> 33 us  [send(): lax.ppermute(pieces[i], GROUP, [(p, p ^ i * step) for p in range(HEADS)])]
    ppermute x60 -> x24, waiting for transfers between devices: 17.9 us -> 29.3 us  [send(): lax.ppermute(pieces[i], GROUP, [(p, p ^ i * step) for p in range(HEADS)])]
    unnamed x16 -> x18, local copies, waits for them, and re-layouts: 8.41 us -> 2.55 us
    pallas_call x7 -> x11, Pallas kernels: 7.07 us -> 7.49 us  [call(): pl.pallas_call(body, out_shape=outs, in_specs=[pl.BlockSpec(memory_space=...]
  transfers between devices with their start and end apart: 62 -> 26, of which waited for: 12 -> 22; matrix products, arithmetic and copies ran while one was open for 0% -> 0% of each run, Pallas kernels for 0% -> 0%
where the time goes in v4:
time: 76.2 us; the launch traced here: 76 us
  starting transfers between devices  33.1 us (43%)
  waiting for transfers between devices  32 us (42%)
  Pallas kernels  7.49 us (10%)
  local copies, waits for them, and re-layouts  2.55 us (3%)
  between operations  0.79 us (1%)
    ppermute x24, starting transfers between devices, send(): lax.ppermute(pieces[i], GROUP, [(p, p ^ i * step) for p in range(HEADS)])  33 us
    ppermute x24, waiting for transfers between devices, send(): lax.ppermute(pieces[i], GROUP, [(p, p ^ i * step) for p in range(HEADS)])  29.3 us
    pallas_call x11, Pallas kernels, call(): pl.pallas_call(body, out_shape=outs, in_specs=[pl.BlockSpec(memory_space=...  7.49 us
    ppermute x2, waiting for transfers between devices, attention(): lax.ppermute(mine, 'core', [(i, (i + 1) % cores) for i in range(cores)])  2.67 us
    unnamed x18, local copies, waits for them, and re-layouts  2.55 us
  transfers between devices with their start and end apart: 26, of which 22 were waited for; matrix products, arithmetic and copies ran while one was open for 0% of the time, Pallas kernels for 0%

profile of v4, /device:TPU:0, one launch (start us, length us, event | category | flops | bytes accessed | tf_op | source)
XLA Modules:
  0.0 76.0 jit_solution(7767556354210478194)
XLA Ops:
  0.6 0.8 %copy-done.3 = bf16[1,32,1024]{2,1,0:T(8,128)(2,1)S(1)} copy-done((bf16[1,32,1024]{2,1,0:T(8,128)(2,1)S(1)}, bf16[1,32,1024]{2,1,0:T(8,128)(2,1)}, u32[]{:S(2)}) %copy-start.3) | copy-done | bytes 65560
  1.5 0.8 %copy-done.4 = bf16[1,32,1024]{2,1,0:T(8,128)(2,1)S(1)} copy-done((bf16[1,32,1024]{2,1,0:T(8,128)(2,1)S(1)}, bf16[1,32,1024]{2,1,0:T(8,128)(2,1)}, u32[]{:S(2)}) %copy-start.4) | copy-done | bytes 65560
  2.3 0.8 %copy-done.5 = bf16[1,32,1024]{2,1,0:T(8,128)(2,1)S(1)} copy-done((bf16[1,32,1024]{2,1,0:T(8,128)(2,1)S(1)}, bf16[1,32,1024]{2,1,0:T(8,128)(2,1)}, u32[]{:S(2)}) %copy-start.5) | copy-done | bytes 65560
  3.2 0.4 shard_map.95
  3.5 3.1 %collective-permute-start = (bf16[4,48,128]{2,1,0:T(8,128)(2,1)S(1)}, bf16[4,48,128]{2,1,0:T(8,128)(2,1)S(1)}, u32[]{:S(2)}, u32[]{:S(2)}) collective-permute-start(bf16[4,48,128]{2,1,0:T(8,128)(2,1)S(1)} %get-tuple-element.36), channel_id=1, source_target_pairs={{0,8},{2,10},{4,12},{6,14},{8,0},{10,2},{12,4},{14,6},{16,24},{18,... | collective-permute-start | bytes 147464 | tf_op jit(solution)/shard_map/ppermute | solution.py:239
  6.6 2.6 %collective-permute-start.1 = (bf16[4,48,128]{2,1,0:T(8,128)(2,1)S(1)}, bf16[4,48,128]{2,1,0:T(8,128)(2,1)S(1)}, u32[]{:S(2)}, u32[]{:S(2)}) collective-permute-start(bf16[4,48,128]{2,1,0:T(8,128)(2,1)S(1)} %get-tuple-element.37), channel_id=1, source_target_pairs={{0,16},{2,18},{4,20},{6,22},{8,24},{10,26},{12,28},{14,30},{16,0},... | collective-permute-start | bytes 147464 | tf_op jit(solution)/shard_map/ppermute | solution.py:239
  9.2 0.0 collective-permute-start.2
  9.2 0.0 collective-permute-done.refs_1_
  9.2 3.3 %collective-permute-done.1.refs_2_ = bf16[4,48,128]{2,1,0:T(8,128)(2,1)S(1)} collective-permute-done((bf16[4,48,128]{2,1,0:T(8,128)(2,1)S(1)}, bf16[4,48,128]{2,1,0:T(8,128)(2,1)S(1)}, u32[]{:S(2)}, u32[]{:S(2)}) %collective-permute-start.1) | collective-permute-done | bytes 49184 | tf_op jit(solution)/shard_map/ppermute | solution.py:239
  12.6 2.6 %collective-permute-done.2.refs_3_ = bf16[4,48,128]{2,1,0:T(8,128)(2,1)S(1)} collective-permute-done((bf16[4,48,128]{2,1,0:T(8,128)(2,1)S(1)}, bf16[4,48,128]{2,1,0:T(8,128)(2,1)S(1)}, u32[]{:S(2)}, u32[]{:S(2)}) %collective-permute-start.2) | collective-permute-done | bytes 49184 | tf_op jit(solution)/shard_map/ppermute | solution.py:239
  15.1 1.6 %collective-permute-start.3 = (bf16[4,48,128]{2,1,0:T(8,128)(2,1)S(1)}, bf16[4,48,128]{2,1,0:T(8,128)(2,1)S(1)}, u32[]{:S(2)}, u32[]{:S(2)}) collective-permute-start(bf16[4,48,128]{2,1,0:T(8,128)(2,1)S(1)} %get-tuple-element.40), channel_id=1, source_target_pairs={{0,2},{2,0},{4,6},{6,4},{8,10},{10,8},{12,14},{14,12},{16,18},{18,... | collective-permute-start | bytes 147464 | tf_op jit(solution)/shard_map/ppermute | solution.py:239
  16.7 1.5 %collective-permute-start.4 = (bf16[4,48,128]{2,1,0:T(8,128)(2,1)S(1)}, bf16[4,48,128]{2,1,0:T(8,128)(2,1)S(1)}, u32[]{:S(2)}, u32[]{:S(2)}) collective-permute-start(bf16[4,48,128]{2,1,0:T(8,128)(2,1)S(1)} %get-tuple-element.41), channel_id=1, source_target_pairs={{0,4},{2,6},{4,0},{6,2},{8,12},{10,14},{12,8},{14,10},{16,20},{18,... | collective-permute-start | bytes 147464 | tf_op jit(solution)/shard_map/ppermute | solution.py:239
  18.2 0.5 collective-permute-start.5
  18.7 0.8 %collective-permute-done.3.refs_1_ = bf16[4,48,128]{2,1,0:T(8,128)(2,1)S(1)} collective-permute-done((bf16[4,48,128]{2,1,0:T(8,128)(2,1)S(1)}, bf16[4,48,128]{2,1,0:T(8,128)(2,1)S(1)}, u32[]{:S(2)}, u32[]{:S(2)}) %collective-permute-start.3) | collective-permute-done | bytes 49184 | tf_op jit(solution)/shard_map/ppermute | solution.py:239
  19.5 1.3 %collective-permute-done.4.refs_2_ = bf16[4,48,128]{2,1,0:T(8,128)(2,1)S(1)} collective-permute-done((bf16[4,48,128]{2,1,0:T(8,128)(2,1)S(1)}, bf16[4,48,128]{2,1,0:T(8,128)(2,1)S(1)}, u32[]{:S(2)}, u32[]{:S(2)}) %collective-permute-start.4) | collective-permute-done | bytes 49184 | tf_op jit(solution)/shard_map/ppermute | solution.py:239
  20.8 2.4 %collective-permute-done.5.refs_3_ = bf16[4,48,128]{2,1,0:T(8,128)(2,1)S(1)} collective-permute-done((bf16[4,48,128]{2,1,0:T(8,128)(2,1)S(1)}, bf16[4,48,128]{2,1,0:T(8,128)(2,1)S(1)}, u32[]{:S(2)}, u32[]{:S(2)}) %collective-permute-start.5) | collective-permute-done | bytes 49184 | tf_op jit(solution)/shard_map/ppermute | solution.py:239
  23.2 0.0 slice-start.1
  23.2 0.0 copy-start.1
  23.2 0.0 copy-start.2
  23.2 0.0 copy-start.6
  23.3 0.1 collective-permute-start.6
  23.3 1.3 %collective-permute-done.6.other_ref = bf16[512,128]{1,0:T(8,128)(2,1)S(1)} collective-permute-done((bf16[512,128]{1,0:T(8,128)(2,1)S(1)}, bf16[512,128]{1,0:T(8,128)(2,1)S(1)}, u32[]{:S(2)}, u32[]{:S(2)}) %collective-permute-start.6) | collective-permute-done | bytes 131104 | tf_op jit(solution)/shard_map/ppermute | solution.py:264
  24.7 1.7 %shard_map.98 = (bf16[4,16,128]{2,1,0:T(8,128)(2,1)S(1)}, bf16[4,16,128]{2,1,0:T(8,128)(2,1)S(1)}, bf16[4,16,128]{2,1,0:T(8,128)(2,1)S(1)}, bf16[4,16,128]{2,1,0:T(8,128)(2,1)S(1)}) custom-call(bf16[512,128]{1,0:T(8,128)(2,1)S(1)} %shard_map.97.mine_ref, bf16[512,128]{1,0:T(8,128)(2,1)S(1)} %collective-permute-done.6.other_ref, ...), custom_call_target="tpu_custom_call" | custom-call | flops 17179869184 | bytes 41943040 | tf_op jit(solution)/shard_map/pallas_call | solution.py:225
  26.4 0.0 collective-permute-start.7
  26.4 1.3 %collective-permute-start.8 = (bf16[4,16,128]{2,1,0:T(8,128)(2,1)S(1)}, bf16[4,16,128]{2,1,0:T(8,128)(2,1)S(1)}, u32[]{:S(2)}, u32[]{:S(2)}) collective-permute-start(bf16[4,16,128]{2,1,0:T(8,128)(2,1)S(1)} %get-tuple-element.45), channel_id=1, source_target_pairs={{0,16},{2,18},{4,20},{6,22},{8,24},{10,26},{12,28},{14,30},{16,0},... | collective-permute-start | bytes 49160 | tf_op jit(solution)/shard_map/ppermute | solution.py:239
  27.7 3.1 %collective-permute-start.9 = (bf16[4,16,128]{2,1,0:T(8,128)(2,1)S(1)}, bf16[4,16,128]{2,1,0:T(8,128)(2,1)S(1)}, u32[]{:S(2)}, u32[]{:S(2)}) collective-permute-start(bf16[4,16,128]{2,1,0:T(8,128)(2,1)S(1)} %get-tuple-element.46), channel_id=1, source_target_pairs={{0,24},{2,26},{4,28},{6,30},{8,16},{10,18},{12,20},{14,22},{16,8},... | collective-permute-start | bytes 49160 | tf_op jit(solution)/shard_map/ppermute | solution.py:239
  30.8 0.0 collective-permute-done.7.refs_1_
  30.8 0.3 collective-permute-done.8.refs_2_
  31.1 2.1 %collective-permute-done.9.refs_3_ = bf16[4,16,128]{2,1,0:T(8,128)(2,1)S(1)} collective-permute-done((bf16[4,16,128]{2,1,0:T(8,128)(2,1)S(1)}, bf16[4,16,128]{2,1,0:T(8,128)(2,1)S(1)}, u32[]{:S(2)}, u32[]{:S(2)}) %collective-permute-start.9) | collective-permute-done | bytes 16416 | tf_op jit(solution)/shard_map/ppermute | solution.py:239
  33.2 0.5 collective-permute-start.10
  33.8 0.5 collective-permute-start.11
  34.3 2.4 %collective-permute-start.12 = (bf16[4,16,128]{2,1,0:T(8,128)(2,1)S(1)}, bf16[4,16,128]{2,1,0:T(8,128)(2,1)S(1)}, u32[]{:S(2)}, u32[]{:S(2)}) collective-permute-start(bf16[4,16,128]{2,1,0:T(8,128)(2,1)S(1)} %get-tuple-element.50), channel_id=1, source_target_pairs={{0,6},{2,4},{4,2},{6,0},{8,14},{10,12},{12,10},{14,8},{16,22},{18,... | collective-permute-start | bytes 49160 | tf_op jit(solution)/shard_map/ppermute | solution.py:239
  36.7 0.2 collective-permute-done.10.refs_1_
  37.0 0.5 collective-permute-done.11.refs_2_
  37.5 1.4 %collective-permute-done.12.refs_3_ = bf16[4,16,128]{2,1,0:T(8,128)(2,1)S(1)} collective-permute-done((bf16[4,16,128]{2,1,0:T(8,128)(2,1)S(1)}, bf16[4,16,128]{2,1,0:T(8,128)(2,1)S(1)}, u32[]{:S(2)}, u32[]{:S(2)}) %collective-permute-start.12) | collective-permute-done | bytes 16416 | tf_op jit(solution)/shard_map/ppermute | solution.py:239
  39.0 2.4 %shard_map.100 = (f32[1,32,1024]{2,1,0:T(8,128)}, bf16[4,48,128]{2,1,0:T(8,128)(2,1)S(1)}, bf16[4,48,128]{2,1,0:T(8,128)(2,1)S(1)}, bf16[4,48,128]{2,1,0:T(8,128)(2,1)S(1)}, bf16[4,48,128]{2,1,0:T(8,128)(2,1)S(1)}) custom-call(bf16[1,32,1024]{2,1,0:T(8,128)(2,1)S(1)} %copy-done.2, bf16[1024,1024]{1,0:T(8,128)(2,1)S(1)} %copy-done.1, f32[1,1024]{1,0:T(1,128)S(1)} %bitcast.3, ...), custom_call_target="tpu_custom_call" | custom-call | tf_op jit(solution)/shard_map/pallas_call | solution.py:225
  41.4 0.0 collective-permute-start.13
  41.4 3.7 %collective-permute-start.14 = (bf16[4,48,128]{2,1,0:T(8,128)(2,1)S(1)}, bf16[4,48,128]{2,1,0:T(8,128)(2,1)S(1)}, u32[]{:S(2)}, u32[]{:S(2)}) collective-permute-start(bf16[4,48,128]{2,1,0:T(8,128)(2,1)S(1)} %get-tuple-element.54), channel_id=1, source_target_pairs={{0,16},{2,18},{4,20},{6,22},{8,24},{10,26},{12,28},{14,30},{16,0},... | collective-permute-start | bytes 147464 | tf_op jit(solution)/shard_map/ppermute | solution.py:239
  45.0 0.7 collective-permute-start.15
  45.8 0.0 collective-permute-done.13.refs_1_
  45.8 1.3 %collective-permute-done.14.refs_2_ = bf16[4,48,128]{2,1,0:T(8,128)(2,1)S(1)} collective-permute-done((bf16[4,48,128]{2,1,0:T(8,128)(2,1)S(1)}, bf16[4,48,128]{2,1,0:T(8,128)(2,1)S(1)}, u32[]{:S(2)}, u32[]{:S(2)}) %collective-permute-start.14) | collective-permute-done | bytes 49184 | tf_op jit(solution)/shard_map/ppermute | solution.py:239
  47.1 3.8 %collective-permute-done.15.refs_3_ = bf16[4,48,128]{2,1,0:T(8,128)(2,1)S(1)} collective-permute-done((bf16[4,48,128]{2,1,0:T(8,128)(2,1)S(1)}, bf16[4,48,128]{2,1,0:T(8,128)(2,1)S(1)}, u32[]{:S(2)}, u32[]{:S(2)}) %collective-permute-start.15) | collective-permute-done | bytes 49184 | tf_op jit(solution)/shard_map/ppermute | solution.py:239
  50.9 1.6 %collective-permute-start.16 = (bf16[4,48,128]{2,1,0:T(8,128)(2,1)S(1)}, bf16[4,48,128]{2,1,0:T(8,128)(2,1)S(1)}, u32[]{:S(2)}, u32[]{:S(2)}) collective-permute-start(bf16[4,48,128]{2,1,0:T(8,128)(2,1)S(1)} %get-tuple-element.57), channel_id=1, source_target_pairs={{0,2},{2,0},{4,6},{6,4},{8,10},{10,8},{12,14},{14,12},{16,18},{18,... | collective-permute-start | bytes 147464 | tf_op jit(solution)/shard_map/ppermute | solution.py:239
  52.5 1.5 %collective-permute-start.17 = (bf16[4,48,128]{2,1,0:T(8,128)(2,1)S(1)}, bf16[4,48,128]{2,1,0:T(8,128)(2,1)S(1)}, u32[]{:S(2)}, u32[]{:S(2)}) collective-permute-start(bf16[4,48,128]{2,1,0:T(8,128)(2,1)S(1)} %get-tuple-element.58), channel_id=1, source_target_pairs={{0,4},{2,6},{4,0},{6,2},{8,12},{10,14},{12,8},{14,10},{16,20},{18,... | collective-permute-start | bytes 147464 | tf_op jit(solution)/shard_map/ppermute | solution.py:239
  54.0 0.5 collective-permute-start.18
  54.5 0.6 collective-permute-done.16.refs_1_
  55.1 1.5 %collective-permute-done.17.refs_2_ = bf16[4,48,128]{2,1,0:T(8,128)(2,1)S(1)} collective-permute-done((bf16[4,48,128]{2,1,0:T(8,128)(2,1)S(1)}, bf16[4,48,128]{2,1,0:T(8,128)(2,1)S(1)}, u32[]{:S(2)}, u32[]{:S(2)}) %collective-permute-start.17) | collective-permute-done | bytes 49184 | tf_op jit(solution)/shard_map/ppermute | solution.py:239
  56.6 2.4 %collective-permute-done.18.refs_3_ = bf16[4,48,128]{2,1,0:T(8,128)(2,1)S(1)} collective-permute-done((bf16[4,48,128]{2,1,0:T(8,128)(2,1)S(1)}, bf16[4,48,128]{2,1,0:T(8,128)(2,1)S(1)}, u32[]{:S(2)}, u32[]{:S(2)}) %collective-permute-start.18) | collective-permute-done | bytes 49184 | tf_op jit(solution)/shard_map/ppermute | solution.py:239
  59.0 0.0 copy-start
  59.0 0.1 collective-permute-start.19
  59.1 1.3 %collective-permute-done.19.other_ref = bf16[512,128]{1,0:T(8,128)(2,1)S(1)} collective-permute-done((bf16[512,128]{1,0:T(8,128)(2,1)S(1)}, bf16[512,128]{1,0:T(8,128)(2,1)S(1)}, u32[]{:S(2)}, u32[]{:S(2)}) %collective-permute-start.19) | collective-permute-done | bytes 131104 | tf_op jit(solution)/shard_map/ppermute | solution.py:264
  60.4 1.7 %shard_map.103 = (bf16[4,16,128]{2,1,0:T(8,128)(2,1)S(1)}, bf16[4,16,128]{2,1,0:T(8,128)(2,1)S(1)}, bf16[4,16,128]{2,1,0:T(8,128)(2,1)S(1)}, bf16[4,16,128]{2,1,0:T(8,128)(2,1)S(1)}) custom-call(bf16[512,128]{1,0:T(8,128)(2,1)S(1)} %shard_map.102.mine_ref, bf16[512,128]{1,0:T(8,128)(2,1)S(1)} %collective-permute-done.19.other_ref, ...), custom_call_target="tpu_custom_call" | custom-call | flops 17179869184 | bytes 41943040 | tf_op jit(solution)/shard_map/pallas_call | solution.py:225
  62.1 0.0 collective-permute-start.20
  62.2 1.3 %collective-permute-start.21 = (bf16[4,16,128]{2,1,0:T(8,128)(2,1)S(1)}, bf16[4,16,128]{2,1,0:T(8,128)(2,1)S(1)}, u32[]{:S(2)}, u32[]{:S(2)}) collective-permute-start(bf16[4,16,128]{2,1,0:T(8,128)(2,1)S(1)} %get-tuple-element.62), channel_id=1, source_target_pairs={{0,16},{2,18},{4,20},{6,22},{8,24},{10,26},{12,28},{14,30},{16,0},... | collective-permute-start | bytes 49160 | tf_op jit(solution)/shard_map/ppermute | solution.py:239
  63.5 3.1 %collective-permute-start.22 = (bf16[4,16,128]{2,1,0:T(8,128)(2,1)S(1)}, bf16[4,16,128]{2,1,0:T(8,128)(2,1)S(1)}, u32[]{:S(2)}, u32[]{:S(2)}) collective-permute-start(bf16[4,16,128]{2,1,0:T(8,128)(2,1)S(1)} %get-tuple-element.63), channel_id=1, source_target_pairs={{0,24},{2,26},{4,28},{6,30},{8,16},{10,18},{12,20},{14,22},{16,8},... | collective-permute-start | bytes 49160 | tf_op jit(solution)/shard_map/ppermute | solution.py:239
  66.6 0.3 collective-permute-done.21.refs_2_
  66.9 2.1 %collective-permute-done.22.refs_3_ = bf16[4,16,128]{2,1,0:T(8,128)(2,1)S(1)} collective-permute-done((bf16[4,16,128]{2,1,0:T(8,128)(2,1)S(1)}, bf16[4,16,128]{2,1,0:T(8,128)(2,1)S(1)}, u32[]{:S(2)}, u32[]{:S(2)}) %collective-permute-start.22) | collective-permute-done | bytes 16416 | tf_op jit(solution)/shard_map/ppermute | solution.py:239
  69.0 0.5 collective-permute-start.23
  69.5 0.5 collective-permute-start.24
  70.0 2.4 %collective-permute-start.25 = (bf16[4,16,128]{2,1,0:T(8,128)(2,1)S(1)}, bf16[4,16,128]{2,1,0:T(8,128)(2,1)S(1)}, u32[]{:S(2)}, u32[]{:S(2)}) collective-permute-start(bf16[4,16,128]{2,1,0:T(8,128)(2,1)S(1)} %get-tuple-element.67), channel_id=1, source_target_pairs={{0,6},{2,4},{4,2},{6,0},{8,14},{10,12},{12,10},{14,8},{16,22},{18,... | collective-permute-start | bytes 49160 | tf_op jit(solution)/shard_map/ppermute | solution.py:239
  72.5 0.2 collective-permute-done.23.refs_1_
  72.7 0.5 collective-permute-done.24.refs_2_
  73.3 1.4 %collective-permute-done.25.refs_3_ = bf16[4,16,128]{2,1,0:T(8,128)(2,1)S(1)} collective-permute-done((bf16[4,16,128]{2,1,0:T(8,128)(2,1)S(1)}, bf16[4,16,128]{2,1,0:T(8,128)(2,1)S(1)}, u32[]{:S(2)}, u32[]{:S(2)}) %collective-permute-start.25) | collective-permute-done | bytes 16416 | tf_op jit(solution)/shard_map/ppermute | solution.py:239
  74.7 1.3 %shard_map.105 = f32[1,32,1024]{2,1,0:T(8,128)} custom-call(bf16[1024,1024]{1,0:T(8,128)(2,1)S(1)} %copy-done, bf16[4,16,128]{2,1,0:T(8,128)(2,1)S(1)} %get-tuple-element.64.refs_0_, bf16[4,16,128]{2,1,0:T(8,128)(2,1)S(1)} %collective-permute-done.23.refs_1_, bf16[4,16,128]{2,1,0:T(8,128)(2,1)S(1)} %collective-permute-done.24.refs_2_, ...), custom_call_target="tpu_custom_call" | custom-call | tf_op jit(solution)/shard_map/pallas_call | solution.py:225
  (18 shorter events, 0.1 us)
Async XLA Ops:
  0.6 0.8 %copy-start.3 = (bf16[1,32,1024]{2,1,0:T(8,128)(2,1)S(1)}, bf16[1,32,1024]{2,1,0:T(8,128)(2,1)}, u32[]{:S(2)}) copy-start(bf16[1,32,1024]{2,1,0:T(8,128)(2,1)} %q_hbm.1) | copy-start | bytes 196612
  1.5 0.8 %copy-start.4 = (bf16[1,32,1024]{2,1,0:T(8,128)(2,1)S(1)}, bf16[1,32,1024]{2,1,0:T(8,128)(2,1)}, u32[]{:S(2)}) copy-start(bf16[1,32,1024]{2,1,0:T(8,128)(2,1)} %k_hbm.1) | copy-start | bytes 196612
  2.3 0.8 %copy-start.5 = (bf16[1,32,1024]{2,1,0:T(8,128)(2,1)S(1)}, bf16[1,32,1024]{2,1,0:T(8,128)(2,1)}, u32[]{:S(2)}) copy-start(bf16[1,32,1024]{2,1,0:T(8,128)(2,1)} %v_hbm.1) | copy-start | bytes 196612
  3.5 5.7 %collective-permute-start = (bf16[4,48,128]{2,1,0:T(8,128)(2,1)S(1)}, bf16[4,48,128]{2,1,0:T(8,128)(2,1)S(1)}, u32[]{:S(2)}, u32[]{:S(2)}) collective-permute-start(bf16[4,48,128]{2,1,0:T(8,128)(2,1)S(1)} %get-tuple-element.36), channel_id=1, source_target_pairs={{0,8},{2,10},{4,12},{6,14},{8,0},{10,2},{12,4},{14,6},{16,24},{18,... | collective-permute-start | bytes 147464 | tf_op jit(solution)/shard_map/ppermute | solution.py:239
  6.6 5.9 %collective-permute-start.1 = (bf16[4,48,128]{2,1,0:T(8,128)(2,1)S(1)}, bf16[4,48,128]{2,1,0:T(8,128)(2,1)S(1)}, u32[]{:S(2)}, u32[]{:S(2)}) collective-permute-start(bf16[4,48,128]{2,1,0:T(8,128)(2,1)S(1)} %get-tuple-element.37), channel_id=1, source_target_pairs={{0,16},{2,18},{4,20},{6,22},{8,24},{10,26},{12,28},{14,30},{16,0},... | collective-permute-start | bytes 147464 | tf_op jit(solution)/shard_map/ppermute | solution.py:239
  9.2 5.9 %collective-permute-start.2 = (bf16[4,48,128]{2,1,0:T(8,128)(2,1)S(1)}, bf16[4,48,128]{2,1,0:T(8,128)(2,1)S(1)}, u32[]{:S(2)}, u32[]{:S(2)}) collective-permute-start(bf16[4,48,128]{2,1,0:T(8,128)(2,1)S(1)} %get-tuple-element.38), channel_id=1, source_target_pairs={{0,24},{2,26},{4,28},{6,30},{8,16},{10,18},{12,20},{14,22},{16,8},... | collective-permute-start | bytes 147464 | tf_op jit(solution)/shard_map/ppermute | solution.py:239
  15.1 4.3 %collective-permute-start.3 = (bf16[4,48,128]{2,1,0:T(8,128)(2,1)S(1)}, bf16[4,48,128]{2,1,0:T(8,128)(2,1)S(1)}, u32[]{:S(2)}, u32[]{:S(2)}) collective-permute-start(bf16[4,48,128]{2,1,0:T(8,128)(2,1)S(1)} %get-tuple-element.40), channel_id=1, source_target_pairs={{0,2},{2,0},{4,6},{6,4},{8,10},{10,8},{12,14},{14,12},{16,18},{18,... | collective-permute-start | bytes 147464 | tf_op jit(solution)/shard_map/ppermute | solution.py:239
  16.7 4.1 %collective-permute-start.4 = (bf16[4,48,128]{2,1,0:T(8,128)(2,1)S(1)}, bf16[4,48,128]{2,1,0:T(8,128)(2,1)S(1)}, u32[]{:S(2)}, u32[]{:S(2)}) collective-permute-start(bf16[4,48,128]{2,1,0:T(8,128)(2,1)S(1)} %get-tuple-element.41), channel_id=1, source_target_pairs={{0,4},{2,6},{4,0},{6,2},{8,12},{10,14},{12,8},{14,10},{16,20},{18,... | collective-permute-start | bytes 147464 | tf_op jit(solution)/shard_map/ppermute | solution.py:239
  18.2 5.0 %collective-permute-start.5 = (bf16[4,48,128]{2,1,0:T(8,128)(2,1)S(1)}, bf16[4,48,128]{2,1,0:T(8,128)(2,1)S(1)}, u32[]{:S(2)}, u32[]{:S(2)}) collective-permute-start(bf16[4,48,128]{2,1,0:T(8,128)(2,1)S(1)} %get-tuple-element.42), channel_id=1, source_target_pairs={{0,6},{2,4},{4,2},{6,0},{8,14},{10,12},{12,10},{14,8},{16,22},{18,... | collective-permute-start | bytes 147464 | tf_op jit(solution)/shard_map/ppermute | solution.py:239
  23.2 15.7 %slice-start = ((s8[6291456]{0:T(1024)(128)(4,1)}), s8[4194304]{0:T(1024)(128)(4,1)S(1)}, s32[]{:S(2)}) async-start(s8[6291456]{0:T(1024)(128)(4,1)} %bitcast.1), calls=%async_computation | async-start | bytes 8388608
  23.2 15.7 %slice-start.1 = ((s8[6291456]{0:T(1024)(128)(4,1)}), s8[2097152]{0:T(1024)(128)(4,1)S(1)}, s32[]{:S(2)}) async-start(s8[6291456]{0:T(1024)(128)(4,1)} %bitcast.1), calls=%async_computation.1 | async-start | bytes 4194304
  23.2 15.7 %copy-start.1 = (bf16[1024,1024]{1,0:T(8,128)(2,1)S(1)}, bf16[1024,1024]{1,0:T(8,128)(2,1)}, u32[]{:S(2)}) copy-start(bf16[1024,1024]{1,0:T(8,128)(2,1)} %wv_ref.1) | copy-start | bytes 6291460
  23.2 15.7 %copy-start.2 = (bf16[1,32,1024]{2,1,0:T(8,128)(2,1)S(1)}, bf16[1,32,1024]{2,1,0:T(8,128)(2,1)}, u32[]{:S(2)}) copy-start(bf16[1,32,1024]{2,1,0:T(8,128)(2,1)} %x2_ref.1) | copy-start | bytes 196612
  23.2 15.7 %copy-start.6 = (f32[1024]{0:T(1024)S(1)}, f32[1024]{0:T(1024)}, u32[]{:S(2)}) copy-start(f32[1024]{0:T(1024)} %param.14) | copy-start | bytes 12292
  23.3 1.4 %collective-permute-start.6 = (bf16[512,128]{1,0:T(8,128)(2,1)S(1)}, bf16[512,128]{1,0:T(8,128)(2,1)S(1)}, u32[]{:S(2)}, u32[]{:S(2)}) collective-permute-start(bf16[512,128]{1,0:T(8,128)(2,1)S(1)} %shard_map.97.mine_ref), channel_id=1, source_target_pairs={{0,1},{1,0},{2,3},{3,2},{4,5},{5,4},{6,7},{7,6},{8,9},{9,8},{10,11... | collective-permute-start | bytes 393224 | tf_op jit(solution)/shard_map/ppermute | solution.py:264
  26.4 4.4 %collective-permute-start.7 = (bf16[4,16,128]{2,1,0:T(8,128)(2,1)S(1)}, bf16[4,16,128]{2,1,0:T(8,128)(2,1)S(1)}, u32[]{:S(2)}, u32[]{:S(2)}) collective-permute-start(bf16[4,16,128]{2,1,0:T(8,128)(2,1)S(1)} %get-tuple-element.44), channel_id=1, source_target_pairs={{0,8},{2,10},{4,12},{6,14},{8,0},{10,2},{12,4},{14,6},{16,24},{18,... | collective-permute-start | bytes 49160 | tf_op jit(solution)/shard_map/ppermute | solution.py:239
  26.4 4.7 %collective-permute-start.8 = (bf16[4,16,128]{2,1,0:T(8,128)(2,1)S(1)}, bf16[4,16,128]{2,1,0:T(8,128)(2,1)S(1)}, u32[]{:S(2)}, u32[]{:S(2)}) collective-permute-start(bf16[4,16,128]{2,1,0:T(8,128)(2,1)S(1)} %get-tuple-element.45), channel_id=1, source_target_pairs={{0,16},{2,18},{4,20},{6,22},{8,24},{10,26},{12,28},{14,30},{16,0},... | collective-permute-start | bytes 49160 | tf_op jit(solution)/shard_map/ppermute | solution.py:239
  27.7 5.5 %collective-permute-start.9 = (bf16[4,16,128]{2,1,0:T(8,128)(2,1)S(1)}, bf16[4,16,128]{2,1,0:T(8,128)(2,1)S(1)}, u32[]{:S(2)}, u32[]{:S(2)}) collective-permute-start(bf16[4,16,128]{2,1,0:T(8,128)(2,1)S(1)} %get-tuple-element.46), channel_id=1, source_target_pairs={{0,24},{2,26},{4,28},{6,30},{8,16},{10,18},{12,20},{14,22},{16,8},... | collective-permute-start | bytes 49160 | tf_op jit(solution)/shard_map/ppermute | solution.py:239
  33.2 3.7 %collective-permute-start.10 = (bf16[4,16,128]{2,1,0:T(8,128)(2,1)S(1)}, bf16[4,16,128]{2,1,0:T(8,128)(2,1)S(1)}, u32[]{:S(2)}, u32[]{:S(2)}) collective-permute-start(bf16[4,16,128]{2,1,0:T(8,128)(2,1)S(1)} %get-tuple-element.48), channel_id=1, source_target_pairs={{0,2},{2,0},{4,6},{6,4},{8,10},{10,8},{12,14},{14,12},{16,18},{18,... | collective-permute-start | bytes 49160 | tf_op jit(solution)/shard_map/ppermute | solution.py:239
  33.8 3.7 %collective-permute-start.11 = (bf16[4,16,128]{2,1,0:T(8,128)(2,1)S(1)}, bf16[4,16,128]{2,1,0:T(8,128)(2,1)S(1)}, u32[]{:S(2)}, u32[]{:S(2)}) collective-permute-start(bf16[4,16,128]{2,1,0:T(8,128)(2,1)S(1)} %get-tuple-element.49), channel_id=1, source_target_pairs={{0,4},{2,6},{4,0},{6,2},{8,12},{10,14},{12,8},{14,10},{16,20},{18,... | collective-permute-start | bytes 49160 | tf_op jit(solution)/shard_map/ppermute | solution.py:239
  34.3 4.6 %collective-permute-start.12 = (bf16[4,16,128]{2,1,0:T(8,128)(2,1)S(1)}, bf16[4,16,128]{2,1,0:T(8,128)(2,1)S(1)}, u32[]{:S(2)}, u32[]{:S(2)}) collective-permute-start(bf16[4,16,128]{2,1,0:T(8,128)(2,1)S(1)} %get-tuple-element.50), channel_id=1, source_target_pairs={{0,6},{2,4},{4,2},{6,0},{8,14},{10,12},{12,10},{14,8},{16,22},{18,... | collective-permute-start | bytes 49160 | tf_op jit(solution)/shard_map/ppermute | solution.py:239
  41.4 4.4 %collective-permute-start.13 = (bf16[4,48,128]{2,1,0:T(8,128)(2,1)S(1)}, bf16[4,48,128]{2,1,0:T(8,128)(2,1)S(1)}, u32[]{:S(2)}, u32[]{:S(2)}) collective-permute-start(bf16[4,48,128]{2,1,0:T(8,128)(2,1)S(1)} %get-tuple-element.53), channel_id=1, source_target_pairs={{0,8},{2,10},{4,12},{6,14},{8,0},{10,2},{12,4},{14,6},{16,24},{18,... | collective-permute-start | bytes 147464 | tf_op jit(solution)/shard_map/ppermute | solution.py:239
  41.4 5.7 %collective-permute-start.14 = (bf16[4,48,128]{2,1,0:T(8,128)(2,1)S(1)}, bf16[4,48,128]{2,1,0:T(8,128)(2,1)S(1)}, u32[]{:S(2)}, u32[]{:S(2)}) collective-permute-start(bf16[4,48,128]{2,1,0:T(8,128)(2,1)S(1)} %get-tuple-element.54), channel_id=1, source_target_pairs={{0,16},{2,18},{4,20},{6,22},{8,24},{10,26},{12,28},{14,30},{16,0},... | collective-permute-start | bytes 147464 | tf_op jit(solution)/shard_map/ppermute | solution.py:239
  45.0 5.9 %collective-permute-start.15 = (bf16[4,48,128]{2,1,0:T(8,128)(2,1)S(1)}, bf16[4,48,128]{2,1,0:T(8,128)(2,1)S(1)}, u32[]{:S(2)}, u32[]{:S(2)}) collective-permute-start(bf16[4,48,128]{2,1,0:T(8,128)(2,1)S(1)} %get-tuple-element.55), channel_id=1, source_target_pairs={{0,24},{2,26},{4,28},{6,30},{8,16},{10,18},{12,20},{14,22},{16,8},... | collective-permute-start | bytes 147464 | tf_op jit(solution)/shard_map/ppermute | solution.py:239
  50.9 4.2 %collective-permute-start.16 = (bf16[4,48,128]{2,1,0:T(8,128)(2,1)S(1)}, bf16[4,48,128]{2,1,0:T(8,128)(2,1)S(1)}, u32[]{:S(2)}, u32[]{:S(2)}) collective-permute-start(bf16[4,48,128]{2,1,0:T(8,128)(2,1)S(1)} %get-tuple-element.57), channel_id=1, source_target_pairs={{0,2},{2,0},{4,6},{6,4},{8,10},{10,8},{12,14},{14,12},{16,18},{18,... | collective-permute-start | bytes 147464 | tf_op jit(solution)/shard_map/ppermute | solution.py:239
  52.5 4.1 %collective-permute-start.17 = (bf16[4,48,128]{2,1,0:T(8,128)(2,1)S(1)}, bf16[4,48,128]{2,1,0:T(8,128)(2,1)S(1)}, u32[]{:S(2)}, u32[]{:S(2)}) collective-permute-start(bf16[4,48,128]{2,1,0:T(8,128)(2,1)S(1)} %get-tuple-element.58), channel_id=1, source_target_pairs={{0,4},{2,6},{4,0},{6,2},{8,12},{10,14},{12,8},{14,10},{16,20},{18,... | collective-permute-start | bytes 147464 | tf_op jit(solution)/shard_map/ppermute | solution.py:239
  54.0 5.0 %collective-permute-start.18 = (bf16[4,48,128]{2,1,0:T(8,128)(2,1)S(1)}, bf16[4,48,128]{2,1,0:T(8,128)(2,1)S(1)}, u32[]{:S(2)}, u32[]{:S(2)}) collective-permute-start(bf16[4,48,128]{2,1,0:T(8,128)(2,1)S(1)} %get-tuple-element.59), channel_id=1, source_target_pairs={{0,6},{2,4},{4,2},{6,0},{8,14},{10,12},{12,10},{14,8},{16,22},{18,... | collective-permute-start | bytes 147464 | tf_op jit(solution)/shard_map/ppermute | solution.py:239
  59.0 15.7 %copy-start = (bf16[1024,1024]{1,0:T(8,128)(2,1)S(1)}, bf16[1024,1024]{1,0:T(8,128)(2,1)}, u32[]{:S(2)}) copy-start(bf16[1024,1024]{1,0:T(8,128)(2,1)} %wout_ref.1) | copy-start | bytes 6291460
  59.0 1.4 %collective-permute-start.19 = (bf16[512,128]{1,0:T(8,128)(2,1)S(1)}, bf16[512,128]{1,0:T(8,128)(2,1)S(1)}, u32[]{:S(2)}, u32[]{:S(2)}) collective-permute-start(bf16[512,128]{1,0:T(8,128)(2,1)S(1)} %shard_map.102.mine_ref), channel_id=1, source_target_pairs={{0,1},{1,0},{2,3},{3,2},{4,5},{5,4},{6,7},{7,6},{8,9},{9,8},{10,11... | collective-permute-start | bytes 393224 | tf_op jit(solution)/shard_map/ppermute | solution.py:264
  62.1 4.4 %collective-permute-start.20 = (bf16[4,16,128]{2,1,0:T(8,128)(2,1)S(1)}, bf16[4,16,128]{2,1,0:T(8,128)(2,1)S(1)}, u32[]{:S(2)}, u32[]{:S(2)}) collective-permute-start(bf16[4,16,128]{2,1,0:T(8,128)(2,1)S(1)} %get-tuple-element.61), channel_id=1, source_target_pairs={{0,8},{2,10},{4,12},{6,14},{8,0},{10,2},{12,4},{14,6},{16,24},{18,... | collective-permute-start | bytes 49160 | tf_op jit(solution)/shard_map/ppermute | solution.py:239
  62.2 4.7 %collective-permute-start.21 = (bf16[4,16,128]{2,1,0:T(8,128)(2,1)S(1)}, bf16[4,16,128]{2,1,0:T(8,128)(2,1)S(1)}, u32[]{:S(2)}, u32[]{:S(2)}) collective-permute-start(bf16[4,16,128]{2,1,0:T(8,128)(2,1)S(1)} %get-tuple-element.62), channel_id=1, source_target_pairs={{0,16},{2,18},{4,20},{6,22},{8,24},{10,26},{12,28},{14,30},{16,0},... | collective-permute-start | bytes 49160 | tf_op jit(solution)/shard_map/ppermute | solution.py:239
  63.5 5.5 %collective-permute-start.22 = (bf16[4,16,128]{2,1,0:T(8,128)(2,1)S(1)}, bf16[4,16,128]{2,1,0:T(8,128)(2,1)S(1)}, u32[]{:S(2)}, u32[]{:S(2)}) collective-permute-start(bf16[4,16,128]{2,1,0:T(8,128)(2,1)S(1)} %get-tuple-element.63), channel_id=1, source_target_pairs={{0,24},{2,26},{4,28},{6,30},{8,16},{10,18},{12,20},{14,22},{16,8},... | collective-permute-start | bytes 49160 | tf_op jit(solution)/shard_map/ppermute | solution.py:239
  69.0 3.7 %collective-permute-start.23 = (bf16[4,16,128]{2,1,0:T(8,128)(2,1)S(1)}, bf16[4,16,128]{2,1,0:T(8,128)(2,1)S(1)}, u32[]{:S(2)}, u32[]{:S(2)}) collective-permute-start(bf16[4,16,128]{2,1,0:T(8,128)(2,1)S(1)} %get-tuple-element.65), channel_id=1, source_target_pairs={{0,2},{2,0},{4,6},{6,4},{8,10},{10,8},{12,14},{14,12},{16,18},{18,... | collective-permute-start | bytes 49160 | tf_op jit(solution)/shard_map/ppermute | solution.py:239
  69.5 3.7 %collective-permute-start.24 = (bf16[4,16,128]{2,1,0:T(8,128)(2,1)S(1)}, bf16[4,16,128]{2,1,0:T(8,128)(2,1)S(1)}, u32[]{:S(2)}, u32[]{:S(2)}) collective-permute-start(bf16[4,16,128]{2,1,0:T(8,128)(2,1)S(1)} %get-tuple-element.66), channel_id=1, source_target_pairs={{0,4},{2,6},{4,0},{6,2},{8,12},{10,14},{12,8},{14,10},{16,20},{18,... | collective-permute-start | bytes 49160 | tf_op jit(solution)/shard_map/ppermute | solution.py:239
  70.0 4.6 %collective-permute-start.25 = (bf16[4,16,128]{2,1,0:T(8,128)(2,1)S(1)}, bf16[4,16,128]{2,1,0:T(8,128)(2,1)S(1)}, u32[]{:S(2)}, u32[]{:S(2)}) collective-permute-start(bf16[4,16,128]{2,1,0:T(8,128)(2,1)S(1)} %get-tuple-element.67), channel_id=1, source_target_pairs={{0,6},{2,4},{4,2},{6,0},{8,14},{10,12},{12,10},{14,8},{16,22},{18,... | collective-permute-start | bytes 49160 | tf_op jit(solution)/shard_map/ppermute | solution.py:239

commit v5 on v3

--- a/solution.py
+++ b/solution.py
@@ -3,7 +3,7 @@
 from jax import lax
 from jax.experimental import pallas as pl
 from jax.experimental.pallas import tpu as pltpu
-from jax.sharding import Mesh, PartitionSpec as P
+from jax.sharding import PartitionSpec as P
 
 HEADS = 16
 HD = 64
@@ -107,20 +107,33 @@
     return (features[None], result[None])
 
 
+ALL = ("view", "tok")
+
+
 def pack_heads(out_ref, q, k, v):
     rows = q.shape[0]
-    half = rows // 2
+    lines = rows // 4
     for h in range(HEADS):
         cols = slice(h * HD, (h + 1) * HD)
-        out_ref[h, 0:rows, :] = jnp.concatenate([k[:, cols], v[:, cols]], axis=-1)
-        out_ref[h, rows : rows + half, :] = jnp.concatenate([q[:half, cols], q[half:, cols]], axis=-1)
+        kv = jnp.concatenate([k[:, cols], v[:, cols]], axis=-1)
+        for part in range(2):
+            at = 2 * part * lines
+            out_ref[2 * h + part, 0:rows, :] = kv
+            out_ref[2 * h + part, rows : rows + lines, :] = jnp.concatenate(
+                [q[at : at + lines, cols], q[at + lines : at + 2 * lines, cols]], axis=-1
+            )
 
 
 def unpack_rows(got_ref):
-    pieces = [got_ref[h].astype(jnp.float32) for h in range(HEADS)]
-    top = jnp.concatenate([p[:, :HD] for p in pieces], axis=-1)
-    low = jnp.concatenate([p[:, HD:] for p in pieces], axis=-1)
-    return jnp.concatenate([top, low], axis=0)
+    wide = got_ref[...].astype(jnp.float32)
+    return jnp.concatenate(
+        [
+            jnp.concatenate([wide[2 * h + part, :, side * HD : (side + 1) * HD] for h in range(HEADS)], axis=-1)
+            for part in range(2)
+            for side in range(2)
+        ],
+        axis=0,
+    )
 
 
 def unit(x):
@@ -139,19 +152,16 @@
     pack_heads(out_ref, q_ref[0], k_ref[0], v_ref[0])
 
 
-def attend_kernel(mine_ref, other_ref, out_ref):
-    sources, lines, _ = mine_ref.shape
-    rows = lines * 2 // 3
-    half = rows // 2
-    kv = jnp.concatenate(
-        [mine_ref[:, 0:rows, :].reshape(-1, 2 * HD), other_ref[:, 0:rows, :].reshape(-1, 2 * HD)], axis=0
-    )
+def attend_kernel(got_ref, out_ref):
+    sources, lines, _ = got_ref.shape
+    rows = lines * 4 // 5
+    kv = got_ref[:, 0:rows, :].reshape(-1, 2 * HD)
     keys = kv[:, :HD]
     vals = kv[:, HD:]
-    step = max(1, 128 // half)
+    step = max(1, 64 // (lines - rows))
     for s in range(0, sources, step):
-        packed = mine_ref[s : s + step, rows:lines, :].reshape(-1, 2 * HD)
-        queries = jnp.concatenate([packed[:, :HD], packed[:, HD:]], axis=0)
+        packed = got_ref[s : s + step, rows:lines, :].astype(jnp.float32).reshape(-1, 2 * HD)
+        queries = jnp.concatenate([packed[:, :HD], packed[:, HD:]], axis=0).astype(jnp.bfloat16)
         scores = lax.dot_general(
             queries, keys, (((1,), (1,)), ((), ())), preferred_element_type=jnp.float32
         ) * (HD ** (-0.5))
@@ -159,9 +169,10 @@
         weights = jnp.exp(scores - peak)
         total = jnp.sum(weights, axis=-1, keepdims=True)
         summed = jnp.dot(weights.astype(jnp.bfloat16), vals, preferred_element_type=jnp.float32)
-        attn = (summed / total).astype(jnp.bfloat16)
+        attn = summed / total
         n = attn.shape[0] // 2
-        out_ref[s : s + step] = jnp.concatenate([attn[:n], attn[n:]], axis=-1).reshape(step, half, 2 * HD)
+        lined = jnp.concatenate([attn[:n], attn[n:]], axis=-1)
+        out_ref[s : s + step] = lined.reshape(step, lines - rows, 2 * HD).astype(jnp.bfloat16)
 
 
 def middle_kernel(got_ref, x2_ref, wv_ref, gain_ref, wqkv_ref, feats_ref, out_ref):
@@ -195,44 +206,34 @@
 
 def by_heads(q1, k1, v1, nbr, x2, w_view_out, norm_gain, w_qkv, w_out):
     rows = q1.shape[1]
-    lines = rows * 3 // 2
-    packed_type = jax.ShapeDtypeStruct((HEADS, lines, 2 * HD), jnp.bfloat16)
-    half_type = jax.ShapeDtypeStruct((HEADS, rows // 2, 2 * HD), jnp.bfloat16)
+    packed_type = jax.ShapeDtypeStruct((2 * HEADS, rows + rows // 4, 2 * HD), jnp.bfloat16)
+    part_type = jax.ShapeDtypeStruct((2 * HEADS, rows // 4, 2 * HD), jnp.bfloat16)
     wide_type = jax.ShapeDtypeStruct((1, rows, HEADS * HD), jnp.float32)
-    group = ("view", "chip")
+
+    def trade(piece):
+        return lax.all_to_all(piece, ALL, split_axis=0, concat_axis=0, tiled=True)
 
     def attention(packed):
-        mine = lax.all_to_all(packed, group, split_axis=0, concat_axis=0, tiled=True)
-        cores = lax.axis_size("core")
-        other = lax.ppermute(mine, "core", [(i, (i + 1) % cores) for i in range(cores)])
         cost = pl.CostEstimate(flops=16 << 30, bytes_accessed=40 << 20, transcendentals=0)
-        half = call(attend_kernel, half_type, (mine, other), cost=cost)
-        return lax.all_to_all(half, group, split_axis=0, concat_axis=0, tiled=True)
+        return trade(call(attend_kernel, part_type, (trade(packed),), cost=cost))
 
     scratch = [pltpu.VMEM(q1.shape, q1.dtype)] * 3 + [pltpu.SemaphoreType.DMA((3,))]
-    got = attention(call(pack_kernel, packed_type, (q1, k1, v1), scratch, space=pltpu.HBM, limit=60 << 20))
+    packed = call(pack_kernel, packed_type, (q1, k1, v1), scratch, space=pltpu.HBM, limit=60 << 20)
     feats, packed = call(
-        middle_kernel, (wide_type, packed_type), (got, x2, w_view_out, norm_gain[None], w_qkv)
-    )
-    result = call(last_kernel, wide_type, (attention(packed), w_out))
-    return feats, result
+        middle_kernel, (wide_type, packed_type), (attention(packed), x2, w_view_out, norm_gain[None], w_qkv)
+    )
+    return feats, call(last_kernel, wide_type, (attention(packed), w_out))
 
 
 def solution(mesh):
-    views, toks = mesh.devices.shape
-    fine = Mesh(mesh.devices.reshape(views, toks // 2, 2), ("view", "chip", "core"))
+    devices = mesh.devices.size
 
     def run(q1, k1, v1, nbr, x2, w_view_out, norm_gain, w_qkv, w_out):
         every_view = q1.shape[0] == nbr.shape[1] + 1
-        one_head = views * (toks // 2) == HEADS
-        if every_view and one_head:
-            body, grid, tok = by_heads, fine, ("chip", "core")
-        else:
-            body, grid, tok = general, mesh, "tok"
-        split = P("view", tok, None)
+        split = P("view", "tok", None)
         return jax.shard_map(
-            body,
-            mesh=grid,
+            by_heads if every_view and devices == 2 * HEADS else general,
+            mesh=mesh,
             in_specs=(split, split, split, P("view", None), split, P(), P(), P(), P()),
             out_specs=(split, split),
             check_vma=False,

time: 60.4 us -> 61.6 us (1.020)
  blocking collectives: 48.8 us -> 52.2 us
  waiting for transfers between devices: 2.87 us -> 0 us
  Pallas kernels: 7.58 us -> 8.41 us
    all_to_all x4, blocking collectives: 48.8 us -> 52.2 us  [trade(): return lax.all_to_all(piece, ALL, split_axis=0, concat_axis=0, tiled=True)]
    ppermute x2 -> x0, waiting for transfers between devices: 2.87 us -> none  [attention(): lax.ppermute(mine, 'core', [(i, (i + 1) % cores) for i in range(cores)])]
    pallas_call x5, Pallas kernels: 7.58 us -> 8.41 us  [call(): pl.pallas_call(body, out_shape=outs, in_specs=[pl.BlockSpec(memory_space=...]
  transfers between devices with their start and end apart: 2 -> 0, of which waited for: 2 -> 0; matrix products, arithmetic and copies ran while one was open for 0% -> 0% of each run, Pallas kernels for 0% -> 0%
where the time goes in v5:
time: 61.6 us; the launch traced here: 61.3 us
  blocking collectives  52.2 us (85%)
  Pallas kernels  8.41 us (14%)
  between operations  0.69 us (1%)
    all_to_all x4, blocking collectives, trade(): return lax.all_to_all(piece, ALL, split_axis=0, concat_axis=0, tiled=True)  52.2 us
    pallas_call x5, Pallas kernels, call(): pl.pallas_call(body, out_shape=outs, in_specs=[pl.BlockSpec(memory_space=...  8.41 us

profile of v5, /device:TPU:0, one launch (start us, length us, event | category | flops | bytes accessed | tf_op | source)
XLA Modules:
  0.0 61.3 jit_solution(15142984307774459455)
XLA Ops:
  0.6 1.8 %shard_map.95 = bf16[32,40,128]{2,1,0:T(8,128)(2,1)} custom-call(bf16[1,32,1024]{2,1,0:T(8,128)(2,1)} %q_hbm.1, bf16[1,32,1024]{2,1,0:T(8,128)(2,1)} %k_hbm.1, bf16[1,32,1024]{2,1,0:T(8,128)(2,1)} %v_hbm.1), custom_call_target="tpu_custom_call" | custom-call | tf_op jit(solution)/shard_map/pallas_call | solution.py:196
  2.4 0.0 slice-start
  2.4 19.3 %all_to_all.20.got_ref = bf16[32,40,128]{2,1,0:T(8,128)(2,1)S(1)} all-to-all(bf16[32,40,128]{2,1,0:T(8,128)(2,1)} %shard_map.95), channel_id=1, replica_groups=mesh['view'=8,'tok'=4] {'view','tok'}, dimensions={0} | all-to-all | bytes 655360 | tf_op jit(solution)/shard_map/all_to_all | solution.py:214
  21.7 0.0 slice-start.1
  21.7 0.0 copy-start.1
  21.7 0.0 copy-start.2
  21.7 0.0 copy-start.3
  21.8 1.7 %shard_map.96 = bf16[32,8,128]{2,1,0:T(8,128)(2,1)S(1)} custom-call(bf16[32,40,128]{2,1,0:T(8,128)(2,1)S(1)} %all_to_all.20.got_ref), custom_call_target="tpu_custom_call" | custom-call | flops 17179869184 | bytes 41943040 | tf_op jit(solution)/shard_map/pallas_call | solution.py:196
  23.5 9.6 %all_to_all.21.got_ref = bf16[32,8,128]{2,1,0:T(8,128)(2,1)S(1)} all-to-all(bf16[32,8,128]{2,1,0:T(8,128)(2,1)S(1)} %shard_map.96), channel_id=1, replica_groups=mesh['view'=8,'tok'=4] {'view','tok'}, dimensions={0} | all-to-all | bytes 131072 | tf_op jit(solution)/shard_map/all_to_all | solution.py:214
  33.1 0.0 slice-done
  33.1 0.0 slice-done.1
  33.1 0.0 copy-done.1
  33.1 0.0 copy-done.2
  33.1 0.0 copy-done.3
  33.1 1.9 %shard_map.97 = (f32[1,32,1024]{2,1,0:T(8,128)}, bf16[32,40,128]{2,1,0:T(8,128)(2,1)S(1)}) custom-call(bf16[32,8,128]{2,1,0:T(8,128)(2,1)S(1)} %all_to_all.21.got_ref, bf16[1,32,1024]{2,1,0:T(8,128)(2,1)S(1)} %copy-done.2, bf16[1024,1024]{1,0:T(8,128)(2,1)S(1)} %copy-done.1, f32[1,1024]{1,0:T(1,128)S(1)} %bitcast.3, bf16[1024,3072]{1,0:T(8,128)(2,1)S(1)} %bitcast.2), custom_call_target="tpu_custom_call" | custom-call | tf_op jit(solution)/shard_map/pallas_call | solution.py:196
  35.1 13.7 %all_to_all.22.got_ref = bf16[32,40,128]{2,1,0:T(8,128)(2,1)S(1)} all-to-all(bf16[32,40,128]{2,1,0:T(8,128)(2,1)S(1)} %get-tuple-element.5), channel_id=1, replica_groups=mesh['view'=8,'tok'=4] {'view','tok'}, dimensions={0} | all-to-all | bytes 655360 | tf_op jit(solution)/shard_map/all_to_all | solution.py:214
  48.8 0.0 copy-start
  48.8 1.7 %shard_map.98 = bf16[32,8,128]{2,1,0:T(8,128)(2,1)S(1)} custom-call(bf16[32,40,128]{2,1,0:T(8,128)(2,1)S(1)} %all_to_all.22.got_ref), custom_call_target="tpu_custom_call" | custom-call | flops 17179869184 | bytes 41943040 | tf_op jit(solution)/shard_map/pallas_call | solution.py:196
  50.5 9.5 %all_to_all.23.got_ref = bf16[32,8,128]{2,1,0:T(8,128)(2,1)S(1)} all-to-all(bf16[32,8,128]{2,1,0:T(8,128)(2,1)S(1)} %shard_map.98), channel_id=1, replica_groups=mesh['view'=8,'tok'=4] {'view','tok'}, dimensions={0} | all-to-all | bytes 131072 | tf_op jit(solution)/shard_map/all_to_all | solution.py:214
  60.0 0.0 copy-done
  60.0 1.3 %shard_map.99 = f32[1,32,1024]{2,1,0:T(8,128)} custom-call(bf16[32,8,128]{2,1,0:T(8,128)(2,1)S(1)} %all_to_all.23.got_ref, bf16[1024,1024]{1,0:T(8,128)(2,1)S(1)} %copy-done), custom_call_target="tpu_custom_call" | custom-call | tf_op jit(solution)/shard_map/pallas_call | solution.py:196
  (1 shorter events, 0.0 us)
Async XLA Ops:
  2.4 30.7 %slice-start = ((s8[6291456]{0:T(1024)(128)(4,1)}), s8[4194304]{0:T(1024)(128)(4,1)S(1)}, s32[]{:S(2)}) async-start(s8[6291456]{0:T(1024)(128)(4,1)} %bitcast.1), calls=%async_computation.4 | async-start | bytes 8388608
  21.7 11.4 %slice-start.1 = ((s8[6291456]{0:T(1024)(128)(4,1)}), s8[2097152]{0:T(1024)(128)(4,1)S(1)}, s32[]{:S(2)}) async-start(s8[6291456]{0:T(1024)(128)(4,1)} %bitcast.1), calls=%async_computation.5 | async-start | bytes 4194304
  21.7 11.4 %copy-start.1 = (bf16[1024,1024]{1,0:T(8,128)(2,1)S(1)}, bf16[1024,1024]{1,0:T(8,128)(2,1)}, u32[]{:S(2)}) copy-start(bf16[1024,1024]{1,0:T(8,128)(2,1)} %wv_ref.1) | copy-start | bytes 6291460
  21.7 11.4 %copy-start.2 = (bf16[1,32,1024]{2,1,0:T(8,128)(2,1)S(1)}, bf16[1,32,1024]{2,1,0:T(8,128)(2,1)}, u32[]{:S(2)}) copy-start(bf16[1,32,1024]{2,1,0:T(8,128)(2,1)} %x2_ref.1) | copy-start | bytes 196612
  21.7 11.4 %copy-start.3 = (f32[1024]{0:T(1024)S(1)}, f32[1024]{0:T(1024)}, u32[]{:S(2)}) copy-start(f32[1024]{0:T(1024)} %param.14) | copy-start | bytes 12292
  48.8 11.2 %copy-start = (bf16[1024,1024]{1,0:T(8,128)(2,1)S(1)}, bf16[1024,1024]{1,0:T(8,128)(2,1)}, u32[]{:S(2)}) copy-start(bf16[1024,1024]{1,0:T(8,128)(2,1)} %wout_ref.1) | copy-start | bytes 6291460

commit v6 on v3

--- a/solution.py
+++ b/solution.py
@@ -3,13 +3,12 @@
 from jax import lax
 from jax.experimental import pallas as pl
 from jax.experimental.pallas import tpu as pltpu
-from jax.sharding import Mesh, PartitionSpec as P
+from jax.sharding import PartitionSpec as P
 
 HEADS = 16
 HD = 64
 EPSILON = 1e-06
 NEGATIVE = -1e30
-VMEM = pl.BlockSpec(memory_space=pltpu.VMEM)
 
 
 def absorb(running, queries, key_piece, val_piece, keep_key, factor_scale):
@@ -107,6 +106,11 @@
     return (features[None], result[None])
 
 
+ALL = ("view", "tok")
+CORES = 2
+SHARP = HD ** (-0.5) * 1.4426950408889634
+
+
 def pack_heads(out_ref, q, k, v):
     rows = q.shape[0]
     half = rows // 2
@@ -139,34 +143,62 @@
     pack_heads(out_ref, q_ref[0], k_ref[0], v_ref[0])
 
 
-def attend_kernel(mine_ref, other_ref, out_ref):
+def key_values(piece_ref):
+    sources, lines, _ = piece_ref.shape
+    kv = piece_ref[:, 0 : lines * 2 // 3, :].reshape(-1, 2 * HD)
+    return kv[:, :HD], jnp.concatenate([kv[:, HD:], jnp.ones((kv.shape[0], HD), kv.dtype)], axis=-1)
+
+
+def some_queries(piece_ref, start, count):
+    lines = piece_ref.shape[1]
+    packed = piece_ref[start : start + count, lines * 2 // 3 : lines, :].reshape(-1, 2 * HD)
+    return jnp.concatenate([packed[:, :HD], packed[:, HD:]], axis=0)
+
+
+def score(queries, keys):
+    return lax.dot_general(queries, keys, (((1,), (1,)), ((), ())), preferred_element_type=jnp.float32)
+
+
+def weigh(scores, peak, vals):
+    weights = jnp.exp2((scores - peak) * SHARP).astype(jnp.bfloat16)
+    return jnp.dot(weights, vals, preferred_element_type=jnp.float32)
+
+
+def begin_kernel(mine_ref, peak_ref, sum_ref):
     sources, lines, _ = mine_ref.shape
-    rows = lines * 2 // 3
-    half = rows // 2
-    kv = jnp.concatenate(
-        [mine_ref[:, 0:rows, :].reshape(-1, 2 * HD), other_ref[:, 0:rows, :].reshape(-1, 2 * HD)], axis=0
-    )
-    keys = kv[:, :HD]
-    vals = kv[:, HD:]
-    step = max(1, 128 // half)
-    for s in range(0, sources, step):
-        packed = mine_ref[s : s + step, rows:lines, :].reshape(-1, 2 * HD)
-        queries = jnp.concatenate([packed[:, :HD], packed[:, HD:]], axis=0)
-        scores = lax.dot_general(
-            queries, keys, (((1,), (1,)), ((), ())), preferred_element_type=jnp.float32
-        ) * (HD ** (-0.5))
+    keys, vals = key_values(mine_ref)
+    step = max(1, 384 // lines)
+    rows = step * lines * 2 // 3
+    for i in range(sources // step):
+        scores = score(some_queries(mine_ref, i * step, step), keys)
         peak = jnp.max(scores, axis=-1, keepdims=True)
-        weights = jnp.exp(scores - peak)
-        total = jnp.sum(weights, axis=-1, keepdims=True)
-        summed = jnp.dot(weights.astype(jnp.bfloat16), vals, preferred_element_type=jnp.float32)
-        attn = (summed / total).astype(jnp.bfloat16)
-        n = attn.shape[0] // 2
-        out_ref[s : s + step] = jnp.concatenate([attn[:n], attn[n:]], axis=-1).reshape(step, half, 2 * HD)
-
-
-def middle_kernel(got_ref, x2_ref, wv_ref, gain_ref, wqkv_ref, feats_ref, out_ref):
+        at = slice(i * rows, (i + 1) * rows)
+        peak_ref[at, :] = peak
+        sum_ref[at, :] = weigh(scores, peak, vals)
+
+
+def finish_kernel(mine_ref, other_ref, peak_ref, sum_ref, out_ref):
+    sources, lines, _ = mine_ref.shape
+    keys, vals = key_values(other_ref)
+    step = max(1, 384 // lines)
+    rows = step * lines * 2 // 3
+    for i in range(sources // step):
+        at = slice(i * rows, (i + 1) * rows)
+        scores = score(some_queries(mine_ref, i * step, step), keys)
+        before = peak_ref[at, :]
+        peak = jnp.maximum(before, jnp.max(scores, axis=-1, keepdims=True))
+        summed = sum_ref[at, :] * jnp.exp2((before - peak) * SHARP) + weigh(scores, peak, vals)
+        attn = (summed[:, :HD] / summed[:, HD:]).astype(jnp.bfloat16)
+        n = rows // 2
+        lined = jnp.concatenate([attn[:n], attn[n:]], axis=-1)
+        out_ref[i * step : (i + 1) * step] = lined.reshape(step, lines // 3, 2 * HD)
+
+
+def middle_kernel(got_ref, x2_ref, wv_ref, gain_ref, wqkv_ref, feats_hbm, out_ref, feats_ref, sem):
     feats = unit(unpack_rows(got_ref))
     feats_ref[0] = feats
+    copy = pltpu.make_async_copy(feats_ref, feats_hbm, sem)
+    copy.start()
     hidden = x2_ref[0].astype(jnp.float32) + jnp.dot(
         feats.astype(jnp.bfloat16), wv_ref[...], preferred_element_type=jnp.float32
     )
@@ -174,19 +206,28 @@
     projected = jnp.dot(normed, wqkv_ref[...], preferred_element_type=jnp.float32).astype(jnp.bfloat16)
     width = HEADS * HD
     pack_heads(out_ref, projected[:, :width], projected[:, width : 2 * width], projected[:, 2 * width :])
-
-
-def last_kernel(got_ref, wout_ref, out_ref):
+    copy.wait()
+
+
+def last_kernel(got_ref, wout_ref, out_hbm, out_ref, sems):
     rows = unit(unpack_rows(got_ref)).astype(jnp.bfloat16)
-    out_ref[0] = jnp.dot(rows, wout_ref[...], preferred_element_type=jnp.float32)
+    copies = []
+    width = wout_ref.shape[1] // 2
+    for i in range(2):
+        cols = slice(i * width, (i + 1) * width)
+        out_ref[0, :, cols] = jnp.dot(rows, wout_ref[:, cols], preferred_element_type=jnp.float32)
+        copies.append(pltpu.make_async_copy(out_ref.at[:, :, cols], out_hbm.at[:, :, cols], sems.at[i]))
+        copies[i].start()
+    for copy in copies:
+        copy.wait()
 
 
 def call(body, outs, args, scratch=(), limit=16 << 20, space=pltpu.VMEM, cost=None):
     return pl.pallas_call(
         body,
-        out_shape=outs,
+        out_shape=[jax.ShapeDtypeStruct(shape, dtype) for shape, dtype, _ in outs],
         in_specs=[pl.BlockSpec(memory_space=space)] * len(args),
-        out_specs=jax.tree.map(lambda _: VMEM, outs),
+        out_specs=[pl.BlockSpec(memory_space=where) for _, _, where in outs],
         scratch_shapes=list(scratch),
         cost_estimate=cost,
         compiler_params=pltpu.CompilerParams(vmem_limit_bytes=limit),
@@ -195,44 +236,52 @@
 
 def by_heads(q1, k1, v1, nbr, x2, w_view_out, norm_gain, w_qkv, w_out):
     rows = q1.shape[1]
-    lines = rows * 3 // 2
-    packed_type = jax.ShapeDtypeStruct((HEADS, lines, 2 * HD), jnp.bfloat16)
-    half_type = jax.ShapeDtypeStruct((HEADS, rows // 2, 2 * HD), jnp.bfloat16)
-    wide_type = jax.ShapeDtypeStruct((1, rows, HEADS * HD), jnp.float32)
-    group = ("view", "chip")
+    packed = ((HEADS, rows * 3 // 2, 2 * HD), jnp.bfloat16, pltpu.VMEM)
+    halves = ((HEADS, rows // 2, 2 * HD), jnp.bfloat16, pltpu.VMEM)
+    peaks = ((HEADS * rows, 1), jnp.float32, pltpu.VMEM)
+    sums = ((HEADS * rows, 2 * HD), jnp.float32, pltpu.VMEM)
+    wide = (1, rows, HEADS * HD)
+    devices = HEADS * CORES
+    groups = [[(p * CORES + core + 8) % devices for p in range(HEADS)] for core in range(CORES)]
+
+    def trade(piece):
+        return lax.all_to_all(piece, ALL, split_axis=0, concat_axis=0, tiled=True, axis_index_groups=groups)
 
     def attention(packed):
-        mine = lax.all_to_all(packed, group, split_axis=0, concat_axis=0, tiled=True)
-        cores = lax.axis_size("core")
-        other = lax.ppermute(mine, "core", [(i, (i + 1) % cores) for i in range(cores)])
+        mine = trade(packed)
+        other = lax.ppermute(mine, ALL, [(i, i ^ 1) for i in range(devices)])
+        peak, summed = call(begin_kernel, [peaks, sums], (mine,), cost=pl.CostEstimate(1 << 30, 0, 1 << 20))
         cost = pl.CostEstimate(flops=16 << 30, bytes_accessed=40 << 20, transcendentals=0)
-        half = call(attend_kernel, half_type, (mine, other), cost=cost)
-        return lax.all_to_all(half, group, split_axis=0, concat_axis=0, tiled=True)
-
+        (half,) = call(finish_kernel, [halves], (mine, other, peak, summed), cost=cost)
+        return trade(half)
+
+    inputs = [pltpu.with_memory_space_constraint(x, pltpu.HBM) for x in (q1, k1, v1)]
     scratch = [pltpu.VMEM(q1.shape, q1.dtype)] * 3 + [pltpu.SemaphoreType.DMA((3,))]
-    got = attention(call(pack_kernel, packed_type, (q1, k1, v1), scratch, space=pltpu.HBM, limit=60 << 20))
-    feats, packed = call(
-        middle_kernel, (wide_type, packed_type), (got, x2, w_view_out, norm_gain[None], w_qkv)
-    )
-    result = call(last_kernel, wide_type, (attention(packed), w_out))
+    (piece,) = call(pack_kernel, [packed], inputs, scratch, space=pltpu.HBM, limit=48 << 20)
+    feats, piece = call(
+        middle_kernel,
+        [(wide, jnp.float32, pltpu.HBM), packed],
+        (attention(piece), x2, w_view_out, norm_gain[None], w_qkv),
+        [pltpu.VMEM(wide, jnp.float32), pltpu.SemaphoreType.DMA],
+    )
+    (result,) = call(
+        last_kernel,
+        [(wide, jnp.float32, pltpu.HBM)],
+        (attention(piece), w_out),
+        [pltpu.VMEM(wide, jnp.float32), pltpu.SemaphoreType.DMA((2,))],
+    )
     return feats, result
 
 
 def solution(mesh):
-    views, toks = mesh.devices.shape
-    fine = Mesh(mesh.devices.reshape(views, toks // 2, 2), ("view", "chip", "core"))
+    devices = mesh.devices.size
 
     def run(q1, k1, v1, nbr, x2, w_view_out, norm_gain, w_qkv, w_out):
         every_view = q1.shape[0] == nbr.shape[1] + 1
-        one_head = views * (toks // 2) == HEADS
-        if every_view and one_head:
-            body, grid, tok = by_heads, fine, ("chip", "core")
-        else:
-            body, grid, tok = general, mesh, "tok"
-        split = P("view", tok, None)
+        split = P("view", "tok", None)
         return jax.shard_map(
-            body,
-            mesh=grid,
+            by_heads if every_view and devices == CORES * HEADS else general,
+            mesh=mesh,
             in_specs=(split, split, split, P("view", None), split, P(), P(), P(), P()),
             out_specs=(split, split),
             check_vma=False,

time: 60.4 us -> 56.6 us (0.937)
  blocking collectives: 48.8 us -> 46.2 us
  waiting for transfers between devices: 2.87 us -> 1.28 us
    all_to_all x4, blocking collectives: 48.8 us -> 46.2 us  [trade(): lax.all_to_all(piece, ALL, split_axis=0, concat_axis=0, tiled=True, axis_...]
    ppermute x2, waiting for transfers between devices: 2.87 us -> 1.28 us  [attention(): other = lax.ppermute(mine, ALL, [(i, i ^ 1) for i in range(devices)])]
    pallas_call x5 -> x7, Pallas kernels: 7.58 us -> 8.17 us  [call(): pl.pallas_call(body, out_shape=[jax.ShapeDtypeStruct(shape, dtype) for sh...]
  transfers between devices with their start and end apart: 2 -> 2, of which waited for: 2 -> 2; matrix products, arithmetic and copies ran while one was open for 0% -> 0% of each run, Pallas kernels for 0% -> 3%
where the time goes in v6:
time: 56.6 us; the launch traced here: 56.3 us
  blocking collectives  46.2 us (82%)
  Pallas kernels  8.17 us (14%)
  waiting for transfers between devices  1.28 us (2%)
  between operations  0.71 us (1%)
    all_to_all x4, blocking collectives, trade(): lax.all_to_all(piece, ALL, split_axis=0, concat_axis=0, tiled=True, axis_...  46.2 us
    pallas_call x7, Pallas kernels, call(): pl.pallas_call(body, out_shape=[jax.ShapeDtypeStruct(shape, dtype) for sh...  8.17 us
    ppermute x2, waiting for transfers between devices, attention(): other = lax.ppermute(mine, ALL, [(i, i ^ 1) for i in range(devices)])  1.28 us
  transfers between devices with their start and end apart: 2, of which 2 were waited for; matrix products, arithmetic and copies ran while one was open for 0% of the time, Pallas kernels for 3%

profile of v6, /device:TPU:0, one launch (start us, length us, event | category | flops | bytes accessed | tf_op | source)
XLA Modules:
  0.0 56.3 jit_solution(15222591310585842995)
XLA Ops:
  0.6 1.1 %shard_map.95 = bf16[16,48,128]{2,1,0:T(8,128)(2,1)S(1)} custom-call(bf16[1,32,1024]{2,1,0:T(8,128)(2,1)} %q_hbm.1, bf16[1,32,1024]{2,1,0:T(8,128)(2,1)} %k_hbm.1, bf16[1,32,1024]{2,1,0:T(8,128)(2,1)} %v_hbm.1), custom_call_target="tpu_custom_call" | custom-call | tf_op jit(solution)/shard_map/pallas_call | solution.py:226
  1.7 15.9 %all_to_all.20.mine_ref = bf16[16,48,128]{2,1,0:T(8,128)(2,1)S(1)} all-to-all(bf16[16,48,128]{2,1,0:T(8,128)(2,1)S(1)} %shard_map.95), channel_id=1, replica_groups={{8,10,12,14,16,18,20,22,24,26,28,30,0,2,4,6},{9,11,13,15,17,19,21,23,25..., dimensions={0} | all-to-all | bytes 393216 | tf_op jit(solution)/shard_map/all_to_all | solution.py:248
  17.5 0.0 collective-permute-start
  17.5 0.8 %shard_map.96 = (f32[512,1]{1,0:T(8,128)S(1)}, f32[512,128]{1,0:T(8,128)S(1)}) custom-call(bf16[16,48,128]{2,1,0:T(8,128)(2,1)S(1)} %all_to_all.20.mine_ref), custom_call_target="tpu_custom_call" | custom-call | flops 1073741824 | bytes 1048576 | tf_op jit(solution)/shard_map/pallas_call | solution.py:226
  18.3 0.6 %collective-permute-done.other_ref = bf16[16,48,128]{2,1,0:T(8,128)(2,1)S(1)} collective-permute-done((bf16[16,48,128]{2,1,0:T(8,128)(2,1)S(1)}, bf16[16,48,128]{2,1,0:T(8,128)(2,1)S(1)}, u32[]{:S(2)}, u32[]{:S(2)}) %collective-permute-start) | collective-permute-done | bytes 196640 | tf_op jit(solution)/shard_map/ppermute | solution.py:252
  19.0 0.0 slice-start
  19.0 0.0 slice-start.1
  19.0 0.0 copy-start.1
  19.0 0.0 copy-start.2
  19.0 0.0 copy-start.3
  19.0 1.2 %shard_map.97 = bf16[16,16,128]{2,1,0:T(8,128)(2,1)S(1)} custom-call(bf16[16,48,128]{2,1,0:T(8,128)(2,1)S(1)} %all_to_all.20.mine_ref, bf16[16,48,128]{2,1,0:T(8,128)(2,1)S(1)} %collective-permute-done.other_ref, f32[512,1]{1,0:T(8,128)S(1)} %get-tuple-element.8.peak_ref, f32[512,128]{1,0:T(8,128)S(1)} %get-tuple-element.9.sum_ref), custom_call_target="tpu_custom_call" | custom-call | flops 17179869184 | bytes 41943040 | tf_op jit(solution)/shard_map/pallas_call | solution.py:226
  20.2 10.2 %all_to_all.21.got_ref = bf16[16,16,128]{2,1,0:T(8,128)(2,1)S(1)} all-to-all(bf16[16,16,128]{2,1,0:T(8,128)(2,1)S(1)} %shard_map.97), channel_id=1, replica_groups={{8,10,12,14,16,18,20,22,24,26,28,30,0,2,4,6},{9,11,13,15,17,19,21,23,25..., dimensions={0} | all-to-all | bytes 131072 | tf_op jit(solution)/shard_map/all_to_all | solution.py:248
  30.3 0.0 slice-done
  30.3 0.0 slice-done.1
  30.3 0.0 copy-done.1
  30.4 0.0 copy-done.2
  30.4 0.0 copy-done.3
  30.4 2.0 %shard_map.98 = (f32[1,32,1024]{2,1,0:T(8,128)}, bf16[16,48,128]{2,1,0:T(8,128)(2,1)S(1)}) custom-call(bf16[16,16,128]{2,1,0:T(8,128)(2,1)S(1)} %all_to_all.21.got_ref, bf16[1,32,1024]{2,1,0:T(8,128)(2,1)S(1)} %copy-done.2, bf16[1024,1024]{1,0:T(8,128)(2,1)S(1)} %copy-done.1, f32[1,1024]{1,0:T(1,128)S(1)} %bitcast.3, bf16[1024,3072]{1,0:T(8,128)(2,1)S(1)} %bitcast.2), custom_call_target="tpu_custom_call" | custom-call | tf_op jit(solution)/shard_map/pallas_call | solution.py:226
  32.3 10.1 %all_to_all.22.mine_ref = bf16[16,48,128]{2,1,0:T(8,128)(2,1)S(1)} all-to-all(bf16[16,48,128]{2,1,0:T(8,128)(2,1)S(1)} %get-tuple-element.11), channel_id=1, replica_groups={{8,10,12,14,16,18,20,22,24,26,28,30,0,2,4,6},{9,11,13,15,17,19,21,23,25..., dimensions={0} | all-to-all | bytes 393216 | tf_op jit(solution)/shard_map/all_to_all | solution.py:248
  42.4 0.0 collective-permute-start.1
  42.4 0.8 %shard_map.99 = (f32[512,1]{1,0:T(8,128)S(1)}, f32[512,128]{1,0:T(8,128)S(1)}) custom-call(bf16[16,48,128]{2,1,0:T(8,128)(2,1)S(1)} %all_to_all.22.mine_ref), custom_call_target="tpu_custom_call" | custom-call | flops 1073741824 | bytes 1048576 | tf_op jit(solution)/shard_map/pallas_call | solution.py:226
  43.2 0.6 %collective-permute-done.1.other_ref = bf16[16,48,128]{2,1,0:T(8,128)(2,1)S(1)} collective-permute-done((bf16[16,48,128]{2,1,0:T(8,128)(2,1)S(1)}, bf16[16,48,128]{2,1,0:T(8,128)(2,1)S(1)}, u32[]{:S(2)}, u32[]{:S(2)}) %collective-permute-start.1) | collective-permute-done | bytes 196640 | tf_op jit(solution)/shard_map/ppermute | solution.py:252
  43.9 0.0 copy-start
  43.9 1.2 %shard_map.100 = bf16[16,16,128]{2,1,0:T(8,128)(2,1)S(1)} custom-call(bf16[16,48,128]{2,1,0:T(8,128)(2,1)S(1)} %all_to_all.22.mine_ref, bf16[16,48,128]{2,1,0:T(8,128)(2,1)S(1)} %collective-permute-done.1.other_ref, f32[512,1]{1,0:T(8,128)S(1)} %get-tuple-element.12.peak_ref, f32[512,128]{1,0:T(8,128)S(1)} %get-tuple-element.13.sum_ref), custom_call_target="tpu_custom_call" | custom-call | flops 17179869184 | bytes 41943040 | tf_op jit(solution)/shard_map/pallas_call | solution.py:226
  45.0 10.0 %all_to_all.23.got_ref = bf16[16,16,128]{2,1,0:T(8,128)(2,1)S(1)} all-to-all(bf16[16,16,128]{2,1,0:T(8,128)(2,1)S(1)} %shard_map.100), channel_id=1, replica_groups={{8,10,12,14,16,18,20,22,24,26,28,30,0,2,4,6},{9,11,13,15,17,19,21,23,25..., dimensions={0} | all-to-all | bytes 131072 | tf_op jit(solution)/shard_map/all_to_all | solution.py:248
  55.1 0.0 copy-done
  55.1 1.3 %shard_map.101 = f32[1,32,1024]{2,1,0:T(8,128)} custom-call(bf16[16,16,128]{2,1,0:T(8,128)(2,1)S(1)} %all_to_all.23.got_ref, bf16[1024,1024]{1,0:T(8,128)(2,1)S(1)} %copy-done), custom_call_target="tpu_custom_call" | custom-call | tf_op jit(solution)/shard_map/pallas_call | solution.py:226
  (1 shorter events, 0.0 us)
Async XLA Ops:
  17.5 1.4 %collective-permute-start = (bf16[16,48,128]{2,1,0:T(8,128)(2,1)S(1)}, bf16[16,48,128]{2,1,0:T(8,128)(2,1)S(1)}, u32[]{:S(2)}, u32[]{:S(2)}) collective-permute-start(bf16[16,48,128]{2,1,0:T(8,128)(2,1)S(1)} %all_to_all.20.mine_ref), channel_id=1, source_target_pairs={{0,1},{1,0},{2,3},{3,2},{4,5},{5,4},{6,7},{7,6},{8,9},{9,8},{10,11... | collective-permute-start | bytes 589832 | tf_op jit(solution)/shard_map/ppermute | solution.py:252
  19.0 11.4 %slice-start = ((s8[6291456]{0:T(1024)(128)(4,1)}), s8[4194304]{0:T(1024)(128)(4,1)S(1)}, s32[]{:S(2)}) async-start(s8[6291456]{0:T(1024)(128)(4,1)} %bitcast.1), calls=%async_computation.4 | async-start | bytes 8388608
  19.0 11.4 %slice-start.1 = ((s8[6291456]{0:T(1024)(128)(4,1)}), s8[2097152]{0:T(1024)(128)(4,1)S(1)}, s32[]{:S(2)}) async-start(s8[6291456]{0:T(1024)(128)(4,1)} %bitcast.1), calls=%async_computation.5 | async-start | bytes 4194304
  19.0 11.4 %copy-start.1 = (bf16[1024,1024]{1,0:T(8,128)(2,1)S(1)}, bf16[1024,1024]{1,0:T(8,128)(2,1)}, u32[]{:S(2)}) copy-start(bf16[1024,1024]{1,0:T(8,128)(2,1)} %wv_ref.1) | copy-start | bytes 6291460
  19.0 11.4 %copy-start.2 = (bf16[1,32,1024]{2,1,0:T(8,128)(2,1)S(1)}, bf16[1,32,1024]{2,1,0:T(8,128)(2,1)}, u32[]{:S(2)}) copy-start(bf16[1,32,1024]{2,1,0:T(8,128)(2,1)} %x2_ref.1) | copy-start | bytes 196612
  19.0 11.4 %copy-start.3 = (f32[1024]{0:T(1024)S(1)}, f32[1024]{0:T(1024)}, u32[]{:S(2)}) copy-start(f32[1024]{0:T(1024)} %param.14) | copy-start | bytes 12292
  42.4 1.4 %collective-permute-start.1 = (bf16[16,48,128]{2,1,0:T(8,128)(2,1)S(1)}, bf16[16,48,128]{2,1,0:T(8,128)(2,1)S(1)}, u32[]{:S(2)}, u32[]{:S(2)}) collective-permute-start(bf16[16,48,128]{2,1,0:T(8,128)(2,1)S(1)} %all_to_all.22.mine_ref), channel_id=1, source_target_pairs={{0,1},{1,0},{2,3},{3,2},{4,5},{5,4},{6,7},{7,6},{8,9},{9,8},{10,11... | collective-permute-start | bytes 589832 | tf_op jit(solution)/shard_map/ppermute | solution.py:252
  43.9 11.2 %copy-start = (bf16[1024,1024]{1,0:T(8,128)(2,1)S(1)}, bf16[1024,1024]{1,0:T(8,128)(2,1)}, u32[]{:S(2)}) copy-start(bf16[1024,1024]{1,0:T(8,128)(2,1)} %wout_ref.1) | copy-start | bytes 6291460

commit v7 on v6

--- a/solution.py
+++ b/solution.py
@@ -108,7 +108,22 @@
 
 ALL = ("view", "tok")
 CORES = 2
+MIDDLE = HEADS // 4
 SHARP = HD ** (-0.5) * 1.4426950408889634
+
+
+def trade_groups():
+    groups = []
+    for s in range(CORES):
+        chips = [(MIDDLE + 1 - s + i) % HEADS for i in range(HEADS)]
+        groups.append([h * CORES + (h + s) % CORES for h in chips])
+    return groups
+
+
+def spot(h):
+    device = lax.axis_index("tok")
+    s = (device + device // CORES) % CORES
+    return (h + HEADS - MIDDLE - 1 + s) % HEADS
 
 
 def pack_heads(out_ref, q, k, v):
@@ -116,12 +131,13 @@
     half = rows // 2
     for h in range(HEADS):
         cols = slice(h * HD, (h + 1) * HD)
-        out_ref[h, 0:rows, :] = jnp.concatenate([k[:, cols], v[:, cols]], axis=-1)
-        out_ref[h, rows : rows + half, :] = jnp.concatenate([q[:half, cols], q[half:, cols]], axis=-1)
+        at = spot(h)
+        out_ref[at, 0:rows, :] = jnp.concatenate([k[:, cols], v[:, cols]], axis=-1)
+        out_ref[at, rows : rows + half, :] = jnp.concatenate([q[:half, cols], q[half:, cols]], axis=-1)
 
 
 def unpack_rows(got_ref):
-    pieces = [got_ref[h].astype(jnp.float32) for h in range(HEADS)]
+    pieces = [got_ref[spot(h)].astype(jnp.float32) for h in range(HEADS)]
     top = jnp.concatenate([p[:, :HD] for p in pieces], axis=-1)
     low = jnp.concatenate([p[:, HD:] for p in pieces], axis=-1)
     return jnp.concatenate([top, low], axis=0)
@@ -143,16 +159,17 @@
     pack_heads(out_ref, q_ref[0], k_ref[0], v_ref[0])
 
 
+def lower_half(shape):
+    return lax.broadcasted_iota(jnp.int32, shape, 1) < HD
+
+
+def turned(x):
+    return jnp.concatenate([x[:, HD:], x[:, :HD]], axis=-1)
+
+
 def key_values(piece_ref):
-    sources, lines, _ = piece_ref.shape
-    kv = piece_ref[:, 0 : lines * 2 // 3, :].reshape(-1, 2 * HD)
-    return kv[:, :HD], jnp.concatenate([kv[:, HD:], jnp.ones((kv.shape[0], HD), kv.dtype)], axis=-1)
-
-
-def some_queries(piece_ref, start, count):
-    lines = piece_ref.shape[1]
-    packed = piece_ref[start : start + count, lines * 2 // 3 : lines, :].reshape(-1, 2 * HD)
-    return jnp.concatenate([packed[:, :HD], packed[:, HD:]], axis=0)
+    kv = piece_ref[:, 0 : piece_ref.shape[1] * 2 // 3, :].reshape(-1, 2 * HD)
+    return kv, jnp.where(lower_half(kv.shape), jnp.ones_like(kv), kv)
 
 
 def score(queries, keys):
@@ -164,34 +181,35 @@
     return jnp.dot(weights, vals, preferred_element_type=jnp.float32)
 
 
-def begin_kernel(mine_ref, peak_ref, sum_ref):
-    sources, lines, _ = mine_ref.shape
+def begin_kernel(mine_ref, query_ref, peak_ref, sum_ref):
+    lines = mine_ref.shape[1]
+    packed = mine_ref[:, lines * 2 // 3 : lines, :].reshape(-1, 2 * HD)
     keys, vals = key_values(mine_ref)
-    step = max(1, 384 // lines)
-    rows = step * lines * 2 // 3
-    for i in range(sources // step):
-        scores = score(some_queries(mine_ref, i * step, step), keys)
+    n = packed.shape[0]
+    for i, part in enumerate((packed, turned(packed))):
+        at = slice(i * n, (i + 1) * n)
+        queries = jnp.where(lower_half(part.shape), part, jnp.zeros_like(part))
+        query_ref[at, :] = queries
+        scores = score(queries, keys)
         peak = jnp.max(scores, axis=-1, keepdims=True)
-        at = slice(i * rows, (i + 1) * rows)
         peak_ref[at, :] = peak
         sum_ref[at, :] = weigh(scores, peak, vals)
 
 
-def finish_kernel(mine_ref, other_ref, peak_ref, sum_ref, out_ref):
-    sources, lines, _ = mine_ref.shape
+def finish_kernel(other_ref, query_ref, peak_ref, sum_ref, out_ref):
     keys, vals = key_values(other_ref)
-    step = max(1, 384 // lines)
-    rows = step * lines * 2 // 3
-    for i in range(sources // step):
-        at = slice(i * rows, (i + 1) * rows)
-        scores = score(some_queries(mine_ref, i * step, step), keys)
+    n = query_ref.shape[0] // 2
+    sums = []
+    for i in range(2):
+        at = slice(i * n, (i + 1) * n)
+        scores = score(query_ref[at, :], keys)
         before = peak_ref[at, :]
         peak = jnp.maximum(before, jnp.max(scores, axis=-1, keepdims=True))
-        summed = sum_ref[at, :] * jnp.exp2((before - peak) * SHARP) + weigh(scores, peak, vals)
-        attn = (summed[:, :HD] / summed[:, HD:]).astype(jnp.bfloat16)
-        n = rows // 2
-        lined = jnp.concatenate([attn[:n], attn[n:]], axis=-1)
-        out_ref[i * step : (i + 1) * step] = lined.reshape(step, lines // 3, 2 * HD)
+        sums.append(sum_ref[at, :] * jnp.exp2((before - peak) * SHARP) + weigh(scores, peak, vals))
+    top, low = sums
+    left = lower_half(top.shape)
+    attn = jnp.where(left, turned(top), low) / jnp.where(left, top, turned(low))
+    out_ref[...] = attn.astype(jnp.bfloat16).reshape(out_ref.shape)
 
 
 def middle_kernel(got_ref, x2_ref, wv_ref, gain_ref, wqkv_ref, feats_hbm, out_ref, feats_ref, sem):
@@ -238,11 +256,12 @@
     rows = q1.shape[1]
     packed = ((HEADS, rows * 3 // 2, 2 * HD), jnp.bfloat16, pltpu.VMEM)
     halves = ((HEADS, rows // 2, 2 * HD), jnp.bfloat16, pltpu.VMEM)
+    queries = ((HEADS * rows, 2 * HD), jnp.bfloat16, pltpu.VMEM)
     peaks = ((HEADS * rows, 1), jnp.float32, pltpu.VMEM)
     sums = ((HEADS * rows, 2 * HD), jnp.float32, pltpu.VMEM)
     wide = (1, rows, HEADS * HD)
     devices = HEADS * CORES
-    groups = [[(p * CORES + core + 8) % devices for p in range(HEADS)] for core in range(CORES)]
+    groups = trade_groups()
 
     def trade(piece):
         return lax.all_to_all(piece, ALL, split_axis=0, concat_axis=0, tiled=True, axis_index_groups=groups)
@@ -250,9 +269,9 @@
     def attention(packed):
         mine = trade(packed)
         other = lax.ppermute(mine, ALL, [(i, i ^ 1) for i in range(devices)])
-        peak, summed = call(begin_kernel, [peaks, sums], (mine,), cost=pl.CostEstimate(1 << 30, 0, 1 << 20))
+        begun = call(begin_kernel, [queries, peaks, sums], (mine,), cost=pl.CostEstimate(1 << 30, 0, 1 << 20))
         cost = pl.CostEstimate(flops=16 << 30, bytes_accessed=40 << 20, transcendentals=0)
-        (half,) = call(finish_kernel, [halves], (mine, other, peak, summed), cost=cost)
+        (half,) = call(finish_kernel, [halves], (other, *begun), cost=cost)
         return trade(half)
 
     inputs = [pltpu.with_memory_space_constraint(x, pltpu.HBM) for x in (q1, k1, v1)]

time: 56.6 us -> 56.3 us (level)
  blocking collectives: 46.2 us -> 45.5 us
    all_to_all x4, blocking collectives: 46.2 us -> 45.5 us  [trade(): lax.all_to_all(piece, ALL, split_axis=0, concat_axis=0, tiled=True, axis_...]
where the time goes in v7:
time: 56.3 us; the launch traced here: 56 us
  blocking collectives  45.5 us (81%)
  Pallas kernels  8.41 us (15%)
  waiting for transfers between devices  1.25 us (2%)
  between operations  0.72 us (1%)
    all_to_all x4, blocking collectives, trade(): lax.all_to_all(piece, ALL, split_axis=0, concat_axis=0, tiled=True, axis_...  45.5 us
    pallas_call x7, Pallas kernels, call(): pl.pallas_call(body, out_shape=[jax.ShapeDtypeStruct(shape, dtype) for sh...  8.41 us
    ppermute x2, waiting for transfers between devices, attention(): other = lax.ppermute(mine, ALL, [(i, i ^ 1) for i in range(devices)])  1.25 us
  transfers between devices with their start and end apart: 2, of which 2 were waited for; matrix products, arithmetic and copies ran while one was open for 0% of the time, Pallas kernels for 3%

profile of v7, /device:TPU:0, one launch (start us, length us, event | category | flops | bytes accessed | tf_op | source)
XLA Modules:
  0.0 56.0 jit_solution(94323923939238539)
XLA Ops:
  0.6 1.1 %shard_map.95 = bf16[16,48,128]{2,1,0:T(8,128)(2,1)S(1)} custom-call(bf16[1,32,1024]{2,1,0:T(8,128)(2,1)} %q_hbm.1, bf16[1,32,1024]{2,1,0:T(8,128)(2,1)} %k_hbm.1, bf16[1,32,1024]{2,1,0:T(8,128)(2,1)} %v_hbm.1), custom_call_target="tpu_custom_call" | custom-call | tf_op jit(solution)/shard_map/pallas_call | solution.py:244
  1.7 15.9 %all_to_all.20.mine_ref = bf16[16,48,128]{2,1,0:T(8,128)(2,1)S(1)} all-to-all(bf16[16,48,128]{2,1,0:T(8,128)(2,1)S(1)} %shard_map.95), channel_id=1, replica_groups={{11,12,15,16,19,20,23,24,27,28,31,0,3,4,7,8},{9,10,13,14,17,18,21,22,25..., dimensions={0} | all-to-all | bytes 393216 | tf_op jit(solution)/shard_map/all_to_all | solution.py:267
  17.6 0.0 collective-permute-start
  17.6 0.8 %shard_map.96 = (bf16[512,128]{1,0:T(8,128)(2,1)S(1)}, f32[512,1]{1,0:T(8,128)S(1)}, f32[512,128]{1,0:T(8,128)S(1)}) custom-call(bf16[16,48,128]{2,1,0:T(8,128)(2,1)S(1)} %all_to_all.20.mine_ref), custom_call_target="tpu_custom_call" | custom-call | flops 1073741824 | bytes 1048576 | tf_op jit(solution)/shard_map/pallas_call | solution.py:244
  18.3 0.7 %collective-permute-done.other_ref = bf16[16,48,128]{2,1,0:T(8,128)(2,1)S(1)} collective-permute-done((bf16[16,48,128]{2,1,0:T(8,128)(2,1)S(1)}, bf16[16,48,128]{2,1,0:T(8,128)(2,1)S(1)}, u32[]{:S(2)}, u32[]{:S(2)}) %collective-permute-start) | collective-permute-done | bytes 196640 | tf_op jit(solution)/shard_map/ppermute | solution.py:271
  19.0 0.0 slice-start
  19.0 0.0 slice-start.1
  19.0 0.0 copy-start.1
  19.0 0.0 copy-start.2
  19.0 0.0 copy-start.3
  19.0 1.1 %shard_map.97 = bf16[16,16,128]{2,1,0:T(8,128)(2,1)S(1)} custom-call(bf16[16,48,128]{2,1,0:T(8,128)(2,1)S(1)} %collective-permute-done.other_ref, bf16[512,128]{1,0:T(8,128)(2,1)S(1)} %get-tuple-element.10.query_ref, f32[512,1]{1,0:T(8,128)S(1)} %get-tuple-element.11.peak_ref, f32[512,128]{1,0:T(8,128)S(1)} %get-tuple-element.12.sum_ref), custom_call_target="tpu_custom_call" | custom-call | flops 17179869184 | bytes 41943040 | tf_op jit(solution)/shard_map/pallas_call | solution.py:244
  20.2 9.5 %all_to_all.21.got_ref = bf16[16,16,128]{2,1,0:T(8,128)(2,1)S(1)} all-to-all(bf16[16,16,128]{2,1,0:T(8,128)(2,1)S(1)} %shard_map.97), channel_id=1, replica_groups={{11,12,15,16,19,20,23,24,27,28,31,0,3,4,7,8},{9,10,13,14,17,18,21,22,25..., dimensions={0} | all-to-all | bytes 131072 | tf_op jit(solution)/shard_map/all_to_all | solution.py:267
  29.7 0.0 slice-done
  29.7 0.0 slice-done.1
  29.7 0.0 copy-done.1
  29.7 0.0 copy-done.2
  29.7 0.0 copy-done.3
  29.7 2.4 %shard_map.98 = (f32[1,32,1024]{2,1,0:T(8,128)}, bf16[16,48,128]{2,1,0:T(8,128)(2,1)S(1)}) custom-call(bf16[16,16,128]{2,1,0:T(8,128)(2,1)S(1)} %all_to_all.21.got_ref, bf16[1,32,1024]{2,1,0:T(8,128)(2,1)S(1)} %copy-done.2, bf16[1024,1024]{1,0:T(8,128)(2,1)S(1)} %copy-done.1, f32[1,1024]{1,0:T(1,128)S(1)} %bitcast.3, bf16[1024,3072]{1,0:T(8,128)(2,1)S(1)} %bitcast.2), custom_call_target="tpu_custom_call" | custom-call | tf_op jit(solution)/shard_map/pallas_call | solution.py:244
  32.1 10.8 %all_to_all.22.mine_ref = bf16[16,48,128]{2,1,0:T(8,128)(2,1)S(1)} all-to-all(bf16[16,48,128]{2,1,0:T(8,128)(2,1)S(1)} %get-tuple-element.14), channel_id=1, replica_groups={{11,12,15,16,19,20,23,24,27,28,31,0,3,4,7,8},{9,10,13,14,17,18,21,22,25..., dimensions={0} | all-to-all | bytes 393216 | tf_op jit(solution)/shard_map/all_to_all | solution.py:267
  43.0 0.1 collective-permute-start.1
  43.1 0.8 %shard_map.99 = (bf16[512,128]{1,0:T(8,128)(2,1)S(1)}, f32[512,1]{1,0:T(8,128)S(1)}, f32[512,128]{1,0:T(8,128)S(1)}) custom-call(bf16[16,48,128]{2,1,0:T(8,128)(2,1)S(1)} %all_to_all.22.mine_ref), custom_call_target="tpu_custom_call" | custom-call | flops 1073741824 | bytes 1048576 | tf_op jit(solution)/shard_map/pallas_call | solution.py:244
  43.8 0.6 %collective-permute-done.1.other_ref = bf16[16,48,128]{2,1,0:T(8,128)(2,1)S(1)} collective-permute-done((bf16[16,48,128]{2,1,0:T(8,128)(2,1)S(1)}, bf16[16,48,128]{2,1,0:T(8,128)(2,1)S(1)}, u32[]{:S(2)}, u32[]{:S(2)}) %collective-permute-start.1) | collective-permute-done | bytes 196640 | tf_op jit(solution)/shard_map/ppermute | solution.py:271
  44.4 0.0 copy-start
  44.4 1.1 %shard_map.100 = bf16[16,16,128]{2,1,0:T(8,128)(2,1)S(1)} custom-call(bf16[16,48,128]{2,1,0:T(8,128)(2,1)S(1)} %collective-permute-done.1.other_ref, bf16[512,128]{1,0:T(8,128)(2,1)S(1)} %get-tuple-element.15.query_ref, f32[512,1]{1,0:T(8,128)S(1)} %get-tuple-element.16.peak_ref, f32[512,128]{1,0:T(8,128)S(1)} %get-tuple-element.17.sum_ref), custom_call_target="tpu_custom_call" | custom-call | flops 17179869184 | bytes 41943040 | tf_op jit(solution)/shard_map/pallas_call | solution.py:244
  45.5 9.3 %all_to_all.23.got_ref = bf16[16,16,128]{2,1,0:T(8,128)(2,1)S(1)} all-to-all(bf16[16,16,128]{2,1,0:T(8,128)(2,1)S(1)} %shard_map.100), channel_id=1, replica_groups={{11,12,15,16,19,20,23,24,27,28,31,0,3,4,7,8},{9,10,13,14,17,18,21,22,25..., dimensions={0} | all-to-all | bytes 131072 | tf_op jit(solution)/shard_map/all_to_all | solution.py:267
  54.8 0.0 copy-done
  54.8 1.2 %shard_map.101 = f32[1,32,1024]{2,1,0:T(8,128)} custom-call(bf16[16,16,128]{2,1,0:T(8,128)(2,1)S(1)} %all_to_all.23.got_ref, bf16[1024,1024]{1,0:T(8,128)(2,1)S(1)} %copy-done), custom_call_target="tpu_custom_call" | custom-call | tf_op jit(solution)/shard_map/pallas_call | solution.py:244
  (1 shorter events, 0.0 us)
Async XLA Ops:
  17.6 1.4 %collective-permute-start = (bf16[16,48,128]{2,1,0:T(8,128)(2,1)S(1)}, bf16[16,48,128]{2,1,0:T(8,128)(2,1)S(1)}, u32[]{:S(2)}, u32[]{:S(2)}) collective-permute-start(bf16[16,48,128]{2,1,0:T(8,128)(2,1)S(1)} %all_to_all.20.mine_ref), channel_id=1, source_target_pairs={{0,1},{1,0},{2,3},{3,2},{4,5},{5,4},{6,7},{7,6},{8,9},{9,8},{10,11... | collective-permute-start | bytes 589832 | tf_op jit(solution)/shard_map/ppermute | solution.py:271
  19.0 10.7 %slice-start = ((s8[6291456]{0:T(1024)(128)(4,1)}), s8[4194304]{0:T(1024)(128)(4,1)S(1)}, s32[]{:S(2)}) async-start(s8[6291456]{0:T(1024)(128)(4,1)} %bitcast.1), calls=%async_computation.4 | async-start | bytes 8388608
  19.0 10.7 %slice-start.1 = ((s8[6291456]{0:T(1024)(128)(4,1)}), s8[2097152]{0:T(1024)(128)(4,1)S(1)}, s32[]{:S(2)}) async-start(s8[6291456]{0:T(1024)(128)(4,1)} %bitcast.1), calls=%async_computation.5 | async-start | bytes 4194304
  19.0 10.7 %copy-start.1 = (bf16[1024,1024]{1,0:T(8,128)(2,1)S(1)}, bf16[1024,1024]{1,0:T(8,128)(2,1)}, u32[]{:S(2)}) copy-start(bf16[1024,1024]{1,0:T(8,128)(2,1)} %wv_ref.1) | copy-start | bytes 6291460
  19.0 10.7 %copy-start.2 = (bf16[1,32,1024]{2,1,0:T(8,128)(2,1)S(1)}, bf16[1,32,1024]{2,1,0:T(8,128)(2,1)}, u32[]{:S(2)}) copy-start(bf16[1,32,1024]{2,1,0:T(8,128)(2,1)} %x2_ref.1) | copy-start | bytes 196612
  19.0 10.7 %copy-start.3 = (f32[1024]{0:T(1024)S(1)}, f32[1024]{0:T(1024)}, u32[]{:S(2)}) copy-start(f32[1024]{0:T(1024)} %param.14) | copy-start | bytes 12292
  43.0 1.4 %collective-permute-start.1 = (bf16[16,48,128]{2,1,0:T(8,128)(2,1)S(1)}, bf16[16,48,128]{2,1,0:T(8,128)(2,1)S(1)}, u32[]{:S(2)}, u32[]{:S(2)}) collective-permute-start(bf16[16,48,128]{2,1,0:T(8,128)(2,1)S(1)} %all_to_all.22.mine_ref), channel_id=1, source_target_pairs={{0,1},{1,0},{2,3},{3,2},{4,5},{5,4},{6,7},{7,6},{8,9},{9,8},{10,11... | collective-permute-start | bytes 589832 | tf_op jit(solution)/shard_map/ppermute | solution.py:271
  44.4 10.4 %copy-start = (bf16[1024,1024]{1,0:T(8,128)(2,1)S(1)}, bf16[1024,1024]{1,0:T(8,128)(2,1)}, u32[]{:S(2)}) copy-start(bf16[1024,1024]{1,0:T(8,128)(2,1)} %wout_ref.1) | copy-start | bytes 6291460

commit v8 on v7

--- a/solution.py
+++ b/solution.py
@@ -108,22 +108,14 @@
 
 ALL = ("view", "tok")
 CORES = 2
-MIDDLE = HEADS // 4
+PLANES = (1, 3, 2, 0)
 SHARP = HD ** (-0.5) * 1.4426950408889634
 
 
 def trade_groups():
-    groups = []
-    for s in range(CORES):
-        chips = [(MIDDLE + 1 - s + i) % HEADS for i in range(HEADS)]
-        groups.append([h * CORES + (h + s) % CORES for h in chips])
-    return groups
-
-
-def spot(h):
-    device = lax.axis_index("tok")
-    s = (device + device // CORES) % CORES
-    return (h + HEADS - MIDDLE - 1 + s) % HEADS
+    plane = HEADS // len(PLANES)
+    chips = [p * plane + (i + 1) % plane for p in PLANES for i in range(plane)]
+    return [[chip * CORES + (chip + s) % CORES for chip in chips] for s in range(CORES)]
 
 
 def pack_heads(out_ref, q, k, v):
@@ -131,13 +123,12 @@
     half = rows // 2
     for h in range(HEADS):
         cols = slice(h * HD, (h + 1) * HD)
-        at = spot(h)
-        out_ref[at, 0:rows, :] = jnp.concatenate([k[:, cols], v[:, cols]], axis=-1)
-        out_ref[at, rows : rows + half, :] = jnp.concatenate([q[:half, cols], q[half:, cols]], axis=-1)
+        out_ref[h, 0:rows, :] = jnp.concatenate([k[:, cols], v[:, cols]], axis=-1)
+        out_ref[h, rows : rows + half, :] = jnp.concatenate([q[:half, cols], q[half:, cols]], axis=-1)
 
 
 def unpack_rows(got_ref):
-    pieces = [got_ref[spot(h)].astype(jnp.float32) for h in range(HEADS)]
+    pieces = [got_ref[h].astype(jnp.float32) for h in range(HEADS)]
     top = jnp.concatenate([p[:, :HD] for p in pieces], axis=-1)
     low = jnp.concatenate([p[:, HD:] for p in pieces], axis=-1)
     return jnp.concatenate([top, low], axis=0)
@@ -208,7 +199,7 @@
         sums.append(sum_ref[at, :] * jnp.exp2((before - peak) * SHARP) + weigh(scores, peak, vals))
     top, low = sums
     left = lower_half(top.shape)
-    attn = jnp.where(left, turned(top), low) / jnp.where(left, top, turned(low))
+    attn = jnp.where(left, pltpu.roll(top, HD, 1), low) / jnp.where(left, top, pltpu.roll(low, HD, 1))
     out_ref[...] = attn.astype(jnp.bfloat16).reshape(out_ref.shape)
 
 

time: 56.3 us -> 56.3 us (level)
  starting transfers between devices: 0.11 us -> 1.63 us
  waiting for transfers between devices: 1.25 us -> 0.61 us
    ppermute x2, starting transfers between devices: 0.11 us -> 1.63 us  [attention(): other = lax.ppermute(mine, ALL, [(i, i ^ 1) for i in range(devices)])]
    ppermute x2, waiting for transfers between devices: 1.25 us -> 0.61 us  [attention(): other = lax.ppermute(mine, ALL, [(i, i ^ 1) for i in range(devices)])]
where the time goes in v8:
time: 56.3 us; the launch traced here: 56 us
  blocking collectives  45 us (80%)
  Pallas kernels  7.96 us (14%)
  starting transfers between devices  1.63 us (3%)
  between operations  0.71 us (1%)
  waiting for transfers between devices  0.61 us (1%)
    all_to_all x4, blocking collectives, trade(): lax.all_to_all(piece, ALL, split_axis=0, concat_axis=0, tiled=True, axis_...  45 us
    pallas_call x7, Pallas kernels, call(): pl.pallas_call(body, out_shape=[jax.ShapeDtypeStruct(shape, dtype) for sh...  7.96 us
    ppermute x2, starting transfers between devices, attention(): other = lax.ppermute(mine, ALL, [(i, i ^ 1) for i in range(devices)])  1.63 us
  transfers between devices with their start and end apart: 2, of which 2 were waited for; matrix products, arithmetic and copies ran while one was open for 0% of the time, Pallas kernels for 3%

profile of v8, /device:TPU:0, one launch (start us, length us, event | category | flops | bytes accessed | tf_op | source)
XLA Modules:
  0.0 56.0 jit_solution(17856586472251717786)
XLA Ops:
  0.6 1.1 %shard_map.95 = bf16[16,48,128]{2,1,0:T(8,128)(2,1)S(1)} custom-call(bf16[1,32,1024]{2,1,0:T(8,128)(2,1)} %q_hbm.1, bf16[1,32,1024]{2,1,0:T(8,128)(2,1)} %k_hbm.1, bf16[1,32,1024]{2,1,0:T(8,128)(2,1)} %v_hbm.1), custom_call_target="tpu_custom_call" | custom-call | tf_op jit(solution)/shard_map/pallas_call | solution.py:235
  1.7 14.4 %all_to_all.20.mine_ref = bf16[16,48,128]{2,1,0:T(8,128)(2,1)S(1)} all-to-all(bf16[16,48,128]{2,1,0:T(8,128)(2,1)S(1)} %shard_map.95), channel_id=1, replica_groups={{11,12,15,8,27,28,31,24,19,20,23,16,3,4,7,0},{10,13,14,9,26,29,30,25,18..., dimensions={0} | all-to-all | bytes 393216 | tf_op jit(solution)/shard_map/all_to_all | solution.py:258
  16.1 0.9 %collective-permute-start = (bf16[16,48,128]{2,1,0:T(8,128)(2,1)S(1)}, bf16[16,48,128]{2,1,0:T(8,128)(2,1)S(1)}, u32[]{:S(2)}, u32[]{:S(2)}) collective-permute-start(bf16[16,48,128]{2,1,0:T(8,128)(2,1)S(1)} %all_to_all.20.mine_ref), channel_id=1, source_target_pairs={{0,1},{1,0},{2,3},{3,2},{4,5},{5,4},{6,7},{7,6},{8,9},{9,8},{10,11... | collective-permute-start | bytes 589832 | tf_op jit(solution)/shard_map/ppermute | solution.py:262
  17.0 0.8 %shard_map.96 = (bf16[512,128]{1,0:T(8,128)(2,1)S(1)}, f32[512,1]{1,0:T(8,128)S(1)}, f32[512,128]{1,0:T(8,128)S(1)}) custom-call(bf16[16,48,128]{2,1,0:T(8,128)(2,1)S(1)} %all_to_all.20.mine_ref), custom_call_target="tpu_custom_call" | custom-call | flops 1073741824 | bytes 1048576 | tf_op jit(solution)/shard_map/pallas_call | solution.py:235
  17.7 0.3 collective-permute-done.other_ref
  18.0 0.0 slice-start
  18.0 0.0 slice-start.1
  18.0 0.0 copy-start.1
  18.1 0.0 copy-start.2
  18.1 0.0 copy-start.3
  18.1 1.1 %shard_map.97 = bf16[16,16,128]{2,1,0:T(8,128)(2,1)S(1)} custom-call(bf16[16,48,128]{2,1,0:T(8,128)(2,1)S(1)} %collective-permute-done.other_ref, bf16[512,128]{1,0:T(8,128)(2,1)S(1)} %get-tuple-element.10.query_ref, f32[512,1]{1,0:T(8,128)S(1)} %get-tuple-element.11.peak_ref, f32[512,128]{1,0:T(8,128)S(1)} %get-tuple-element.12.sum_ref), custom_call_target="tpu_custom_call" | custom-call | flops 17179869184 | bytes 41943040 | tf_op jit(solution)/shard_map/pallas_call | solution.py:235
  19.2 10.6 %all_to_all.21.got_ref = bf16[16,16,128]{2,1,0:T(8,128)(2,1)S(1)} all-to-all(bf16[16,16,128]{2,1,0:T(8,128)(2,1)S(1)} %shard_map.97), channel_id=1, replica_groups={{11,12,15,8,27,28,31,24,19,20,23,16,3,4,7,0},{10,13,14,9,26,29,30,25,18..., dimensions={0} | all-to-all | bytes 131072 | tf_op jit(solution)/shard_map/all_to_all | solution.py:258
  29.8 0.0 slice-done
  29.8 0.0 slice-done.1
  29.8 0.0 copy-done.1
  29.8 0.0 copy-done.2
  29.8 0.0 copy-done.3
  29.8 2.0 %shard_map.98 = (f32[1,32,1024]{2,1,0:T(8,128)}, bf16[16,48,128]{2,1,0:T(8,128)(2,1)S(1)}) custom-call(bf16[16,16,128]{2,1,0:T(8,128)(2,1)S(1)} %all_to_all.21.got_ref, bf16[1,32,1024]{2,1,0:T(8,128)(2,1)S(1)} %copy-done.2, bf16[1024,1024]{1,0:T(8,128)(2,1)S(1)} %copy-done.1, f32[1,1024]{1,0:T(1,128)S(1)} %bitcast.3, bf16[1024,3072]{1,0:T(8,128)(2,1)S(1)} %bitcast.2), custom_call_target="tpu_custom_call" | custom-call | tf_op jit(solution)/shard_map/pallas_call | solution.py:235
  31.7 10.0 %all_to_all.22.mine_ref = bf16[16,48,128]{2,1,0:T(8,128)(2,1)S(1)} all-to-all(bf16[16,48,128]{2,1,0:T(8,128)(2,1)S(1)} %get-tuple-element.14), channel_id=1, replica_groups={{11,12,15,8,27,28,31,24,19,20,23,16,3,4,7,0},{10,13,14,9,26,29,30,25,18..., dimensions={0} | all-to-all | bytes 393216 | tf_op jit(solution)/shard_map/all_to_all | solution.py:258
  41.7 0.8 %collective-permute-start.1 = (bf16[16,48,128]{2,1,0:T(8,128)(2,1)S(1)}, bf16[16,48,128]{2,1,0:T(8,128)(2,1)S(1)}, u32[]{:S(2)}, u32[]{:S(2)}) collective-permute-start(bf16[16,48,128]{2,1,0:T(8,128)(2,1)S(1)} %all_to_all.22.mine_ref), channel_id=1, source_target_pairs={{0,1},{1,0},{2,3},{3,2},{4,5},{5,4},{6,7},{7,6},{8,9},{9,8},{10,11... | collective-permute-start | bytes 589832 | tf_op jit(solution)/shard_map/ppermute | solution.py:262
  42.5 0.8 %shard_map.99 = (bf16[512,128]{1,0:T(8,128)(2,1)S(1)}, f32[512,1]{1,0:T(8,128)S(1)}, f32[512,128]{1,0:T(8,128)S(1)}) custom-call(bf16[16,48,128]{2,1,0:T(8,128)(2,1)S(1)} %all_to_all.22.mine_ref), custom_call_target="tpu_custom_call" | custom-call | flops 1073741824 | bytes 1048576 | tf_op jit(solution)/shard_map/pallas_call | solution.py:235
  43.3 0.3 collective-permute-done.1.other_ref
  43.6 0.0 copy-start
  43.6 1.1 %shard_map.100 = bf16[16,16,128]{2,1,0:T(8,128)(2,1)S(1)} custom-call(bf16[16,48,128]{2,1,0:T(8,128)(2,1)S(1)} %collective-permute-done.1.other_ref, bf16[512,128]{1,0:T(8,128)(2,1)S(1)} %get-tuple-element.15.query_ref, f32[512,1]{1,0:T(8,128)S(1)} %get-tuple-element.16.peak_ref, f32[512,128]{1,0:T(8,128)S(1)} %get-tuple-element.17.sum_ref), custom_call_target="tpu_custom_call" | custom-call | flops 17179869184 | bytes 41943040 | tf_op jit(solution)/shard_map/pallas_call | solution.py:235
  44.7 10.0 %all_to_all.23.got_ref = bf16[16,16,128]{2,1,0:T(8,128)(2,1)S(1)} all-to-all(bf16[16,16,128]{2,1,0:T(8,128)(2,1)S(1)} %shard_map.100), channel_id=1, replica_groups={{11,12,15,8,27,28,31,24,19,20,23,16,3,4,7,0},{10,13,14,9,26,29,30,25,18..., dimensions={0} | all-to-all | bytes 131072 | tf_op jit(solution)/shard_map/all_to_all | solution.py:258
  54.7 0.0 copy-done
  54.7 1.3 %shard_map.101 = f32[1,32,1024]{2,1,0:T(8,128)} custom-call(bf16[16,16,128]{2,1,0:T(8,128)(2,1)S(1)} %all_to_all.23.got_ref, bf16[1024,1024]{1,0:T(8,128)(2,1)S(1)} %copy-done), custom_call_target="tpu_custom_call" | custom-call | tf_op jit(solution)/shard_map/pallas_call | solution.py:235
  (1 shorter events, 0.0 us)
Async XLA Ops:
  16.1 1.9 %collective-permute-start = (bf16[16,48,128]{2,1,0:T(8,128)(2,1)S(1)}, bf16[16,48,128]{2,1,0:T(8,128)(2,1)S(1)}, u32[]{:S(2)}, u32[]{:S(2)}) collective-permute-start(bf16[16,48,128]{2,1,0:T(8,128)(2,1)S(1)} %all_to_all.20.mine_ref), channel_id=1, source_target_pairs={{0,1},{1,0},{2,3},{3,2},{4,5},{5,4},{6,7},{7,6},{8,9},{9,8},{10,11... | collective-permute-start | bytes 589832 | tf_op jit(solution)/shard_map/ppermute | solution.py:262
  18.0 11.7 %slice-start = ((s8[6291456]{0:T(1024)(128)(4,1)}), s8[4194304]{0:T(1024)(128)(4,1)S(1)}, s32[]{:S(2)}) async-start(s8[6291456]{0:T(1024)(128)(4,1)} %bitcast.1), calls=%async_computation.4 | async-start | bytes 8388608
  18.0 11.7 %slice-start.1 = ((s8[6291456]{0:T(1024)(128)(4,1)}), s8[2097152]{0:T(1024)(128)(4,1)S(1)}, s32[]{:S(2)}) async-start(s8[6291456]{0:T(1024)(128)(4,1)} %bitcast.1), calls=%async_computation.5 | async-start | bytes 4194304
  18.0 11.7 %copy-start.1 = (bf16[1024,1024]{1,0:T(8,128)(2,1)S(1)}, bf16[1024,1024]{1,0:T(8,128)(2,1)}, u32[]{:S(2)}) copy-start(bf16[1024,1024]{1,0:T(8,128)(2,1)} %wv_ref.1) | copy-start | bytes 6291460
  18.1 11.7 %copy-start.2 = (bf16[1,32,1024]{2,1,0:T(8,128)(2,1)S(1)}, bf16[1,32,1024]{2,1,0:T(8,128)(2,1)}, u32[]{:S(2)}) copy-start(bf16[1,32,1024]{2,1,0:T(8,128)(2,1)} %x2_ref.1) | copy-start | bytes 196612
  18.1 11.7 %copy-start.3 = (f32[1024]{0:T(1024)S(1)}, f32[1024]{0:T(1024)}, u32[]{:S(2)}) copy-start(f32[1024]{0:T(1024)} %param.14) | copy-start | bytes 12292
  41.7 1.8 %collective-permute-start.1 = (bf16[16,48,128]{2,1,0:T(8,128)(2,1)S(1)}, bf16[16,48,128]{2,1,0:T(8,128)(2,1)S(1)}, u32[]{:S(2)}, u32[]{:S(2)}) collective-permute-start(bf16[16,48,128]{2,1,0:T(8,128)(2,1)S(1)} %all_to_all.22.mine_ref), channel_id=1, source_target_pairs={{0,1},{1,0},{2,3},{3,2},{4,5},{5,4},{6,7},{7,6},{8,9},{9,8},{10,11... | collective-permute-start | bytes 589832 | tf_op jit(solution)/shard_map/ppermute | solution.py:262
  43.6 11.1 %copy-start = (bf16[1024,1024]{1,0:T(8,128)(2,1)S(1)}, bf16[1024,1024]{1,0:T(8,128)(2,1)}, u32[]{:S(2)}) copy-start(bf16[1024,1024]{1,0:T(8,128)(2,1)} %wout_ref.1) | copy-start | bytes 6291460

commit v9 on v8

--- a/solution.py
+++ b/solution.py
@@ -108,7 +108,7 @@
 
 ALL = ("view", "tok")
 CORES = 2
-PLANES = (1, 3, 2, 0)
+PLANES = (1, 2, 3, 0)
 SHARP = HD ** (-0.5) * 1.4426950408889634
 
 

time: 56.3 us -> 55.9 us (level)
  blocking collectives: 45 us -> 43.8 us
  starting transfers between devices: 1.63 us -> 2.52 us
    all_to_all x4, blocking collectives: 45 us -> 43.8 us  [trade(): lax.all_to_all(piece, ALL, split_axis=0, concat_axis=0, tiled=True, axis_...]
    ppermute x2, starting transfers between devices: 1.63 us -> 2.52 us  [attention(): other = lax.ppermute(mine, ALL, [(i, i ^ 1) for i in range(devices)])]
where the time goes in v9:
time: 55.9 us; the launch traced here: 55.7 us
  blocking collectives  43.8 us (78%)
  Pallas kernels  7.96 us (14%)
  starting transfers between devices  2.52 us (5%)
  between operations  0.71 us (1%)
  waiting for transfers between devices  0.62 us (1%)
    all_to_all x4, blocking collectives, trade(): lax.all_to_all(piece, ALL, split_axis=0, concat_axis=0, tiled=True, axis_...  43.8 us
    pallas_call x7, Pallas kernels, call(): pl.pallas_call(body, out_shape=[jax.ShapeDtypeStruct(shape, dtype) for sh...  7.96 us
    ppermute x2, starting transfers between devices, attention(): other = lax.ppermute(mine, ALL, [(i, i ^ 1) for i in range(devices)])  2.52 us
  transfers between devices with their start and end apart: 2, of which 2 were waited for; matrix products, arithmetic and copies ran while one was open for 0% of the time, Pallas kernels for 3%

profile of v9, /device:TPU:0, one launch (start us, length us, event | category | flops | bytes accessed | tf_op | source)
XLA Modules:
  0.0 55.7 jit_solution(2930708518003208560)
XLA Ops:
  0.6 1.1 %shard_map.95 = bf16[16,48,128]{2,1,0:T(8,128)(2,1)S(1)} custom-call(bf16[1,32,1024]{2,1,0:T(8,128)(2,1)} %q_hbm.1, bf16[1,32,1024]{2,1,0:T(8,128)(2,1)} %k_hbm.1, bf16[1,32,1024]{2,1,0:T(8,128)(2,1)} %v_hbm.1), custom_call_target="tpu_custom_call" | custom-call | tf_op jit(solution)/shard_map/pallas_call | solution.py:235
  1.7 13.9 %all_to_all.20.mine_ref = bf16[16,48,128]{2,1,0:T(8,128)(2,1)S(1)} all-to-all(bf16[16,48,128]{2,1,0:T(8,128)(2,1)S(1)} %shard_map.95), channel_id=1, replica_groups={{11,12,15,8,19,20,23,16,27,28,31,24,3,4,7,0},{10,13,14,9,18,21,22,17,26..., dimensions={0} | all-to-all | bytes 393216 | tf_op jit(solution)/shard_map/all_to_all | solution.py:258
  15.6 1.5 %collective-permute-start = (bf16[16,48,128]{2,1,0:T(8,128)(2,1)S(1)}, bf16[16,48,128]{2,1,0:T(8,128)(2,1)S(1)}, u32[]{:S(2)}, u32[]{:S(2)}) collective-permute-start(bf16[16,48,128]{2,1,0:T(8,128)(2,1)S(1)} %all_to_all.20.mine_ref), channel_id=1, source_target_pairs={{0,1},{1,0},{2,3},{3,2},{4,5},{5,4},{6,7},{7,6},{8,9},{9,8},{10,11... | collective-permute-start | bytes 589832 | tf_op jit(solution)/shard_map/ppermute | solution.py:262
  17.1 0.8 %shard_map.96 = (bf16[512,128]{1,0:T(8,128)(2,1)S(1)}, f32[512,1]{1,0:T(8,128)S(1)}, f32[512,128]{1,0:T(8,128)S(1)}) custom-call(bf16[16,48,128]{2,1,0:T(8,128)(2,1)S(1)} %all_to_all.20.mine_ref), custom_call_target="tpu_custom_call" | custom-call | flops 1073741824 | bytes 1048576 | tf_op jit(solution)/shard_map/pallas_call | solution.py:235
  17.9 0.3 collective-permute-done.other_ref
  18.2 0.0 slice-start
  18.2 0.0 slice-start.1
  18.2 0.0 copy-start.1
  18.2 0.0 copy-start.2
  18.2 0.0 copy-start.3
  18.2 1.1 %shard_map.97 = bf16[16,16,128]{2,1,0:T(8,128)(2,1)S(1)} custom-call(bf16[16,48,128]{2,1,0:T(8,128)(2,1)S(1)} %collective-permute-done.other_ref, bf16[512,128]{1,0:T(8,128)(2,1)S(1)} %get-tuple-element.10.query_ref, f32[512,1]{1,0:T(8,128)S(1)} %get-tuple-element.11.peak_ref, f32[512,128]{1,0:T(8,128)S(1)} %get-tuple-element.12.sum_ref), custom_call_target="tpu_custom_call" | custom-call | flops 17179869184 | bytes 41943040 | tf_op jit(solution)/shard_map/pallas_call | solution.py:235
  19.3 10.2 %all_to_all.21.got_ref = bf16[16,16,128]{2,1,0:T(8,128)(2,1)S(1)} all-to-all(bf16[16,16,128]{2,1,0:T(8,128)(2,1)S(1)} %shard_map.97), channel_id=1, replica_groups={{11,12,15,8,19,20,23,16,27,28,31,24,3,4,7,0},{10,13,14,9,18,21,22,17,26..., dimensions={0} | all-to-all | bytes 131072 | tf_op jit(solution)/shard_map/all_to_all | solution.py:258
  29.5 0.0 slice-done
  29.5 0.0 slice-done.1
  29.5 0.0 copy-done.1
  29.5 0.0 copy-done.2
  29.5 0.0 copy-done.3
  29.6 2.0 %shard_map.98 = (f32[1,32,1024]{2,1,0:T(8,128)}, bf16[16,48,128]{2,1,0:T(8,128)(2,1)S(1)}) custom-call(bf16[16,16,128]{2,1,0:T(8,128)(2,1)S(1)} %all_to_all.21.got_ref, bf16[1,32,1024]{2,1,0:T(8,128)(2,1)S(1)} %copy-done.2, bf16[1024,1024]{1,0:T(8,128)(2,1)S(1)} %copy-done.1, f32[1,1024]{1,0:T(1,128)S(1)} %bitcast.3, bf16[1024,3072]{1,0:T(8,128)(2,1)S(1)} %bitcast.2), custom_call_target="tpu_custom_call" | custom-call | tf_op jit(solution)/shard_map/pallas_call | solution.py:235
  31.5 10.3 %all_to_all.22.mine_ref = bf16[16,48,128]{2,1,0:T(8,128)(2,1)S(1)} all-to-all(bf16[16,48,128]{2,1,0:T(8,128)(2,1)S(1)} %get-tuple-element.14), channel_id=1, replica_groups={{11,12,15,8,19,20,23,16,27,28,31,24,3,4,7,0},{10,13,14,9,18,21,22,17,26..., dimensions={0} | all-to-all | bytes 393216 | tf_op jit(solution)/shard_map/all_to_all | solution.py:258
  41.9 1.0 %collective-permute-start.1 = (bf16[16,48,128]{2,1,0:T(8,128)(2,1)S(1)}, bf16[16,48,128]{2,1,0:T(8,128)(2,1)S(1)}, u32[]{:S(2)}, u32[]{:S(2)}) collective-permute-start(bf16[16,48,128]{2,1,0:T(8,128)(2,1)S(1)} %all_to_all.22.mine_ref), channel_id=1, source_target_pairs={{0,1},{1,0},{2,3},{3,2},{4,5},{5,4},{6,7},{7,6},{8,9},{9,8},{10,11... | collective-permute-start | bytes 589832 | tf_op jit(solution)/shard_map/ppermute | solution.py:262
  42.8 0.7 %shard_map.99 = (bf16[512,128]{1,0:T(8,128)(2,1)S(1)}, f32[512,1]{1,0:T(8,128)S(1)}, f32[512,128]{1,0:T(8,128)S(1)}) custom-call(bf16[16,48,128]{2,1,0:T(8,128)(2,1)S(1)} %all_to_all.22.mine_ref), custom_call_target="tpu_custom_call" | custom-call | flops 1073741824 | bytes 1048576 | tf_op jit(solution)/shard_map/pallas_call | solution.py:235
  43.6 0.3 collective-permute-done.1.other_ref
  43.9 0.0 copy-start
  43.9 1.1 %shard_map.100 = bf16[16,16,128]{2,1,0:T(8,128)(2,1)S(1)} custom-call(bf16[16,48,128]{2,1,0:T(8,128)(2,1)S(1)} %collective-permute-done.1.other_ref, bf16[512,128]{1,0:T(8,128)(2,1)S(1)} %get-tuple-element.15.query_ref, f32[512,1]{1,0:T(8,128)S(1)} %get-tuple-element.16.peak_ref, f32[512,128]{1,0:T(8,128)S(1)} %get-tuple-element.17.sum_ref), custom_call_target="tpu_custom_call" | custom-call | flops 17179869184 | bytes 41943040 | tf_op jit(solution)/shard_map/pallas_call | solution.py:235
  45.0 9.4 %all_to_all.23.got_ref = bf16[16,16,128]{2,1,0:T(8,128)(2,1)S(1)} all-to-all(bf16[16,16,128]{2,1,0:T(8,128)(2,1)S(1)} %shard_map.100), channel_id=1, replica_groups={{11,12,15,8,19,20,23,16,27,28,31,24,3,4,7,0},{10,13,14,9,18,21,22,17,26..., dimensions={0} | all-to-all | bytes 131072 | tf_op jit(solution)/shard_map/all_to_all | solution.py:258
  54.4 0.0 copy-done
  54.4 1.3 %shard_map.101 = f32[1,32,1024]{2,1,0:T(8,128)} custom-call(bf16[16,16,128]{2,1,0:T(8,128)(2,1)S(1)} %all_to_all.23.got_ref, bf16[1024,1024]{1,0:T(8,128)(2,1)S(1)} %copy-done), custom_call_target="tpu_custom_call" | custom-call | tf_op jit(solution)/shard_map/pallas_call | solution.py:235
  (1 shorter events, 0.0 us)
Async XLA Ops:
  15.6 2.6 %collective-permute-start = (bf16[16,48,128]{2,1,0:T(8,128)(2,1)S(1)}, bf16[16,48,128]{2,1,0:T(8,128)(2,1)S(1)}, u32[]{:S(2)}, u32[]{:S(2)}) collective-permute-start(bf16[16,48,128]{2,1,0:T(8,128)(2,1)S(1)} %all_to_all.20.mine_ref), channel_id=1, source_target_pairs={{0,1},{1,0},{2,3},{3,2},{4,5},{5,4},{6,7},{7,6},{8,9},{9,8},{10,11... | collective-permute-start | bytes 589832 | tf_op jit(solution)/shard_map/ppermute | solution.py:262
  18.2 11.3 %slice-start = ((s8[6291456]{0:T(1024)(128)(4,1)}), s8[4194304]{0:T(1024)(128)(4,1)S(1)}, s32[]{:S(2)}) async-start(s8[6291456]{0:T(1024)(128)(4,1)} %bitcast.1), calls=%async_computation.4 | async-start | bytes 8388608
  18.2 11.3 %slice-start.1 = ((s8[6291456]{0:T(1024)(128)(4,1)}), s8[2097152]{0:T(1024)(128)(4,1)S(1)}, s32[]{:S(2)}) async-start(s8[6291456]{0:T(1024)(128)(4,1)} %bitcast.1), calls=%async_computation.5 | async-start | bytes 4194304
  18.2 11.3 %copy-start.1 = (bf16[1024,1024]{1,0:T(8,128)(2,1)S(1)}, bf16[1024,1024]{1,0:T(8,128)(2,1)}, u32[]{:S(2)}) copy-start(bf16[1024,1024]{1,0:T(8,128)(2,1)} %wv_ref.1) | copy-start | bytes 6291460
  18.2 11.3 %copy-start.2 = (bf16[1,32,1024]{2,1,0:T(8,128)(2,1)S(1)}, bf16[1,32,1024]{2,1,0:T(8,128)(2,1)}, u32[]{:S(2)}) copy-start(bf16[1,32,1024]{2,1,0:T(8,128)(2,1)} %x2_ref.1) | copy-start | bytes 196612
  18.2 11.3 %copy-start.3 = (f32[1024]{0:T(1024)S(1)}, f32[1024]{0:T(1024)}, u32[]{:S(2)}) copy-start(f32[1024]{0:T(1024)} %param.14) | copy-start | bytes 12292
  41.9 2.1 %collective-permute-start.1 = (bf16[16,48,128]{2,1,0:T(8,128)(2,1)S(1)}, bf16[16,48,128]{2,1,0:T(8,128)(2,1)S(1)}, u32[]{:S(2)}, u32[]{:S(2)}) collective-permute-start(bf16[16,48,128]{2,1,0:T(8,128)(2,1)S(1)} %all_to_all.22.mine_ref), channel_id=1, source_target_pairs={{0,1},{1,0},{2,3},{3,2},{4,5},{5,4},{6,7},{7,6},{8,9},{9,8},{10,11... | collective-permute-start | bytes 589832 | tf_op jit(solution)/shard_map/ppermute | solution.py:262
  43.9 10.5 %copy-start = (bf16[1024,1024]{1,0:T(8,128)(2,1)S(1)}, bf16[1024,1024]{1,0:T(8,128)(2,1)}, u32[]{:S(2)}) copy-start(bf16[1024,1024]{1,0:T(8,128)(2,1)} %wout_ref.1) | copy-start | bytes 6291460

commit v10 on v9

--- a/solution.py
+++ b/solution.py
@@ -119,16 +119,16 @@
 
 
 def pack_heads(out_ref, q, k, v):
-    rows = q.shape[0]
-    half = rows // 2
+    rows = k.shape[0]
+    half = q.shape[0] // 2
     for h in range(HEADS):
         cols = slice(h * HD, (h + 1) * HD)
         out_ref[h, 0:rows, :] = jnp.concatenate([k[:, cols], v[:, cols]], axis=-1)
         out_ref[h, rows : rows + half, :] = jnp.concatenate([q[:half, cols], q[half:, cols]], axis=-1)
 
 
-def unpack_rows(got_ref):
-    pieces = [got_ref[h].astype(jnp.float32) for h in range(HEADS)]
+def unpack_rows(got_ref, start, count):
+    pieces = [got_ref[h, start : start + count, :].astype(jnp.float32) for h in range(HEADS)]
     top = jnp.concatenate([p[:, :HD] for p in pieces], axis=-1)
     low = jnp.concatenate([p[:, HD:] for p in pieces], axis=-1)
     return jnp.concatenate([top, low], axis=0)
@@ -158,8 +158,8 @@
     return jnp.concatenate([x[:, HD:], x[:, :HD]], axis=-1)
 
 
-def key_values(piece_ref):
-    kv = piece_ref[:, 0 : piece_ref.shape[1] * 2 // 3, :].reshape(-1, 2 * HD)
+def key_values(piece_ref, rows):
+    kv = piece_ref[:, 0:rows, :].reshape(-1, 2 * HD)
     return kv, jnp.where(lower_half(kv.shape), jnp.ones_like(kv), kv)
 
 
@@ -172,14 +172,24 @@
     return jnp.dot(weights, vals, preferred_element_type=jnp.float32)
 
 
+def two_queries(piece_ref, rows):
+    packed = piece_ref[:, rows:, :].reshape(-1, 2 * HD)
+    return [jnp.where(lower_half(part.shape), part, jnp.zeros_like(part)) for part in (packed, turned(packed))]
+
+
+def lined(sums):
+    top, low = sums
+    left = lower_half(top.shape)
+    attn = jnp.where(left, pltpu.roll(top, HD, 1), low) / jnp.where(left, top, pltpu.roll(low, HD, 1))
+    return attn.astype(jnp.bfloat16).reshape(HEADS, -1, 2 * HD)
+
+
 def begin_kernel(mine_ref, query_ref, peak_ref, sum_ref):
-    lines = mine_ref.shape[1]
-    packed = mine_ref[:, lines * 2 // 3 : lines, :].reshape(-1, 2 * HD)
-    keys, vals = key_values(mine_ref)
-    n = packed.shape[0]
-    for i, part in enumerate((packed, turned(packed))):
+    rows = mine_ref.shape[1] * 2 // 3
+    keys, vals = key_values(mine_ref, rows)
+    for i, queries in enumerate(two_queries(mine_ref, rows)):
+        n = queries.shape[0]
         at = slice(i * n, (i + 1) * n)
-        queries = jnp.where(lower_half(part.shape), part, jnp.zeros_like(part))
         query_ref[at, :] = queries
         scores = score(queries, keys)
         peak = jnp.max(scores, axis=-1, keepdims=True)
@@ -188,7 +198,7 @@
 
 
 def finish_kernel(other_ref, query_ref, peak_ref, sum_ref, out_ref):
-    keys, vals = key_values(other_ref)
+    keys, vals = key_values(other_ref, other_ref.shape[1] * 2 // 3)
     n = query_ref.shape[0] // 2
     sums = []
     for i in range(2):
@@ -197,29 +207,44 @@
         before = peak_ref[at, :]
         peak = jnp.maximum(before, jnp.max(scores, axis=-1, keepdims=True))
         sums.append(sum_ref[at, :] * jnp.exp2((before - peak) * SHARP) + weigh(scores, peak, vals))
-    top, low = sums
-    left = lower_half(top.shape)
-    attn = jnp.where(left, pltpu.roll(top, HD, 1), low) / jnp.where(left, top, pltpu.roll(low, HD, 1))
-    out_ref[...] = attn.astype(jnp.bfloat16).reshape(out_ref.shape)
-
-
-def middle_kernel(got_ref, x2_ref, wv_ref, gain_ref, wqkv_ref, feats_hbm, out_ref, feats_ref, sem):
-    feats = unit(unpack_rows(got_ref))
-    feats_ref[0] = feats
+    attn = lined(sums)
+    half, away = attn.shape[1], HEADS // 2
+    out_ref[:, 0:half, :] = attn
+    out_ref[:away, half:, :] = attn[away:]
+    out_ref[away:, half:, :] = attn[:away]
+
+
+def whole_kernel(got_ref, out_ref):
+    rows = got_ref.shape[1] * 4 // 5
+    keys, vals = key_values(got_ref, rows)
+    sums = []
+    for queries in two_queries(got_ref, rows):
+        scores = score(queries, keys)
+        sums.append(weigh(scores, jnp.max(scores, axis=-1, keepdims=True), vals))
+    out_ref[...] = lined(sums)
+
+
+def middle_kernel(got_ref, x2_ref, mate_ref, wv_ref, gain_ref, wqkv_ref, feats_hbm, out_ref, feats_ref, sem):
+    rows = x2_ref.shape[1]
+    half = rows // 2
+    own = unit(unpack_rows(got_ref, 0, half))
+    feats_ref[0] = own
     copy = pltpu.make_async_copy(feats_ref, feats_hbm, sem)
     copy.start()
-    hidden = x2_ref[0].astype(jnp.float32) + jnp.dot(
-        feats.astype(jnp.bfloat16), wv_ref[...], preferred_element_type=jnp.float32
-    )
+    feats = jnp.concatenate([own, unit(unpack_rows(got_ref, half, half))], axis=0)
+    before = jnp.concatenate([x2_ref[0], mate_ref[0]], axis=0).astype(jnp.float32)
+    hidden = before + jnp.dot(feats.astype(jnp.bfloat16), wv_ref[...], preferred_element_type=jnp.float32)
     normed = (unit(hidden) * gain_ref[...]).astype(jnp.bfloat16)
     projected = jnp.dot(normed, wqkv_ref[...], preferred_element_type=jnp.float32).astype(jnp.bfloat16)
     width = HEADS * HD
-    pack_heads(out_ref, projected[:, :width], projected[:, width : 2 * width], projected[:, 2 * width :])
+    pack_heads(
+        out_ref, projected[:rows, :width], projected[:, width : 2 * width], projected[:, 2 * width :]
+    )
     copy.wait()
 
 
 def last_kernel(got_ref, wout_ref, out_hbm, out_ref, sems):
-    rows = unit(unpack_rows(got_ref)).astype(jnp.bfloat16)
+    rows = unit(unpack_rows(got_ref, 0, got_ref.shape[1])).astype(jnp.bfloat16)
     copies = []
     width = wout_ref.shape[1] // 2
     for i in range(2):
@@ -245,39 +270,41 @@
 
 def by_heads(q1, k1, v1, nbr, x2, w_view_out, norm_gain, w_qkv, w_out):
     rows = q1.shape[1]
-    packed = ((HEADS, rows * 3 // 2, 2 * HD), jnp.bfloat16, pltpu.VMEM)
-    halves = ((HEADS, rows // 2, 2 * HD), jnp.bfloat16, pltpu.VMEM)
+    devices = HEADS * CORES
+
+    def kept(lines):
+        return ((HEADS, lines, 2 * HD), jnp.bfloat16, pltpu.VMEM)
+
     queries = ((HEADS * rows, 2 * HD), jnp.bfloat16, pltpu.VMEM)
     peaks = ((HEADS * rows, 1), jnp.float32, pltpu.VMEM)
     sums = ((HEADS * rows, 2 * HD), jnp.float32, pltpu.VMEM)
     wide = (1, rows, HEADS * HD)
-    devices = HEADS * CORES
-    groups = trade_groups()
-
-    def trade(piece):
+    across = trade_groups()
+    halves = [[s * HEADS + i for i in range(HEADS)] for s in range(CORES)]
+    cost = pl.CostEstimate(flops=16 << 30, bytes_accessed=40 << 20, transcendentals=0)
+
+    def trade(piece, groups):
         return lax.all_to_all(piece, ALL, split_axis=0, concat_axis=0, tiled=True, axis_index_groups=groups)
-
-    def attention(packed):
-        mine = trade(packed)
-        other = lax.ppermute(mine, ALL, [(i, i ^ 1) for i in range(devices)])
-        begun = call(begin_kernel, [queries, peaks, sums], (mine,), cost=pl.CostEstimate(1 << 30, 0, 1 << 20))
-        cost = pl.CostEstimate(flops=16 << 30, bytes_accessed=40 << 20, transcendentals=0)
-        (half,) = call(finish_kernel, [halves], (other, *begun), cost=cost)
-        return trade(half)
 
     inputs = [pltpu.with_memory_space_constraint(x, pltpu.HBM) for x in (q1, k1, v1)]
     scratch = [pltpu.VMEM(q1.shape, q1.dtype)] * 3 + [pltpu.SemaphoreType.DMA((3,))]
-    (piece,) = call(pack_kernel, [packed], inputs, scratch, space=pltpu.HBM, limit=48 << 20)
+    (piece,) = call(pack_kernel, [kept(rows * 3 // 2)], inputs, scratch, space=pltpu.HBM, limit=48 << 20)
+    mine = trade(piece, across)
+    other = lax.ppermute(mine, ALL, [(i, i ^ 1) for i in range(devices)])
+    mate = lax.ppermute(x2, ALL, [(i, i ^ HEADS) for i in range(devices)])
+    begun = call(begin_kernel, [queries, peaks, sums], (mine,), cost=pl.CostEstimate(1 << 30, 0, 1 << 20))
+    (part,) = call(finish_kernel, [kept(rows)], (other, *begun), cost=cost)
     feats, piece = call(
         middle_kernel,
-        [(wide, jnp.float32, pltpu.HBM), packed],
-        (attention(piece), x2, w_view_out, norm_gain[None], w_qkv),
+        [(wide, jnp.float32, pltpu.HBM), kept(rows * 5 // 2)],
+        (trade(part, across), x2, mate, w_view_out, norm_gain[None], w_qkv),
         [pltpu.VMEM(wide, jnp.float32), pltpu.SemaphoreType.DMA],
     )
+    (part,) = call(whole_kernel, [kept(rows // 2)], (trade(piece, halves),), cost=cost)
     (result,) = call(
         last_kernel,
         [(wide, jnp.float32, pltpu.HBM)],
-        (attention(piece), w_out),
+        (trade(part, halves), w_out),
         [pltpu.VMEM(wide, jnp.float32), pltpu.SemaphoreType.DMA((2,))],
     )
     return feats, result

time: 55.9 us -> 60.7 us (1.086)
  blocking collectives: 43.8 us -> 33.4 us
  waiting for transfers between devices: 0.62 us -> 7.07 us
  starting transfers between devices: 2.52 us -> 8.42 us
  local copies, waits for them, and re-layouts: 0.02 us -> 2.79 us
    all_to_all x4 -> x3, blocking collectives: 43.8 us -> 33.4 us  [trade(): lax.all_to_all(piece, ALL, split_axis=0, concat_axis=0, tiled=True, axis_...]
    ppermute x2, waiting for transfers between devices: 0.62 us -> 7.07 us  [the longest x1 6.77 us: by_heads(): mate = lax.ppermute(x2, ALL, [(i, i ^ HEADS) for i in range(devices)])]
    all_to_all x0 -> x1, starting transfers between devices: none -> 5.41 us  [trade(): lax.all_to_all(piece, ALL, split_axis=0, concat_axis=0, tiled=True, axis_...]
    unnamed x12 -> x10, local copies, waits for them, and re-layouts: 0.02 us -> 2.79 us
    pallas_call x7 -> x6, Pallas kernels: 7.96 us -> 7.93 us  [call(): pl.pallas_call(body, out_shape=[jax.ShapeDtypeStruct(shape, dtype) for sh...]
  transfers between devices with their start and end apart: 2 -> 3, of which waited for: 2 -> 2; matrix products, arithmetic and copies ran while one was open for 0% -> 0% of each run, Pallas kernels for 3% -> 1%
where the time goes in v10:
time: 60.7 us; the launch traced here: 60.3 us
  blocking collectives  33.4 us (55%)
  starting transfers between devices  8.42 us (14%)
  Pallas kernels  7.93 us (13%)
  waiting for transfers between devices  7.07 us (12%)
  local copies, waits for them, and re-layouts  2.79 us (5%)
  between operations  0.68 us (1%)
    all_to_all x3, blocking collectives, trade(): lax.all_to_all(piece, ALL, split_axis=0, concat_axis=0, tiled=True, axis_...  33.4 us
    pallas_call x6, Pallas kernels, call(): pl.pallas_call(body, out_shape=[jax.ShapeDtypeStruct(shape, dtype) for sh...  7.93 us
    ppermute x1, waiting for transfers between devices, by_heads(): mate = lax.ppermute(x2, ALL, [(i, i ^ HEADS) for i in range(devices)])  6.77 us
    all_to_all x1, starting transfers between devices, trade(): lax.all_to_all(piece, ALL, split_axis=0, concat_axis=0, tiled=True, axis_...  5.41 us
    unnamed x10, local copies, waits for them, and re-layouts  2.79 us
    ppermute x1, starting transfers between devices, by_heads(): other = lax.ppermute(mine, ALL, [(i, i ^ 1) for i in range(devices)])  1.54 us
    ppermute x1, starting transfers between devices, by_heads(): mate = lax.ppermute(x2, ALL, [(i, i ^ HEADS) for i in range(devices)])  1.47 us
  transfers between devices with their start and end apart: 3, of which 2 were waited for; matrix products, arithmetic and copies ran while one was open for 0% of the time, Pallas kernels for 1%

profile of v10, /device:TPU:0, one launch (start us, length us, event | category | flops | bytes accessed | tf_op | source)
XLA Modules:
  0.0 60.3 jit_solution(6254508095868376092)
XLA Ops:
  0.6 1.1 %shard_map.95 = bf16[16,48,128]{2,1,0:T(8,128)(2,1)S(1)} custom-call(bf16[1,32,1024]{2,1,0:T(8,128)(2,1)} %q_hbm.1, bf16[1,32,1024]{2,1,0:T(8,128)(2,1)} %k_hbm.1, bf16[1,32,1024]{2,1,0:T(8,128)(2,1)} %v_hbm.1), custom_call_target="tpu_custom_call" | custom-call | tf_op jit(solution)/shard_map/pallas_call | solution.py:260
  1.7 13.9 %all_to_all.20.mine_ref = bf16[16,48,128]{2,1,0:T(8,128)(2,1)S(1)} all-to-all(bf16[16,48,128]{2,1,0:T(8,128)(2,1)S(1)} %shard_map.95), channel_id=1, replica_groups={{11,12,15,8,19,20,23,16,27,28,31,24,3,4,7,0},{10,13,14,9,18,21,22,17,26..., dimensions={0} | all-to-all | bytes 393216 | tf_op jit(solution)/shard_map/all_to_all | solution.py:287
  15.6 1.5 %collective-permute-start = (bf16[16,48,128]{2,1,0:T(8,128)(2,1)S(1)}, bf16[16,48,128]{2,1,0:T(8,128)(2,1)S(1)}, u32[]{:S(2)}, u32[]{:S(2)}) collective-permute-start(bf16[16,48,128]{2,1,0:T(8,128)(2,1)S(1)} %all_to_all.20.mine_ref), channel_id=1, source_target_pairs={{0,1},{1,0},{2,3},{3,2},{4,5},{5,4},{6,7},{7,6},{8,9},{9,8},{10,11... | collective-permute-start | bytes 589832 | tf_op jit(solution)/shard_map/ppermute | solution.py:293
  17.1 0.8 %shard_map.96 = (bf16[512,128]{1,0:T(8,128)(2,1)S(1)}, f32[512,1]{1,0:T(8,128)S(1)}, f32[512,128]{1,0:T(8,128)S(1)}) custom-call(bf16[16,48,128]{2,1,0:T(8,128)(2,1)S(1)} %all_to_all.20.mine_ref), custom_call_target="tpu_custom_call" | custom-call | flops 1073741824 | bytes 1048576 | tf_op jit(solution)/shard_map/pallas_call | solution.py:260
  17.9 0.3 collective-permute-done.other_ref
  18.2 0.0 copy-start.3
  18.2 0.0 copy-start.2
  18.2 0.0 copy-start.4
  18.2 1.8 %shard_map.97 = bf16[16,32,128]{2,1,0:T(8,128)(2,1)} custom-call(bf16[16,48,128]{2,1,0:T(8,128)(2,1)S(1)} %collective-permute-done.other_ref, bf16[512,128]{1,0:T(8,128)(2,1)S(1)} %get-tuple-element.7.query_ref, f32[512,1]{1,0:T(8,128)S(1)} %get-tuple-element.8.peak_ref, f32[512,128]{1,0:T(8,128)S(1)} %get-tuple-element.9.sum_ref), custom_call_target="tpu_custom_call" | custom-call | flops 17179869184 | bytes 41943040 | tf_op jit(solution)/shard_map/pallas_call | solution.py:260
  20.0 5.4 %all-to-all-start.1 = ((bf16[16,32,128]{2,1,0:T(8,128)(2,1)}), bf16[16,32,128]{2,1,0:T(8,128)(2,1)S(1)}, u32[]{:S(2)}, u32[]{:S(2)}) async-start(bf16[16,32,128]{2,1,0:T(8,128)(2,1)} %shard_map.97), calls=%async_computation.1 | async-start | bytes 262144 | tf_op jit(solution)/shard_map/all_to_all | solution.py:287
  25.4 0.0 copy-done.3
  25.4 1.5 %collective-permute-start.1 = (bf16[1,32,1024]{2,1,0:T(8,128)(2,1)S(1)}, bf16[1,32,1024]{2,1,0:T(8,128)(2,1)S(1)}, u32[]{:S(2)}, u32[]{:S(2)}) collective-permute-start(bf16[1,32,1024]{2,1,0:T(8,128)(2,1)S(1)} %copy-done.3), channel_id=1, source_target_pairs={{0,16},{1,17},{2,18},{3,19},{4,20},{5,21},{6,22},{7,23},{8,24},{9,... | collective-permute-start | bytes 196616 | tf_op jit(solution)/shard_map/ppermute | solution.py:294
  26.8 6.8 %collective-permute-done.1.mate_ref = bf16[1,32,1024]{2,1,0:T(8,128)(2,1)S(1)} collective-permute-done((bf16[1,32,1024]{2,1,0:T(8,128)(2,1)S(1)}, bf16[1,32,1024]{2,1,0:T(8,128)(2,1)S(1)}, u32[]{:S(2)}, u32[]{:S(2)}) %collective-permute-start.1) | collective-permute-done | bytes 65568 | tf_op jit(solution)/shard_map/ppermute | solution.py:294
  33.6 0.0 all-to-all-done.1.got_ref
  33.6 0.0 copy-done.2
  33.6 0.0 copy-done.4
  33.6 0.0 copy-start
  33.6 2.8 %copy-done = bf16[1024,3072]{1,0:T(8,128)(2,1)S(1)} copy-done((bf16[1024,3072]{1,0:T(8,128)(2,1)S(1)}, bf16[1024,3072]{1,0:T(8,128)(2,1)}, u32[]{:S(2)}) %copy-start) | copy-done | bytes 6291480
  36.4 2.0 %shard_map.98 = (f32[1,32,1024]{2,1,0:T(8,128)}, bf16[16,80,128]{2,1,0:T(8,128)(2,1)S(1)}) custom-call(bf16[16,32,128]{2,1,0:T(8,128)(2,1)S(1)} %all-to-all-done.1.got_ref, bf16[1,32,1024]{2,1,0:T(8,128)(2,1)S(1)} %copy-done.3, bf16[1,32,1024]{2,1,0:T(8,128)(2,1)S(1)} %collective-permute-done.1.mate_ref, bf16[1024,1024]{1,0:T(8,128)(2,1)S(1)} %copy-done.2, ...), custom_call_target="tpu_custom_call" | custom-call | tf_op jit(solution)/shard_map/pallas_call | solution.py:260
  38.4 11.1 %all_to_all.21.got_ref = bf16[16,80,128]{2,1,0:T(8,128)(2,1)S(1)} all-to-all(bf16[16,80,128]{2,1,0:T(8,128)(2,1)S(1)} %get-tuple-element.11), channel_id=1, replica_groups={{0,1,2,3,4,5,6,7,8,9,10,11,12,13,14,15},{16,17,18,19,20,21,22,23,24,25,..., dimensions={0} | all-to-all | bytes 655360 | tf_op jit(solution)/shard_map/all_to_all | solution.py:287
  49.5 0.0 copy-start.1
  49.5 1.1 %shard_map.99 = bf16[16,16,128]{2,1,0:T(8,128)(2,1)S(1)} custom-call(bf16[16,80,128]{2,1,0:T(8,128)(2,1)S(1)} %all_to_all.21.got_ref), custom_call_target="tpu_custom_call" | custom-call | flops 17179869184 | bytes 41943040 | tf_op jit(solution)/shard_map/pallas_call | solution.py:260
  50.6 8.4 %all_to_all.22.got_ref = bf16[16,16,128]{2,1,0:T(8,128)(2,1)S(1)} all-to-all(bf16[16,16,128]{2,1,0:T(8,128)(2,1)S(1)} %shard_map.99), channel_id=1, replica_groups={{0,1,2,3,4,5,6,7,8,9,10,11,12,13,14,15},{16,17,18,19,20,21,22,23,24,25,..., dimensions={0} | all-to-all | bytes 131072 | tf_op jit(solution)/shard_map/all_to_all | solution.py:287
  59.0 0.0 copy-done.1
  59.0 1.3 %shard_map.100 = f32[1,32,1024]{2,1,0:T(8,128)} custom-call(bf16[16,16,128]{2,1,0:T(8,128)(2,1)S(1)} %all_to_all.22.got_ref, bf16[1024,1024]{1,0:T(8,128)(2,1)S(1)} %copy-done.1), custom_call_target="tpu_custom_call" | custom-call | tf_op jit(solution)/shard_map/pallas_call | solution.py:260
Async XLA Ops:
  15.6 2.6 %collective-permute-start = (bf16[16,48,128]{2,1,0:T(8,128)(2,1)S(1)}, bf16[16,48,128]{2,1,0:T(8,128)(2,1)S(1)}, u32[]{:S(2)}, u32[]{:S(2)}) collective-permute-start(bf16[16,48,128]{2,1,0:T(8,128)(2,1)S(1)} %all_to_all.20.mine_ref), channel_id=1, source_target_pairs={{0,1},{1,0},{2,3},{3,2},{4,5},{5,4},{6,7},{7,6},{8,9},{9,8},{10,11... | collective-permute-start | bytes 589832 | tf_op jit(solution)/shard_map/ppermute | solution.py:293
  18.2 7.2 %copy-start.3 = (bf16[1,32,1024]{2,1,0:T(8,128)(2,1)S(1)}, bf16[1,32,1024]{2,1,0:T(8,128)(2,1)}, u32[]{:S(2)}) copy-start(bf16[1,32,1024]{2,1,0:T(8,128)(2,1)} %x2_ref.1) | copy-start | bytes 196612
  18.2 15.4 %copy-start.2 = (bf16[1024,1024]{1,0:T(8,128)(2,1)S(1)}, bf16[1024,1024]{1,0:T(8,128)(2,1)}, u32[]{:S(2)}) copy-start(bf16[1024,1024]{1,0:T(8,128)(2,1)} %wv_ref.1) | copy-start | bytes 6291460
  18.2 15.4 %copy-start.4 = (f32[1024]{0:T(1024)S(1)}, f32[1024]{0:T(1024)}, u32[]{:S(2)}) copy-start(f32[1024]{0:T(1024)} %param.14) | copy-start | bytes 12292
  20.0 13.7 %all-to-all-start.1 = ((bf16[16,32,128]{2,1,0:T(8,128)(2,1)}), bf16[16,32,128]{2,1,0:T(8,128)(2,1)S(1)}, u32[]{:S(2)}, u32[]{:S(2)}) async-start(bf16[16,32,128]{2,1,0:T(8,128)(2,1)} %shard_map.97), calls=%async_computation.1 | async-start | bytes 262144 | tf_op jit(solution)/shard_map/all_to_all | solution.py:287
  25.4 8.2 %collective-permute-start.1 = (bf16[1,32,1024]{2,1,0:T(8,128)(2,1)S(1)}, bf16[1,32,1024]{2,1,0:T(8,128)(2,1)S(1)}, u32[]{:S(2)}, u32[]{:S(2)}) collective-permute-start(bf16[1,32,1024]{2,1,0:T(8,128)(2,1)S(1)} %copy-done.3), channel_id=1, source_target_pairs={{0,16},{1,17},{2,18},{3,19},{4,20},{5,21},{6,22},{7,23},{8,24},{9,... | collective-permute-start | bytes 196616 | tf_op jit(solution)/shard_map/ppermute | solution.py:294
  33.6 2.8 %copy-start = (bf16[1024,3072]{1,0:T(8,128)(2,1)S(1)}, bf16[1024,3072]{1,0:T(8,128)(2,1)}, u32[]{:S(2)}) copy-start(bf16[1024,3072]{1,0:T(8,128)(2,1)} %wqkv_ref.1) | copy-start | bytes 18874372
  49.5 9.6 %copy-start.1 = (bf16[1024,1024]{1,0:T(8,128)(2,1)S(1)}, bf16[1024,1024]{1,0:T(8,128)(2,1)}, u32[]{:S(2)}) copy-start(bf16[1024,1024]{1,0:T(8,128)(2,1)} %wout_ref.1) | copy-start | bytes 6291460

commit v11 on v9

--- a/solution.py
+++ b/solution.py
@@ -114,7 +114,7 @@
 
 def trade_groups():
     plane = HEADS // len(PLANES)
-    chips = [p * plane + (i + 1) % plane for p in PLANES for i in range(plane)]
+    chips = [p * plane + (i + 1) % plane for i in range(plane) for p in PLANES]
     return [[chip * CORES + (chip + s) % CORES for chip in chips] for s in range(CORES)]
 
 
@@ -183,7 +183,7 @@
         query_ref[at, :] = queries
         scores = score(queries, keys)
         peak = jnp.max(scores, axis=-1, keepdims=True)
-        peak_ref[at, :] = peak
+        peak_ref[at, :] = jnp.broadcast_to(peak, (n, 2 * HD))
         sum_ref[at, :] = weigh(scores, peak, vals)
 
 
@@ -195,8 +195,9 @@
         at = slice(i * n, (i + 1) * n)
         scores = score(query_ref[at, :], keys)
         before = peak_ref[at, :]
-        peak = jnp.maximum(before, jnp.max(scores, axis=-1, keepdims=True))
-        sums.append(sum_ref[at, :] * jnp.exp2((before - peak) * SHARP) + weigh(scores, peak, vals))
+        peak = jnp.maximum(before, jnp.broadcast_to(jnp.max(scores, axis=-1, keepdims=True), before.shape))
+        wide_peak = jnp.concatenate([peak] * (scores.shape[1] // peak.shape[1]), axis=-1)
+        sums.append(sum_ref[at, :] * jnp.exp2((before - peak) * SHARP) + weigh(scores, wide_peak, vals))
     top, low = sums
     left = lower_half(top.shape)
     attn = jnp.where(left, pltpu.roll(top, HD, 1), low) / jnp.where(left, top, pltpu.roll(low, HD, 1))
@@ -248,8 +249,7 @@
     packed = ((HEADS, rows * 3 // 2, 2 * HD), jnp.bfloat16, pltpu.VMEM)
     halves = ((HEADS, rows // 2, 2 * HD), jnp.bfloat16, pltpu.VMEM)
     queries = ((HEADS * rows, 2 * HD), jnp.bfloat16, pltpu.VMEM)
-    peaks = ((HEADS * rows, 1), jnp.float32, pltpu.VMEM)
-    sums = ((HEADS * rows, 2 * HD), jnp.float32, pltpu.VMEM)
+    lines = ((HEADS * rows, 2 * HD), jnp.float32, pltpu.VMEM)
     wide = (1, rows, HEADS * HD)
     devices = HEADS * CORES
     groups = trade_groups()
@@ -260,7 +260,7 @@
     def attention(packed):
         mine = trade(packed)
         other = lax.ppermute(mine, ALL, [(i, i ^ 1) for i in range(devices)])
-        begun = call(begin_kernel, [queries, peaks, sums], (mine,), cost=pl.CostEstimate(1 << 30, 0, 1 << 20))
+        begun = call(begin_kernel, [queries, lines, lines], (mine,), cost=pl.CostEstimate(1 << 30, 0, 1 << 20))
         cost = pl.CostEstimate(flops=16 << 30, bytes_accessed=40 << 20, transcendentals=0)
         (half,) = call(finish_kernel, [halves], (other, *begun), cost=cost)
         return trade(half)

time: 55.9 us -> 56.1 us (level)
  starting transfers between devices: 2.52 us -> 0.01 us
  blocking collectives: 43.8 us -> 46.2 us
  waiting for transfers between devices: 0.62 us -> 1.34 us
    ppermute x2, starting transfers between devices: 2.52 us -> 0.01 us  [attention(): other = lax.ppermute(mine, ALL, [(i, i ^ 1) for i in range(devices)])]
    all_to_all x4, blocking collectives: 43.8 us -> 46.2 us  [trade(): lax.all_to_all(piece, ALL, split_axis=0, concat_axis=0, tiled=True, axis_...]
    ppermute x2, waiting for transfers between devices: 0.62 us -> 1.34 us  [attention(): other = lax.ppermute(mine, ALL, [(i, i ^ 1) for i in range(devices)])]
where the time goes in v11:
time: 56.1 us; the launch traced here: 55.8 us
  blocking collectives  46.2 us (82%)
  Pallas kernels  7.45 us (13%)
  waiting for transfers between devices  1.34 us (2%)
  between operations  0.72 us (1%)
    all_to_all x4, blocking collectives, trade(): lax.all_to_all(piece, ALL, split_axis=0, concat_axis=0, tiled=True, axis_...  46.2 us
    pallas_call x7, Pallas kernels, call(): pl.pallas_call(body, out_shape=[jax.ShapeDtypeStruct(shape, dtype) for sh...  7.45 us
    ppermute x2, waiting for transfers between devices, attention(): other = lax.ppermute(mine, ALL, [(i, i ^ 1) for i in range(devices)])  1.34 us
  transfers between devices with their start and end apart: 2, of which 2 were waited for; matrix products, arithmetic and copies ran while one was open for 0% of the time, Pallas kernels for 3%

profile of v11, /device:TPU:0, one launch (start us, length us, event | category | flops | bytes accessed | tf_op | source)
XLA Modules:
  0.0 55.8 jit_solution(5692009742796293855)
XLA Ops:
  0.6 1.1 %shard_map.95 = bf16[16,48,128]{2,1,0:T(8,128)(2,1)S(1)} custom-call(bf16[1,32,1024]{2,1,0:T(8,128)(2,1)} %q_hbm.1, bf16[1,32,1024]{2,1,0:T(8,128)(2,1)} %k_hbm.1, bf16[1,32,1024]{2,1,0:T(8,128)(2,1)} %v_hbm.1), custom_call_target="tpu_custom_call" | custom-call | tf_op jit(solution)/shard_map/pallas_call | solution.py:236
  1.7 15.4 %all_to_all.20.mine_ref = bf16[16,48,128]{2,1,0:T(8,128)(2,1)S(1)} all-to-all(bf16[16,48,128]{2,1,0:T(8,128)(2,1)S(1)} %shard_map.95), channel_id=1, replica_groups={{11,19,27,3,12,20,28,4,15,23,31,7,8,16,24,0},{10,18,26,2,13,21,29,5,14,..., dimensions={0} | all-to-all | bytes 393216 | tf_op jit(solution)/shard_map/all_to_all | solution.py:258
  17.1 0.0 collective-permute-start
  17.1 0.8 %shard_map.96 = (bf16[512,128]{1,0:T(8,128)(2,1)S(1)}, f32[512,128]{1,0:T(8,128)S(1)}, f32[512,128]{1,0:T(8,128)S(1)}) custom-call(bf16[16,48,128]{2,1,0:T(8,128)(2,1)S(1)} %all_to_all.20.mine_ref), custom_call_target="tpu_custom_call" | custom-call | flops 1073741824 | bytes 1048576 | tf_op jit(solution)/shard_map/pallas_call | solution.py:236
  17.9 0.7 %collective-permute-done.other_ref = bf16[16,48,128]{2,1,0:T(8,128)(2,1)S(1)} collective-permute-done((bf16[16,48,128]{2,1,0:T(8,128)(2,1)S(1)}, bf16[16,48,128]{2,1,0:T(8,128)(2,1)S(1)}, u32[]{:S(2)}, u32[]{:S(2)}) %collective-permute-start) | collective-permute-done | bytes 196640 | tf_op jit(solution)/shard_map/ppermute | solution.py:262
  18.6 0.0 slice-start
  18.6 0.0 slice-start.1
  18.6 0.0 copy-start.1
  18.6 0.0 copy-start.2
  18.6 0.0 copy-start.3
  18.6 0.8 %shard_map.97 = bf16[16,16,128]{2,1,0:T(8,128)(2,1)S(1)} custom-call(bf16[16,48,128]{2,1,0:T(8,128)(2,1)S(1)} %collective-permute-done.other_ref, bf16[512,128]{1,0:T(8,128)(2,1)S(1)} %get-tuple-element.10.query_ref, f32[512,128]{1,0:T(8,128)S(1)} %get-tuple-element.11.peak_ref, f32[512,128]{1,0:T(8,128)S(1)} %get-tuple-element.12.sum_ref), custom_call_target="tpu_custom_call" | custom-call | flops 17179869184 | bytes 41943040 | tf_op jit(solution)/shard_map/pallas_call | solution.py:236
  19.4 10.2 %all_to_all.21.got_ref = bf16[16,16,128]{2,1,0:T(8,128)(2,1)S(1)} all-to-all(bf16[16,16,128]{2,1,0:T(8,128)(2,1)S(1)} %shard_map.97), channel_id=1, replica_groups={{11,19,27,3,12,20,28,4,15,23,31,7,8,16,24,0},{10,18,26,2,13,21,29,5,14,..., dimensions={0} | all-to-all | bytes 131072 | tf_op jit(solution)/shard_map/all_to_all | solution.py:258
  29.7 0.0 slice-done
  29.7 0.0 slice-done.1
  29.7 0.0 copy-done.1
  29.7 0.0 copy-done.2
  29.7 0.0 copy-done.3
  29.7 2.0 %shard_map.98 = (f32[1,32,1024]{2,1,0:T(8,128)}, bf16[16,48,128]{2,1,0:T(8,128)(2,1)S(1)}) custom-call(bf16[16,16,128]{2,1,0:T(8,128)(2,1)S(1)} %all_to_all.21.got_ref, bf16[1,32,1024]{2,1,0:T(8,128)(2,1)S(1)} %copy-done.2, bf16[1024,1024]{1,0:T(8,128)(2,1)S(1)} %copy-done.1, f32[1,1024]{1,0:T(1,128)S(1)} %bitcast.3, bf16[1024,3072]{1,0:T(8,128)(2,1)S(1)} %bitcast.2), custom_call_target="tpu_custom_call" | custom-call | tf_op jit(solution)/shard_map/pallas_call | solution.py:236
  31.7 10.8 %all_to_all.22.mine_ref = bf16[16,48,128]{2,1,0:T(8,128)(2,1)S(1)} all-to-all(bf16[16,48,128]{2,1,0:T(8,128)(2,1)S(1)} %get-tuple-element.14), channel_id=1, replica_groups={{11,19,27,3,12,20,28,4,15,23,31,7,8,16,24,0},{10,18,26,2,13,21,29,5,14,..., dimensions={0} | all-to-all | bytes 393216 | tf_op jit(solution)/shard_map/all_to_all | solution.py:258
  42.5 0.0 collective-permute-start.1
  42.5 0.8 %shard_map.99 = (bf16[512,128]{1,0:T(8,128)(2,1)S(1)}, f32[512,128]{1,0:T(8,128)S(1)}, f32[512,128]{1,0:T(8,128)S(1)}) custom-call(bf16[16,48,128]{2,1,0:T(8,128)(2,1)S(1)} %all_to_all.22.mine_ref), custom_call_target="tpu_custom_call" | custom-call | flops 1073741824 | bytes 1048576 | tf_op jit(solution)/shard_map/pallas_call | solution.py:236
  43.2 0.7 %collective-permute-done.1.other_ref = bf16[16,48,128]{2,1,0:T(8,128)(2,1)S(1)} collective-permute-done((bf16[16,48,128]{2,1,0:T(8,128)(2,1)S(1)}, bf16[16,48,128]{2,1,0:T(8,128)(2,1)S(1)}, u32[]{:S(2)}, u32[]{:S(2)}) %collective-permute-start.1) | collective-permute-done | bytes 196640 | tf_op jit(solution)/shard_map/ppermute | solution.py:262
  43.9 0.0 copy-start
  43.9 0.8 %shard_map.100 = bf16[16,16,128]{2,1,0:T(8,128)(2,1)S(1)} custom-call(bf16[16,48,128]{2,1,0:T(8,128)(2,1)S(1)} %collective-permute-done.1.other_ref, bf16[512,128]{1,0:T(8,128)(2,1)S(1)} %get-tuple-element.15.query_ref, f32[512,128]{1,0:T(8,128)S(1)} %get-tuple-element.16.peak_ref, f32[512,128]{1,0:T(8,128)S(1)} %get-tuple-element.17.sum_ref), custom_call_target="tpu_custom_call" | custom-call | flops 17179869184 | bytes 41943040 | tf_op jit(solution)/shard_map/pallas_call | solution.py:236
  44.7 9.8 %all_to_all.23.got_ref = bf16[16,16,128]{2,1,0:T(8,128)(2,1)S(1)} all-to-all(bf16[16,16,128]{2,1,0:T(8,128)(2,1)S(1)} %shard_map.100), channel_id=1, replica_groups={{11,19,27,3,12,20,28,4,15,23,31,7,8,16,24,0},{10,18,26,2,13,21,29,5,14,..., dimensions={0} | all-to-all | bytes 131072 | tf_op jit(solution)/shard_map/all_to_all | solution.py:258
  54.5 0.0 copy-done
  54.5 1.3 %shard_map.101 = f32[1,32,1024]{2,1,0:T(8,128)} custom-call(bf16[16,16,128]{2,1,0:T(8,128)(2,1)S(1)} %all_to_all.23.got_ref, bf16[1024,1024]{1,0:T(8,128)(2,1)S(1)} %copy-done), custom_call_target="tpu_custom_call" | custom-call | tf_op jit(solution)/shard_map/pallas_call | solution.py:236
  (1 shorter events, 0.0 us)
Async XLA Ops:
  17.1 1.4 %collective-permute-start = (bf16[16,48,128]{2,1,0:T(8,128)(2,1)S(1)}, bf16[16,48,128]{2,1,0:T(8,128)(2,1)S(1)}, u32[]{:S(2)}, u32[]{:S(2)}) collective-permute-start(bf16[16,48,128]{2,1,0:T(8,128)(2,1)S(1)} %all_to_all.20.mine_ref), channel_id=1, source_target_pairs={{0,1},{1,0},{2,3},{3,2},{4,5},{5,4},{6,7},{7,6},{8,9},{9,8},{10,11... | collective-permute-start | bytes 589832 | tf_op jit(solution)/shard_map/ppermute | solution.py:262
  18.6 11.1 %slice-start = ((s8[6291456]{0:T(1024)(128)(4,1)}), s8[4194304]{0:T(1024)(128)(4,1)S(1)}, s32[]{:S(2)}) async-start(s8[6291456]{0:T(1024)(128)(4,1)} %bitcast.1), calls=%async_computation.4 | async-start | bytes 8388608
  18.6 11.1 %slice-start.1 = ((s8[6291456]{0:T(1024)(128)(4,1)}), s8[2097152]{0:T(1024)(128)(4,1)S(1)}, s32[]{:S(2)}) async-start(s8[6291456]{0:T(1024)(128)(4,1)} %bitcast.1), calls=%async_computation.5 | async-start | bytes 4194304
  18.6 11.1 %copy-start.1 = (bf16[1024,1024]{1,0:T(8,128)(2,1)S(1)}, bf16[1024,1024]{1,0:T(8,128)(2,1)}, u32[]{:S(2)}) copy-start(bf16[1024,1024]{1,0:T(8,128)(2,1)} %wv_ref.1) | copy-start | bytes 6291460
  18.6 11.1 %copy-start.2 = (bf16[1,32,1024]{2,1,0:T(8,128)(2,1)S(1)}, bf16[1,32,1024]{2,1,0:T(8,128)(2,1)}, u32[]{:S(2)}) copy-start(bf16[1,32,1024]{2,1,0:T(8,128)(2,1)} %x2_ref.1) | copy-start | bytes 196612
  18.6 11.1 %copy-start.3 = (f32[1024]{0:T(1024)S(1)}, f32[1024]{0:T(1024)}, u32[]{:S(2)}) copy-start(f32[1024]{0:T(1024)} %param.14) | copy-start | bytes 12292
  42.5 1.4 %collective-permute-start.1 = (bf16[16,48,128]{2,1,0:T(8,128)(2,1)S(1)}, bf16[16,48,128]{2,1,0:T(8,128)(2,1)S(1)}, u32[]{:S(2)}, u32[]{:S(2)}) collective-permute-start(bf16[16,48,128]{2,1,0:T(8,128)(2,1)S(1)} %all_to_all.22.mine_ref), channel_id=1, source_target_pairs={{0,1},{1,0},{2,3},{3,2},{4,5},{5,4},{6,7},{7,6},{8,9},{9,8},{10,11... | collective-permute-start | bytes 589832 | tf_op jit(solution)/shard_map/ppermute | solution.py:262
  43.9 10.6 %copy-start = (bf16[1024,1024]{1,0:T(8,128)(2,1)S(1)}, bf16[1024,1024]{1,0:T(8,128)(2,1)}, u32[]{:S(2)}) copy-start(bf16[1024,1024]{1,0:T(8,128)(2,1)} %wout_ref.1) | copy-start | bytes 6291460

commit v12 on v11

--- a/solution.py
+++ b/solution.py
@@ -108,23 +108,23 @@
 
 ALL = ("view", "tok")
 CORES = 2
-PLANES = (1, 2, 3, 0)
+BLOCK = 4
+FIRST = HEADS // 4 + 1
 SHARP = HD ** (-0.5) * 1.4426950408889634
 
 
 def trade_groups():
-    plane = HEADS // len(PLANES)
-    chips = [p * plane + (i + 1) % plane for i in range(plane) for p in PLANES]
+    chips = [(FIRST + i) % HEADS for i in range(HEADS)]
     return [[chip * CORES + (chip + s) % CORES for chip in chips] for s in range(CORES)]
 
 
-def pack_heads(out_ref, q, k, v):
+def pack_heads(out_ref, first, q, k, v):
     rows = q.shape[0]
     half = rows // 2
-    for h in range(HEADS):
-        cols = slice(h * HD, (h + 1) * HD)
-        out_ref[h, 0:rows, :] = jnp.concatenate([k[:, cols], v[:, cols]], axis=-1)
-        out_ref[h, rows : rows + half, :] = jnp.concatenate([q[:half, cols], q[half:, cols]], axis=-1)
+    for i in range(q.shape[1] // HD):
+        cols = slice(i * HD, (i + 1) * HD)
+        out_ref[first + i, 0:rows, :] = jnp.concatenate([k[:, cols], v[:, cols]], axis=-1)
+        out_ref[first + i, rows : rows + half, :] = jnp.concatenate([q[:half, cols], q[half:, cols]], axis=-1)
 
 
 def unpack_rows(got_ref):
@@ -147,7 +147,7 @@
         copy.start()
     for copy in copies:
         copy.wait()
-    pack_heads(out_ref, q_ref[0], k_ref[0], v_ref[0])
+    pack_heads(out_ref, 0, q_ref[0], k_ref[0], v_ref[0])
 
 
 def lower_half(shape):
@@ -158,8 +158,12 @@
     return jnp.concatenate([x[:, HD:], x[:, :HD]], axis=-1)
 
 
-def key_values(piece_ref):
-    kv = piece_ref[:, 0 : piece_ref.shape[1] * 2 // 3, :].reshape(-1, 2 * HD)
+def collect_kernel(piece_ref, kv_ref):
+    kv_ref[...] = piece_ref[:, 0 : piece_ref.shape[1] * 2 // 3, :].reshape(-1, 2 * HD)
+
+
+def key_values(kv_ref):
+    kv = kv_ref[...]
     return kv, jnp.where(lower_half(kv.shape), jnp.ones_like(kv), kv)
 
 
@@ -172,10 +176,10 @@
     return jnp.dot(weights, vals, preferred_element_type=jnp.float32)
 
 
-def begin_kernel(mine_ref, query_ref, peak_ref, sum_ref):
+def begin_kernel(mine_ref, kv_ref, query_ref, peak_ref, sum_ref):
     lines = mine_ref.shape[1]
     packed = mine_ref[:, lines * 2 // 3 : lines, :].reshape(-1, 2 * HD)
-    keys, vals = key_values(mine_ref)
+    keys, vals = key_values(kv_ref)
     n = packed.shape[0]
     for i, part in enumerate((packed, turned(packed))):
         at = slice(i * n, (i + 1) * n)
@@ -213,9 +217,15 @@
         feats.astype(jnp.bfloat16), wv_ref[...], preferred_element_type=jnp.float32
     )
     normed = (unit(hidden) * gain_ref[...]).astype(jnp.bfloat16)
-    projected = jnp.dot(normed, wqkv_ref[...], preferred_element_type=jnp.float32).astype(jnp.bfloat16)
     width = HEADS * HD
-    pack_heads(out_ref, projected[:, :width], projected[:, width : 2 * width], projected[:, 2 * width :])
+    some = BLOCK * HD
+    for first in range(0, HEADS, BLOCK):
+        parts = []
+        for i in range(3):
+            at = i * width + first * HD
+            part = jnp.dot(normed, wqkv_ref[:, at : at + some], preferred_element_type=jnp.float32)
+            parts.append(part.astype(jnp.bfloat16))
+        pack_heads(out_ref, first, *parts)
     copy.wait()
 
 
@@ -259,8 +269,9 @@
 
     def attention(packed):
         mine = trade(packed)
-        other = lax.ppermute(mine, ALL, [(i, i ^ 1) for i in range(devices)])
-        begun = call(begin_kernel, [queries, lines, lines], (mine,), cost=pl.CostEstimate(1 << 30, 0, 1 << 20))
+        (own,) = call(collect_kernel, [queries], (mine,))
+        other = lax.ppermute(own, ALL, [(i, i ^ 1) for i in range(devices)])
+        begun = call(begin_kernel, [queries, lines, lines], (mine, own), cost=pl.CostEstimate(1 << 30, 0, 1 << 20))
         cost = pl.CostEstimate(flops=16 << 30, bytes_accessed=40 << 20, transcendentals=0)
         (half,) = call(finish_kernel, [halves], (other, *begun), cost=cost)
         return trade(half)

time: 56.1 us -> 56.3 us (level)
    pallas_call x7 -> x9, Pallas kernels: 7.45 us -> 7.91 us  [call(): pl.pallas_call(body, out_shape=[jax.ShapeDtypeStruct(shape, dtype) for sh...]
where the time goes in v12:
time: 56.3 us; the launch traced here: 56 us
  blocking collectives  46 us (82%)
  Pallas kernels  7.91 us (14%)
  waiting for transfers between devices  1.15 us (2%)
  between operations  0.74 us (1%)
    all_to_all x4, blocking collectives, trade(): lax.all_to_all(piece, ALL, split_axis=0, concat_axis=0, tiled=True, axis_...  46 us
    pallas_call x9, Pallas kernels, call(): pl.pallas_call(body, out_shape=[jax.ShapeDtypeStruct(shape, dtype) for sh...  7.91 us
    ppermute x2, waiting for transfers between devices, attention(): other = lax.ppermute(own, ALL, [(i, i ^ 1) for i in range(devices)])  1.15 us
  transfers between devices with their start and end apart: 2, of which 2 were waited for; matrix products, arithmetic and copies ran while one was open for 0% of the time, Pallas kernels for 3%

profile of v12, /device:TPU:0, one launch (start us, length us, event | category | flops | bytes accessed | tf_op | source)
XLA Modules:
  0.0 56.0 jit_solution(7516983041587369279)
XLA Ops:
  0.6 1.1 %shard_map.95 = bf16[16,48,128]{2,1,0:T(8,128)(2,1)S(1)} custom-call(bf16[1,32,1024]{2,1,0:T(8,128)(2,1)} %q_hbm.1, bf16[1,32,1024]{2,1,0:T(8,128)(2,1)} %k_hbm.1, bf16[1,32,1024]{2,1,0:T(8,128)(2,1)} %v_hbm.1), custom_call_target="tpu_custom_call" | custom-call | tf_op jit(solution)/shard_map/pallas_call | solution.py:246
  1.7 16.2 %all_to_all.20.piece_ref.mine_ref = bf16[16,48,128]{2,1,0:T(8,128)(2,1)S(1)} all-to-all(bf16[16,48,128]{2,1,0:T(8,128)(2,1)S(1)} %shard_map.95), channel_id=1, replica_groups={{11,12,15,16,19,20,23,24,27,28,31,0,3,4,7,8},{10,13,14,17,18,21,22,25,2..., dimensions={0} | all-to-all | bytes 393216 | tf_op jit(solution)/shard_map/all_to_all | solution.py:268
  17.9 0.1 collective-permute-start
  18.0 0.8 %shard_map.97 = (bf16[512,128]{1,0:T(8,128)(2,1)S(1)}, f32[512,128]{1,0:T(8,128)S(1)}, f32[512,128]{1,0:T(8,128)S(1)}) custom-call(bf16[16,48,128]{2,1,0:T(8,128)(2,1)S(1)} %all_to_all.20.piece_ref.mine_ref, bf16[512,128]{1,0:T(8,128)(2,1)S(1)} %shard_map.96.kv_ref), custom_call_target="tpu_custom_call" | custom-call | flops 1073741824 | bytes 1048576 | tf_op jit(solution)/shard_map/pallas_call | solution.py:246
  18.7 0.6 %collective-permute-done.other_ref = bf16[512,128]{1,0:T(8,128)(2,1)S(1)} collective-permute-done((bf16[512,128]{1,0:T(8,128)(2,1)S(1)}, bf16[512,128]{1,0:T(8,128)(2,1)S(1)}, u32[]{:S(2)}, u32[]{:S(2)}) %collective-permute-start) | collective-permute-done | bytes 131104 | tf_op jit(solution)/shard_map/ppermute | solution.py:273
  19.3 0.0 slice-start
  19.3 0.0 slice-start.1
  19.3 0.0 copy-start.1
  19.3 0.0 copy-start.2
  19.3 0.0 copy-start.3
  19.3 0.8 %shard_map.98 = bf16[16,16,128]{2,1,0:T(8,128)(2,1)S(1)} custom-call(bf16[512,128]{1,0:T(8,128)(2,1)S(1)} %collective-permute-done.other_ref, bf16[512,128]{1,0:T(8,128)(2,1)S(1)} %get-tuple-element.10.query_ref, f32[512,128]{1,0:T(8,128)S(1)} %get-tuple-element.11.peak_ref, f32[512,128]{1,0:T(8,128)S(1)} %get-tuple-element.12.sum_ref), custom_call_target="tpu_custom_call" | custom-call | flops 17179869184 | bytes 41943040 | tf_op jit(solution)/shard_map/pallas_call | solution.py:246
  20.2 9.5 %all_to_all.21.got_ref = bf16[16,16,128]{2,1,0:T(8,128)(2,1)S(1)} all-to-all(bf16[16,16,128]{2,1,0:T(8,128)(2,1)S(1)} %shard_map.98), channel_id=1, replica_groups={{11,12,15,16,19,20,23,24,27,28,31,0,3,4,7,8},{10,13,14,17,18,21,22,25,2..., dimensions={0} | all-to-all | bytes 131072 | tf_op jit(solution)/shard_map/all_to_all | solution.py:268
  29.7 0.0 slice-done
  29.7 0.0 slice-done.1
  29.7 0.0 copy-done.1
  29.7 0.0 copy-done.2
  29.7 0.0 copy-done.3
  29.7 2.4 %shard_map.99 = (f32[1,32,1024]{2,1,0:T(8,128)}, bf16[16,48,128]{2,1,0:T(8,128)(2,1)S(1)}) custom-call(bf16[16,16,128]{2,1,0:T(8,128)(2,1)S(1)} %all_to_all.21.got_ref, bf16[1,32,1024]{2,1,0:T(8,128)(2,1)S(1)} %copy-done.2, bf16[1024,1024]{1,0:T(8,128)(2,1)S(1)} %copy-done.1, f32[1,1024]{1,0:T(1,128)S(1)} %bitcast.3, bf16[1024,3072]{1,0:T(8,128)(2,1)S(1)} %bitcast.2), custom_call_target="tpu_custom_call" | custom-call | tf_op jit(solution)/shard_map/pallas_call | solution.py:246
  32.1 11.1 %all_to_all.22.piece_ref.mine_ref = bf16[16,48,128]{2,1,0:T(8,128)(2,1)S(1)} all-to-all(bf16[16,48,128]{2,1,0:T(8,128)(2,1)S(1)} %get-tuple-element.14), channel_id=1, replica_groups={{11,12,15,16,19,20,23,24,27,28,31,0,3,4,7,8},{10,13,14,17,18,21,22,25,2..., dimensions={0} | all-to-all | bytes 393216 | tf_op jit(solution)/shard_map/all_to_all | solution.py:268
  43.2 0.1 collective-permute-start.1
  43.3 0.8 %shard_map.101 = (bf16[512,128]{1,0:T(8,128)(2,1)S(1)}, f32[512,128]{1,0:T(8,128)S(1)}, f32[512,128]{1,0:T(8,128)S(1)}) custom-call(bf16[16,48,128]{2,1,0:T(8,128)(2,1)S(1)} %all_to_all.22.piece_ref.mine_ref, bf16[512,128]{1,0:T(8,128)(2,1)S(1)} %shard_map.100.kv_ref), custom_call_target="tpu_custom_call" | custom-call | flops 1073741824 | bytes 1048576 | tf_op jit(solution)/shard_map/pallas_call | solution.py:246
  44.1 0.6 %collective-permute-done.1.other_ref = bf16[512,128]{1,0:T(8,128)(2,1)S(1)} collective-permute-done((bf16[512,128]{1,0:T(8,128)(2,1)S(1)}, bf16[512,128]{1,0:T(8,128)(2,1)S(1)}, u32[]{:S(2)}, u32[]{:S(2)}) %collective-permute-start.1) | collective-permute-done | bytes 131104 | tf_op jit(solution)/shard_map/ppermute | solution.py:273
  44.6 0.0 copy-start
  44.6 0.8 %shard_map.102 = bf16[16,16,128]{2,1,0:T(8,128)(2,1)S(1)} custom-call(bf16[512,128]{1,0:T(8,128)(2,1)S(1)} %collective-permute-done.1.other_ref, bf16[512,128]{1,0:T(8,128)(2,1)S(1)} %get-tuple-element.15.query_ref, f32[512,128]{1,0:T(8,128)S(1)} %get-tuple-element.16.peak_ref, f32[512,128]{1,0:T(8,128)S(1)} %get-tuple-element.17.sum_ref), custom_call_target="tpu_custom_call" | custom-call | flops 17179869184 | bytes 41943040 | tf_op jit(solution)/shard_map/pallas_call | solution.py:246
  45.5 9.3 %all_to_all.23.got_ref = bf16[16,16,128]{2,1,0:T(8,128)(2,1)S(1)} all-to-all(bf16[16,16,128]{2,1,0:T(8,128)(2,1)S(1)} %shard_map.102), channel_id=1, replica_groups={{11,12,15,16,19,20,23,24,27,28,31,0,3,4,7,8},{10,13,14,17,18,21,22,25,2..., dimensions={0} | all-to-all | bytes 131072 | tf_op jit(solution)/shard_map/all_to_all | solution.py:268
  54.7 0.0 copy-done
  54.7 1.3 %shard_map.103 = f32[1,32,1024]{2,1,0:T(8,128)} custom-call(bf16[16,16,128]{2,1,0:T(8,128)(2,1)S(1)} %all_to_all.23.got_ref, bf16[1024,1024]{1,0:T(8,128)(2,1)S(1)} %copy-done), custom_call_target="tpu_custom_call" | custom-call | tf_op jit(solution)/shard_map/pallas_call | solution.py:246
  (3 shorter events, 0.0 us)
Async XLA Ops:
  17.9 1.4 %collective-permute-start = (bf16[512,128]{1,0:T(8,128)(2,1)S(1)}, bf16[512,128]{1,0:T(8,128)(2,1)S(1)}, u32[]{:S(2)}, u32[]{:S(2)}) collective-permute-start(bf16[512,128]{1,0:T(8,128)(2,1)S(1)} %shard_map.96.kv_ref), channel_id=1, source_target_pairs={{0,1},{1,0},{2,3},{3,2},{4,5},{5,4},{6,7},{7,6},{8,9},{9,8},{10,11... | collective-permute-start | bytes 393224 | tf_op jit(solution)/shard_map/ppermute | solution.py:273
  19.3 10.4 %slice-start = ((s8[6291456]{0:T(1024)(128)(4,1)}), s8[4194304]{0:T(1024)(128)(4,1)S(1)}, s32[]{:S(2)}) async-start(s8[6291456]{0:T(1024)(128)(4,1)} %bitcast.1), calls=%async_computation.4 | async-start | bytes 8388608
  19.3 10.4 %slice-start.1 = ((s8[6291456]{0:T(1024)(128)(4,1)}), s8[2097152]{0:T(1024)(128)(4,1)S(1)}, s32[]{:S(2)}) async-start(s8[6291456]{0:T(1024)(128)(4,1)} %bitcast.1), calls=%async_computation.5 | async-start | bytes 4194304
  19.3 10.4 %copy-start.1 = (bf16[1024,1024]{1,0:T(8,128)(2,1)S(1)}, bf16[1024,1024]{1,0:T(8,128)(2,1)}, u32[]{:S(2)}) copy-start(bf16[1024,1024]{1,0:T(8,128)(2,1)} %wv_ref.1) | copy-start | bytes 6291460
  19.3 10.4 %copy-start.2 = (bf16[1,32,1024]{2,1,0:T(8,128)(2,1)S(1)}, bf16[1,32,1024]{2,1,0:T(8,128)(2,1)}, u32[]{:S(2)}) copy-start(bf16[1,32,1024]{2,1,0:T(8,128)(2,1)} %x2_ref.1) | copy-start | bytes 196612
  19.3 10.4 %copy-start.3 = (f32[1024]{0:T(1024)S(1)}, f32[1024]{0:T(1024)}, u32[]{:S(2)}) copy-start(f32[1024]{0:T(1024)} %param.14) | copy-start | bytes 12292
  43.2 1.4 %collective-permute-start.1 = (bf16[512,128]{1,0:T(8,128)(2,1)S(1)}, bf16[512,128]{1,0:T(8,128)(2,1)S(1)}, u32[]{:S(2)}, u32[]{:S(2)}) collective-permute-start(bf16[512,128]{1,0:T(8,128)(2,1)S(1)} %shard_map.100.kv_ref), channel_id=1, source_target_pairs={{0,1},{1,0},{2,3},{3,2},{4,5},{5,4},{6,7},{7,6},{8,9},{9,8},{10,11... | collective-permute-start | bytes 393224 | tf_op jit(solution)/shard_map/ppermute | solution.py:273
  44.6 10.1 %copy-start = (bf16[1024,1024]{1,0:T(8,128)(2,1)S(1)}, bf16[1024,1024]{1,0:T(8,128)(2,1)}, u32[]{:S(2)}) copy-start(bf16[1024,1024]{1,0:T(8,128)(2,1)} %wout_ref.1) | copy-start | bytes 6291460

commit v13 on v11

--- a/solution.py
+++ b/solution.py
@@ -108,13 +108,12 @@
 
 ALL = ("view", "tok")
 CORES = 2
-PLANES = (1, 2, 3, 0)
+FIRST = HEADS // 4 + 1
 SHARP = HD ** (-0.5) * 1.4426950408889634
 
 
 def trade_groups():
-    plane = HEADS // len(PLANES)
-    chips = [p * plane + (i + 1) % plane for i in range(plane) for p in PLANES]
+    chips = [(FIRST + i) % HEADS for i in range(HEADS)]
     return [[chip * CORES + (chip + s) % CORES for chip in chips] for s in range(CORES)]
 
 
@@ -139,9 +138,11 @@
 
 
 def pack_kernel(q_hbm, k_hbm, v_hbm, out_ref, q_ref, k_ref, v_ref, sems):
+    half = q_ref.shape[1] // 2
     copies = [
-        pltpu.make_async_copy(src, dst, sems.at[i])
+        pltpu.make_async_copy(src.at[:, at : at + half], dst.at[:, at : at + half], sems.at[i, at // half])
         for i, (src, dst) in enumerate(((q_hbm, q_ref), (k_hbm, k_ref), (v_hbm, v_ref)))
+        for at in (0, half)
     ]
     for copy in copies:
         copy.start()
@@ -222,8 +223,8 @@
 def last_kernel(got_ref, wout_ref, out_hbm, out_ref, sems):
     rows = unit(unpack_rows(got_ref)).astype(jnp.bfloat16)
     copies = []
-    width = wout_ref.shape[1] // 2
-    for i in range(2):
+    width = wout_ref.shape[1] // 4
+    for i in range(4):
         cols = slice(i * width, (i + 1) * width)
         out_ref[0, :, cols] = jnp.dot(rows, wout_ref[:, cols], preferred_element_type=jnp.float32)
         copies.append(pltpu.make_async_copy(out_ref.at[:, :, cols], out_hbm.at[:, :, cols], sems.at[i]))
@@ -266,7 +267,7 @@
         return trade(half)
 
     inputs = [pltpu.with_memory_space_constraint(x, pltpu.HBM) for x in (q1, k1, v1)]
-    scratch = [pltpu.VMEM(q1.shape, q1.dtype)] * 3 + [pltpu.SemaphoreType.DMA((3,))]
+    scratch = [pltpu.VMEM(q1.shape, q1.dtype)] * 3 + [pltpu.SemaphoreType.DMA((3, 2))]
     (piece,) = call(pack_kernel, [packed], inputs, scratch, space=pltpu.HBM, limit=48 << 20)
     feats, piece = call(
         middle_kernel,
@@ -278,7 +279,7 @@
         last_kernel,
         [(wide, jnp.float32, pltpu.HBM)],
         (attention(piece), w_out),
-        [pltpu.VMEM(wide, jnp.float32), pltpu.SemaphoreType.DMA((2,))],
+        [pltpu.VMEM(wide, jnp.float32), pltpu.SemaphoreType.DMA((4,))],
     )
     return feats, result
 

time: 56.1 us -> 55.9 us (level)
  no operation moved by 1% of the time
where the time goes in v13:
time: 55.9 us; the launch traced here: 55.6 us
  blocking collectives  46 us (82%)
  Pallas kernels  7.42 us (13%)
  waiting for transfers between devices  1.36 us (2%)
  between operations  0.72 us (1%)
    all_to_all x4, blocking collectives, trade(): lax.all_to_all(piece, ALL, split_axis=0, concat_axis=0, tiled=True, axis_...  46 us
    pallas_call x7, Pallas kernels, call(): pl.pallas_call(body, out_shape=[jax.ShapeDtypeStruct(shape, dtype) for sh...  7.42 us
    ppermute x2, waiting for transfers between devices, attention(): other = lax.ppermute(mine, ALL, [(i, i ^ 1) for i in range(devices)])  1.36 us
  transfers between devices with their start and end apart: 2, of which 2 were waited for; matrix products, arithmetic and copies ran while one was open for 0% of the time, Pallas kernels for 3%

profile of v13, /device:TPU:0, one launch (start us, length us, event | category | flops | bytes accessed | tf_op | source)
XLA Modules:
  0.0 55.6 jit_solution(5066807018198395240)
XLA Ops:
  0.6 1.0 %shard_map.95 = bf16[16,48,128]{2,1,0:T(8,128)(2,1)S(1)} custom-call(bf16[1,32,1024]{2,1,0:T(8,128)(2,1)} %q_hbm.1, bf16[1,32,1024]{2,1,0:T(8,128)(2,1)} %k_hbm.1, bf16[1,32,1024]{2,1,0:T(8,128)(2,1)} %v_hbm.1), custom_call_target="tpu_custom_call" | custom-call | tf_op jit(solution)/shard_map/pallas_call | solution.py:237
  1.7 16.2 %all_to_all.20.mine_ref = bf16[16,48,128]{2,1,0:T(8,128)(2,1)S(1)} all-to-all(bf16[16,48,128]{2,1,0:T(8,128)(2,1)S(1)} %shard_map.95), channel_id=1, replica_groups={{11,12,15,16,19,20,23,24,27,28,31,0,3,4,7,8},{10,13,14,17,18,21,22,25,2..., dimensions={0} | all-to-all | bytes 393216 | tf_op jit(solution)/shard_map/all_to_all | solution.py:259
  17.8 0.0 collective-permute-start
  17.8 0.8 %shard_map.96 = (bf16[512,128]{1,0:T(8,128)(2,1)S(1)}, f32[512,128]{1,0:T(8,128)S(1)}, f32[512,128]{1,0:T(8,128)S(1)}) custom-call(bf16[16,48,128]{2,1,0:T(8,128)(2,1)S(1)} %all_to_all.20.mine_ref), custom_call_target="tpu_custom_call" | custom-call | flops 1073741824 | bytes 1048576 | tf_op jit(solution)/shard_map/pallas_call | solution.py:237
  18.6 0.7 %collective-permute-done.other_ref = bf16[16,48,128]{2,1,0:T(8,128)(2,1)S(1)} collective-permute-done((bf16[16,48,128]{2,1,0:T(8,128)(2,1)S(1)}, bf16[16,48,128]{2,1,0:T(8,128)(2,1)S(1)}, u32[]{:S(2)}, u32[]{:S(2)}) %collective-permute-start) | collective-permute-done | bytes 196640 | tf_op jit(solution)/shard_map/ppermute | solution.py:263
  19.3 0.0 slice-start
  19.3 0.0 slice-start.1
  19.3 0.0 copy-start.1
  19.3 0.0 copy-start.2
  19.3 0.0 copy-start.3
  19.3 0.8 %shard_map.97 = bf16[16,16,128]{2,1,0:T(8,128)(2,1)S(1)} custom-call(bf16[16,48,128]{2,1,0:T(8,128)(2,1)S(1)} %collective-permute-done.other_ref, bf16[512,128]{1,0:T(8,128)(2,1)S(1)} %get-tuple-element.10.query_ref, f32[512,128]{1,0:T(8,128)S(1)} %get-tuple-element.11.peak_ref, f32[512,128]{1,0:T(8,128)S(1)} %get-tuple-element.12.sum_ref), custom_call_target="tpu_custom_call" | custom-call | flops 17179869184 | bytes 41943040 | tf_op jit(solution)/shard_map/pallas_call | solution.py:237
  20.1 9.5 %all_to_all.21.got_ref = bf16[16,16,128]{2,1,0:T(8,128)(2,1)S(1)} all-to-all(bf16[16,16,128]{2,1,0:T(8,128)(2,1)S(1)} %shard_map.97), channel_id=1, replica_groups={{11,12,15,16,19,20,23,24,27,28,31,0,3,4,7,8},{10,13,14,17,18,21,22,25,2..., dimensions={0} | all-to-all | bytes 131072 | tf_op jit(solution)/shard_map/all_to_all | solution.py:259
  29.7 0.0 slice-done
  29.7 0.0 slice-done.1
  29.7 0.0 copy-done.1
  29.7 0.0 copy-done.2
  29.7 0.0 copy-done.3
  29.7 2.0 %shard_map.98 = (f32[1,32,1024]{2,1,0:T(8,128)}, bf16[16,48,128]{2,1,0:T(8,128)(2,1)S(1)}) custom-call(bf16[16,16,128]{2,1,0:T(8,128)(2,1)S(1)} %all_to_all.21.got_ref, bf16[1,32,1024]{2,1,0:T(8,128)(2,1)S(1)} %copy-done.2, bf16[1024,1024]{1,0:T(8,128)(2,1)S(1)} %copy-done.1, f32[1,1024]{1,0:T(1,128)S(1)} %bitcast.3, bf16[1024,3072]{1,0:T(8,128)(2,1)S(1)} %bitcast.2), custom_call_target="tpu_custom_call" | custom-call | tf_op jit(solution)/shard_map/pallas_call | solution.py:237
  31.7 11.1 %all_to_all.22.mine_ref = bf16[16,48,128]{2,1,0:T(8,128)(2,1)S(1)} all-to-all(bf16[16,48,128]{2,1,0:T(8,128)(2,1)S(1)} %get-tuple-element.14), channel_id=1, replica_groups={{11,12,15,16,19,20,23,24,27,28,31,0,3,4,7,8},{10,13,14,17,18,21,22,25,2..., dimensions={0} | all-to-all | bytes 393216 | tf_op jit(solution)/shard_map/all_to_all | solution.py:259
  42.7 0.0 collective-permute-start.1
  42.7 0.8 %shard_map.99 = (bf16[512,128]{1,0:T(8,128)(2,1)S(1)}, f32[512,128]{1,0:T(8,128)S(1)}, f32[512,128]{1,0:T(8,128)S(1)}) custom-call(bf16[16,48,128]{2,1,0:T(8,128)(2,1)S(1)} %all_to_all.22.mine_ref), custom_call_target="tpu_custom_call" | custom-call | flops 1073741824 | bytes 1048576 | tf_op jit(solution)/shard_map/pallas_call | solution.py:237
  43.5 0.7 %collective-permute-done.1.other_ref = bf16[16,48,128]{2,1,0:T(8,128)(2,1)S(1)} collective-permute-done((bf16[16,48,128]{2,1,0:T(8,128)(2,1)S(1)}, bf16[16,48,128]{2,1,0:T(8,128)(2,1)S(1)}, u32[]{:S(2)}, u32[]{:S(2)}) %collective-permute-start.1) | collective-permute-done | bytes 196640 | tf_op jit(solution)/shard_map/ppermute | solution.py:263
  44.2 0.0 copy-start
  44.2 0.8 %shard_map.100 = bf16[16,16,128]{2,1,0:T(8,128)(2,1)S(1)} custom-call(bf16[16,48,128]{2,1,0:T(8,128)(2,1)S(1)} %collective-permute-done.1.other_ref, bf16[512,128]{1,0:T(8,128)(2,1)S(1)} %get-tuple-element.15.query_ref, f32[512,128]{1,0:T(8,128)S(1)} %get-tuple-element.16.peak_ref, f32[512,128]{1,0:T(8,128)S(1)} %get-tuple-element.17.sum_ref), custom_call_target="tpu_custom_call" | custom-call | flops 17179869184 | bytes 41943040 | tf_op jit(solution)/shard_map/pallas_call | solution.py:237
  45.0 9.3 %all_to_all.23.got_ref = bf16[16,16,128]{2,1,0:T(8,128)(2,1)S(1)} all-to-all(bf16[16,16,128]{2,1,0:T(8,128)(2,1)S(1)} %shard_map.100), channel_id=1, replica_groups={{11,12,15,16,19,20,23,24,27,28,31,0,3,4,7,8},{10,13,14,17,18,21,22,25,2..., dimensions={0} | all-to-all | bytes 131072 | tf_op jit(solution)/shard_map/all_to_all | solution.py:259
  54.3 0.0 copy-done
  54.3 1.3 %shard_map.101 = f32[1,32,1024]{2,1,0:T(8,128)} custom-call(bf16[16,16,128]{2,1,0:T(8,128)(2,1)S(1)} %all_to_all.23.got_ref, bf16[1024,1024]{1,0:T(8,128)(2,1)S(1)} %copy-done), custom_call_target="tpu_custom_call" | custom-call | tf_op jit(solution)/shard_map/pallas_call | solution.py:237
  (1 shorter events, 0.0 us)
Async XLA Ops:
  17.8 1.4 %collective-permute-start = (bf16[16,48,128]{2,1,0:T(8,128)(2,1)S(1)}, bf16[16,48,128]{2,1,0:T(8,128)(2,1)S(1)}, u32[]{:S(2)}, u32[]{:S(2)}) collective-permute-start(bf16[16,48,128]{2,1,0:T(8,128)(2,1)S(1)} %all_to_all.20.mine_ref), channel_id=1, source_target_pairs={{0,1},{1,0},{2,3},{3,2},{4,5},{5,4},{6,7},{7,6},{8,9},{9,8},{10,11... | collective-permute-start | bytes 589832 | tf_op jit(solution)/shard_map/ppermute | solution.py:263
  19.3 10.4 %slice-start = ((s8[6291456]{0:T(1024)(128)(4,1)}), s8[4194304]{0:T(1024)(128)(4,1)S(1)}, s32[]{:S(2)}) async-start(s8[6291456]{0:T(1024)(128)(4,1)} %bitcast.1), calls=%async_computation.4 | async-start | bytes 8388608
  19.3 10.4 %slice-start.1 = ((s8[6291456]{0:T(1024)(128)(4,1)}), s8[2097152]{0:T(1024)(128)(4,1)S(1)}, s32[]{:S(2)}) async-start(s8[6291456]{0:T(1024)(128)(4,1)} %bitcast.1), calls=%async_computation.5 | async-start | bytes 4194304
  19.3 10.4 %copy-start.1 = (bf16[1024,1024]{1,0:T(8,128)(2,1)S(1)}, bf16[1024,1024]{1,0:T(8,128)(2,1)}, u32[]{:S(2)}) copy-start(bf16[1024,1024]{1,0:T(8,128)(2,1)} %wv_ref.1) | copy-start | bytes 6291460
  19.3 10.4 %copy-start.2 = (bf16[1,32,1024]{2,1,0:T(8,128)(2,1)S(1)}, bf16[1,32,1024]{2,1,0:T(8,128)(2,1)}, u32[]{:S(2)}) copy-start(bf16[1,32,1024]{2,1,0:T(8,128)(2,1)} %x2_ref.1) | copy-start | bytes 196612
  19.3 10.4 %copy-start.3 = (f32[1024]{0:T(1024)S(1)}, f32[1024]{0:T(1024)}, u32[]{:S(2)}) copy-start(f32[1024]{0:T(1024)} %param.14) | copy-start | bytes 12292
  42.7 1.4 %collective-permute-start.1 = (bf16[16,48,128]{2,1,0:T(8,128)(2,1)S(1)}, bf16[16,48,128]{2,1,0:T(8,128)(2,1)S(1)}, u32[]{:S(2)}, u32[]{:S(2)}) collective-permute-start(bf16[16,48,128]{2,1,0:T(8,128)(2,1)S(1)} %all_to_all.22.mine_ref), channel_id=1, source_target_pairs={{0,1},{1,0},{2,3},{3,2},{4,5},{5,4},{6,7},{7,6},{8,9},{9,8},{10,11... | collective-permute-start | bytes 589832 | tf_op jit(solution)/shard_map/ppermute | solution.py:263
  44.2 10.1 %copy-start = (bf16[1024,1024]{1,0:T(8,128)(2,1)S(1)}, bf16[1024,1024]{1,0:T(8,128)(2,1)}, u32[]{:S(2)}) copy-start(bf16[1024,1024]{1,0:T(8,128)(2,1)} %wout_ref.1) | copy-start | bytes 6291460

commit v14 on v13

--- a/solution.py
+++ b/solution.py
@@ -114,7 +114,7 @@
 
 def trade_groups():
     chips = [(FIRST + i) % HEADS for i in range(HEADS)]
-    return [[chip * CORES + (chip + s) % CORES for chip in chips] for s in range(CORES)]
+    return [[chip * CORES + (chip // (HEADS // 2) + s) % CORES for chip in chips] for s in range(CORES)]
 
 
 def pack_heads(out_ref, q, k, v):

time: 55.9 us -> 55.7 us (level)
  starting transfers between devices: 0.01 us -> 0.67 us
    ppermute x2, starting transfers between devices: 0.01 us -> 0.67 us  [attention(): other = lax.ppermute(mine, ALL, [(i, i ^ 1) for i in range(devices)])]
where the time goes in v14:
time: 55.7 us; the launch traced here: 55.4 us
  blocking collectives  45.7 us (82%)
  Pallas kernels  7.43 us (13%)
  waiting for transfers between devices  0.88 us (2%)
  between operations  0.72 us (1%)
  starting transfers between devices  0.67 us (1%)
    all_to_all x4, blocking collectives, trade(): lax.all_to_all(piece, ALL, split_axis=0, concat_axis=0, tiled=True, axis_...  45.7 us
    pallas_call x7, Pallas kernels, call(): pl.pallas_call(body, out_shape=[jax.ShapeDtypeStruct(shape, dtype) for sh...  7.43 us
  transfers between devices with their start and end apart: 2, of which 2 were waited for; matrix products, arithmetic and copies ran while one was open for 0% of the time, Pallas kernels for 3%

profile of v14, /device:TPU:0, one launch (start us, length us, event | category | flops | bytes accessed | tf_op | source)
XLA Modules:
  0.0 55.4 jit_solution(15785611429775761206)
XLA Ops:
  0.6 1.0 %shard_map.95 = bf16[16,48,128]{2,1,0:T(8,128)(2,1)S(1)} custom-call(bf16[1,32,1024]{2,1,0:T(8,128)(2,1)} %q_hbm.1, bf16[1,32,1024]{2,1,0:T(8,128)(2,1)} %k_hbm.1, bf16[1,32,1024]{2,1,0:T(8,128)(2,1)} %v_hbm.1), custom_call_target="tpu_custom_call" | custom-call | tf_op jit(solution)/shard_map/pallas_call | solution.py:237
  1.7 14.9 %all_to_all.20.mine_ref = bf16[16,48,128]{2,1,0:T(8,128)(2,1)S(1)} all-to-all(bf16[16,48,128]{2,1,0:T(8,128)(2,1)S(1)} %shard_map.95), channel_id=1, replica_groups={{10,12,14,17,19,21,23,25,27,29,31,0,2,4,6,8},{11,13,15,16,18,20,22,24,2..., dimensions={0} | all-to-all | bytes 393216 | tf_op jit(solution)/shard_map/all_to_all | solution.py:259
  16.5 0.6 %collective-permute-start = (bf16[16,48,128]{2,1,0:T(8,128)(2,1)S(1)}, bf16[16,48,128]{2,1,0:T(8,128)(2,1)S(1)}, u32[]{:S(2)}, u32[]{:S(2)}) collective-permute-start(bf16[16,48,128]{2,1,0:T(8,128)(2,1)S(1)} %all_to_all.20.mine_ref), channel_id=1, source_target_pairs={{0,1},{1,0},{2,3},{3,2},{4,5},{5,4},{6,7},{7,6},{8,9},{9,8},{10,11... | collective-permute-start | bytes 589832 | tf_op jit(solution)/shard_map/ppermute | solution.py:263
  17.1 0.8 %shard_map.96 = (bf16[512,128]{1,0:T(8,128)(2,1)S(1)}, f32[512,128]{1,0:T(8,128)S(1)}, f32[512,128]{1,0:T(8,128)S(1)}) custom-call(bf16[16,48,128]{2,1,0:T(8,128)(2,1)S(1)} %all_to_all.20.mine_ref), custom_call_target="tpu_custom_call" | custom-call | flops 1073741824 | bytes 1048576 | tf_op jit(solution)/shard_map/pallas_call | solution.py:237
  17.8 0.3 collective-permute-done.other_ref
  18.2 0.0 slice-start
  18.2 0.0 slice-start.1
  18.2 0.0 copy-start.1
  18.2 0.0 copy-start.2
  18.2 0.0 copy-start.3
  18.2 0.8 %shard_map.97 = bf16[16,16,128]{2,1,0:T(8,128)(2,1)S(1)} custom-call(bf16[16,48,128]{2,1,0:T(8,128)(2,1)S(1)} %collective-permute-done.other_ref, bf16[512,128]{1,0:T(8,128)(2,1)S(1)} %get-tuple-element.10.query_ref, f32[512,128]{1,0:T(8,128)S(1)} %get-tuple-element.11.peak_ref, f32[512,128]{1,0:T(8,128)S(1)} %get-tuple-element.12.sum_ref), custom_call_target="tpu_custom_call" | custom-call | flops 17179869184 | bytes 41943040 | tf_op jit(solution)/shard_map/pallas_call | solution.py:237
  19.0 9.8 %all_to_all.21.got_ref = bf16[16,16,128]{2,1,0:T(8,128)(2,1)S(1)} all-to-all(bf16[16,16,128]{2,1,0:T(8,128)(2,1)S(1)} %shard_map.97), channel_id=1, replica_groups={{10,12,14,17,19,21,23,25,27,29,31,0,2,4,6,8},{11,13,15,16,18,20,22,24,2..., dimensions={0} | all-to-all | bytes 131072 | tf_op jit(solution)/shard_map/all_to_all | solution.py:259
  28.8 0.0 slice-done
  28.9 0.0 slice-done.1
  28.9 0.0 copy-done.1
  28.9 0.0 copy-done.2
  28.9 0.0 copy-done.3
  28.9 2.0 %shard_map.98 = (f32[1,32,1024]{2,1,0:T(8,128)}, bf16[16,48,128]{2,1,0:T(8,128)(2,1)S(1)}) custom-call(bf16[16,16,128]{2,1,0:T(8,128)(2,1)S(1)} %all_to_all.21.got_ref, bf16[1,32,1024]{2,1,0:T(8,128)(2,1)S(1)} %copy-done.2, bf16[1024,1024]{1,0:T(8,128)(2,1)S(1)} %copy-done.1, f32[1,1024]{1,0:T(1,128)S(1)} %bitcast.3, bf16[1024,3072]{1,0:T(8,128)(2,1)S(1)} %bitcast.2), custom_call_target="tpu_custom_call" | custom-call | tf_op jit(solution)/shard_map/pallas_call | solution.py:237
  30.8 11.5 %all_to_all.22.mine_ref = bf16[16,48,128]{2,1,0:T(8,128)(2,1)S(1)} all-to-all(bf16[16,48,128]{2,1,0:T(8,128)(2,1)S(1)} %get-tuple-element.14), channel_id=1, replica_groups={{10,12,14,17,19,21,23,25,27,29,31,0,2,4,6,8},{11,13,15,16,18,20,22,24,2..., dimensions={0} | all-to-all | bytes 393216 | tf_op jit(solution)/shard_map/all_to_all | solution.py:259
  42.4 0.1 collective-permute-start.1
  42.5 0.7 %shard_map.99 = (bf16[512,128]{1,0:T(8,128)(2,1)S(1)}, f32[512,128]{1,0:T(8,128)S(1)}, f32[512,128]{1,0:T(8,128)S(1)}) custom-call(bf16[16,48,128]{2,1,0:T(8,128)(2,1)S(1)} %all_to_all.22.mine_ref), custom_call_target="tpu_custom_call" | custom-call | flops 1073741824 | bytes 1048576 | tf_op jit(solution)/shard_map/pallas_call | solution.py:237
  43.2 0.6 %collective-permute-done.1.other_ref = bf16[16,48,128]{2,1,0:T(8,128)(2,1)S(1)} collective-permute-done((bf16[16,48,128]{2,1,0:T(8,128)(2,1)S(1)}, bf16[16,48,128]{2,1,0:T(8,128)(2,1)S(1)}, u32[]{:S(2)}, u32[]{:S(2)}) %collective-permute-start.1) | collective-permute-done | bytes 196640 | tf_op jit(solution)/shard_map/ppermute | solution.py:263
  43.8 0.0 copy-start
  43.8 0.8 %shard_map.100 = bf16[16,16,128]{2,1,0:T(8,128)(2,1)S(1)} custom-call(bf16[16,48,128]{2,1,0:T(8,128)(2,1)S(1)} %collective-permute-done.1.other_ref, bf16[512,128]{1,0:T(8,128)(2,1)S(1)} %get-tuple-element.15.query_ref, f32[512,128]{1,0:T(8,128)S(1)} %get-tuple-element.16.peak_ref, f32[512,128]{1,0:T(8,128)S(1)} %get-tuple-element.17.sum_ref), custom_call_target="tpu_custom_call" | custom-call | flops 17179869184 | bytes 41943040 | tf_op jit(solution)/shard_map/pallas_call | solution.py:237
  44.7 9.5 %all_to_all.23.got_ref = bf16[16,16,128]{2,1,0:T(8,128)(2,1)S(1)} all-to-all(bf16[16,16,128]{2,1,0:T(8,128)(2,1)S(1)} %shard_map.100), channel_id=1, replica_groups={{10,12,14,17,19,21,23,25,27,29,31,0,2,4,6,8},{11,13,15,16,18,20,22,24,2..., dimensions={0} | all-to-all | bytes 131072 | tf_op jit(solution)/shard_map/all_to_all | solution.py:259
  54.1 0.0 copy-done
  54.1 1.3 %shard_map.101 = f32[1,32,1024]{2,1,0:T(8,128)} custom-call(bf16[16,16,128]{2,1,0:T(8,128)(2,1)S(1)} %all_to_all.23.got_ref, bf16[1024,1024]{1,0:T(8,128)(2,1)S(1)} %copy-done), custom_call_target="tpu_custom_call" | custom-call | tf_op jit(solution)/shard_map/pallas_call | solution.py:237
  (1 shorter events, 0.0 us)
Async XLA Ops:
  16.5 1.6 %collective-permute-start = (bf16[16,48,128]{2,1,0:T(8,128)(2,1)S(1)}, bf16[16,48,128]{2,1,0:T(8,128)(2,1)S(1)}, u32[]{:S(2)}, u32[]{:S(2)}) collective-permute-start(bf16[16,48,128]{2,1,0:T(8,128)(2,1)S(1)} %all_to_all.20.mine_ref), channel_id=1, source_target_pairs={{0,1},{1,0},{2,3},{3,2},{4,5},{5,4},{6,7},{7,6},{8,9},{9,8},{10,11... | collective-permute-start | bytes 589832 | tf_op jit(solution)/shard_map/ppermute | solution.py:263
  18.2 10.7 %slice-start = ((s8[6291456]{0:T(1024)(128)(4,1)}), s8[4194304]{0:T(1024)(128)(4,1)S(1)}, s32[]{:S(2)}) async-start(s8[6291456]{0:T(1024)(128)(4,1)} %bitcast.1), calls=%async_computation.4 | async-start | bytes 8388608
  18.2 10.7 %slice-start.1 = ((s8[6291456]{0:T(1024)(128)(4,1)}), s8[2097152]{0:T(1024)(128)(4,1)S(1)}, s32[]{:S(2)}) async-start(s8[6291456]{0:T(1024)(128)(4,1)} %bitcast.1), calls=%async_computation.5 | async-start | bytes 4194304
  18.2 10.7 %copy-start.1 = (bf16[1024,1024]{1,0:T(8,128)(2,1)S(1)}, bf16[1024,1024]{1,0:T(8,128)(2,1)}, u32[]{:S(2)}) copy-start(bf16[1024,1024]{1,0:T(8,128)(2,1)} %wv_ref.1) | copy-start | bytes 6291460
  18.2 10.7 %copy-start.2 = (bf16[1,32,1024]{2,1,0:T(8,128)(2,1)S(1)}, bf16[1,32,1024]{2,1,0:T(8,128)(2,1)}, u32[]{:S(2)}) copy-start(bf16[1,32,1024]{2,1,0:T(8,128)(2,1)} %x2_ref.1) | copy-start | bytes 196612
  18.2 10.7 %copy-start.3 = (f32[1024]{0:T(1024)S(1)}, f32[1024]{0:T(1024)}, u32[]{:S(2)}) copy-start(f32[1024]{0:T(1024)} %param.14) | copy-start | bytes 12292
  42.4 1.4 %collective-permute-start.1 = (bf16[16,48,128]{2,1,0:T(8,128)(2,1)S(1)}, bf16[16,48,128]{2,1,0:T(8,128)(2,1)S(1)}, u32[]{:S(2)}, u32[]{:S(2)}) collective-permute-start(bf16[16,48,128]{2,1,0:T(8,128)(2,1)S(1)} %all_to_all.22.mine_ref), channel_id=1, source_target_pairs={{0,1},{1,0},{2,3},{3,2},{4,5},{5,4},{6,7},{7,6},{8,9},{9,8},{10,11... | collective-permute-start | bytes 589832 | tf_op jit(solution)/shard_map/ppermute | solution.py:263
  43.8 10.3 %copy-start = (bf16[1024,1024]{1,0:T(8,128)(2,1)S(1)}, bf16[1024,1024]{1,0:T(8,128)(2,1)}, u32[]{:S(2)}) copy-start(bf16[1024,1024]{1,0:T(8,128)(2,1)} %wout_ref.1) | copy-start | bytes 6291460

commit v15 on v10

--- a/solution.py
+++ b/solution.py
@@ -108,13 +108,12 @@
 
 ALL = ("view", "tok")
 CORES = 2
-PLANES = (1, 2, 3, 0)
+FIRST = HEADS // 4 + 1
 SHARP = HD ** (-0.5) * 1.4426950408889634
 
 
 def trade_groups():
-    plane = HEADS // len(PLANES)
-    chips = [p * plane + (i + 1) % plane for p in PLANES for i in range(plane)]
+    chips = [(FIRST + i) % HEADS for i in range(HEADS)]
     return [[chip * CORES + (chip + s) % CORES for chip in chips] for s in range(CORES)]
 
 
@@ -139,9 +138,11 @@
 
 
 def pack_kernel(q_hbm, k_hbm, v_hbm, out_ref, q_ref, k_ref, v_ref, sems):
+    half = q_ref.shape[1] // 2
     copies = [
-        pltpu.make_async_copy(src, dst, sems.at[i])
+        pltpu.make_async_copy(src.at[:, at : at + half], dst.at[:, at : at + half], sems.at[i, at // half])
         for i, (src, dst) in enumerate(((q_hbm, q_ref), (k_hbm, k_ref), (v_hbm, v_ref)))
+        for at in (0, half)
     ]
     for copy in copies:
         copy.start()
@@ -181,10 +182,10 @@
     top, low = sums
     left = lower_half(top.shape)
     attn = jnp.where(left, pltpu.roll(top, HD, 1), low) / jnp.where(left, top, pltpu.roll(low, HD, 1))
-    return attn.astype(jnp.bfloat16).reshape(HEADS, -1, 2 * HD)
-
-
-def begin_kernel(mine_ref, query_ref, peak_ref, sum_ref):
+    return attn.astype(jnp.bfloat16)
+
+
+def begin_kernel(mine_ref, mate_ref, query_ref, peak_ref, sum_ref):
     rows = mine_ref.shape[1] * 2 // 3
     keys, vals = key_values(mine_ref, rows)
     for i, queries in enumerate(two_queries(mine_ref, rows)):
@@ -193,7 +194,7 @@
         query_ref[at, :] = queries
         scores = score(queries, keys)
         peak = jnp.max(scores, axis=-1, keepdims=True)
-        peak_ref[at, :] = peak
+        peak_ref[at, :] = jnp.broadcast_to(peak, (n, 2 * HD))
         sum_ref[at, :] = weigh(scores, peak, vals)
 
 
@@ -205,13 +206,15 @@
         at = slice(i * n, (i + 1) * n)
         scores = score(query_ref[at, :], keys)
         before = peak_ref[at, :]
-        peak = jnp.maximum(before, jnp.max(scores, axis=-1, keepdims=True))
-        sums.append(sum_ref[at, :] * jnp.exp2((before - peak) * SHARP) + weigh(scores, peak, vals))
+        peak = jnp.maximum(before, jnp.broadcast_to(jnp.max(scores, axis=-1, keepdims=True), before.shape))
+        wide_peak = jnp.concatenate([peak] * (scores.shape[1] // peak.shape[1]), axis=-1)
+        sums.append(sum_ref[at, :] * jnp.exp2((before - peak) * SHARP) + weigh(scores, wide_peak, vals))
     attn = lined(sums)
-    half, away = attn.shape[1], HEADS // 2
-    out_ref[:, 0:half, :] = attn
-    out_ref[:away, half:, :] = attn[away:]
-    out_ref[away:, half:, :] = attn[:away]
+    half = n // HEADS
+    for i in range(HEADS):
+        block = attn[i * half : (i + 1) * half]
+        out_ref[i, 0:half, :] = block
+        out_ref[(i + HEADS // 2) % HEADS, half : 2 * half, :] = block
 
 
 def whole_kernel(got_ref, out_ref):
@@ -221,7 +224,7 @@
     for queries in two_queries(got_ref, rows):
         scores = score(queries, keys)
         sums.append(weigh(scores, jnp.max(scores, axis=-1, keepdims=True), vals))
-    out_ref[...] = lined(sums)
+    out_ref[...] = lined(sums).reshape(out_ref.shape)
 
 
 def middle_kernel(got_ref, x2_ref, mate_ref, wv_ref, gain_ref, wqkv_ref, feats_hbm, out_ref, feats_ref, sem):
@@ -246,8 +249,8 @@
 def last_kernel(got_ref, wout_ref, out_hbm, out_ref, sems):
     rows = unit(unpack_rows(got_ref, 0, got_ref.shape[1])).astype(jnp.bfloat16)
     copies = []
-    width = wout_ref.shape[1] // 2
-    for i in range(2):
+    width = wout_ref.shape[1] // 4
+    for i in range(4):
         cols = slice(i * width, (i + 1) * width)
         out_ref[0, :, cols] = jnp.dot(rows, wout_ref[:, cols], preferred_element_type=jnp.float32)
         copies.append(pltpu.make_async_copy(out_ref.at[:, :, cols], out_hbm.at[:, :, cols], sems.at[i]))
@@ -276,8 +279,7 @@
         return ((HEADS, lines, 2 * HD), jnp.bfloat16, pltpu.VMEM)
 
     queries = ((HEADS * rows, 2 * HD), jnp.bfloat16, pltpu.VMEM)
-    peaks = ((HEADS * rows, 1), jnp.float32, pltpu.VMEM)
-    sums = ((HEADS * rows, 2 * HD), jnp.float32, pltpu.VMEM)
+    lines = ((HEADS * rows, 2 * HD), jnp.float32, pltpu.VMEM)
     wide = (1, rows, HEADS * HD)
     across = trade_groups()
     halves = [[s * HEADS + i for i in range(HEADS)] for s in range(CORES)]
@@ -287,12 +289,12 @@
         return lax.all_to_all(piece, ALL, split_axis=0, concat_axis=0, tiled=True, axis_index_groups=groups)
 
     inputs = [pltpu.with_memory_space_constraint(x, pltpu.HBM) for x in (q1, k1, v1)]
-    scratch = [pltpu.VMEM(q1.shape, q1.dtype)] * 3 + [pltpu.SemaphoreType.DMA((3,))]
+    scratch = [pltpu.VMEM(q1.shape, q1.dtype)] * 3 + [pltpu.SemaphoreType.DMA((3, 2))]
     (piece,) = call(pack_kernel, [kept(rows * 3 // 2)], inputs, scratch, space=pltpu.HBM, limit=48 << 20)
     mine = trade(piece, across)
     other = lax.ppermute(mine, ALL, [(i, i ^ 1) for i in range(devices)])
     mate = lax.ppermute(x2, ALL, [(i, i ^ HEADS) for i in range(devices)])
-    begun = call(begin_kernel, [queries, peaks, sums], (mine,), cost=pl.CostEstimate(1 << 30, 0, 1 << 20))
+    begun = call(begin_kernel, [queries, lines, lines], (mine, mate), cost=pl.CostEstimate(1 << 30, 0, 1 << 20))
     (part,) = call(finish_kernel, [kept(rows)], (other, *begun), cost=cost)
     feats, piece = call(
         middle_kernel,
@@ -305,7 +307,7 @@
         last_kernel,
         [(wide, jnp.float32, pltpu.HBM)],
         (trade(part, halves), w_out),
-        [pltpu.VMEM(wide, jnp.float32), pltpu.SemaphoreType.DMA((2,))],
+        [pltpu.VMEM(wide, jnp.float32), pltpu.SemaphoreType.DMA((4,))],
     )
     return feats, result
 

time: 60.7 us -> 61.2 us (level)
  blocking collectives: 33.4 us -> 46.8 us
  starting transfers between devices: 8.42 us -> 0.71 us
  local copies, waits for them, and re-layouts: 2.79 us -> 0.03 us
  waiting for transfers between devices: 7.07 us -> 5.6 us
  Pallas kernels: 7.93 us -> 6.99 us
    all_to_all x3 -> x4, blocking collectives: 33.4 us -> 46.8 us  [trade(): lax.all_to_all(piece, ALL, split_axis=0, concat_axis=0, tiled=True, axis_...]
    all_to_all x1 -> x0, starting transfers between devices: 5.41 us -> none  [trade(): lax.all_to_all(piece, ALL, split_axis=0, concat_axis=0, tiled=True, axis_...]
    unnamed x10 -> x12, local copies, waits for them, and re-layouts: 2.79 us -> 0.03 us
    ppermute x1, starting transfers between devices: 1.54 us -> 0.01 us  [by_heads(): other = lax.ppermute(mine, ALL, [(i, i ^ 1) for i in range(devices)])]
    ppermute x1, waiting for transfers between devices: 6.77 us -> 5.6 us  [by_heads(): mate = lax.ppermute(x2, ALL, [(i, i ^ HEADS) for i in range(devices)])]
    pallas_call x6, Pallas kernels: 7.93 us -> 6.99 us  [call(): pl.pallas_call(body, out_shape=[jax.ShapeDtypeStruct(shape, dtype) for sh...]
    ppermute x1, starting transfers between devices: 1.47 us -> 0.71 us  [by_heads(): mate = lax.ppermute(x2, ALL, [(i, i ^ HEADS) for i in range(devices)])]
  transfers between devices with their start and end apart: 3 -> 2, of which waited for: 2 -> 1; matrix products, arithmetic and copies ran while one was open for 0% -> 0% of each run, Pallas kernels for 1% -> 1%
where the time goes in v15:
time: 61.2 us; the launch traced here: 60.8 us
  blocking collectives  46.8 us (76%)
  Pallas kernels  6.99 us (11%)
  waiting for transfers between devices  5.6 us (9%)
  between operations  0.75 us (1%)
  starting transfers between devices  0.71 us (1%)
    all_to_all x4, blocking collectives, trade(): lax.all_to_all(piece, ALL, split_axis=0, concat_axis=0, tiled=True, axis_...  46.8 us
    pallas_call x6, Pallas kernels, call(): pl.pallas_call(body, out_shape=[jax.ShapeDtypeStruct(shape, dtype) for sh...  6.99 us
    ppermute x1, waiting for transfers between devices, by_heads(): mate = lax.ppermute(x2, ALL, [(i, i ^ HEADS) for i in range(devices)])  5.6 us
  transfers between devices with their start and end apart: 2, of which 1 were waited for; matrix products, arithmetic and copies ran while one was open for 0% of the time, Pallas kernels for 1%

profile of v15, /device:TPU:0, one launch (start us, length us, event | category | flops | bytes accessed | tf_op | source)
XLA Modules:
  0.0 60.8 jit_solution(8758975783858078409)
XLA Ops:
  0.6 1.0 %shard_map.95 = bf16[16,48,128]{2,1,0:T(8,128)(2,1)S(1)} custom-call(bf16[1,32,1024]{2,1,0:T(8,128)(2,1)} %q_hbm.1, bf16[1,32,1024]{2,1,0:T(8,128)(2,1)} %k_hbm.1, bf16[1,32,1024]{2,1,0:T(8,128)(2,1)} %v_hbm.1), custom_call_target="tpu_custom_call" | custom-call | tf_op jit(solution)/shard_map/pallas_call | solution.py:263
  1.7 16.2 %all_to_all.20.mine_ref = bf16[16,48,128]{2,1,0:T(8,128)(2,1)S(1)} all-to-all(bf16[16,48,128]{2,1,0:T(8,128)(2,1)S(1)} %shard_map.95), channel_id=1, replica_groups={{11,12,15,16,19,20,23,24,27,28,31,0,3,4,7,8},{10,13,14,17,18,21,22,25,2..., dimensions={0} | all-to-all | bytes 393216 | tf_op jit(solution)/shard_map/all_to_all | solution.py:289
  17.8 0.0 collective-permute-start
  17.8 0.7 %collective-permute-start.1 = (bf16[1,32,1024]{2,1,0:T(8,128)(2,1)}, bf16[1,32,1024]{2,1,0:T(8,128)(2,1)S(1)}, u32[]{:S(2)}, u32[]{:S(2)}) collective-permute-start(bf16[1,32,1024]{2,1,0:T(8,128)(2,1)} %x2_ref.1), channel_id=1, source_target_pairs={{0,16},{1,17},{2,18},{3,19},{4,20},{5,21},{6,22},{7,23},{8,24},{9,... | collective-permute-start | bytes 196616 | tf_op jit(solution)/shard_map/ppermute | solution.py:296
  18.5 5.6 %collective-permute-done.1.mate_ref = bf16[1,32,1024]{2,1,0:T(8,128)(2,1)S(1)} collective-permute-done((bf16[1,32,1024]{2,1,0:T(8,128)(2,1)}, bf16[1,32,1024]{2,1,0:T(8,128)(2,1)S(1)}, u32[]{:S(2)}, u32[]{:S(2)}) %collective-permute-start.1) | collective-permute-done | bytes 65568 | tf_op jit(solution)/shard_map/ppermute | solution.py:296
  24.1 0.8 %shard_map.96 = (bf16[512,128]{1,0:T(8,128)(2,1)S(1)}, f32[512,128]{1,0:T(8,128)S(1)}, f32[512,128]{1,0:T(8,128)S(1)}) custom-call(bf16[16,48,128]{2,1,0:T(8,128)(2,1)S(1)} %all_to_all.20.mine_ref, bf16[1,32,1024]{2,1,0:T(8,128)(2,1)S(1)} %collective-permute-done.1.mate_ref), custom_call_target="tpu_custom_call" | custom-call | flops 1073741824 | bytes 1048576 | tf_op jit(solution)/shard_map/pallas_call | solution.py:263
  24.9 0.0 collective-permute-done.other_ref
  24.9 0.0 slice-start
  24.9 0.0 slice-start.1
  24.9 0.0 copy-start.1
  24.9 0.0 copy-start.2
  24.9 0.0 copy-start.3
  25.0 0.8 %shard_map.97 = bf16[16,32,128]{2,1,0:T(8,128)(2,1)S(1)} custom-call(bf16[16,48,128]{2,1,0:T(8,128)(2,1)S(1)} %collective-permute-done.other_ref, bf16[512,128]{1,0:T(8,128)(2,1)S(1)} %get-tuple-element.7.query_ref, f32[512,128]{1,0:T(8,128)S(1)} %get-tuple-element.8.peak_ref, f32[512,128]{1,0:T(8,128)S(1)} %get-tuple-element.9.sum_ref), custom_call_target="tpu_custom_call" | custom-call | flops 17179869184 | bytes 41943040 | tf_op jit(solution)/shard_map/pallas_call | solution.py:263
  25.8 11.1 %all_to_all.21.got_ref = bf16[16,32,128]{2,1,0:T(8,128)(2,1)S(1)} all-to-all(bf16[16,32,128]{2,1,0:T(8,128)(2,1)S(1)} %shard_map.97), channel_id=1, replica_groups={{11,12,15,16,19,20,23,24,27,28,31,0,3,4,7,8},{10,13,14,17,18,21,22,25,2..., dimensions={0} | all-to-all | bytes 262144 | tf_op jit(solution)/shard_map/all_to_all | solution.py:289
  37.0 0.0 slice-done
  37.0 0.0 slice-done.1
  37.0 0.0 copy-done.1
  37.0 0.0 copy-done.2
  37.0 0.0 copy-done.3
  37.0 2.0 %shard_map.98 = (f32[1,32,1024]{2,1,0:T(8,128)}, bf16[16,80,128]{2,1,0:T(8,128)(2,1)S(1)}) custom-call(bf16[16,32,128]{2,1,0:T(8,128)(2,1)S(1)} %all_to_all.21.got_ref, bf16[1,32,1024]{2,1,0:T(8,128)(2,1)S(1)} %copy-done.2, bf16[1,32,1024]{2,1,0:T(8,128)(2,1)S(1)} %collective-permute-done.1.mate_ref, bf16[1024,1024]{1,0:T(8,128)(2,1)S(1)} %copy-done.1, ...), custom_call_target="tpu_custom_call" | custom-call | tf_op jit(solution)/shard_map/pallas_call | solution.py:263
  39.0 11.0 %all_to_all.22.got_ref = bf16[16,80,128]{2,1,0:T(8,128)(2,1)S(1)} all-to-all(bf16[16,80,128]{2,1,0:T(8,128)(2,1)S(1)} %get-tuple-element.11), channel_id=1, replica_groups={{0,1,2,3,4,5,6,7,8,9,10,11,12,13,14,15},{16,17,18,19,20,21,22,23,24,25,..., dimensions={0} | all-to-all | bytes 655360 | tf_op jit(solution)/shard_map/all_to_all | solution.py:289
  50.0 0.0 copy-start
  50.0 1.1 %shard_map.99 = bf16[16,16,128]{2,1,0:T(8,128)(2,1)S(1)} custom-call(bf16[16,80,128]{2,1,0:T(8,128)(2,1)S(1)} %all_to_all.22.got_ref), custom_call_target="tpu_custom_call" | custom-call | flops 17179869184 | bytes 41943040 | tf_op jit(solution)/shard_map/pallas_call | solution.py:263
  51.2 8.4 %all_to_all.23.got_ref = bf16[16,16,128]{2,1,0:T(8,128)(2,1)S(1)} all-to-all(bf16[16,16,128]{2,1,0:T(8,128)(2,1)S(1)} %shard_map.99), channel_id=1, replica_groups={{0,1,2,3,4,5,6,7,8,9,10,11,12,13,14,15},{16,17,18,19,20,21,22,23,24,25,..., dimensions={0} | all-to-all | bytes 131072 | tf_op jit(solution)/shard_map/all_to_all | solution.py:289
  59.6 0.0 copy-done
  59.6 1.3 %shard_map.100 = f32[1,32,1024]{2,1,0:T(8,128)} custom-call(bf16[16,16,128]{2,1,0:T(8,128)(2,1)S(1)} %all_to_all.23.got_ref, bf16[1024,1024]{1,0:T(8,128)(2,1)S(1)} %copy-done), custom_call_target="tpu_custom_call" | custom-call | tf_op jit(solution)/shard_map/pallas_call | solution.py:263
  (1 shorter events, 0.0 us)
Async XLA Ops:
  17.8 7.1 %collective-permute-start = (bf16[16,48,128]{2,1,0:T(8,128)(2,1)S(1)}, bf16[16,48,128]{2,1,0:T(8,128)(2,1)S(1)}, u32[]{:S(2)}, u32[]{:S(2)}) collective-permute-start(bf16[16,48,128]{2,1,0:T(8,128)(2,1)S(1)} %all_to_all.20.mine_ref), channel_id=1, source_target_pairs={{0,1},{1,0},{2,3},{3,2},{4,5},{5,4},{6,7},{7,6},{8,9},{9,8},{10,11... | collective-permute-start | bytes 589832 | tf_op jit(solution)/shard_map/ppermute | solution.py:295
  17.8 6.3 %collective-permute-start.1 = (bf16[1,32,1024]{2,1,0:T(8,128)(2,1)}, bf16[1,32,1024]{2,1,0:T(8,128)(2,1)S(1)}, u32[]{:S(2)}, u32[]{:S(2)}) collective-permute-start(bf16[1,32,1024]{2,1,0:T(8,128)(2,1)} %x2_ref.1), channel_id=1, source_target_pairs={{0,16},{1,17},{2,18},{3,19},{4,20},{5,21},{6,22},{7,23},{8,24},{9,... | collective-permute-start | bytes 196616 | tf_op jit(solution)/shard_map/ppermute | solution.py:296
  24.9 12.1 %slice-start = ((s8[6291456]{0:T(1024)(128)(4,1)}), s8[4194304]{0:T(1024)(128)(4,1)S(1)}, s32[]{:S(2)}) async-start(s8[6291456]{0:T(1024)(128)(4,1)} %bitcast.1), calls=%async_computation.4 | async-start | bytes 8388608
  24.9 12.0 %slice-start.1 = ((s8[6291456]{0:T(1024)(128)(4,1)}), s8[2097152]{0:T(1024)(128)(4,1)S(1)}, s32[]{:S(2)}) async-start(s8[6291456]{0:T(1024)(128)(4,1)} %bitcast.1), calls=%async_computation.5 | async-start | bytes 4194304
  24.9 12.0 %copy-start.1 = (bf16[1024,1024]{1,0:T(8,128)(2,1)S(1)}, bf16[1024,1024]{1,0:T(8,128)(2,1)}, u32[]{:S(2)}) copy-start(bf16[1024,1024]{1,0:T(8,128)(2,1)} %wv_ref.1) | copy-start | bytes 6291460
  24.9 12.0 %copy-start.2 = (bf16[1,32,1024]{2,1,0:T(8,128)(2,1)S(1)}, bf16[1,32,1024]{2,1,0:T(8,128)(2,1)}, u32[]{:S(2)}) copy-start(bf16[1,32,1024]{2,1,0:T(8,128)(2,1)} %x2_ref.1) | copy-start | bytes 196612
  24.9 12.0 %copy-start.3 = (f32[1024]{0:T(1024)S(1)}, f32[1024]{0:T(1024)}, u32[]{:S(2)}) copy-start(f32[1024]{0:T(1024)} %param.14) | copy-start | bytes 12292
  50.0 9.6 %copy-start = (bf16[1024,1024]{1,0:T(8,128)(2,1)S(1)}, bf16[1024,1024]{1,0:T(8,128)(2,1)}, u32[]{:S(2)}) copy-start(bf16[1024,1024]{1,0:T(8,128)(2,1)} %wout_ref.1) | copy-start | bytes 6291460

commit v16 on v13

--- a/solution.py
+++ b/solution.py
@@ -127,14 +127,18 @@
 
 
 def unpack_rows(got_ref):
-    pieces = [got_ref[h].astype(jnp.float32) for h in range(HEADS)]
+    pieces = [got_ref[h] for h in range(HEADS)]
     top = jnp.concatenate([p[:, :HD] for p in pieces], axis=-1)
     low = jnp.concatenate([p[:, HD:] for p in pieces], axis=-1)
     return jnp.concatenate([top, low], axis=0)
 
 
-def unit(x):
-    return x * lax.rsqrt(jnp.mean(x * x, axis=-1, keepdims=True) + EPSILON)
+def factor(x):
+    return lax.rsqrt(jnp.mean(x * x, axis=-1, keepdims=True) + EPSILON)
+
+
+def times(x, weight):
+    return jnp.dot(x, weight, preferred_element_type=jnp.float32)
 
 
 def pack_kernel(q_hbm, k_hbm, v_hbm, out_ref, q_ref, k_ref, v_ref, sems):
@@ -206,27 +210,28 @@
 
 
 def middle_kernel(got_ref, x2_ref, wv_ref, gain_ref, wqkv_ref, feats_hbm, out_ref, feats_ref, sem):
-    feats = unit(unpack_rows(got_ref))
-    feats_ref[0] = feats
+    rows = unpack_rows(got_ref)
+    wide = rows.astype(jnp.float32)
+    scale = factor(wide)
+    feats_ref[0] = wide * scale
     copy = pltpu.make_async_copy(feats_ref, feats_hbm, sem)
     copy.start()
-    hidden = x2_ref[0].astype(jnp.float32) + jnp.dot(
-        feats.astype(jnp.bfloat16), wv_ref[...], preferred_element_type=jnp.float32
-    )
-    normed = (unit(hidden) * gain_ref[...]).astype(jnp.bfloat16)
-    projected = jnp.dot(normed, wqkv_ref[...], preferred_element_type=jnp.float32).astype(jnp.bfloat16)
+    hidden = x2_ref[0].astype(jnp.float32) + times(rows, wv_ref[...]) * scale
+    gained = (hidden * gain_ref[...]).astype(jnp.bfloat16)
+    projected = (times(gained, wqkv_ref[...]) * factor(hidden)).astype(jnp.bfloat16)
     width = HEADS * HD
     pack_heads(out_ref, projected[:, :width], projected[:, width : 2 * width], projected[:, 2 * width :])
     copy.wait()
 
 
 def last_kernel(got_ref, wout_ref, out_hbm, out_ref, sems):
-    rows = unit(unpack_rows(got_ref)).astype(jnp.bfloat16)
+    rows = unpack_rows(got_ref)
+    scale = factor(rows.astype(jnp.float32))
     copies = []
     width = wout_ref.shape[1] // 4
     for i in range(4):
         cols = slice(i * width, (i + 1) * width)
-        out_ref[0, :, cols] = jnp.dot(rows, wout_ref[:, cols], preferred_element_type=jnp.float32)
+        out_ref[0, :, cols] = times(rows, wout_ref[:, cols]) * scale
         copies.append(pltpu.make_async_copy(out_ref.at[:, :, cols], out_hbm.at[:, :, cols], sems.at[i]))
         copies[i].start()
     for copy in copies:

time: 55.9 us -> 55.5 us (level)
  no operation moved by 1% of the time
where the time goes in v16:
time: 55.5 us; the launch traced here: 55.2 us
  blocking collectives  46 us (83%)
  Pallas kernels  7.08 us (13%)
  waiting for transfers between devices  1.35 us (2%)
  between operations  0.72 us (1%)
    all_to_all x4, blocking collectives, trade(): lax.all_to_all(piece, ALL, split_axis=0, concat_axis=0, tiled=True, axis_...  46 us
    pallas_call x7, Pallas kernels, call(): pl.pallas_call(body, out_shape=[jax.ShapeDtypeStruct(shape, dtype) for sh...  7.08 us
    ppermute x2, waiting for transfers between devices, attention(): other = lax.ppermute(mine, ALL, [(i, i ^ 1) for i in range(devices)])  1.35 us
  transfers between devices with their start and end apart: 2, of which 2 were waited for; matrix products, arithmetic and copies ran while one was open for 0% of the time, Pallas kernels for 3%

profile of v16, /device:TPU:0, one launch (start us, length us, event | category | flops | bytes accessed | tf_op | source)
XLA Modules:
  0.0 55.2 jit_solution(16373534283310967403)
XLA Ops:
  0.6 1.0 %shard_map.95 = bf16[16,48,128]{2,1,0:T(8,128)(2,1)S(1)} custom-call(bf16[1,32,1024]{2,1,0:T(8,128)(2,1)} %q_hbm.1, bf16[1,32,1024]{2,1,0:T(8,128)(2,1)} %k_hbm.1, bf16[1,32,1024]{2,1,0:T(8,128)(2,1)} %v_hbm.1), custom_call_target="tpu_custom_call" | custom-call | tf_op jit(solution)/shard_map/pallas_call | solution.py:242
  1.7 16.2 %all_to_all.20.mine_ref = bf16[16,48,128]{2,1,0:T(8,128)(2,1)S(1)} all-to-all(bf16[16,48,128]{2,1,0:T(8,128)(2,1)S(1)} %shard_map.95), channel_id=1, replica_groups={{11,12,15,16,19,20,23,24,27,28,31,0,3,4,7,8},{10,13,14,17,18,21,22,25,2..., dimensions={0} | all-to-all | bytes 393216 | tf_op jit(solution)/shard_map/all_to_all | solution.py:264
  17.8 0.0 collective-permute-start
  17.8 0.8 %shard_map.96 = (bf16[512,128]{1,0:T(8,128)(2,1)S(1)}, f32[512,128]{1,0:T(8,128)S(1)}, f32[512,128]{1,0:T(8,128)S(1)}) custom-call(bf16[16,48,128]{2,1,0:T(8,128)(2,1)S(1)} %all_to_all.20.mine_ref), custom_call_target="tpu_custom_call" | custom-call | flops 1073741824 | bytes 1048576 | tf_op jit(solution)/shard_map/pallas_call | solution.py:242
  18.6 0.7 %collective-permute-done.other_ref = bf16[16,48,128]{2,1,0:T(8,128)(2,1)S(1)} collective-permute-done((bf16[16,48,128]{2,1,0:T(8,128)(2,1)S(1)}, bf16[16,48,128]{2,1,0:T(8,128)(2,1)S(1)}, u32[]{:S(2)}, u32[]{:S(2)}) %collective-permute-start) | collective-permute-done | bytes 196640 | tf_op jit(solution)/shard_map/ppermute | solution.py:268
  19.3 0.0 slice-start
  19.3 0.0 slice-start.1
  19.3 0.0 copy-start.1
  19.3 0.0 copy-start.2
  19.3 0.0 copy-start.3
  19.3 0.8 %shard_map.97 = bf16[16,16,128]{2,1,0:T(8,128)(2,1)S(1)} custom-call(bf16[16,48,128]{2,1,0:T(8,128)(2,1)S(1)} %collective-permute-done.other_ref, bf16[512,128]{1,0:T(8,128)(2,1)S(1)} %get-tuple-element.10.query_ref, f32[512,128]{1,0:T(8,128)S(1)} %get-tuple-element.11.peak_ref, f32[512,128]{1,0:T(8,128)S(1)} %get-tuple-element.12.sum_ref), custom_call_target="tpu_custom_call" | custom-call | flops 17179869184 | bytes 41943040 | tf_op jit(solution)/shard_map/pallas_call | solution.py:242
  20.1 9.5 %all_to_all.21.got_ref = bf16[16,16,128]{2,1,0:T(8,128)(2,1)S(1)} all-to-all(bf16[16,16,128]{2,1,0:T(8,128)(2,1)S(1)} %shard_map.97), channel_id=1, replica_groups={{11,12,15,16,19,20,23,24,27,28,31,0,3,4,7,8},{10,13,14,17,18,21,22,25,2..., dimensions={0} | all-to-all | bytes 131072 | tf_op jit(solution)/shard_map/all_to_all | solution.py:264
  29.7 0.0 slice-done
  29.7 0.0 slice-done.1
  29.7 0.0 copy-done.1
  29.7 0.0 copy-done.2
  29.7 0.0 copy-done.3
  29.7 1.7 %shard_map.98 = (f32[1,32,1024]{2,1,0:T(8,128)}, bf16[16,48,128]{2,1,0:T(8,128)(2,1)S(1)}) custom-call(bf16[16,16,128]{2,1,0:T(8,128)(2,1)S(1)} %all_to_all.21.got_ref, bf16[1,32,1024]{2,1,0:T(8,128)(2,1)S(1)} %copy-done.2, bf16[1024,1024]{1,0:T(8,128)(2,1)S(1)} %copy-done.1, f32[1,1024]{1,0:T(1,128)S(1)} %bitcast.3, bf16[1024,3072]{1,0:T(8,128)(2,1)S(1)} %bitcast.2), custom_call_target="tpu_custom_call" | custom-call | tf_op jit(solution)/shard_map/pallas_call | solution.py:242
  31.4 11.1 %all_to_all.22.mine_ref = bf16[16,48,128]{2,1,0:T(8,128)(2,1)S(1)} all-to-all(bf16[16,48,128]{2,1,0:T(8,128)(2,1)S(1)} %get-tuple-element.14), channel_id=1, replica_groups={{11,12,15,16,19,20,23,24,27,28,31,0,3,4,7,8},{10,13,14,17,18,21,22,25,2..., dimensions={0} | all-to-all | bytes 393216 | tf_op jit(solution)/shard_map/all_to_all | solution.py:264
  42.5 0.0 collective-permute-start.1
  42.5 0.8 %shard_map.99 = (bf16[512,128]{1,0:T(8,128)(2,1)S(1)}, f32[512,128]{1,0:T(8,128)S(1)}, f32[512,128]{1,0:T(8,128)S(1)}) custom-call(bf16[16,48,128]{2,1,0:T(8,128)(2,1)S(1)} %all_to_all.22.mine_ref), custom_call_target="tpu_custom_call" | custom-call | flops 1073741824 | bytes 1048576 | tf_op jit(solution)/shard_map/pallas_call | solution.py:242
  43.3 0.7 %collective-permute-done.1.other_ref = bf16[16,48,128]{2,1,0:T(8,128)(2,1)S(1)} collective-permute-done((bf16[16,48,128]{2,1,0:T(8,128)(2,1)S(1)}, bf16[16,48,128]{2,1,0:T(8,128)(2,1)S(1)}, u32[]{:S(2)}, u32[]{:S(2)}) %collective-permute-start.1) | collective-permute-done | bytes 196640 | tf_op jit(solution)/shard_map/ppermute | solution.py:268
  43.9 0.0 copy-start
  43.9 0.8 %shard_map.100 = bf16[16,16,128]{2,1,0:T(8,128)(2,1)S(1)} custom-call(bf16[16,48,128]{2,1,0:T(8,128)(2,1)S(1)} %collective-permute-done.1.other_ref, bf16[512,128]{1,0:T(8,128)(2,1)S(1)} %get-tuple-element.15.query_ref, f32[512,128]{1,0:T(8,128)S(1)} %get-tuple-element.16.peak_ref, f32[512,128]{1,0:T(8,128)S(1)} %get-tuple-element.17.sum_ref), custom_call_target="tpu_custom_call" | custom-call | flops 17179869184 | bytes 41943040 | tf_op jit(solution)/shard_map/pallas_call | solution.py:242
  44.8 9.3 %all_to_all.23.got_ref = bf16[16,16,128]{2,1,0:T(8,128)(2,1)S(1)} all-to-all(bf16[16,16,128]{2,1,0:T(8,128)(2,1)S(1)} %shard_map.100), channel_id=1, replica_groups={{11,12,15,16,19,20,23,24,27,28,31,0,3,4,7,8},{10,13,14,17,18,21,22,25,2..., dimensions={0} | all-to-all | bytes 131072 | tf_op jit(solution)/shard_map/all_to_all | solution.py:264
  54.0 0.0 copy-done
  54.0 1.2 %shard_map.101 = f32[1,32,1024]{2,1,0:T(8,128)} custom-call(bf16[16,16,128]{2,1,0:T(8,128)(2,1)S(1)} %all_to_all.23.got_ref, bf16[1024,1024]{1,0:T(8,128)(2,1)S(1)} %copy-done), custom_call_target="tpu_custom_call" | custom-call | tf_op jit(solution)/shard_map/pallas_call | solution.py:242
  (1 shorter events, 0.0 us)
Async XLA Ops:
  17.8 1.4 %collective-permute-start = (bf16[16,48,128]{2,1,0:T(8,128)(2,1)S(1)}, bf16[16,48,128]{2,1,0:T(8,128)(2,1)S(1)}, u32[]{:S(2)}, u32[]{:S(2)}) collective-permute-start(bf16[16,48,128]{2,1,0:T(8,128)(2,1)S(1)} %all_to_all.20.mine_ref), channel_id=1, source_target_pairs={{0,1},{1,0},{2,3},{3,2},{4,5},{5,4},{6,7},{7,6},{8,9},{9,8},{10,11... | collective-permute-start | bytes 589832 | tf_op jit(solution)/shard_map/ppermute | solution.py:268
  19.3 10.4 %slice-start = ((s8[6291456]{0:T(1024)(128)(4,1)}), s8[4194304]{0:T(1024)(128)(4,1)S(1)}, s32[]{:S(2)}) async-start(s8[6291456]{0:T(1024)(128)(4,1)} %bitcast.1), calls=%async_computation.4 | async-start | bytes 8388608
  19.3 10.4 %slice-start.1 = ((s8[6291456]{0:T(1024)(128)(4,1)}), s8[2097152]{0:T(1024)(128)(4,1)S(1)}, s32[]{:S(2)}) async-start(s8[6291456]{0:T(1024)(128)(4,1)} %bitcast.1), calls=%async_computation.5 | async-start | bytes 4194304
  19.3 10.4 %copy-start.1 = (bf16[1024,1024]{1,0:T(8,128)(2,1)S(1)}, bf16[1024,1024]{1,0:T(8,128)(2,1)}, u32[]{:S(2)}) copy-start(bf16[1024,1024]{1,0:T(8,128)(2,1)} %wv_ref.1) | copy-start | bytes 6291460
  19.3 10.4 %copy-start.2 = (bf16[1,32,1024]{2,1,0:T(8,128)(2,1)S(1)}, bf16[1,32,1024]{2,1,0:T(8,128)(2,1)}, u32[]{:S(2)}) copy-start(bf16[1,32,1024]{2,1,0:T(8,128)(2,1)} %x2_ref.1) | copy-start | bytes 196612
  19.3 10.4 %copy-start.3 = (f32[1024]{0:T(1024)S(1)}, f32[1024]{0:T(1024)}, u32[]{:S(2)}) copy-start(f32[1024]{0:T(1024)} %param.14) | copy-start | bytes 12292
  42.5 1.4 %collective-permute-start.1 = (bf16[16,48,128]{2,1,0:T(8,128)(2,1)S(1)}, bf16[16,48,128]{2,1,0:T(8,128)(2,1)S(1)}, u32[]{:S(2)}, u32[]{:S(2)}) collective-permute-start(bf16[16,48,128]{2,1,0:T(8,128)(2,1)S(1)} %all_to_all.22.mine_ref), channel_id=1, source_target_pairs={{0,1},{1,0},{2,3},{3,2},{4,5},{5,4},{6,7},{7,6},{8,9},{9,8},{10,11... | collective-permute-start | bytes 589832 | tf_op jit(solution)/shard_map/ppermute | solution.py:268
  43.9 10.1 %copy-start = (bf16[1024,1024]{1,0:T(8,128)(2,1)S(1)}, bf16[1024,1024]{1,0:T(8,128)(2,1)}, u32[]{:S(2)}) copy-start(bf16[1024,1024]{1,0:T(8,128)(2,1)} %wout_ref.1) | copy-start | bytes 6291460

commit v17 on v16

--- a/solution.py
+++ b/solution.py
@@ -108,12 +108,11 @@
 
 ALL = ("view", "tok")
 CORES = 2
-FIRST = HEADS // 4 + 1
 SHARP = HD ** (-0.5) * 1.4426950408889634
 
 
-def trade_groups():
-    chips = [(FIRST + i) % HEADS for i in range(HEADS)]
+def trade_groups(first, step):
+    chips = [(first + i * step) % HEADS for i in range(HEADS)]
     return [[chip * CORES + (chip + s) % CORES for chip in chips] for s in range(CORES)]
 
 
@@ -258,18 +257,17 @@
     lines = ((HEADS * rows, 2 * HD), jnp.float32, pltpu.VMEM)
     wide = (1, rows, HEADS * HD)
     devices = HEADS * CORES
-    groups = trade_groups()
-
-    def trade(piece):
+
+    def trade(piece, groups):
         return lax.all_to_all(piece, ALL, split_axis=0, concat_axis=0, tiled=True, axis_index_groups=groups)
 
-    def attention(packed):
-        mine = trade(packed)
+    def attention(packed, groups):
+        mine = trade(packed, groups)
         other = lax.ppermute(mine, ALL, [(i, i ^ 1) for i in range(devices)])
         begun = call(begin_kernel, [queries, lines, lines], (mine,), cost=pl.CostEstimate(1 << 30, 0, 1 << 20))
         cost = pl.CostEstimate(flops=16 << 30, bytes_accessed=40 << 20, transcendentals=0)
         (half,) = call(finish_kernel, [halves], (other, *begun), cost=cost)
-        return trade(half)
+        return trade(half, groups)
 
     inputs = [pltpu.with_memory_space_constraint(x, pltpu.HBM) for x in (q1, k1, v1)]
     scratch = [pltpu.VMEM(q1.shape, q1.dtype)] * 3 + [pltpu.SemaphoreType.DMA((3, 2))]
@@ -277,13 +275,13 @@
     feats, piece = call(
         middle_kernel,
         [(wide, jnp.float32, pltpu.HBM), packed],
-        (attention(piece), x2, w_view_out, norm_gain[None], w_qkv),
+        (attention(piece, trade_groups(HEADS * 3 // 4 + 1, 1)), x2, w_view_out, norm_gain[None], w_qkv),
         [pltpu.VMEM(wide, jnp.float32), pltpu.SemaphoreType.DMA],
     )
     (result,) = call(
         last_kernel,
         [(wide, jnp.float32, pltpu.HBM)],
-        (attention(piece), w_out),
+        (attention(piece, trade_groups(HEADS // 4 + 1, -1)), w_out),
         [pltpu.VMEM(wide, jnp.float32), pltpu.SemaphoreType.DMA((4,))],
     )
     return feats, result

time: 55.5 us -> 56.2 us (1.013)
  starting transfers between devices: 0.01 us -> 0.87 us
    ppermute x2, starting transfers between devices: 0.01 us -> 0.87 us  [attention(): other = lax.ppermute(mine, ALL, [(i, i ^ 1) for i in range(devices)])]
where the time goes in v17:
time: 56.2 us; the launch traced here: 55.9 us
  blocking collectives  46.3 us (82%)
  Pallas kernels  7.08 us (13%)
  waiting for transfers between devices  0.89 us (2%)
  starting transfers between devices  0.87 us (2%)
  between operations  0.72 us (1%)
    all_to_all x4, blocking collectives, trade(): lax.all_to_all(piece, ALL, split_axis=0, concat_axis=0, tiled=True, axis_...  46.3 us
    pallas_call x7, Pallas kernels, call(): pl.pallas_call(body, out_shape=[jax.ShapeDtypeStruct(shape, dtype) for sh...  7.08 us
  transfers between devices with their start and end apart: 2, of which 2 were waited for; matrix products, arithmetic and copies ran while one was open for 0% of the time, Pallas kernels for 3%

profile of v17, /device:TPU:0, one launch (start us, length us, event | category | flops | bytes accessed | tf_op | source)
XLA Modules:
  0.0 55.9 jit_solution(10742159909534810582)
XLA Ops:
  0.6 1.0 %shard_map.95 = bf16[16,48,128]{2,1,0:T(8,128)(2,1)S(1)} custom-call(bf16[1,32,1024]{2,1,0:T(8,128)(2,1)} %q_hbm.1, bf16[1,32,1024]{2,1,0:T(8,128)(2,1)} %k_hbm.1, bf16[1,32,1024]{2,1,0:T(8,128)(2,1)} %v_hbm.1), custom_call_target="tpu_custom_call" | custom-call | tf_op jit(solution)/shard_map/pallas_call | solution.py:241
  1.7 14.4 %all_to_all.20.mine_ref = bf16[16,48,128]{2,1,0:T(8,128)(2,1)S(1)} all-to-all(bf16[16,48,128]{2,1,0:T(8,128)(2,1)S(1)} %shard_map.95), channel_id=1, replica_groups={{27,28,31,0,3,4,7,8,11,12,15,16,19,20,23,24},{26,29,30,1,2,5,6,9,10,13,..., dimensions={0} | all-to-all | bytes 393216 | tf_op jit(solution)/shard_map/all_to_all | solution.py:262
  16.0 0.1 collective-permute-start
  16.1 0.8 %shard_map.96 = (bf16[512,128]{1,0:T(8,128)(2,1)S(1)}, f32[512,128]{1,0:T(8,128)S(1)}, f32[512,128]{1,0:T(8,128)S(1)}) custom-call(bf16[16,48,128]{2,1,0:T(8,128)(2,1)S(1)} %all_to_all.20.mine_ref), custom_call_target="tpu_custom_call" | custom-call | flops 1073741824 | bytes 1048576 | tf_op jit(solution)/shard_map/pallas_call | solution.py:241
  16.9 0.6 %collective-permute-done.other_ref = bf16[16,48,128]{2,1,0:T(8,128)(2,1)S(1)} collective-permute-done((bf16[16,48,128]{2,1,0:T(8,128)(2,1)S(1)}, bf16[16,48,128]{2,1,0:T(8,128)(2,1)S(1)}, u32[]{:S(2)}, u32[]{:S(2)}) %collective-permute-start) | collective-permute-done | bytes 196640 | tf_op jit(solution)/shard_map/ppermute | solution.py:266
  17.5 0.0 slice-start
  17.5 0.0 slice-start.1
  17.5 0.0 copy-start.1
  17.5 0.0 copy-start.2
  17.5 0.0 copy-start.3
  17.5 0.8 %shard_map.97 = bf16[16,16,128]{2,1,0:T(8,128)(2,1)S(1)} custom-call(bf16[16,48,128]{2,1,0:T(8,128)(2,1)S(1)} %collective-permute-done.other_ref, bf16[512,128]{1,0:T(8,128)(2,1)S(1)} %get-tuple-element.10.query_ref, f32[512,128]{1,0:T(8,128)S(1)} %get-tuple-element.11.peak_ref, f32[512,128]{1,0:T(8,128)S(1)} %get-tuple-element.12.sum_ref), custom_call_target="tpu_custom_call" | custom-call | flops 17179869184 | bytes 41943040 | tf_op jit(solution)/shard_map/pallas_call | solution.py:241
  18.4 10.2 %all_to_all.21.got_ref = bf16[16,16,128]{2,1,0:T(8,128)(2,1)S(1)} all-to-all(bf16[16,16,128]{2,1,0:T(8,128)(2,1)S(1)} %shard_map.97), channel_id=1, replica_groups={{27,28,31,0,3,4,7,8,11,12,15,16,19,20,23,24},{26,29,30,1,2,5,6,9,10,13,..., dimensions={0} | all-to-all | bytes 131072 | tf_op jit(solution)/shard_map/all_to_all | solution.py:262
  28.6 0.0 slice-done
  28.6 0.0 slice-done.1
  28.6 0.0 copy-done.1
  28.6 0.0 copy-done.2
  28.6 0.0 copy-done.3
  28.6 1.7 %shard_map.98 = (f32[1,32,1024]{2,1,0:T(8,128)}, bf16[16,48,128]{2,1,0:T(8,128)(2,1)S(1)}) custom-call(bf16[16,16,128]{2,1,0:T(8,128)(2,1)S(1)} %all_to_all.21.got_ref, bf16[1,32,1024]{2,1,0:T(8,128)(2,1)S(1)} %copy-done.2, bf16[1024,1024]{1,0:T(8,128)(2,1)S(1)} %copy-done.1, f32[1,1024]{1,0:T(1,128)S(1)} %bitcast.3, bf16[1024,3072]{1,0:T(8,128)(2,1)S(1)} %bitcast.2), custom_call_target="tpu_custom_call" | custom-call | tf_op jit(solution)/shard_map/pallas_call | solution.py:241
  30.3 12.1 %all_to_all.22.mine_ref = bf16[16,48,128]{2,1,0:T(8,128)(2,1)S(1)} all-to-all(bf16[16,48,128]{2,1,0:T(8,128)(2,1)S(1)} %get-tuple-element.14), channel_id=1, replica_groups={{11,8,7,4,3,0,31,28,27,24,23,20,19,16,15,12},{10,9,6,5,2,1,30,29,26,25,..., dimensions={0} | all-to-all | bytes 393216 | tf_op jit(solution)/shard_map/all_to_all | solution.py:262
  42.4 0.8 %collective-permute-start.1 = (bf16[16,48,128]{2,1,0:T(8,128)(2,1)S(1)}, bf16[16,48,128]{2,1,0:T(8,128)(2,1)S(1)}, u32[]{:S(2)}, u32[]{:S(2)}) collective-permute-start(bf16[16,48,128]{2,1,0:T(8,128)(2,1)S(1)} %all_to_all.22.mine_ref), channel_id=1, source_target_pairs={{0,1},{1,0},{2,3},{3,2},{4,5},{5,4},{6,7},{7,6},{8,9},{9,8},{10,11... | collective-permute-start | bytes 589832 | tf_op jit(solution)/shard_map/ppermute | solution.py:266
  43.2 0.8 %shard_map.99 = (bf16[512,128]{1,0:T(8,128)(2,1)S(1)}, f32[512,128]{1,0:T(8,128)S(1)}, f32[512,128]{1,0:T(8,128)S(1)}) custom-call(bf16[16,48,128]{2,1,0:T(8,128)(2,1)S(1)} %all_to_all.22.mine_ref), custom_call_target="tpu_custom_call" | custom-call | flops 1073741824 | bytes 1048576 | tf_op jit(solution)/shard_map/pallas_call | solution.py:241
  43.9 0.3 collective-permute-done.1.other_ref
  44.2 0.0 copy-start
  44.2 0.8 %shard_map.100 = bf16[16,16,128]{2,1,0:T(8,128)(2,1)S(1)} custom-call(bf16[16,48,128]{2,1,0:T(8,128)(2,1)S(1)} %collective-permute-done.1.other_ref, bf16[512,128]{1,0:T(8,128)(2,1)S(1)} %get-tuple-element.15.query_ref, f32[512,128]{1,0:T(8,128)S(1)} %get-tuple-element.16.peak_ref, f32[512,128]{1,0:T(8,128)S(1)} %get-tuple-element.17.sum_ref), custom_call_target="tpu_custom_call" | custom-call | flops 17179869184 | bytes 41943040 | tf_op jit(solution)/shard_map/pallas_call | solution.py:241
  45.1 9.7 %all_to_all.23.got_ref = bf16[16,16,128]{2,1,0:T(8,128)(2,1)S(1)} all-to-all(bf16[16,16,128]{2,1,0:T(8,128)(2,1)S(1)} %shard_map.100), channel_id=1, replica_groups={{11,8,7,4,3,0,31,28,27,24,23,20,19,16,15,12},{10,9,6,5,2,1,30,29,26,25,..., dimensions={0} | all-to-all | bytes 131072 | tf_op jit(solution)/shard_map/all_to_all | solution.py:262
  54.7 0.0 copy-done
  54.7 1.2 %shard_map.101 = f32[1,32,1024]{2,1,0:T(8,128)} custom-call(bf16[16,16,128]{2,1,0:T(8,128)(2,1)S(1)} %all_to_all.23.got_ref, bf16[1024,1024]{1,0:T(8,128)(2,1)S(1)} %copy-done), custom_call_target="tpu_custom_call" | custom-call | tf_op jit(solution)/shard_map/pallas_call | solution.py:241
  (1 shorter events, 0.0 us)
Async XLA Ops:
  16.0 1.4 %collective-permute-start = (bf16[16,48,128]{2,1,0:T(8,128)(2,1)S(1)}, bf16[16,48,128]{2,1,0:T(8,128)(2,1)S(1)}, u32[]{:S(2)}, u32[]{:S(2)}) collective-permute-start(bf16[16,48,128]{2,1,0:T(8,128)(2,1)S(1)} %all_to_all.20.mine_ref), channel_id=1, source_target_pairs={{0,1},{1,0},{2,3},{3,2},{4,5},{5,4},{6,7},{7,6},{8,9},{9,8},{10,11... | collective-permute-start | bytes 589832 | tf_op jit(solution)/shard_map/ppermute | solution.py:266
  17.5 11.1 %slice-start = ((s8[6291456]{0:T(1024)(128)(4,1)}), s8[4194304]{0:T(1024)(128)(4,1)S(1)}, s32[]{:S(2)}) async-start(s8[6291456]{0:T(1024)(128)(4,1)} %bitcast.1), calls=%async_computation.4 | async-start | bytes 8388608
  17.5 11.1 %slice-start.1 = ((s8[6291456]{0:T(1024)(128)(4,1)}), s8[2097152]{0:T(1024)(128)(4,1)S(1)}, s32[]{:S(2)}) async-start(s8[6291456]{0:T(1024)(128)(4,1)} %bitcast.1), calls=%async_computation.5 | async-start | bytes 4194304
  17.5 11.1 %copy-start.1 = (bf16[1024,1024]{1,0:T(8,128)(2,1)S(1)}, bf16[1024,1024]{1,0:T(8,128)(2,1)}, u32[]{:S(2)}) copy-start(bf16[1024,1024]{1,0:T(8,128)(2,1)} %wv_ref.1) | copy-start | bytes 6291460
  17.5 11.1 %copy-start.2 = (bf16[1,32,1024]{2,1,0:T(8,128)(2,1)S(1)}, bf16[1,32,1024]{2,1,0:T(8,128)(2,1)}, u32[]{:S(2)}) copy-start(bf16[1,32,1024]{2,1,0:T(8,128)(2,1)} %x2_ref.1) | copy-start | bytes 196612
  17.5 11.1 %copy-start.3 = (f32[1024]{0:T(1024)S(1)}, f32[1024]{0:T(1024)}, u32[]{:S(2)}) copy-start(f32[1024]{0:T(1024)} %param.14) | copy-start | bytes 12292
  42.4 1.8 %collective-permute-start.1 = (bf16[16,48,128]{2,1,0:T(8,128)(2,1)S(1)}, bf16[16,48,128]{2,1,0:T(8,128)(2,1)S(1)}, u32[]{:S(2)}, u32[]{:S(2)}) collective-permute-start(bf16[16,48,128]{2,1,0:T(8,128)(2,1)S(1)} %all_to_all.22.mine_ref), channel_id=1, source_target_pairs={{0,1},{1,0},{2,3},{3,2},{4,5},{5,4},{6,7},{7,6},{8,9},{9,8},{10,11... | collective-permute-start | bytes 589832 | tf_op jit(solution)/shard_map/ppermute | solution.py:266
  44.2 10.5 %copy-start = (bf16[1024,1024]{1,0:T(8,128)(2,1)S(1)}, bf16[1024,1024]{1,0:T(8,128)(2,1)}, u32[]{:S(2)}) copy-start(bf16[1024,1024]{1,0:T(8,128)(2,1)} %wout_ref.1) | copy-start | bytes 6291460

commit v18 on v17

--- a/solution.py
+++ b/solution.py
@@ -1,3 +1,5 @@
+import functools
+
 import jax
 import jax.numpy as jnp
 from jax import lax
@@ -108,11 +110,12 @@
 
 ALL = ("view", "tok")
 CORES = 2
+MIDDLE, LATE = HEADS // 4 + 1, HEADS - 1
 SHARP = HD ** (-0.5) * 1.4426950408889634
 
 
-def trade_groups(first, step):
-    chips = [(first + i * step) % HEADS for i in range(HEADS)]
+def trade_groups(first):
+    chips = [(first + i) % HEADS for i in range(HEADS)]
     return [[chip * CORES + (chip + s) % CORES for chip in chips] for s in range(CORES)]
 
 
@@ -125,8 +128,8 @@
         out_ref[h, rows : rows + half, :] = jnp.concatenate([q[:half, cols], q[half:, cols]], axis=-1)
 
 
-def unpack_rows(got_ref):
-    pieces = [got_ref[h] for h in range(HEADS)]
+def unpack_rows(got_ref, turn=0):
+    pieces = [got_ref[(h + turn) % HEADS] for h in range(HEADS)]
     top = jnp.concatenate([p[:, :HD] for p in pieces], axis=-1)
     low = jnp.concatenate([p[:, HD:] for p in pieces], axis=-1)
     return jnp.concatenate([top, low], axis=0)
@@ -191,7 +194,7 @@
         sum_ref[at, :] = weigh(scores, peak, vals)
 
 
-def finish_kernel(other_ref, query_ref, peak_ref, sum_ref, out_ref):
+def finish_kernel(turn, other_ref, query_ref, peak_ref, sum_ref, out_ref):
     keys, vals = key_values(other_ref)
     n = query_ref.shape[0] // 2
     sums = []
@@ -205,11 +208,14 @@
     top, low = sums
     left = lower_half(top.shape)
     attn = jnp.where(left, pltpu.roll(top, HD, 1), low) / jnp.where(left, top, pltpu.roll(low, HD, 1))
-    out_ref[...] = attn.astype(jnp.bfloat16).reshape(out_ref.shape)
-
-
-def middle_kernel(got_ref, x2_ref, wv_ref, gain_ref, wqkv_ref, feats_hbm, out_ref, feats_ref, sem):
-    rows = unpack_rows(got_ref)
+    attn = attn.astype(jnp.bfloat16).reshape(out_ref.shape)
+    out_ref[turn:] = attn[: HEADS - turn]
+    if turn:
+        out_ref[:turn] = attn[HEADS - turn :]
+
+
+def middle_kernel(turn, got_ref, x2_ref, wv_ref, gain_ref, wqkv_ref, feats_hbm, out_ref, feats_ref, sem):
+    rows = unpack_rows(got_ref, turn)
     wide = rows.astype(jnp.float32)
     scale = factor(wide)
     feats_ref[0] = wide * scale
@@ -257,31 +263,33 @@
     lines = ((HEADS * rows, 2 * HD), jnp.float32, pltpu.VMEM)
     wide = (1, rows, HEADS * HD)
     devices = HEADS * CORES
+    middle = trade_groups(MIDDLE)
+    turn = (LATE - MIDDLE) % HEADS
 
     def trade(piece, groups):
         return lax.all_to_all(piece, ALL, split_axis=0, concat_axis=0, tiled=True, axis_index_groups=groups)
 
-    def attention(packed, groups):
+    def attention(packed, groups, turn):
         mine = trade(packed, groups)
         other = lax.ppermute(mine, ALL, [(i, i ^ 1) for i in range(devices)])
         begun = call(begin_kernel, [queries, lines, lines], (mine,), cost=pl.CostEstimate(1 << 30, 0, 1 << 20))
         cost = pl.CostEstimate(flops=16 << 30, bytes_accessed=40 << 20, transcendentals=0)
-        (half,) = call(finish_kernel, [halves], (other, *begun), cost=cost)
-        return trade(half, groups)
+        (half,) = call(functools.partial(finish_kernel, turn), [halves], (other, *begun), cost=cost)
+        return trade(half, middle)
 
     inputs = [pltpu.with_memory_space_constraint(x, pltpu.HBM) for x in (q1, k1, v1)]
     scratch = [pltpu.VMEM(q1.shape, q1.dtype)] * 3 + [pltpu.SemaphoreType.DMA((3, 2))]
     (piece,) = call(pack_kernel, [packed], inputs, scratch, space=pltpu.HBM, limit=48 << 20)
     feats, piece = call(
-        middle_kernel,
+        functools.partial(middle_kernel, turn),
         [(wide, jnp.float32, pltpu.HBM), packed],
-        (attention(piece, trade_groups(HEADS * 3 // 4 + 1, 1)), x2, w_view_out, norm_gain[None], w_qkv),
+        (attention(piece, trade_groups(LATE), turn), x2, w_view_out, norm_gain[None], w_qkv),
         [pltpu.VMEM(wide, jnp.float32), pltpu.SemaphoreType.DMA],
     )
     (result,) = call(
         last_kernel,
         [(wide, jnp.float32, pltpu.HBM)],
-        (attention(piece, trade_groups(HEADS // 4 + 1, -1)), w_out),
+        (attention(piece, middle, 0), w_out),
         [pltpu.VMEM(wide, jnp.float32), pltpu.SemaphoreType.DMA((4,))],
     )
     return feats, result

time: 56.2 us -> 57.2 us (1.018)
  blocking collectives: 46.3 us -> 47.7 us
  starting transfers between devices: 0.87 us -> 0.01 us
    all_to_all x4, blocking collectives: 46.3 us -> 47.7 us  [trade(): lax.all_to_all(piece, ALL, split_axis=0, concat_axis=0, tiled=True, axis_...]
    ppermute x2, starting transfers between devices: 0.87 us -> 0.01 us  [attention(): other = lax.ppermute(mine, ALL, [(i, i ^ 1) for i in range(devices)])]
where the time goes in v18:
time: 57.2 us; the launch traced here: 56.9 us
  blocking collectives  47.7 us (83%)
  Pallas kernels  7.07 us (12%)
  waiting for transfers between devices  1.36 us (2%)
  between operations  0.72 us (1%)
    all_to_all x4, blocking collectives, trade(): lax.all_to_all(piece, ALL, split_axis=0, concat_axis=0, tiled=True, axis_...  47.7 us
    pallas_call x7, Pallas kernels, call(): pl.pallas_call(body, out_shape=[jax.ShapeDtypeStruct(shape, dtype) for sh...  7.07 us
    ppermute x2, waiting for transfers between devices, attention(): other = lax.ppermute(mine, ALL, [(i, i ^ 1) for i in range(devices)])  1.36 us
  transfers between devices with their start and end apart: 2, of which 2 were waited for; matrix products, arithmetic and copies ran while one was open for 0% of the time, Pallas kernels for 3%

profile of v18, /device:TPU:0, one launch (start us, length us, event | category | flops | bytes accessed | tf_op | source)
XLA Modules:
  0.0 56.9 jit_solution(14067303022991087999)
XLA Ops:
  0.6 1.0 %shard_map.95 = bf16[16,48,128]{2,1,0:T(8,128)(2,1)S(1)} custom-call(bf16[1,32,1024]{2,1,0:T(8,128)(2,1)} %q_hbm.1, bf16[1,32,1024]{2,1,0:T(8,128)(2,1)} %k_hbm.1, bf16[1,32,1024]{2,1,0:T(8,128)(2,1)} %v_hbm.1), custom_call_target="tpu_custom_call" | custom-call | tf_op jit(solution)/shard_map/pallas_call | solution.py:247
  1.7 14.4 %all_to_all.20.mine_ref = bf16[16,48,128]{2,1,0:T(8,128)(2,1)S(1)} all-to-all(bf16[16,48,128]{2,1,0:T(8,128)(2,1)S(1)} %shard_map.95), channel_id=1, replica_groups={{31,0,3,4,7,8,11,12,15,16,19,20,23,24,27,28},{30,1,2,5,6,9,10,13,14,17,..., dimensions={0} | all-to-all | bytes 393216 | tf_op jit(solution)/shard_map/all_to_all | solution.py:270
  16.1 0.0 collective-permute-start
  16.1 0.8 %shard_map.96 = (bf16[512,128]{1,0:T(8,128)(2,1)S(1)}, f32[512,128]{1,0:T(8,128)S(1)}, f32[512,128]{1,0:T(8,128)S(1)}) custom-call(bf16[16,48,128]{2,1,0:T(8,128)(2,1)S(1)} %all_to_all.20.mine_ref), custom_call_target="tpu_custom_call" | custom-call | flops 1073741824 | bytes 1048576 | tf_op jit(solution)/shard_map/pallas_call | solution.py:247
  16.8 0.7 %collective-permute-done.other_ref = bf16[16,48,128]{2,1,0:T(8,128)(2,1)S(1)} collective-permute-done((bf16[16,48,128]{2,1,0:T(8,128)(2,1)S(1)}, bf16[16,48,128]{2,1,0:T(8,128)(2,1)S(1)}, u32[]{:S(2)}, u32[]{:S(2)}) %collective-permute-start) | collective-permute-done | bytes 196640 | tf_op jit(solution)/shard_map/ppermute | solution.py:274
  17.5 0.0 slice-start
  17.5 0.0 slice-start.1
  17.5 0.0 copy-start.1
  17.5 0.0 copy-start.2
  17.5 0.0 copy-start.3
  17.5 0.8 %shard_map.97 = bf16[16,16,128]{2,1,0:T(8,128)(2,1)S(1)} custom-call(bf16[16,48,128]{2,1,0:T(8,128)(2,1)S(1)} %collective-permute-done.other_ref, bf16[512,128]{1,0:T(8,128)(2,1)S(1)} %get-tuple-element.10.query_ref, f32[512,128]{1,0:T(8,128)S(1)} %get-tuple-element.11.peak_ref, f32[512,128]{1,0:T(8,128)S(1)} %get-tuple-element.12.sum_ref), custom_call_target="tpu_custom_call" | custom-call | flops 17179869184 | bytes 41943040 | tf_op jit(solution)/shard_map/pallas_call | solution.py:247
  18.4 12.4 %all_to_all.21.got_ref = bf16[16,16,128]{2,1,0:T(8,128)(2,1)S(1)} all-to-all(bf16[16,16,128]{2,1,0:T(8,128)(2,1)S(1)} %shard_map.97), channel_id=1, replica_groups={{11,12,15,16,19,20,23,24,27,28,31,0,3,4,7,8},{10,13,14,17,18,21,22,25,2..., dimensions={0} | all-to-all | bytes 131072 | tf_op jit(solution)/shard_map/all_to_all | solution.py:270
  30.8 0.0 slice-done
  30.8 0.0 slice-done.1
  30.8 0.0 copy-done.1
  30.8 0.0 copy-done.2
  30.8 0.0 copy-done.3
  30.9 1.7 %shard_map.98 = (f32[1,32,1024]{2,1,0:T(8,128)}, bf16[16,48,128]{2,1,0:T(8,128)(2,1)S(1)}) custom-call(bf16[16,16,128]{2,1,0:T(8,128)(2,1)S(1)} %all_to_all.21.got_ref, bf16[1,32,1024]{2,1,0:T(8,128)(2,1)S(1)} %copy-done.2, bf16[1024,1024]{1,0:T(8,128)(2,1)S(1)} %copy-done.1, f32[1,1024]{1,0:T(1,128)S(1)} %bitcast.3, bf16[1024,3072]{1,0:T(8,128)(2,1)S(1)} %bitcast.2), custom_call_target="tpu_custom_call" | custom-call | tf_op jit(solution)/shard_map/pallas_call | solution.py:247
  32.6 11.6 %all_to_all.22.mine_ref = bf16[16,48,128]{2,1,0:T(8,128)(2,1)S(1)} all-to-all(bf16[16,48,128]{2,1,0:T(8,128)(2,1)S(1)} %get-tuple-element.14), channel_id=1, replica_groups={{11,12,15,16,19,20,23,24,27,28,31,0,3,4,7,8},{10,13,14,17,18,21,22,25,2..., dimensions={0} | all-to-all | bytes 393216 | tf_op jit(solution)/shard_map/all_to_all | solution.py:270
  44.1 0.0 collective-permute-start.1
  44.1 0.8 %shard_map.99 = (bf16[512,128]{1,0:T(8,128)(2,1)S(1)}, f32[512,128]{1,0:T(8,128)S(1)}, f32[512,128]{1,0:T(8,128)S(1)}) custom-call(bf16[16,48,128]{2,1,0:T(8,128)(2,1)S(1)} %all_to_all.22.mine_ref), custom_call_target="tpu_custom_call" | custom-call | flops 1073741824 | bytes 1048576 | tf_op jit(solution)/shard_map/pallas_call | solution.py:247
  44.9 0.7 %collective-permute-done.1.other_ref = bf16[16,48,128]{2,1,0:T(8,128)(2,1)S(1)} collective-permute-done((bf16[16,48,128]{2,1,0:T(8,128)(2,1)S(1)}, bf16[16,48,128]{2,1,0:T(8,128)(2,1)S(1)}, u32[]{:S(2)}, u32[]{:S(2)}) %collective-permute-start.1) | collective-permute-done | bytes 196640 | tf_op jit(solution)/shard_map/ppermute | solution.py:274
  45.6 0.0 copy-start
  45.6 0.8 %shard_map.100 = bf16[16,16,128]{2,1,0:T(8,128)(2,1)S(1)} custom-call(bf16[16,48,128]{2,1,0:T(8,128)(2,1)S(1)} %collective-permute-done.1.other_ref, bf16[512,128]{1,0:T(8,128)(2,1)S(1)} %get-tuple-element.15.query_ref, f32[512,128]{1,0:T(8,128)S(1)} %get-tuple-element.16.peak_ref, f32[512,128]{1,0:T(8,128)S(1)} %get-tuple-element.17.sum_ref), custom_call_target="tpu_custom_call" | custom-call | flops 17179869184 | bytes 41943040 | tf_op jit(solution)/shard_map/pallas_call | solution.py:247
  46.4 9.3 %all_to_all.23.got_ref = bf16[16,16,128]{2,1,0:T(8,128)(2,1)S(1)} all-to-all(bf16[16,16,128]{2,1,0:T(8,128)(2,1)S(1)} %shard_map.100), channel_id=1, replica_groups={{11,12,15,16,19,20,23,24,27,28,31,0,3,4,7,8},{10,13,14,17,18,21,22,25,2..., dimensions={0} | all-to-all | bytes 131072 | tf_op jit(solution)/shard_map/all_to_all | solution.py:270
  55.7 0.0 copy-done
  55.7 1.2 %shard_map.101 = f32[1,32,1024]{2,1,0:T(8,128)} custom-call(bf16[16,16,128]{2,1,0:T(8,128)(2,1)S(1)} %all_to_all.23.got_ref, bf16[1024,1024]{1,0:T(8,128)(2,1)S(1)} %copy-done), custom_call_target="tpu_custom_call" | custom-call | tf_op jit(solution)/shard_map/pallas_call | solution.py:247
  (1 shorter events, 0.0 us)
Async XLA Ops:
  16.1 1.4 %collective-permute-start = (bf16[16,48,128]{2,1,0:T(8,128)(2,1)S(1)}, bf16[16,48,128]{2,1,0:T(8,128)(2,1)S(1)}, u32[]{:S(2)}, u32[]{:S(2)}) collective-permute-start(bf16[16,48,128]{2,1,0:T(8,128)(2,1)S(1)} %all_to_all.20.mine_ref), channel_id=1, source_target_pairs={{0,1},{1,0},{2,3},{3,2},{4,5},{5,4},{6,7},{7,6},{8,9},{9,8},{10,11... | collective-permute-start | bytes 589832 | tf_op jit(solution)/shard_map/ppermute | solution.py:274
  17.5 13.3 %slice-start = ((s8[6291456]{0:T(1024)(128)(4,1)}), s8[4194304]{0:T(1024)(128)(4,1)S(1)}, s32[]{:S(2)}) async-start(s8[6291456]{0:T(1024)(128)(4,1)} %bitcast.1), calls=%async_computation.4 | async-start | bytes 8388608
  17.5 13.3 %slice-start.1 = ((s8[6291456]{0:T(1024)(128)(4,1)}), s8[2097152]{0:T(1024)(128)(4,1)S(1)}, s32[]{:S(2)}) async-start(s8[6291456]{0:T(1024)(128)(4,1)} %bitcast.1), calls=%async_computation.5 | async-start | bytes 4194304
  17.5 13.3 %copy-start.1 = (bf16[1024,1024]{1,0:T(8,128)(2,1)S(1)}, bf16[1024,1024]{1,0:T(8,128)(2,1)}, u32[]{:S(2)}) copy-start(bf16[1024,1024]{1,0:T(8,128)(2,1)} %wv_ref.1) | copy-start | bytes 6291460
  17.5 13.3 %copy-start.2 = (bf16[1,32,1024]{2,1,0:T(8,128)(2,1)S(1)}, bf16[1,32,1024]{2,1,0:T(8,128)(2,1)}, u32[]{:S(2)}) copy-start(bf16[1,32,1024]{2,1,0:T(8,128)(2,1)} %x2_ref.1) | copy-start | bytes 196612
  17.5 13.3 %copy-start.3 = (f32[1024]{0:T(1024)S(1)}, f32[1024]{0:T(1024)}, u32[]{:S(2)}) copy-start(f32[1024]{0:T(1024)} %param.14) | copy-start | bytes 12292
  44.1 1.4 %collective-permute-start.1 = (bf16[16,48,128]{2,1,0:T(8,128)(2,1)S(1)}, bf16[16,48,128]{2,1,0:T(8,128)(2,1)S(1)}, u32[]{:S(2)}, u32[]{:S(2)}) collective-permute-start(bf16[16,48,128]{2,1,0:T(8,128)(2,1)S(1)} %all_to_all.22.mine_ref), channel_id=1, source_target_pairs={{0,1},{1,0},{2,3},{3,2},{4,5},{5,4},{6,7},{7,6},{8,9},{9,8},{10,11... | collective-permute-start | bytes 589832 | tf_op jit(solution)/shard_map/ppermute | solution.py:274
  45.6 10.1 %copy-start = (bf16[1024,1024]{1,0:T(8,128)(2,1)S(1)}, bf16[1024,1024]{1,0:T(8,128)(2,1)}, u32[]{:S(2)}) copy-start(bf16[1024,1024]{1,0:T(8,128)(2,1)} %wout_ref.1) | copy-start | bytes 6291460

commit v19 on v18

--- a/solution.py
+++ b/solution.py
@@ -110,7 +110,7 @@
 
 ALL = ("view", "tok")
 CORES = 2
-MIDDLE, LATE = HEADS // 4 + 1, HEADS - 1
+MIDDLE, LATE = HEADS // 4 + 1, HEADS * 3 // 4 + 1
 SHARP = HD ** (-0.5) * 1.4426950408889634
 
 

time: 57.2 us -> 55.9 us (0.977)
  blocking collectives: 47.7 us -> 46.4 us
    all_to_all x4, blocking collectives: 47.7 us -> 46.4 us  [trade(): lax.all_to_all(piece, ALL, split_axis=0, concat_axis=0, tiled=True, axis_...]
where the time goes in v19:
time: 55.9 us; the launch traced here: 55.5 us
  blocking collectives  46.4 us (83%)
  Pallas kernels  7.08 us (13%)
  waiting for transfers between devices  1.26 us (2%)
  between operations  0.72 us (1%)
    all_to_all x4, blocking collectives, trade(): lax.all_to_all(piece, ALL, split_axis=0, concat_axis=0, tiled=True, axis_...  46.4 us
    pallas_call x7, Pallas kernels, call(): pl.pallas_call(body, out_shape=[jax.ShapeDtypeStruct(shape, dtype) for sh...  7.08 us
    ppermute x2, waiting for transfers between devices, attention(): other = lax.ppermute(mine, ALL, [(i, i ^ 1) for i in range(devices)])  1.26 us
  transfers between devices with their start and end apart: 2, of which 2 were waited for; matrix products, arithmetic and copies ran while one was open for 0% of the time, Pallas kernels for 3%

profile of v19, /device:TPU:0, one launch (start us, length us, event | category | flops | bytes accessed | tf_op | source)
XLA Modules:
  0.0 55.5 jit_solution(1722334704258927723)
XLA Ops:
  0.6 1.0 %shard_map.95 = bf16[16,48,128]{2,1,0:T(8,128)(2,1)S(1)} custom-call(bf16[1,32,1024]{2,1,0:T(8,128)(2,1)} %q_hbm.1, bf16[1,32,1024]{2,1,0:T(8,128)(2,1)} %k_hbm.1, bf16[1,32,1024]{2,1,0:T(8,128)(2,1)} %v_hbm.1), custom_call_target="tpu_custom_call" | custom-call | tf_op jit(solution)/shard_map/pallas_call | solution.py:247
  1.7 14.4 %all_to_all.20.mine_ref = bf16[16,48,128]{2,1,0:T(8,128)(2,1)S(1)} all-to-all(bf16[16,48,128]{2,1,0:T(8,128)(2,1)S(1)} %shard_map.95), channel_id=1, replica_groups={{27,28,31,0,3,4,7,8,11,12,15,16,19,20,23,24},{26,29,30,1,2,5,6,9,10,13,..., dimensions={0} | all-to-all | bytes 393216 | tf_op jit(solution)/shard_map/all_to_all | solution.py:270
  16.0 0.1 collective-permute-start
  16.1 0.8 %shard_map.96 = (bf16[512,128]{1,0:T(8,128)(2,1)S(1)}, f32[512,128]{1,0:T(8,128)S(1)}, f32[512,128]{1,0:T(8,128)S(1)}) custom-call(bf16[16,48,128]{2,1,0:T(8,128)(2,1)S(1)} %all_to_all.20.mine_ref), custom_call_target="tpu_custom_call" | custom-call | flops 1073741824 | bytes 1048576 | tf_op jit(solution)/shard_map/pallas_call | solution.py:247
  16.9 0.6 %collective-permute-done.other_ref = bf16[16,48,128]{2,1,0:T(8,128)(2,1)S(1)} collective-permute-done((bf16[16,48,128]{2,1,0:T(8,128)(2,1)S(1)}, bf16[16,48,128]{2,1,0:T(8,128)(2,1)S(1)}, u32[]{:S(2)}, u32[]{:S(2)}) %collective-permute-start) | collective-permute-done | bytes 196640 | tf_op jit(solution)/shard_map/ppermute | solution.py:274
  17.5 0.0 slice-start
  17.5 0.0 slice-start.1
  17.5 0.0 copy-start.1
  17.5 0.0 copy-start.2
  17.5 0.0 copy-start.3
  17.5 0.8 %shard_map.97 = bf16[16,16,128]{2,1,0:T(8,128)(2,1)S(1)} custom-call(bf16[16,48,128]{2,1,0:T(8,128)(2,1)S(1)} %collective-permute-done.other_ref, bf16[512,128]{1,0:T(8,128)(2,1)S(1)} %get-tuple-element.10.query_ref, f32[512,128]{1,0:T(8,128)S(1)} %get-tuple-element.11.peak_ref, f32[512,128]{1,0:T(8,128)S(1)} %get-tuple-element.12.sum_ref), custom_call_target="tpu_custom_call" | custom-call | flops 17179869184 | bytes 41943040 | tf_op jit(solution)/shard_map/pallas_call | solution.py:247
  18.4 11.3 %all_to_all.21.got_ref = bf16[16,16,128]{2,1,0:T(8,128)(2,1)S(1)} all-to-all(bf16[16,16,128]{2,1,0:T(8,128)(2,1)S(1)} %shard_map.97), channel_id=1, replica_groups={{11,12,15,16,19,20,23,24,27,28,31,0,3,4,7,8},{10,13,14,17,18,21,22,25,2..., dimensions={0} | all-to-all | bytes 131072 | tf_op jit(solution)/shard_map/all_to_all | solution.py:270
  29.6 0.0 slice-done
  29.6 0.0 slice-done.1
  29.6 0.0 copy-done.1
  29.6 0.0 copy-done.2
  29.6 0.0 copy-done.3
  29.7 1.7 %shard_map.98 = (f32[1,32,1024]{2,1,0:T(8,128)}, bf16[16,48,128]{2,1,0:T(8,128)(2,1)S(1)}) custom-call(bf16[16,16,128]{2,1,0:T(8,128)(2,1)S(1)} %all_to_all.21.got_ref, bf16[1,32,1024]{2,1,0:T(8,128)(2,1)S(1)} %copy-done.2, bf16[1024,1024]{1,0:T(8,128)(2,1)S(1)} %copy-done.1, f32[1,1024]{1,0:T(1,128)S(1)} %bitcast.3, bf16[1024,3072]{1,0:T(8,128)(2,1)S(1)} %bitcast.2), custom_call_target="tpu_custom_call" | custom-call | tf_op jit(solution)/shard_map/pallas_call | solution.py:247
  31.4 11.5 %all_to_all.22.mine_ref = bf16[16,48,128]{2,1,0:T(8,128)(2,1)S(1)} all-to-all(bf16[16,48,128]{2,1,0:T(8,128)(2,1)S(1)} %get-tuple-element.14), channel_id=1, replica_groups={{11,12,15,16,19,20,23,24,27,28,31,0,3,4,7,8},{10,13,14,17,18,21,22,25,2..., dimensions={0} | all-to-all | bytes 393216 | tf_op jit(solution)/shard_map/all_to_all | solution.py:270
  42.8 0.0 collective-permute-start.1
  42.8 0.8 %shard_map.99 = (bf16[512,128]{1,0:T(8,128)(2,1)S(1)}, f32[512,128]{1,0:T(8,128)S(1)}, f32[512,128]{1,0:T(8,128)S(1)}) custom-call(bf16[16,48,128]{2,1,0:T(8,128)(2,1)S(1)} %all_to_all.22.mine_ref), custom_call_target="tpu_custom_call" | custom-call | flops 1073741824 | bytes 1048576 | tf_op jit(solution)/shard_map/pallas_call | solution.py:247
  43.6 0.7 %collective-permute-done.1.other_ref = bf16[16,48,128]{2,1,0:T(8,128)(2,1)S(1)} collective-permute-done((bf16[16,48,128]{2,1,0:T(8,128)(2,1)S(1)}, bf16[16,48,128]{2,1,0:T(8,128)(2,1)S(1)}, u32[]{:S(2)}, u32[]{:S(2)}) %collective-permute-start.1) | collective-permute-done | bytes 196640 | tf_op jit(solution)/shard_map/ppermute | solution.py:274
  44.3 0.0 copy-start
  44.3 0.8 %shard_map.100 = bf16[16,16,128]{2,1,0:T(8,128)(2,1)S(1)} custom-call(bf16[16,48,128]{2,1,0:T(8,128)(2,1)S(1)} %collective-permute-done.1.other_ref, bf16[512,128]{1,0:T(8,128)(2,1)S(1)} %get-tuple-element.15.query_ref, f32[512,128]{1,0:T(8,128)S(1)} %get-tuple-element.16.peak_ref, f32[512,128]{1,0:T(8,128)S(1)} %get-tuple-element.17.sum_ref), custom_call_target="tpu_custom_call" | custom-call | flops 17179869184 | bytes 41943040 | tf_op jit(solution)/shard_map/pallas_call | solution.py:247
  45.1 9.3 %all_to_all.23.got_ref = bf16[16,16,128]{2,1,0:T(8,128)(2,1)S(1)} all-to-all(bf16[16,16,128]{2,1,0:T(8,128)(2,1)S(1)} %shard_map.100), channel_id=1, replica_groups={{11,12,15,16,19,20,23,24,27,28,31,0,3,4,7,8},{10,13,14,17,18,21,22,25,2..., dimensions={0} | all-to-all | bytes 131072 | tf_op jit(solution)/shard_map/all_to_all | solution.py:270
  54.4 0.0 copy-done
  54.4 1.2 %shard_map.101 = f32[1,32,1024]{2,1,0:T(8,128)} custom-call(bf16[16,16,128]{2,1,0:T(8,128)(2,1)S(1)} %all_to_all.23.got_ref, bf16[1024,1024]{1,0:T(8,128)(2,1)S(1)} %copy-done), custom_call_target="tpu_custom_call" | custom-call | tf_op jit(solution)/shard_map/pallas_call | solution.py:247
  (1 shorter events, 0.0 us)
Async XLA Ops:
  16.0 1.4 %collective-permute-start = (bf16[16,48,128]{2,1,0:T(8,128)(2,1)S(1)}, bf16[16,48,128]{2,1,0:T(8,128)(2,1)S(1)}, u32[]{:S(2)}, u32[]{:S(2)}) collective-permute-start(bf16[16,48,128]{2,1,0:T(8,128)(2,1)S(1)} %all_to_all.20.mine_ref), channel_id=1, source_target_pairs={{0,1},{1,0},{2,3},{3,2},{4,5},{5,4},{6,7},{7,6},{8,9},{9,8},{10,11... | collective-permute-start | bytes 589832 | tf_op jit(solution)/shard_map/ppermute | solution.py:274
  17.5 12.1 %slice-start = ((s8[6291456]{0:T(1024)(128)(4,1)}), s8[4194304]{0:T(1024)(128)(4,1)S(1)}, s32[]{:S(2)}) async-start(s8[6291456]{0:T(1024)(128)(4,1)} %bitcast.1), calls=%async_computation.4 | async-start | bytes 8388608
  17.5 12.1 %slice-start.1 = ((s8[6291456]{0:T(1024)(128)(4,1)}), s8[2097152]{0:T(1024)(128)(4,1)S(1)}, s32[]{:S(2)}) async-start(s8[6291456]{0:T(1024)(128)(4,1)} %bitcast.1), calls=%async_computation.5 | async-start | bytes 4194304
  17.5 12.1 %copy-start.1 = (bf16[1024,1024]{1,0:T(8,128)(2,1)S(1)}, bf16[1024,1024]{1,0:T(8,128)(2,1)}, u32[]{:S(2)}) copy-start(bf16[1024,1024]{1,0:T(8,128)(2,1)} %wv_ref.1) | copy-start | bytes 6291460
  17.5 12.1 %copy-start.2 = (bf16[1,32,1024]{2,1,0:T(8,128)(2,1)S(1)}, bf16[1,32,1024]{2,1,0:T(8,128)(2,1)}, u32[]{:S(2)}) copy-start(bf16[1,32,1024]{2,1,0:T(8,128)(2,1)} %x2_ref.1) | copy-start | bytes 196612
  17.5 12.1 %copy-start.3 = (f32[1024]{0:T(1024)S(1)}, f32[1024]{0:T(1024)}, u32[]{:S(2)}) copy-start(f32[1024]{0:T(1024)} %param.14) | copy-start | bytes 12292
  42.8 1.4 %collective-permute-start.1 = (bf16[16,48,128]{2,1,0:T(8,128)(2,1)S(1)}, bf16[16,48,128]{2,1,0:T(8,128)(2,1)S(1)}, u32[]{:S(2)}, u32[]{:S(2)}) collective-permute-start(bf16[16,48,128]{2,1,0:T(8,128)(2,1)S(1)} %all_to_all.22.mine_ref), channel_id=1, source_target_pairs={{0,1},{1,0},{2,3},{3,2},{4,5},{5,4},{6,7},{7,6},{8,9},{9,8},{10,11... | collective-permute-start | bytes 589832 | tf_op jit(solution)/shard_map/ppermute | solution.py:274
  44.3 10.1 %copy-start = (bf16[1024,1024]{1,0:T(8,128)(2,1)S(1)}, bf16[1024,1024]{1,0:T(8,128)(2,1)}, u32[]{:S(2)}) copy-start(bf16[1024,1024]{1,0:T(8,128)(2,1)} %wout_ref.1) | copy-start | bytes 6291460

commit v20 on v16

--- a/solution.py
+++ b/solution.py
@@ -108,26 +108,35 @@
 
 ALL = ("view", "tok")
 CORES = 2
-FIRST = HEADS // 4 + 1
+MIDDLE = HEADS // 4
 SHARP = HD ** (-0.5) * 1.4426950408889634
 
 
 def trade_groups():
-    chips = [(FIRST + i) % HEADS for i in range(HEADS)]
-    return [[chip * CORES + (chip + s) % CORES for chip in chips] for s in range(CORES)]
+    groups = []
+    for s in range(CORES):
+        chips = [(MIDDLE + 1 - s + i) % HEADS for i in range(HEADS)]
+        groups.append([chip * CORES + (chip + s) % CORES for chip in chips])
+    return groups
+
+
+def spots():
+    device = lax.axis_index("tok")
+    s = (device ^ (device >> 1)) & 1
+    return [(h + s) & (HEADS - 1) for h in range(HEADS)]
 
 
 def pack_heads(out_ref, q, k, v):
     rows = q.shape[0]
     half = rows // 2
-    for h in range(HEADS):
+    for h, at in enumerate(spots()):
         cols = slice(h * HD, (h + 1) * HD)
-        out_ref[h, 0:rows, :] = jnp.concatenate([k[:, cols], v[:, cols]], axis=-1)
-        out_ref[h, rows : rows + half, :] = jnp.concatenate([q[:half, cols], q[half:, cols]], axis=-1)
+        out_ref[at, 0:rows, :] = jnp.concatenate([k[:, cols], v[:, cols]], axis=-1)
+        out_ref[at, rows : rows + half, :] = jnp.concatenate([q[:half, cols], q[half:, cols]], axis=-1)
 
 
 def unpack_rows(got_ref):
-    pieces = [got_ref[h] for h in range(HEADS)]
+    pieces = [got_ref[at] for at in spots()]
     top = jnp.concatenate([p[:, :HD] for p in pieces], axis=-1)
     low = jnp.concatenate([p[:, HD:] for p in pieces], axis=-1)
     return jnp.concatenate([top, low], axis=0)

time: 55.5 us -> 55.6 us (level)
  no operation moved by 1% of the time
where the time goes in v20:
time: 55.6 us; the launch traced here: 55.2 us
  blocking collectives  45.5 us (82%)
  Pallas kernels  7.61 us (14%)
  waiting for transfers between devices  1.24 us (2%)
  between operations  0.72 us (1%)
    all_to_all x4, blocking collectives, trade(): lax.all_to_all(piece, ALL, split_axis=0, concat_axis=0, tiled=True, axis_...  45.5 us
    pallas_call x7, Pallas kernels, call(): pl.pallas_call(body, out_shape=[jax.ShapeDtypeStruct(shape, dtype) for sh...  7.61 us
    ppermute x2, waiting for transfers between devices, attention(): other = lax.ppermute(mine, ALL, [(i, i ^ 1) for i in range(devices)])  1.24 us
  transfers between devices with their start and end apart: 2, of which 2 were waited for; matrix products, arithmetic and copies ran while one was open for 0% of the time, Pallas kernels for 3%

profile of v20, /device:TPU:0, one launch (start us, length us, event | category | flops | bytes accessed | tf_op | source)
XLA Modules:
  0.0 55.2 jit_solution(14006597553101782572)
XLA Ops:
  0.6 1.0 %shard_map.95 = bf16[16,48,128]{2,1,0:T(8,128)(2,1)S(1)} custom-call(bf16[1,32,1024]{2,1,0:T(8,128)(2,1)} %q_hbm.1, bf16[1,32,1024]{2,1,0:T(8,128)(2,1)} %k_hbm.1, bf16[1,32,1024]{2,1,0:T(8,128)(2,1)} %v_hbm.1), custom_call_target="tpu_custom_call" | custom-call | tf_op jit(solution)/shard_map/pallas_call | solution.py:251
  1.7 15.9 %all_to_all.20.mine_ref = bf16[16,48,128]{2,1,0:T(8,128)(2,1)S(1)} all-to-all(bf16[16,48,128]{2,1,0:T(8,128)(2,1)S(1)} %shard_map.95), channel_id=1, replica_groups={{11,12,15,16,19,20,23,24,27,28,31,0,3,4,7,8},{9,10,13,14,17,18,21,22,25..., dimensions={0} | all-to-all | bytes 393216 | tf_op jit(solution)/shard_map/all_to_all | solution.py:273
  17.5 0.0 collective-permute-start
  17.5 0.8 %shard_map.96 = (bf16[512,128]{1,0:T(8,128)(2,1)S(1)}, f32[512,128]{1,0:T(8,128)S(1)}, f32[512,128]{1,0:T(8,128)S(1)}) custom-call(bf16[16,48,128]{2,1,0:T(8,128)(2,1)S(1)} %all_to_all.20.mine_ref), custom_call_target="tpu_custom_call" | custom-call | flops 1073741824 | bytes 1048576 | tf_op jit(solution)/shard_map/pallas_call | solution.py:251
  18.3 0.7 %collective-permute-done.other_ref = bf16[16,48,128]{2,1,0:T(8,128)(2,1)S(1)} collective-permute-done((bf16[16,48,128]{2,1,0:T(8,128)(2,1)S(1)}, bf16[16,48,128]{2,1,0:T(8,128)(2,1)S(1)}, u32[]{:S(2)}, u32[]{:S(2)}) %collective-permute-start) | collective-permute-done | bytes 196640 | tf_op jit(solution)/shard_map/ppermute | solution.py:277
  19.0 0.0 slice-start
  19.0 0.0 slice-start.1
  19.0 0.0 copy-start.1
  19.0 0.0 copy-start.2
  19.0 0.0 copy-start.3
  19.0 0.8 %shard_map.97 = bf16[16,16,128]{2,1,0:T(8,128)(2,1)S(1)} custom-call(bf16[16,48,128]{2,1,0:T(8,128)(2,1)S(1)} %collective-permute-done.other_ref, bf16[512,128]{1,0:T(8,128)(2,1)S(1)} %get-tuple-element.10.query_ref, f32[512,128]{1,0:T(8,128)S(1)} %get-tuple-element.11.peak_ref, f32[512,128]{1,0:T(8,128)S(1)} %get-tuple-element.12.sum_ref), custom_call_target="tpu_custom_call" | custom-call | flops 17179869184 | bytes 41943040 | tf_op jit(solution)/shard_map/pallas_call | solution.py:251
  19.9 9.5 %all_to_all.21.got_ref = bf16[16,16,128]{2,1,0:T(8,128)(2,1)S(1)} all-to-all(bf16[16,16,128]{2,1,0:T(8,128)(2,1)S(1)} %shard_map.97), channel_id=1, replica_groups={{11,12,15,16,19,20,23,24,27,28,31,0,3,4,7,8},{9,10,13,14,17,18,21,22,25..., dimensions={0} | all-to-all | bytes 131072 | tf_op jit(solution)/shard_map/all_to_all | solution.py:273
  29.4 0.0 slice-done
  29.4 0.0 slice-done.1
  29.4 0.0 copy-done.1
  29.4 0.0 copy-done.2
  29.4 0.0 copy-done.3
  29.4 2.2 %shard_map.98 = (f32[1,32,1024]{2,1,0:T(8,128)}, bf16[16,48,128]{2,1,0:T(8,128)(2,1)S(1)}) custom-call(bf16[16,16,128]{2,1,0:T(8,128)(2,1)S(1)} %all_to_all.21.got_ref, bf16[1,32,1024]{2,1,0:T(8,128)(2,1)S(1)} %copy-done.2, bf16[1024,1024]{1,0:T(8,128)(2,1)S(1)} %copy-done.1, f32[1,1024]{1,0:T(1,128)S(1)} %bitcast.3, bf16[1024,3072]{1,0:T(8,128)(2,1)S(1)} %bitcast.2), custom_call_target="tpu_custom_call" | custom-call | tf_op jit(solution)/shard_map/pallas_call | solution.py:251
  31.6 10.8 %all_to_all.22.mine_ref = bf16[16,48,128]{2,1,0:T(8,128)(2,1)S(1)} all-to-all(bf16[16,48,128]{2,1,0:T(8,128)(2,1)S(1)} %get-tuple-element.14), channel_id=1, replica_groups={{11,12,15,16,19,20,23,24,27,28,31,0,3,4,7,8},{9,10,13,14,17,18,21,22,25..., dimensions={0} | all-to-all | bytes 393216 | tf_op jit(solution)/shard_map/all_to_all | solution.py:273
  42.5 0.1 collective-permute-start.1
  42.6 0.8 %shard_map.99 = (bf16[512,128]{1,0:T(8,128)(2,1)S(1)}, f32[512,128]{1,0:T(8,128)S(1)}, f32[512,128]{1,0:T(8,128)S(1)}) custom-call(bf16[16,48,128]{2,1,0:T(8,128)(2,1)S(1)} %all_to_all.22.mine_ref), custom_call_target="tpu_custom_call" | custom-call | flops 1073741824 | bytes 1048576 | tf_op jit(solution)/shard_map/pallas_call | solution.py:251
  43.4 0.6 %collective-permute-done.1.other_ref = bf16[16,48,128]{2,1,0:T(8,128)(2,1)S(1)} collective-permute-done((bf16[16,48,128]{2,1,0:T(8,128)(2,1)S(1)}, bf16[16,48,128]{2,1,0:T(8,128)(2,1)S(1)}, u32[]{:S(2)}, u32[]{:S(2)}) %collective-permute-start.1) | collective-permute-done | bytes 196640 | tf_op jit(solution)/shard_map/ppermute | solution.py:277
  43.9 0.0 copy-start
  43.9 0.8 %shard_map.100 = bf16[16,16,128]{2,1,0:T(8,128)(2,1)S(1)} custom-call(bf16[16,48,128]{2,1,0:T(8,128)(2,1)S(1)} %collective-permute-done.1.other_ref, bf16[512,128]{1,0:T(8,128)(2,1)S(1)} %get-tuple-element.15.query_ref, f32[512,128]{1,0:T(8,128)S(1)} %get-tuple-element.16.peak_ref, f32[512,128]{1,0:T(8,128)S(1)} %get-tuple-element.17.sum_ref), custom_call_target="tpu_custom_call" | custom-call | flops 17179869184 | bytes 41943040 | tf_op jit(solution)/shard_map/pallas_call | solution.py:251
  44.8 9.3 %all_to_all.23.got_ref = bf16[16,16,128]{2,1,0:T(8,128)(2,1)S(1)} all-to-all(bf16[16,16,128]{2,1,0:T(8,128)(2,1)S(1)} %shard_map.100), channel_id=1, replica_groups={{11,12,15,16,19,20,23,24,27,28,31,0,3,4,7,8},{9,10,13,14,17,18,21,22,25..., dimensions={0} | all-to-all | bytes 131072 | tf_op jit(solution)/shard_map/all_to_all | solution.py:273
  54.1 0.0 copy-done
  54.1 1.2 %shard_map.101 = f32[1,32,1024]{2,1,0:T(8,128)} custom-call(bf16[16,16,128]{2,1,0:T(8,128)(2,1)S(1)} %all_to_all.23.got_ref, bf16[1024,1024]{1,0:T(8,128)(2,1)S(1)} %copy-done), custom_call_target="tpu_custom_call" | custom-call | tf_op jit(solution)/shard_map/pallas_call | solution.py:251
  (1 shorter events, 0.0 us)
Async XLA Ops:
  17.5 1.4 %collective-permute-start = (bf16[16,48,128]{2,1,0:T(8,128)(2,1)S(1)}, bf16[16,48,128]{2,1,0:T(8,128)(2,1)S(1)}, u32[]{:S(2)}, u32[]{:S(2)}) collective-permute-start(bf16[16,48,128]{2,1,0:T(8,128)(2,1)S(1)} %all_to_all.20.mine_ref), channel_id=1, source_target_pairs={{0,1},{1,0},{2,3},{3,2},{4,5},{5,4},{6,7},{7,6},{8,9},{9,8},{10,11... | collective-permute-start | bytes 589832 | tf_op jit(solution)/shard_map/ppermute | solution.py:277
  19.0 10.4 %slice-start = ((s8[6291456]{0:T(1024)(128)(4,1)}), s8[4194304]{0:T(1024)(128)(4,1)S(1)}, s32[]{:S(2)}) async-start(s8[6291456]{0:T(1024)(128)(4,1)} %bitcast.1), calls=%async_computation.4 | async-start | bytes 8388608
  19.0 10.4 %slice-start.1 = ((s8[6291456]{0:T(1024)(128)(4,1)}), s8[2097152]{0:T(1024)(128)(4,1)S(1)}, s32[]{:S(2)}) async-start(s8[6291456]{0:T(1024)(128)(4,1)} %bitcast.1), calls=%async_computation.5 | async-start | bytes 4194304
  19.0 10.4 %copy-start.1 = (bf16[1024,1024]{1,0:T(8,128)(2,1)S(1)}, bf16[1024,1024]{1,0:T(8,128)(2,1)}, u32[]{:S(2)}) copy-start(bf16[1024,1024]{1,0:T(8,128)(2,1)} %wv_ref.1) | copy-start | bytes 6291460
  19.0 10.4 %copy-start.2 = (bf16[1,32,1024]{2,1,0:T(8,128)(2,1)S(1)}, bf16[1,32,1024]{2,1,0:T(8,128)(2,1)}, u32[]{:S(2)}) copy-start(bf16[1,32,1024]{2,1,0:T(8,128)(2,1)} %x2_ref.1) | copy-start | bytes 196612
  19.0 10.4 %copy-start.3 = (f32[1024]{0:T(1024)S(1)}, f32[1024]{0:T(1024)}, u32[]{:S(2)}) copy-start(f32[1024]{0:T(1024)} %param.14) | copy-start | bytes 12292
  42.5 1.4 %collective-permute-start.1 = (bf16[16,48,128]{2,1,0:T(8,128)(2,1)S(1)}, bf16[16,48,128]{2,1,0:T(8,128)(2,1)S(1)}, u32[]{:S(2)}, u32[]{:S(2)}) collective-permute-start(bf16[16,48,128]{2,1,0:T(8,128)(2,1)S(1)} %all_to_all.22.mine_ref), channel_id=1, source_target_pairs={{0,1},{1,0},{2,3},{3,2},{4,5},{5,4},{6,7},{7,6},{8,9},{9,8},{10,11... | collective-permute-start | bytes 589832 | tf_op jit(solution)/shard_map/ppermute | solution.py:277
  43.9 10.1 %copy-start = (bf16[1024,1024]{1,0:T(8,128)(2,1)S(1)}, bf16[1024,1024]{1,0:T(8,128)(2,1)}, u32[]{:S(2)}) copy-start(bf16[1024,1024]{1,0:T(8,128)(2,1)} %wout_ref.1) | copy-start | bytes 6291460

commit v21 on v20

--- a/solution.py
+++ b/solution.py
@@ -120,23 +120,28 @@
     return groups
 
 
-def spots():
+def own_group():
     device = lax.axis_index("tok")
-    s = (device ^ (device >> 1)) & 1
-    return [(h + s) & (HEADS - 1) for h in range(HEADS)]
-
-
-def pack_heads(out_ref, q, k, v):
+    return (device ^ (device >> 1)) & 1
+
+
+def pack_heads(out_ref, packed_ref, q, k, v):
     rows = q.shape[0]
     half = rows // 2
-    for h, at in enumerate(spots()):
+    for h in range(HEADS):
         cols = slice(h * HD, (h + 1) * HD)
-        out_ref[at, 0:rows, :] = jnp.concatenate([k[:, cols], v[:, cols]], axis=-1)
-        out_ref[at, rows : rows + half, :] = jnp.concatenate([q[:half, cols], q[half:, cols]], axis=-1)
+        packed_ref[h, 0:rows, :] = jnp.concatenate([k[:, cols], v[:, cols]], axis=-1)
+        packed_ref[h, rows : rows + half, :] = jnp.concatenate([q[:half, cols], q[half:, cols]], axis=-1)
+    for s in range(CORES):
+
+        @pl.when(own_group() == s)
+        def _():
+            for h in range(HEADS):
+                out_ref[(h + s) % HEADS] = packed_ref[h]
 
 
 def unpack_rows(got_ref):
-    pieces = [got_ref[at] for at in spots()]
+    pieces = [got_ref[(h + own_group()) & (HEADS - 1)] for h in range(HEADS)]
     top = jnp.concatenate([p[:, :HD] for p in pieces], axis=-1)
     low = jnp.concatenate([p[:, HD:] for p in pieces], axis=-1)
     return jnp.concatenate([top, low], axis=0)
@@ -150,7 +155,7 @@
     return jnp.dot(x, weight, preferred_element_type=jnp.float32)
 
 
-def pack_kernel(q_hbm, k_hbm, v_hbm, out_ref, q_ref, k_ref, v_ref, sems):
+def pack_kernel(q_hbm, k_hbm, v_hbm, out_ref, packed_ref, q_ref, k_ref, v_ref, sems):
     half = q_ref.shape[1] // 2
     copies = [
         pltpu.make_async_copy(src.at[:, at : at + half], dst.at[:, at : at + half], sems.at[i, at // half])
@@ -161,7 +166,7 @@
         copy.start()
     for copy in copies:
         copy.wait()
-    pack_heads(out_ref, q_ref[0], k_ref[0], v_ref[0])
+    pack_heads(out_ref, packed_ref, q_ref[0], k_ref[0], v_ref[0])
 
 
 def lower_half(shape):
@@ -218,7 +223,7 @@
     out_ref[...] = attn.astype(jnp.bfloat16).reshape(out_ref.shape)
 
 
-def middle_kernel(got_ref, x2_ref, wv_ref, gain_ref, wqkv_ref, feats_hbm, out_ref, feats_ref, sem):
+def middle_kernel(got_ref, x2_ref, wv_ref, gain_ref, wqkv_ref, feats_hbm, out_ref, packed_ref, feats_ref, sem):
     rows = unpack_rows(got_ref)
     wide = rows.astype(jnp.float32)
     scale = factor(wide)
@@ -229,7 +234,7 @@
     gained = (hidden * gain_ref[...]).astype(jnp.bfloat16)
     projected = (times(gained, wqkv_ref[...]) * factor(hidden)).astype(jnp.bfloat16)
     width = HEADS * HD
-    pack_heads(out_ref, projected[:, :width], projected[:, width : 2 * width], projected[:, 2 * width :])
+    pack_heads(out_ref, packed_ref, projected[:, :width], projected[:, width : 2 * width], projected[:, 2 * width :])
     copy.wait()
 
 
@@ -281,13 +286,14 @@
         return trade(half)
 
     inputs = [pltpu.with_memory_space_constraint(x, pltpu.HBM) for x in (q1, k1, v1)]
-    scratch = [pltpu.VMEM(q1.shape, q1.dtype)] * 3 + [pltpu.SemaphoreType.DMA((3, 2))]
+    lay = pltpu.VMEM(packed[0], packed[1])
+    scratch = [lay] + [pltpu.VMEM(q1.shape, q1.dtype)] * 3 + [pltpu.SemaphoreType.DMA((3, 2))]
     (piece,) = call(pack_kernel, [packed], inputs, scratch, space=pltpu.HBM, limit=48 << 20)
     feats, piece = call(
         middle_kernel,
         [(wide, jnp.float32, pltpu.HBM), packed],
         (attention(piece), x2, w_view_out, norm_gain[None], w_qkv),
-        [pltpu.VMEM(wide, jnp.float32), pltpu.SemaphoreType.DMA],
+        [lay, pltpu.VMEM(wide, jnp.float32), pltpu.SemaphoreType.DMA],
     )
     (result,) = call(
         last_kernel,

time: 55.6 us -> 55.5 us (level)
  no operation moved by 1% of the time
where the time goes in v21:
time: 55.5 us; the launch traced here: 55.2 us
  blocking collectives  45.5 us (82%)
  Pallas kernels  7.53 us (14%)
  waiting for transfers between devices  1.25 us (2%)
  between operations  0.72 us (1%)
    all_to_all x4, blocking collectives, trade(): lax.all_to_all(piece, ALL, split_axis=0, concat_axis=0, tiled=True, axis_...  45.5 us
    pallas_call x7, Pallas kernels, call(): pl.pallas_call(body, out_shape=[jax.ShapeDtypeStruct(shape, dtype) for sh...  7.53 us
    ppermute x2, waiting for transfers between devices, attention(): other = lax.ppermute(mine, ALL, [(i, i ^ 1) for i in range(devices)])  1.25 us
  transfers between devices with their start and end apart: 2, of which 2 were waited for; matrix products, arithmetic and copies ran while one was open for 0% of the time, Pallas kernels for 3%

profile of v21, /device:TPU:0, one launch (start us, length us, event | category | flops | bytes accessed | tf_op | source)
XLA Modules:
  0.0 55.2 jit_solution(11071740362150982830)
XLA Ops:
  0.6 1.0 %shard_map.95 = bf16[16,48,128]{2,1,0:T(8,128)(2,1)S(1)} custom-call(bf16[1,32,1024]{2,1,0:T(8,128)(2,1)} %q_hbm.1, bf16[1,32,1024]{2,1,0:T(8,128)(2,1)} %k_hbm.1, bf16[1,32,1024]{2,1,0:T(8,128)(2,1)} %v_hbm.1), custom_call_target="tpu_custom_call" | custom-call | tf_op jit(solution)/shard_map/pallas_call | solution.py:256
  1.7 15.9 %all_to_all.20.mine_ref = bf16[16,48,128]{2,1,0:T(8,128)(2,1)S(1)} all-to-all(bf16[16,48,128]{2,1,0:T(8,128)(2,1)S(1)} %shard_map.95), channel_id=1, replica_groups={{11,12,15,16,19,20,23,24,27,28,31,0,3,4,7,8},{9,10,13,14,17,18,21,22,25..., dimensions={0} | all-to-all | bytes 393216 | tf_op jit(solution)/shard_map/all_to_all | solution.py:278
  17.6 0.0 collective-permute-start
  17.6 0.8 %shard_map.96 = (bf16[512,128]{1,0:T(8,128)(2,1)S(1)}, f32[512,128]{1,0:T(8,128)S(1)}, f32[512,128]{1,0:T(8,128)S(1)}) custom-call(bf16[16,48,128]{2,1,0:T(8,128)(2,1)S(1)} %all_to_all.20.mine_ref), custom_call_target="tpu_custom_call" | custom-call | flops 1073741824 | bytes 1048576 | tf_op jit(solution)/shard_map/pallas_call | solution.py:256
  18.3 0.7 %collective-permute-done.other_ref = bf16[16,48,128]{2,1,0:T(8,128)(2,1)S(1)} collective-permute-done((bf16[16,48,128]{2,1,0:T(8,128)(2,1)S(1)}, bf16[16,48,128]{2,1,0:T(8,128)(2,1)S(1)}, u32[]{:S(2)}, u32[]{:S(2)}) %collective-permute-start) | collective-permute-done | bytes 196640 | tf_op jit(solution)/shard_map/ppermute | solution.py:282
  19.0 0.0 slice-start
  19.0 0.0 slice-start.1
  19.0 0.0 copy-start.1
  19.0 0.0 copy-start.2
  19.0 0.0 copy-start.3
  19.0 0.8 %shard_map.97 = bf16[16,16,128]{2,1,0:T(8,128)(2,1)S(1)} custom-call(bf16[16,48,128]{2,1,0:T(8,128)(2,1)S(1)} %collective-permute-done.other_ref, bf16[512,128]{1,0:T(8,128)(2,1)S(1)} %get-tuple-element.10.query_ref, f32[512,128]{1,0:T(8,128)S(1)} %get-tuple-element.11.peak_ref, f32[512,128]{1,0:T(8,128)S(1)} %get-tuple-element.12.sum_ref), custom_call_target="tpu_custom_call" | custom-call | flops 17179869184 | bytes 41943040 | tf_op jit(solution)/shard_map/pallas_call | solution.py:256
  19.9 9.5 %all_to_all.21.got_ref = bf16[16,16,128]{2,1,0:T(8,128)(2,1)S(1)} all-to-all(bf16[16,16,128]{2,1,0:T(8,128)(2,1)S(1)} %shard_map.97), channel_id=1, replica_groups={{11,12,15,16,19,20,23,24,27,28,31,0,3,4,7,8},{9,10,13,14,17,18,21,22,25..., dimensions={0} | all-to-all | bytes 131072 | tf_op jit(solution)/shard_map/all_to_all | solution.py:278
  29.4 0.0 slice-done
  29.4 0.0 slice-done.1
  29.4 0.0 copy-done.1
  29.4 0.0 copy-done.2
  29.4 0.0 copy-done.3
  29.4 2.2 %shard_map.98 = (f32[1,32,1024]{2,1,0:T(8,128)}, bf16[16,48,128]{2,1,0:T(8,128)(2,1)S(1)}) custom-call(bf16[16,16,128]{2,1,0:T(8,128)(2,1)S(1)} %all_to_all.21.got_ref, bf16[1,32,1024]{2,1,0:T(8,128)(2,1)S(1)} %copy-done.2, bf16[1024,1024]{1,0:T(8,128)(2,1)S(1)} %copy-done.1, f32[1,1024]{1,0:T(1,128)S(1)} %bitcast.3, bf16[1024,3072]{1,0:T(8,128)(2,1)S(1)} %bitcast.2), custom_call_target="tpu_custom_call" | custom-call | tf_op jit(solution)/shard_map/pallas_call | solution.py:256
  31.6 10.8 %all_to_all.22.mine_ref = bf16[16,48,128]{2,1,0:T(8,128)(2,1)S(1)} all-to-all(bf16[16,48,128]{2,1,0:T(8,128)(2,1)S(1)} %get-tuple-element.14), channel_id=1, replica_groups={{11,12,15,16,19,20,23,24,27,28,31,0,3,4,7,8},{9,10,13,14,17,18,21,22,25..., dimensions={0} | all-to-all | bytes 393216 | tf_op jit(solution)/shard_map/all_to_all | solution.py:278
  42.4 0.1 collective-permute-start.1
  42.5 0.7 %shard_map.99 = (bf16[512,128]{1,0:T(8,128)(2,1)S(1)}, f32[512,128]{1,0:T(8,128)S(1)}, f32[512,128]{1,0:T(8,128)S(1)}) custom-call(bf16[16,48,128]{2,1,0:T(8,128)(2,1)S(1)} %all_to_all.22.mine_ref), custom_call_target="tpu_custom_call" | custom-call | flops 1073741824 | bytes 1048576 | tf_op jit(solution)/shard_map/pallas_call | solution.py:256
  43.3 0.6 %collective-permute-done.1.other_ref = bf16[16,48,128]{2,1,0:T(8,128)(2,1)S(1)} collective-permute-done((bf16[16,48,128]{2,1,0:T(8,128)(2,1)S(1)}, bf16[16,48,128]{2,1,0:T(8,128)(2,1)S(1)}, u32[]{:S(2)}, u32[]{:S(2)}) %collective-permute-start.1) | collective-permute-done | bytes 196640 | tf_op jit(solution)/shard_map/ppermute | solution.py:282
  43.9 0.0 copy-start
  43.9 0.8 %shard_map.100 = bf16[16,16,128]{2,1,0:T(8,128)(2,1)S(1)} custom-call(bf16[16,48,128]{2,1,0:T(8,128)(2,1)S(1)} %collective-permute-done.1.other_ref, bf16[512,128]{1,0:T(8,128)(2,1)S(1)} %get-tuple-element.15.query_ref, f32[512,128]{1,0:T(8,128)S(1)} %get-tuple-element.16.peak_ref, f32[512,128]{1,0:T(8,128)S(1)} %get-tuple-element.17.sum_ref), custom_call_target="tpu_custom_call" | custom-call | flops 17179869184 | bytes 41943040 | tf_op jit(solution)/shard_map/pallas_call | solution.py:256
  44.7 9.3 %all_to_all.23.got_ref = bf16[16,16,128]{2,1,0:T(8,128)(2,1)S(1)} all-to-all(bf16[16,16,128]{2,1,0:T(8,128)(2,1)S(1)} %shard_map.100), channel_id=1, replica_groups={{11,12,15,16,19,20,23,24,27,28,31,0,3,4,7,8},{9,10,13,14,17,18,21,22,25..., dimensions={0} | all-to-all | bytes 131072 | tf_op jit(solution)/shard_map/all_to_all | solution.py:278
  54.0 0.0 copy-done
  54.0 1.2 %shard_map.101 = f32[1,32,1024]{2,1,0:T(8,128)} custom-call(bf16[16,16,128]{2,1,0:T(8,128)(2,1)S(1)} %all_to_all.23.got_ref, bf16[1024,1024]{1,0:T(8,128)(2,1)S(1)} %copy-done), custom_call_target="tpu_custom_call" | custom-call | tf_op jit(solution)/shard_map/pallas_call | solution.py:256
  (1 shorter events, 0.0 us)
Async XLA Ops:
  17.6 1.4 %collective-permute-start = (bf16[16,48,128]{2,1,0:T(8,128)(2,1)S(1)}, bf16[16,48,128]{2,1,0:T(8,128)(2,1)S(1)}, u32[]{:S(2)}, u32[]{:S(2)}) collective-permute-start(bf16[16,48,128]{2,1,0:T(8,128)(2,1)S(1)} %all_to_all.20.mine_ref), channel_id=1, source_target_pairs={{0,1},{1,0},{2,3},{3,2},{4,5},{5,4},{6,7},{7,6},{8,9},{9,8},{10,11... | collective-permute-start | bytes 589832 | tf_op jit(solution)/shard_map/ppermute | solution.py:282
  19.0 10.4 %slice-start = ((s8[6291456]{0:T(1024)(128)(4,1)}), s8[4194304]{0:T(1024)(128)(4,1)S(1)}, s32[]{:S(2)}) async-start(s8[6291456]{0:T(1024)(128)(4,1)} %bitcast.1), calls=%async_computation.4 | async-start | bytes 8388608
  19.0 10.4 %slice-start.1 = ((s8[6291456]{0:T(1024)(128)(4,1)}), s8[2097152]{0:T(1024)(128)(4,1)S(1)}, s32[]{:S(2)}) async-start(s8[6291456]{0:T(1024)(128)(4,1)} %bitcast.1), calls=%async_computation.5 | async-start | bytes 4194304
  19.0 10.4 %copy-start.1 = (bf16[1024,1024]{1,0:T(8,128)(2,1)S(1)}, bf16[1024,1024]{1,0:T(8,128)(2,1)}, u32[]{:S(2)}) copy-start(bf16[1024,1024]{1,0:T(8,128)(2,1)} %wv_ref.1) | copy-start | bytes 6291460
  19.0 10.4 %copy-start.2 = (bf16[1,32,1024]{2,1,0:T(8,128)(2,1)S(1)}, bf16[1,32,1024]{2,1,0:T(8,128)(2,1)}, u32[]{:S(2)}) copy-start(bf16[1,32,1024]{2,1,0:T(8,128)(2,1)} %x2_ref.1) | copy-start | bytes 196612
  19.0 10.4 %copy-start.3 = (f32[1024]{0:T(1024)S(1)}, f32[1024]{0:T(1024)}, u32[]{:S(2)}) copy-start(f32[1024]{0:T(1024)} %param.14) | copy-start | bytes 12292
  42.4 1.4 %collective-permute-start.1 = (bf16[16,48,128]{2,1,0:T(8,128)(2,1)S(1)}, bf16[16,48,128]{2,1,0:T(8,128)(2,1)S(1)}, u32[]{:S(2)}, u32[]{:S(2)}) collective-permute-start(bf16[16,48,128]{2,1,0:T(8,128)(2,1)S(1)} %all_to_all.22.mine_ref), channel_id=1, source_target_pairs={{0,1},{1,0},{2,3},{3,2},{4,5},{5,4},{6,7},{7,6},{8,9},{9,8},{10,11... | collective-permute-start | bytes 589832 | tf_op jit(solution)/shard_map/ppermute | solution.py:282
  43.9 10.1 %copy-start = (bf16[1024,1024]{1,0:T(8,128)(2,1)S(1)}, bf16[1024,1024]{1,0:T(8,128)(2,1)}, u32[]{:S(2)}) copy-start(bf16[1024,1024]{1,0:T(8,128)(2,1)} %wout_ref.1) | copy-start | bytes 6291460

commit v22 on v20

--- a/solution.py
+++ b/solution.py
@@ -120,23 +120,28 @@
     return groups
 
 
-def spots():
+def first_group():
     device = lax.axis_index("tok")
-    s = (device ^ (device >> 1)) & 1
-    return [(h + s) & (HEADS - 1) for h in range(HEADS)]
+    return ((device ^ (device >> 1)) & 1) == 0
 
 
 def pack_heads(out_ref, q, k, v):
     rows = q.shape[0]
     half = rows // 2
-    for h, at in enumerate(spots()):
+    first = first_group()
+    kv, lines = [], []
+    for h in range(HEADS):
         cols = slice(h * HD, (h + 1) * HD)
-        out_ref[at, 0:rows, :] = jnp.concatenate([k[:, cols], v[:, cols]], axis=-1)
-        out_ref[at, rows : rows + half, :] = jnp.concatenate([q[:half, cols], q[half:, cols]], axis=-1)
+        kv.append(jnp.concatenate([k[:, cols], v[:, cols]], axis=-1))
+        lines.append(jnp.concatenate([q[:half, cols], q[half:, cols]], axis=-1))
+    for at in range(HEADS):
+        out_ref[at, 0:rows, :] = jnp.where(first, kv[at], kv[at - 1])
+        out_ref[at, rows : rows + half, :] = jnp.where(first, lines[at], lines[at - 1])
 
 
 def unpack_rows(got_ref):
-    pieces = [got_ref[at] for at in spots()]
+    first = first_group()
+    pieces = [jnp.where(first, got_ref[h], got_ref[(h + 1) % HEADS]) for h in range(HEADS)]
     top = jnp.concatenate([p[:, :HD] for p in pieces], axis=-1)
     low = jnp.concatenate([p[:, HD:] for p in pieces], axis=-1)
     return jnp.concatenate([top, low], axis=0)

time: 55.6 us -> 55 us (0.989)
  no operation moved by 1% of the time
where the time goes in v22:
time: 55 us; the launch traced here: 54.7 us
  blocking collectives  45.5 us (83%)
  Pallas kernels  7.09 us (13%)
  waiting for transfers between devices  1.26 us (2%)
  between operations  0.72 us (1%)
    all_to_all x4, blocking collectives, trade(): lax.all_to_all(piece, ALL, split_axis=0, concat_axis=0, tiled=True, axis_...  45.5 us
    pallas_call x7, Pallas kernels, call(): pl.pallas_call(body, out_shape=[jax.ShapeDtypeStruct(shape, dtype) for sh...  7.09 us
    ppermute x2, waiting for transfers between devices, attention(): other = lax.ppermute(mine, ALL, [(i, i ^ 1) for i in range(devices)])  1.26 us
  transfers between devices with their start and end apart: 2, of which 2 were waited for; matrix products, arithmetic and copies ran while one was open for 0% of the time, Pallas kernels for 3%

profile of v22, /device:TPU:0, one launch (start us, length us, event | category | flops | bytes accessed | tf_op | source)
XLA Modules:
  0.0 54.7 jit_solution(1657227836770539804)
XLA Ops:
  0.6 1.0 %shard_map.95 = bf16[16,48,128]{2,1,0:T(8,128)(2,1)S(1)} custom-call(bf16[1,32,1024]{2,1,0:T(8,128)(2,1)} %q_hbm.1, bf16[1,32,1024]{2,1,0:T(8,128)(2,1)} %k_hbm.1, bf16[1,32,1024]{2,1,0:T(8,128)(2,1)} %v_hbm.1), custom_call_target="tpu_custom_call" | custom-call | tf_op jit(solution)/shard_map/pallas_call | solution.py:256
  1.7 15.9 %all_to_all.20.mine_ref = bf16[16,48,128]{2,1,0:T(8,128)(2,1)S(1)} all-to-all(bf16[16,48,128]{2,1,0:T(8,128)(2,1)S(1)} %shard_map.95), channel_id=1, replica_groups={{11,12,15,16,19,20,23,24,27,28,31,0,3,4,7,8},{9,10,13,14,17,18,21,22,25..., dimensions={0} | all-to-all | bytes 393216 | tf_op jit(solution)/shard_map/all_to_all | solution.py:278
  17.5 0.0 collective-permute-start
  17.5 0.8 %shard_map.96 = (bf16[512,128]{1,0:T(8,128)(2,1)S(1)}, f32[512,128]{1,0:T(8,128)S(1)}, f32[512,128]{1,0:T(8,128)S(1)}) custom-call(bf16[16,48,128]{2,1,0:T(8,128)(2,1)S(1)} %all_to_all.20.mine_ref), custom_call_target="tpu_custom_call" | custom-call | flops 1073741824 | bytes 1048576 | tf_op jit(solution)/shard_map/pallas_call | solution.py:256
  18.3 0.7 %collective-permute-done.other_ref = bf16[16,48,128]{2,1,0:T(8,128)(2,1)S(1)} collective-permute-done((bf16[16,48,128]{2,1,0:T(8,128)(2,1)S(1)}, bf16[16,48,128]{2,1,0:T(8,128)(2,1)S(1)}, u32[]{:S(2)}, u32[]{:S(2)}) %collective-permute-start) | collective-permute-done | bytes 196640 | tf_op jit(solution)/shard_map/ppermute | solution.py:282
  19.0 0.0 slice-start
  19.0 0.0 slice-start.1
  19.0 0.0 copy-start.1
  19.0 0.0 copy-start.2
  19.0 0.0 copy-start.3
  19.0 0.8 %shard_map.97 = bf16[16,16,128]{2,1,0:T(8,128)(2,1)S(1)} custom-call(bf16[16,48,128]{2,1,0:T(8,128)(2,1)S(1)} %collective-permute-done.other_ref, bf16[512,128]{1,0:T(8,128)(2,1)S(1)} %get-tuple-element.10.query_ref, f32[512,128]{1,0:T(8,128)S(1)} %get-tuple-element.11.peak_ref, f32[512,128]{1,0:T(8,128)S(1)} %get-tuple-element.12.sum_ref), custom_call_target="tpu_custom_call" | custom-call | flops 17179869184 | bytes 41943040 | tf_op jit(solution)/shard_map/pallas_call | solution.py:256
  19.9 9.5 %all_to_all.21.got_ref = bf16[16,16,128]{2,1,0:T(8,128)(2,1)S(1)} all-to-all(bf16[16,16,128]{2,1,0:T(8,128)(2,1)S(1)} %shard_map.97), channel_id=1, replica_groups={{11,12,15,16,19,20,23,24,27,28,31,0,3,4,7,8},{9,10,13,14,17,18,21,22,25..., dimensions={0} | all-to-all | bytes 131072 | tf_op jit(solution)/shard_map/all_to_all | solution.py:278
  29.4 0.0 slice-done
  29.4 0.0 slice-done.1
  29.4 0.0 copy-done.1
  29.4 0.0 copy-done.2
  29.4 0.0 copy-done.3
  29.4 1.7 %shard_map.98 = (f32[1,32,1024]{2,1,0:T(8,128)}, bf16[16,48,128]{2,1,0:T(8,128)(2,1)S(1)}) custom-call(bf16[16,16,128]{2,1,0:T(8,128)(2,1)S(1)} %all_to_all.21.got_ref, bf16[1,32,1024]{2,1,0:T(8,128)(2,1)S(1)} %copy-done.2, bf16[1024,1024]{1,0:T(8,128)(2,1)S(1)} %copy-done.1, f32[1,1024]{1,0:T(1,128)S(1)} %bitcast.3, bf16[1024,3072]{1,0:T(8,128)(2,1)S(1)} %bitcast.2), custom_call_target="tpu_custom_call" | custom-call | tf_op jit(solution)/shard_map/pallas_call | solution.py:256
  31.1 10.8 %all_to_all.22.mine_ref = bf16[16,48,128]{2,1,0:T(8,128)(2,1)S(1)} all-to-all(bf16[16,48,128]{2,1,0:T(8,128)(2,1)S(1)} %get-tuple-element.14), channel_id=1, replica_groups={{11,12,15,16,19,20,23,24,27,28,31,0,3,4,7,8},{9,10,13,14,17,18,21,22,25..., dimensions={0} | all-to-all | bytes 393216 | tf_op jit(solution)/shard_map/all_to_all | solution.py:278
  42.0 0.1 collective-permute-start.1
  42.1 0.7 %shard_map.99 = (bf16[512,128]{1,0:T(8,128)(2,1)S(1)}, f32[512,128]{1,0:T(8,128)S(1)}, f32[512,128]{1,0:T(8,128)S(1)}) custom-call(bf16[16,48,128]{2,1,0:T(8,128)(2,1)S(1)} %all_to_all.22.mine_ref), custom_call_target="tpu_custom_call" | custom-call | flops 1073741824 | bytes 1048576 | tf_op jit(solution)/shard_map/pallas_call | solution.py:256
  42.8 0.6 %collective-permute-done.1.other_ref = bf16[16,48,128]{2,1,0:T(8,128)(2,1)S(1)} collective-permute-done((bf16[16,48,128]{2,1,0:T(8,128)(2,1)S(1)}, bf16[16,48,128]{2,1,0:T(8,128)(2,1)S(1)}, u32[]{:S(2)}, u32[]{:S(2)}) %collective-permute-start.1) | collective-permute-done | bytes 196640 | tf_op jit(solution)/shard_map/ppermute | solution.py:282
  43.4 0.0 copy-start
  43.4 0.8 %shard_map.100 = bf16[16,16,128]{2,1,0:T(8,128)(2,1)S(1)} custom-call(bf16[16,48,128]{2,1,0:T(8,128)(2,1)S(1)} %collective-permute-done.1.other_ref, bf16[512,128]{1,0:T(8,128)(2,1)S(1)} %get-tuple-element.15.query_ref, f32[512,128]{1,0:T(8,128)S(1)} %get-tuple-element.16.peak_ref, f32[512,128]{1,0:T(8,128)S(1)} %get-tuple-element.17.sum_ref), custom_call_target="tpu_custom_call" | custom-call | flops 17179869184 | bytes 41943040 | tf_op jit(solution)/shard_map/pallas_call | solution.py:256
  44.3 9.3 %all_to_all.23.got_ref = bf16[16,16,128]{2,1,0:T(8,128)(2,1)S(1)} all-to-all(bf16[16,16,128]{2,1,0:T(8,128)(2,1)S(1)} %shard_map.100), channel_id=1, replica_groups={{11,12,15,16,19,20,23,24,27,28,31,0,3,4,7,8},{9,10,13,14,17,18,21,22,25..., dimensions={0} | all-to-all | bytes 131072 | tf_op jit(solution)/shard_map/all_to_all | solution.py:278
  53.5 0.0 copy-done
  53.5 1.2 %shard_map.101 = f32[1,32,1024]{2,1,0:T(8,128)} custom-call(bf16[16,16,128]{2,1,0:T(8,128)(2,1)S(1)} %all_to_all.23.got_ref, bf16[1024,1024]{1,0:T(8,128)(2,1)S(1)} %copy-done), custom_call_target="tpu_custom_call" | custom-call | tf_op jit(solution)/shard_map/pallas_call | solution.py:256
  (1 shorter events, 0.0 us)
Async XLA Ops:
  17.5 1.4 %collective-permute-start = (bf16[16,48,128]{2,1,0:T(8,128)(2,1)S(1)}, bf16[16,48,128]{2,1,0:T(8,128)(2,1)S(1)}, u32[]{:S(2)}, u32[]{:S(2)}) collective-permute-start(bf16[16,48,128]{2,1,0:T(8,128)(2,1)S(1)} %all_to_all.20.mine_ref), channel_id=1, source_target_pairs={{0,1},{1,0},{2,3},{3,2},{4,5},{5,4},{6,7},{7,6},{8,9},{9,8},{10,11... | collective-permute-start | bytes 589832 | tf_op jit(solution)/shard_map/ppermute | solution.py:282
  19.0 10.4 %slice-start = ((s8[6291456]{0:T(1024)(128)(4,1)}), s8[4194304]{0:T(1024)(128)(4,1)S(1)}, s32[]{:S(2)}) async-start(s8[6291456]{0:T(1024)(128)(4,1)} %bitcast.1), calls=%async_computation.4 | async-start | bytes 8388608
  19.0 10.4 %slice-start.1 = ((s8[6291456]{0:T(1024)(128)(4,1)}), s8[2097152]{0:T(1024)(128)(4,1)S(1)}, s32[]{:S(2)}) async-start(s8[6291456]{0:T(1024)(128)(4,1)} %bitcast.1), calls=%async_computation.5 | async-start | bytes 4194304
  19.0 10.4 %copy-start.1 = (bf16[1024,1024]{1,0:T(8,128)(2,1)S(1)}, bf16[1024,1024]{1,0:T(8,128)(2,1)}, u32[]{:S(2)}) copy-start(bf16[1024,1024]{1,0:T(8,128)(2,1)} %wv_ref.1) | copy-start | bytes 6291460
  19.0 10.4 %copy-start.2 = (bf16[1,32,1024]{2,1,0:T(8,128)(2,1)S(1)}, bf16[1,32,1024]{2,1,0:T(8,128)(2,1)}, u32[]{:S(2)}) copy-start(bf16[1,32,1024]{2,1,0:T(8,128)(2,1)} %x2_ref.1) | copy-start | bytes 196612
  19.0 10.4 %copy-start.3 = (f32[1024]{0:T(1024)S(1)}, f32[1024]{0:T(1024)}, u32[]{:S(2)}) copy-start(f32[1024]{0:T(1024)} %param.14) | copy-start | bytes 12292
  42.0 1.4 %collective-permute-start.1 = (bf16[16,48,128]{2,1,0:T(8,128)(2,1)S(1)}, bf16[16,48,128]{2,1,0:T(8,128)(2,1)S(1)}, u32[]{:S(2)}, u32[]{:S(2)}) collective-permute-start(bf16[16,48,128]{2,1,0:T(8,128)(2,1)S(1)} %all_to_all.22.mine_ref), channel_id=1, source_target_pairs={{0,1},{1,0},{2,3},{3,2},{4,5},{5,4},{6,7},{7,6},{8,9},{9,8},{10,11... | collective-permute-start | bytes 589832 | tf_op jit(solution)/shard_map/ppermute | solution.py:282
  43.4 10.1 %copy-start = (bf16[1024,1024]{1,0:T(8,128)(2,1)S(1)}, bf16[1024,1024]{1,0:T(8,128)(2,1)}, u32[]{:S(2)}) copy-start(bf16[1024,1024]{1,0:T(8,128)(2,1)} %wout_ref.1) | copy-start | bytes 6291460

commit v23 on v22

--- a/solution.py
+++ b/solution.py
@@ -108,7 +108,7 @@
 
 ALL = ("view", "tok")
 CORES = 2
-MIDDLE = HEADS // 4
+MIDDLE = HEADS // 2
 SHARP = HD ** (-0.5) * 1.4426950408889634
 
 

time: 55 us -> 54.2 us (0.985)
  blocking collectives: 45.5 us -> 44.7 us
    all_to_all x4, blocking collectives: 45.5 us -> 44.7 us  [trade(): lax.all_to_all(piece, ALL, split_axis=0, concat_axis=0, tiled=True, axis_...]
where the time goes in v23:
time: 54.2 us; the launch traced here: 53.9 us
  blocking collectives  44.7 us (82%)
  Pallas kernels  7.1 us (13%)
  waiting for transfers between devices  1.25 us (2%)
  between operations  0.72 us (1%)
    all_to_all x4, blocking collectives, trade(): lax.all_to_all(piece, ALL, split_axis=0, concat_axis=0, tiled=True, axis_...  44.7 us
    pallas_call x7, Pallas kernels, call(): pl.pallas_call(body, out_shape=[jax.ShapeDtypeStruct(shape, dtype) for sh...  7.1 us
    ppermute x2, waiting for transfers between devices, attention(): other = lax.ppermute(mine, ALL, [(i, i ^ 1) for i in range(devices)])  1.25 us
  transfers between devices with their start and end apart: 2, of which 2 were waited for; matrix products, arithmetic and copies ran while one was open for 0% of the time, Pallas kernels for 3%

profile of v23, /device:TPU:0, one launch (start us, length us, event | category | flops | bytes accessed | tf_op | source)
XLA Modules:
  0.0 53.9 jit_solution(8850463300021380558)
XLA Ops:
  0.6 1.0 %shard_map.95 = bf16[16,48,128]{2,1,0:T(8,128)(2,1)S(1)} custom-call(bf16[1,32,1024]{2,1,0:T(8,128)(2,1)} %q_hbm.1, bf16[1,32,1024]{2,1,0:T(8,128)(2,1)} %k_hbm.1, bf16[1,32,1024]{2,1,0:T(8,128)(2,1)} %v_hbm.1), custom_call_target="tpu_custom_call" | custom-call | tf_op jit(solution)/shard_map/pallas_call | solution.py:256
  1.7 15.0 %all_to_all.20.mine_ref = bf16[16,48,128]{2,1,0:T(8,128)(2,1)S(1)} all-to-all(bf16[16,48,128]{2,1,0:T(8,128)(2,1)S(1)} %shard_map.95), channel_id=1, replica_groups={{19,20,23,24,27,28,31,0,3,4,7,8,11,12,15,16},{17,18,21,22,25,26,29,30,1..., dimensions={0} | all-to-all | bytes 393216 | tf_op jit(solution)/shard_map/all_to_all | solution.py:278
  16.6 0.0 collective-permute-start
  16.6 0.8 %shard_map.96 = (bf16[512,128]{1,0:T(8,128)(2,1)S(1)}, f32[512,128]{1,0:T(8,128)S(1)}, f32[512,128]{1,0:T(8,128)S(1)}) custom-call(bf16[16,48,128]{2,1,0:T(8,128)(2,1)S(1)} %all_to_all.20.mine_ref), custom_call_target="tpu_custom_call" | custom-call | flops 1073741824 | bytes 1048576 | tf_op jit(solution)/shard_map/pallas_call | solution.py:256
  17.4 0.7 %collective-permute-done.other_ref = bf16[16,48,128]{2,1,0:T(8,128)(2,1)S(1)} collective-permute-done((bf16[16,48,128]{2,1,0:T(8,128)(2,1)S(1)}, bf16[16,48,128]{2,1,0:T(8,128)(2,1)S(1)}, u32[]{:S(2)}, u32[]{:S(2)}) %collective-permute-start) | collective-permute-done | bytes 196640 | tf_op jit(solution)/shard_map/ppermute | solution.py:282
  18.1 0.0 slice-start
  18.1 0.0 slice-start.1
  18.1 0.0 copy-start.1
  18.1 0.0 copy-start.2
  18.1 0.0 copy-start.3
  18.1 0.8 %shard_map.97 = bf16[16,16,128]{2,1,0:T(8,128)(2,1)S(1)} custom-call(bf16[16,48,128]{2,1,0:T(8,128)(2,1)S(1)} %collective-permute-done.other_ref, bf16[512,128]{1,0:T(8,128)(2,1)S(1)} %get-tuple-element.10.query_ref, f32[512,128]{1,0:T(8,128)S(1)} %get-tuple-element.11.peak_ref, f32[512,128]{1,0:T(8,128)S(1)} %get-tuple-element.12.sum_ref), custom_call_target="tpu_custom_call" | custom-call | flops 17179869184 | bytes 41943040 | tf_op jit(solution)/shard_map/pallas_call | solution.py:256
  19.0 9.5 %all_to_all.21.got_ref = bf16[16,16,128]{2,1,0:T(8,128)(2,1)S(1)} all-to-all(bf16[16,16,128]{2,1,0:T(8,128)(2,1)S(1)} %shard_map.97), channel_id=1, replica_groups={{19,20,23,24,27,28,31,0,3,4,7,8,11,12,15,16},{17,18,21,22,25,26,29,30,1..., dimensions={0} | all-to-all | bytes 131072 | tf_op jit(solution)/shard_map/all_to_all | solution.py:278
  28.5 0.0 slice-done
  28.5 0.0 slice-done.1
  28.5 0.0 copy-done.1
  28.5 0.0 copy-done.2
  28.5 0.0 copy-done.3
  28.5 1.7 %shard_map.98 = (f32[1,32,1024]{2,1,0:T(8,128)}, bf16[16,48,128]{2,1,0:T(8,128)(2,1)S(1)}) custom-call(bf16[16,16,128]{2,1,0:T(8,128)(2,1)S(1)} %all_to_all.21.got_ref, bf16[1,32,1024]{2,1,0:T(8,128)(2,1)S(1)} %copy-done.2, bf16[1024,1024]{1,0:T(8,128)(2,1)S(1)} %copy-done.1, f32[1,1024]{1,0:T(1,128)S(1)} %bitcast.3, bf16[1024,3072]{1,0:T(8,128)(2,1)S(1)} %bitcast.2), custom_call_target="tpu_custom_call" | custom-call | tf_op jit(solution)/shard_map/pallas_call | solution.py:256
  30.2 10.9 %all_to_all.22.mine_ref = bf16[16,48,128]{2,1,0:T(8,128)(2,1)S(1)} all-to-all(bf16[16,48,128]{2,1,0:T(8,128)(2,1)S(1)} %get-tuple-element.14), channel_id=1, replica_groups={{19,20,23,24,27,28,31,0,3,4,7,8,11,12,15,16},{17,18,21,22,25,26,29,30,1..., dimensions={0} | all-to-all | bytes 393216 | tf_op jit(solution)/shard_map/all_to_all | solution.py:278
  41.2 0.1 collective-permute-start.1
  41.3 0.8 %shard_map.99 = (bf16[512,128]{1,0:T(8,128)(2,1)S(1)}, f32[512,128]{1,0:T(8,128)S(1)}, f32[512,128]{1,0:T(8,128)S(1)}) custom-call(bf16[16,48,128]{2,1,0:T(8,128)(2,1)S(1)} %all_to_all.22.mine_ref), custom_call_target="tpu_custom_call" | custom-call | flops 1073741824 | bytes 1048576 | tf_op jit(solution)/shard_map/pallas_call | solution.py:256
  42.0 0.6 %collective-permute-done.1.other_ref = bf16[16,48,128]{2,1,0:T(8,128)(2,1)S(1)} collective-permute-done((bf16[16,48,128]{2,1,0:T(8,128)(2,1)S(1)}, bf16[16,48,128]{2,1,0:T(8,128)(2,1)S(1)}, u32[]{:S(2)}, u32[]{:S(2)}) %collective-permute-start.1) | collective-permute-done | bytes 196640 | tf_op jit(solution)/shard_map/ppermute | solution.py:282
  42.6 0.0 copy-start
  42.6 0.8 %shard_map.100 = bf16[16,16,128]{2,1,0:T(8,128)(2,1)S(1)} custom-call(bf16[16,48,128]{2,1,0:T(8,128)(2,1)S(1)} %collective-permute-done.1.other_ref, bf16[512,128]{1,0:T(8,128)(2,1)S(1)} %get-tuple-element.15.query_ref, f32[512,128]{1,0:T(8,128)S(1)} %get-tuple-element.16.peak_ref, f32[512,128]{1,0:T(8,128)S(1)} %get-tuple-element.17.sum_ref), custom_call_target="tpu_custom_call" | custom-call | flops 17179869184 | bytes 41943040 | tf_op jit(solution)/shard_map/pallas_call | solution.py:256
  43.4 9.3 %all_to_all.23.got_ref = bf16[16,16,128]{2,1,0:T(8,128)(2,1)S(1)} all-to-all(bf16[16,16,128]{2,1,0:T(8,128)(2,1)S(1)} %shard_map.100), channel_id=1, replica_groups={{19,20,23,24,27,28,31,0,3,4,7,8,11,12,15,16},{17,18,21,22,25,26,29,30,1..., dimensions={0} | all-to-all | bytes 131072 | tf_op jit(solution)/shard_map/all_to_all | solution.py:278
  52.7 0.0 copy-done
  52.7 1.2 %shard_map.101 = f32[1,32,1024]{2,1,0:T(8,128)} custom-call(bf16[16,16,128]{2,1,0:T(8,128)(2,1)S(1)} %all_to_all.23.got_ref, bf16[1024,1024]{1,0:T(8,128)(2,1)S(1)} %copy-done), custom_call_target="tpu_custom_call" | custom-call | tf_op jit(solution)/shard_map/pallas_call | solution.py:256
  (1 shorter events, 0.0 us)
Async XLA Ops:
  16.6 1.4 %collective-permute-start = (bf16[16,48,128]{2,1,0:T(8,128)(2,1)S(1)}, bf16[16,48,128]{2,1,0:T(8,128)(2,1)S(1)}, u32[]{:S(2)}, u32[]{:S(2)}) collective-permute-start(bf16[16,48,128]{2,1,0:T(8,128)(2,1)S(1)} %all_to_all.20.mine_ref), channel_id=1, source_target_pairs={{0,1},{1,0},{2,3},{3,2},{4,5},{5,4},{6,7},{7,6},{8,9},{9,8},{10,11... | collective-permute-start | bytes 589832 | tf_op jit(solution)/shard_map/ppermute | solution.py:282
  18.1 10.4 %slice-start = ((s8[6291456]{0:T(1024)(128)(4,1)}), s8[4194304]{0:T(1024)(128)(4,1)S(1)}, s32[]{:S(2)}) async-start(s8[6291456]{0:T(1024)(128)(4,1)} %bitcast.1), calls=%async_computation.4 | async-start | bytes 8388608
  18.1 10.4 %slice-start.1 = ((s8[6291456]{0:T(1024)(128)(4,1)}), s8[2097152]{0:T(1024)(128)(4,1)S(1)}, s32[]{:S(2)}) async-start(s8[6291456]{0:T(1024)(128)(4,1)} %bitcast.1), calls=%async_computation.5 | async-start | bytes 4194304
  18.1 10.4 %copy-start.1 = (bf16[1024,1024]{1,0:T(8,128)(2,1)S(1)}, bf16[1024,1024]{1,0:T(8,128)(2,1)}, u32[]{:S(2)}) copy-start(bf16[1024,1024]{1,0:T(8,128)(2,1)} %wv_ref.1) | copy-start | bytes 6291460
  18.1 10.4 %copy-start.2 = (bf16[1,32,1024]{2,1,0:T(8,128)(2,1)S(1)}, bf16[1,32,1024]{2,1,0:T(8,128)(2,1)}, u32[]{:S(2)}) copy-start(bf16[1,32,1024]{2,1,0:T(8,128)(2,1)} %x2_ref.1) | copy-start | bytes 196612
  18.1 10.4 %copy-start.3 = (f32[1024]{0:T(1024)S(1)}, f32[1024]{0:T(1024)}, u32[]{:S(2)}) copy-start(f32[1024]{0:T(1024)} %param.14) | copy-start | bytes 12292
  41.2 1.4 %collective-permute-start.1 = (bf16[16,48,128]{2,1,0:T(8,128)(2,1)S(1)}, bf16[16,48,128]{2,1,0:T(8,128)(2,1)S(1)}, u32[]{:S(2)}, u32[]{:S(2)}) collective-permute-start(bf16[16,48,128]{2,1,0:T(8,128)(2,1)S(1)} %all_to_all.22.mine_ref), channel_id=1, source_target_pairs={{0,1},{1,0},{2,3},{3,2},{4,5},{5,4},{6,7},{7,6},{8,9},{9,8},{10,11... | collective-permute-start | bytes 589832 | tf_op jit(solution)/shard_map/ppermute | solution.py:282
  42.6 10.1 %copy-start = (bf16[1024,1024]{1,0:T(8,128)(2,1)S(1)}, bf16[1024,1024]{1,0:T(8,128)(2,1)}, u32[]{:S(2)}) copy-start(bf16[1024,1024]{1,0:T(8,128)(2,1)} %wout_ref.1) | copy-start | bytes 6291460

commit v24 on v23

--- a/solution.py
+++ b/solution.py
@@ -108,7 +108,7 @@
 
 ALL = ("view", "tok")
 CORES = 2
-MIDDLE = HEADS // 2
+MIDDLE = HEADS // 2 + 2
 SHARP = HD ** (-0.5) * 1.4426950408889634
 
 

time: 54.2 us -> 53.3 us (0.983)
  blocking collectives: 44.7 us -> 43.8 us
    all_to_all x4, blocking collectives: 44.7 us -> 43.8 us  [trade(): lax.all_to_all(piece, ALL, split_axis=0, concat_axis=0, tiled=True, axis_...]
where the time goes in v24:
time: 53.3 us; the launch traced here: 53 us
  blocking collectives  43.8 us (82%)
  Pallas kernels  7.11 us (13%)
  waiting for transfers between devices  1.23 us (2%)
  between operations  0.72 us (1%)
    all_to_all x4, blocking collectives, trade(): lax.all_to_all(piece, ALL, split_axis=0, concat_axis=0, tiled=True, axis_...  43.8 us
    pallas_call x7, Pallas kernels, call(): pl.pallas_call(body, out_shape=[jax.ShapeDtypeStruct(shape, dtype) for sh...  7.11 us
    ppermute x2, waiting for transfers between devices, attention(): other = lax.ppermute(mine, ALL, [(i, i ^ 1) for i in range(devices)])  1.23 us
  transfers between devices with their start and end apart: 2, of which 2 were waited for; matrix products, arithmetic and copies ran while one was open for 0% of the time, Pallas kernels for 3%

profile of v24, /device:TPU:0, one launch (start us, length us, event | category | flops | bytes accessed | tf_op | source)
XLA Modules:
  0.0 53.0 jit_solution(5025289643952788127)
XLA Ops:
  0.6 1.0 %shard_map.95 = bf16[16,48,128]{2,1,0:T(8,128)(2,1)S(1)} custom-call(bf16[1,32,1024]{2,1,0:T(8,128)(2,1)} %q_hbm.1, bf16[1,32,1024]{2,1,0:T(8,128)(2,1)} %k_hbm.1, bf16[1,32,1024]{2,1,0:T(8,128)(2,1)} %v_hbm.1), custom_call_target="tpu_custom_call" | custom-call | tf_op jit(solution)/shard_map/pallas_call | solution.py:256
  1.7 14.1 %all_to_all.20.mine_ref = bf16[16,48,128]{2,1,0:T(8,128)(2,1)S(1)} all-to-all(bf16[16,48,128]{2,1,0:T(8,128)(2,1)S(1)} %shard_map.95), channel_id=1, replica_groups={{23,24,27,28,31,0,3,4,7,8,11,12,15,16,19,20},{21,22,25,26,29,30,1,2,5,6..., dimensions={0} | all-to-all | bytes 393216 | tf_op jit(solution)/shard_map/all_to_all | solution.py:278
  15.7 0.0 collective-permute-start
  15.7 0.8 %shard_map.96 = (bf16[512,128]{1,0:T(8,128)(2,1)S(1)}, f32[512,128]{1,0:T(8,128)S(1)}, f32[512,128]{1,0:T(8,128)S(1)}) custom-call(bf16[16,48,128]{2,1,0:T(8,128)(2,1)S(1)} %all_to_all.20.mine_ref), custom_call_target="tpu_custom_call" | custom-call | flops 1073741824 | bytes 1048576 | tf_op jit(solution)/shard_map/pallas_call | solution.py:256
  16.5 0.7 %collective-permute-done.other_ref = bf16[16,48,128]{2,1,0:T(8,128)(2,1)S(1)} collective-permute-done((bf16[16,48,128]{2,1,0:T(8,128)(2,1)S(1)}, bf16[16,48,128]{2,1,0:T(8,128)(2,1)S(1)}, u32[]{:S(2)}, u32[]{:S(2)}) %collective-permute-start) | collective-permute-done | bytes 196640 | tf_op jit(solution)/shard_map/ppermute | solution.py:282
  17.2 0.0 slice-start
  17.2 0.0 slice-start.1
  17.2 0.0 copy-start.1
  17.2 0.0 copy-start.2
  17.2 0.0 copy-start.3
  17.2 0.8 %shard_map.97 = bf16[16,16,128]{2,1,0:T(8,128)(2,1)S(1)} custom-call(bf16[16,48,128]{2,1,0:T(8,128)(2,1)S(1)} %collective-permute-done.other_ref, bf16[512,128]{1,0:T(8,128)(2,1)S(1)} %get-tuple-element.10.query_ref, f32[512,128]{1,0:T(8,128)S(1)} %get-tuple-element.11.peak_ref, f32[512,128]{1,0:T(8,128)S(1)} %get-tuple-element.12.sum_ref), custom_call_target="tpu_custom_call" | custom-call | flops 17179869184 | bytes 41943040 | tf_op jit(solution)/shard_map/pallas_call | solution.py:256
  18.1 9.5 %all_to_all.21.got_ref = bf16[16,16,128]{2,1,0:T(8,128)(2,1)S(1)} all-to-all(bf16[16,16,128]{2,1,0:T(8,128)(2,1)S(1)} %shard_map.97), channel_id=1, replica_groups={{23,24,27,28,31,0,3,4,7,8,11,12,15,16,19,20},{21,22,25,26,29,30,1,2,5,6..., dimensions={0} | all-to-all | bytes 131072 | tf_op jit(solution)/shard_map/all_to_all | solution.py:278
  27.6 0.0 slice-done
  27.6 0.0 slice-done.1
  27.6 0.0 copy-done.1
  27.6 0.0 copy-done.2
  27.6 0.0 copy-done.3
  27.6 1.7 %shard_map.98 = (f32[1,32,1024]{2,1,0:T(8,128)}, bf16[16,48,128]{2,1,0:T(8,128)(2,1)S(1)}) custom-call(bf16[16,16,128]{2,1,0:T(8,128)(2,1)S(1)} %all_to_all.21.got_ref, bf16[1,32,1024]{2,1,0:T(8,128)(2,1)S(1)} %copy-done.2, bf16[1024,1024]{1,0:T(8,128)(2,1)S(1)} %copy-done.1, f32[1,1024]{1,0:T(1,128)S(1)} %bitcast.3, bf16[1024,3072]{1,0:T(8,128)(2,1)S(1)} %bitcast.2), custom_call_target="tpu_custom_call" | custom-call | tf_op jit(solution)/shard_map/pallas_call | solution.py:256
  29.3 10.9 %all_to_all.22.mine_ref = bf16[16,48,128]{2,1,0:T(8,128)(2,1)S(1)} all-to-all(bf16[16,48,128]{2,1,0:T(8,128)(2,1)S(1)} %get-tuple-element.14), channel_id=1, replica_groups={{23,24,27,28,31,0,3,4,7,8,11,12,15,16,19,20},{21,22,25,26,29,30,1,2,5,6..., dimensions={0} | all-to-all | bytes 393216 | tf_op jit(solution)/shard_map/all_to_all | solution.py:278
  40.3 0.1 collective-permute-start.1
  40.4 0.8 %shard_map.99 = (bf16[512,128]{1,0:T(8,128)(2,1)S(1)}, f32[512,128]{1,0:T(8,128)S(1)}, f32[512,128]{1,0:T(8,128)S(1)}) custom-call(bf16[16,48,128]{2,1,0:T(8,128)(2,1)S(1)} %all_to_all.22.mine_ref), custom_call_target="tpu_custom_call" | custom-call | flops 1073741824 | bytes 1048576 | tf_op jit(solution)/shard_map/pallas_call | solution.py:256
  41.1 0.6 %collective-permute-done.1.other_ref = bf16[16,48,128]{2,1,0:T(8,128)(2,1)S(1)} collective-permute-done((bf16[16,48,128]{2,1,0:T(8,128)(2,1)S(1)}, bf16[16,48,128]{2,1,0:T(8,128)(2,1)S(1)}, u32[]{:S(2)}, u32[]{:S(2)}) %collective-permute-start.1) | collective-permute-done | bytes 196640 | tf_op jit(solution)/shard_map/ppermute | solution.py:282
  41.7 0.0 copy-start
  41.7 0.8 %shard_map.100 = bf16[16,16,128]{2,1,0:T(8,128)(2,1)S(1)} custom-call(bf16[16,48,128]{2,1,0:T(8,128)(2,1)S(1)} %collective-permute-done.1.other_ref, bf16[512,128]{1,0:T(8,128)(2,1)S(1)} %get-tuple-element.15.query_ref, f32[512,128]{1,0:T(8,128)S(1)} %get-tuple-element.16.peak_ref, f32[512,128]{1,0:T(8,128)S(1)} %get-tuple-element.17.sum_ref), custom_call_target="tpu_custom_call" | custom-call | flops 17179869184 | bytes 41943040 | tf_op jit(solution)/shard_map/pallas_call | solution.py:256
  42.5 9.3 %all_to_all.23.got_ref = bf16[16,16,128]{2,1,0:T(8,128)(2,1)S(1)} all-to-all(bf16[16,16,128]{2,1,0:T(8,128)(2,1)S(1)} %shard_map.100), channel_id=1, replica_groups={{23,24,27,28,31,0,3,4,7,8,11,12,15,16,19,20},{21,22,25,26,29,30,1,2,5,6..., dimensions={0} | all-to-all | bytes 131072 | tf_op jit(solution)/shard_map/all_to_all | solution.py:278
  51.8 0.0 copy-done
  51.8 1.2 %shard_map.101 = f32[1,32,1024]{2,1,0:T(8,128)} custom-call(bf16[16,16,128]{2,1,0:T(8,128)(2,1)S(1)} %all_to_all.23.got_ref, bf16[1024,1024]{1,0:T(8,128)(2,1)S(1)} %copy-done), custom_call_target="tpu_custom_call" | custom-call | tf_op jit(solution)/shard_map/pallas_call | solution.py:256
  (1 shorter events, 0.0 us)
Async XLA Ops:
  15.7 1.4 %collective-permute-start = (bf16[16,48,128]{2,1,0:T(8,128)(2,1)S(1)}, bf16[16,48,128]{2,1,0:T(8,128)(2,1)S(1)}, u32[]{:S(2)}, u32[]{:S(2)}) collective-permute-start(bf16[16,48,128]{2,1,0:T(8,128)(2,1)S(1)} %all_to_all.20.mine_ref), channel_id=1, source_target_pairs={{0,1},{1,0},{2,3},{3,2},{4,5},{5,4},{6,7},{7,6},{8,9},{9,8},{10,11... | collective-permute-start | bytes 589832 | tf_op jit(solution)/shard_map/ppermute | solution.py:282
  17.2 10.4 %slice-start = ((s8[6291456]{0:T(1024)(128)(4,1)}), s8[4194304]{0:T(1024)(128)(4,1)S(1)}, s32[]{:S(2)}) async-start(s8[6291456]{0:T(1024)(128)(4,1)} %bitcast.1), calls=%async_computation.4 | async-start | bytes 8388608
  17.2 10.4 %slice-start.1 = ((s8[6291456]{0:T(1024)(128)(4,1)}), s8[2097152]{0:T(1024)(128)(4,1)S(1)}, s32[]{:S(2)}) async-start(s8[6291456]{0:T(1024)(128)(4,1)} %bitcast.1), calls=%async_computation.5 | async-start | bytes 4194304
  17.2 10.4 %copy-start.1 = (bf16[1024,1024]{1,0:T(8,128)(2,1)S(1)}, bf16[1024,1024]{1,0:T(8,128)(2,1)}, u32[]{:S(2)}) copy-start(bf16[1024,1024]{1,0:T(8,128)(2,1)} %wv_ref.1) | copy-start | bytes 6291460
  17.2 10.4 %copy-start.2 = (bf16[1,32,1024]{2,1,0:T(8,128)(2,1)S(1)}, bf16[1,32,1024]{2,1,0:T(8,128)(2,1)}, u32[]{:S(2)}) copy-start(bf16[1,32,1024]{2,1,0:T(8,128)(2,1)} %x2_ref.1) | copy-start | bytes 196612
  17.2 10.4 %copy-start.3 = (f32[1024]{0:T(1024)S(1)}, f32[1024]{0:T(1024)}, u32[]{:S(2)}) copy-start(f32[1024]{0:T(1024)} %param.14) | copy-start | bytes 12292
  40.3 1.4 %collective-permute-start.1 = (bf16[16,48,128]{2,1,0:T(8,128)(2,1)S(1)}, bf16[16,48,128]{2,1,0:T(8,128)(2,1)S(1)}, u32[]{:S(2)}, u32[]{:S(2)}) collective-permute-start(bf16[16,48,128]{2,1,0:T(8,128)(2,1)S(1)} %all_to_all.22.mine_ref), channel_id=1, source_target_pairs={{0,1},{1,0},{2,3},{3,2},{4,5},{5,4},{6,7},{7,6},{8,9},{9,8},{10,11... | collective-permute-start | bytes 589832 | tf_op jit(solution)/shard_map/ppermute | solution.py:282
  41.7 10.1 %copy-start = (bf16[1024,1024]{1,0:T(8,128)(2,1)S(1)}, bf16[1024,1024]{1,0:T(8,128)(2,1)}, u32[]{:S(2)}) copy-start(bf16[1024,1024]{1,0:T(8,128)(2,1)} %wout_ref.1) | copy-start | bytes 6291460

commit v25 on v24

--- a/solution.py
+++ b/solution.py
@@ -108,16 +108,14 @@
 
 ALL = ("view", "tok")
 CORES = 2
-MIDDLE = HEADS // 2 + 2
+PLANES, ROUND = (2, 3, 0, 1), (2, 3, 1, 0)
 SHARP = HD ** (-0.5) * 1.4426950408889634
 
 
 def trade_groups():
-    groups = []
-    for s in range(CORES):
-        chips = [(MIDDLE + 1 - s + i) % HEADS for i in range(HEADS)]
-        groups.append([chip * CORES + (chip + s) % CORES for chip in chips])
-    return groups
+    chips = [z * len(ROUND) + i for z in PLANES for i in ROUND]
+    turned = chips[1:] + chips[:1]
+    return [[chip * CORES + (chip + s) % CORES for chip in order] for s, order in enumerate((turned, chips))]
 
 
 def first_group():

time: 53.3 us -> 53.3 us (level)
  starting transfers between devices: 0.12 us -> 0.96 us
    ppermute x2, starting transfers between devices: 0.12 us -> 0.96 us  [attention(): other = lax.ppermute(mine, ALL, [(i, i ^ 1) for i in range(devices)])]
where the time goes in v25:
time: 53.3 us; the launch traced here: 53 us
  blocking collectives  43.4 us (81%)
  Pallas kernels  7.09 us (13%)
  starting transfers between devices  0.96 us (2%)
  waiting for transfers between devices  0.82 us (2%)
  between operations  0.72 us (1%)
    all_to_all x4, blocking collectives, trade(): lax.all_to_all(piece, ALL, split_axis=0, concat_axis=0, tiled=True, axis_...  43.4 us
    pallas_call x7, Pallas kernels, call(): pl.pallas_call(body, out_shape=[jax.ShapeDtypeStruct(shape, dtype) for sh...  7.09 us
  transfers between devices with their start and end apart: 2, of which 2 were waited for; matrix products, arithmetic and copies ran while one was open for 0% of the time, Pallas kernels for 3%

profile of v25, /device:TPU:0, one launch (start us, length us, event | category | flops | bytes accessed | tf_op | source)
XLA Modules:
  0.0 53.0 jit_solution(10809943272621935551)
XLA Ops:
  0.6 1.0 %shard_map.95 = bf16[16,48,128]{2,1,0:T(8,128)(2,1)S(1)} custom-call(bf16[1,32,1024]{2,1,0:T(8,128)(2,1)} %q_hbm.1, bf16[1,32,1024]{2,1,0:T(8,128)(2,1)} %k_hbm.1, bf16[1,32,1024]{2,1,0:T(8,128)(2,1)} %v_hbm.1), custom_call_target="tpu_custom_call" | custom-call | tf_op jit(solution)/shard_map/pallas_call | solution.py:254
  1.7 13.5 %all_to_all.20.mine_ref = bf16[16,48,128]{2,1,0:T(8,128)(2,1)S(1)} all-to-all(bf16[16,48,128]{2,1,0:T(8,128)(2,1)S(1)} %shard_map.95), channel_id=1, replica_groups={{23,19,16,28,31,27,24,4,7,3,0,12,15,11,8,20},{21,22,18,17,29,30,26,25,5..., dimensions={0} | all-to-all | bytes 393216 | tf_op jit(solution)/shard_map/all_to_all | solution.py:276
  15.2 0.2 collective-permute-start
  15.3 0.8 %shard_map.96 = (bf16[512,128]{1,0:T(8,128)(2,1)S(1)}, f32[512,128]{1,0:T(8,128)S(1)}, f32[512,128]{1,0:T(8,128)S(1)}) custom-call(bf16[16,48,128]{2,1,0:T(8,128)(2,1)S(1)} %all_to_all.20.mine_ref), custom_call_target="tpu_custom_call" | custom-call | flops 1073741824 | bytes 1048576 | tf_op jit(solution)/shard_map/pallas_call | solution.py:254
  16.1 0.5 collective-permute-done.other_ref
  16.6 0.0 slice-start
  16.6 0.0 slice-start.1
  16.6 0.0 copy-start.1
  16.6 0.0 copy-start.2
  16.6 0.0 copy-start.3
  16.6 0.8 %shard_map.97 = bf16[16,16,128]{2,1,0:T(8,128)(2,1)S(1)} custom-call(bf16[16,48,128]{2,1,0:T(8,128)(2,1)S(1)} %collective-permute-done.other_ref, bf16[512,128]{1,0:T(8,128)(2,1)S(1)} %get-tuple-element.10.query_ref, f32[512,128]{1,0:T(8,128)S(1)} %get-tuple-element.11.peak_ref, f32[512,128]{1,0:T(8,128)S(1)} %get-tuple-element.12.sum_ref), custom_call_target="tpu_custom_call" | custom-call | flops 17179869184 | bytes 41943040 | tf_op jit(solution)/shard_map/pallas_call | solution.py:254
  17.5 10.1 %all_to_all.21.got_ref = bf16[16,16,128]{2,1,0:T(8,128)(2,1)S(1)} all-to-all(bf16[16,16,128]{2,1,0:T(8,128)(2,1)S(1)} %shard_map.97), channel_id=1, replica_groups={{23,19,16,28,31,27,24,4,7,3,0,12,15,11,8,20},{21,22,18,17,29,30,26,25,5..., dimensions={0} | all-to-all | bytes 131072 | tf_op jit(solution)/shard_map/all_to_all | solution.py:276
  27.6 0.0 slice-done
  27.6 0.0 slice-done.1
  27.6 0.0 copy-done.1
  27.6 0.0 copy-done.2
  27.6 0.0 copy-done.3
  27.6 1.7 %shard_map.98 = (f32[1,32,1024]{2,1,0:T(8,128)}, bf16[16,48,128]{2,1,0:T(8,128)(2,1)S(1)}) custom-call(bf16[16,16,128]{2,1,0:T(8,128)(2,1)S(1)} %all_to_all.21.got_ref, bf16[1,32,1024]{2,1,0:T(8,128)(2,1)S(1)} %copy-done.2, bf16[1024,1024]{1,0:T(8,128)(2,1)S(1)} %copy-done.1, f32[1,1024]{1,0:T(1,128)S(1)} %bitcast.3, bf16[1024,3072]{1,0:T(8,128)(2,1)S(1)} %bitcast.2), custom_call_target="tpu_custom_call" | custom-call | tf_op jit(solution)/shard_map/pallas_call | solution.py:254
  29.4 10.3 %all_to_all.22.mine_ref = bf16[16,48,128]{2,1,0:T(8,128)(2,1)S(1)} all-to-all(bf16[16,48,128]{2,1,0:T(8,128)(2,1)S(1)} %get-tuple-element.14), channel_id=1, replica_groups={{23,19,16,28,31,27,24,4,7,3,0,12,15,11,8,20},{21,22,18,17,29,30,26,25,5..., dimensions={0} | all-to-all | bytes 393216 | tf_op jit(solution)/shard_map/all_to_all | solution.py:276
  39.7 0.8 %collective-permute-start.1 = (bf16[16,48,128]{2,1,0:T(8,128)(2,1)S(1)}, bf16[16,48,128]{2,1,0:T(8,128)(2,1)S(1)}, u32[]{:S(2)}, u32[]{:S(2)}) collective-permute-start(bf16[16,48,128]{2,1,0:T(8,128)(2,1)S(1)} %all_to_all.22.mine_ref), channel_id=1, source_target_pairs={{0,1},{1,0},{2,3},{3,2},{4,5},{5,4},{6,7},{7,6},{8,9},{9,8},{10,11... | collective-permute-start | bytes 589832 | tf_op jit(solution)/shard_map/ppermute | solution.py:280
  40.4 0.8 %shard_map.99 = (bf16[512,128]{1,0:T(8,128)(2,1)S(1)}, f32[512,128]{1,0:T(8,128)S(1)}, f32[512,128]{1,0:T(8,128)S(1)}) custom-call(bf16[16,48,128]{2,1,0:T(8,128)(2,1)S(1)} %all_to_all.22.mine_ref), custom_call_target="tpu_custom_call" | custom-call | flops 1073741824 | bytes 1048576 | tf_op jit(solution)/shard_map/pallas_call | solution.py:254
  41.2 0.3 collective-permute-done.1.other_ref
  41.5 0.0 copy-start
  41.5 0.8 %shard_map.100 = bf16[16,16,128]{2,1,0:T(8,128)(2,1)S(1)} custom-call(bf16[16,48,128]{2,1,0:T(8,128)(2,1)S(1)} %collective-permute-done.1.other_ref, bf16[512,128]{1,0:T(8,128)(2,1)S(1)} %get-tuple-element.15.query_ref, f32[512,128]{1,0:T(8,128)S(1)} %get-tuple-element.16.peak_ref, f32[512,128]{1,0:T(8,128)S(1)} %get-tuple-element.17.sum_ref), custom_call_target="tpu_custom_call" | custom-call | flops 17179869184 | bytes 41943040 | tf_op jit(solution)/shard_map/pallas_call | solution.py:254
  42.3 9.5 %all_to_all.23.got_ref = bf16[16,16,128]{2,1,0:T(8,128)(2,1)S(1)} all-to-all(bf16[16,16,128]{2,1,0:T(8,128)(2,1)S(1)} %shard_map.100), channel_id=1, replica_groups={{23,19,16,28,31,27,24,4,7,3,0,12,15,11,8,20},{21,22,18,17,29,30,26,25,5..., dimensions={0} | all-to-all | bytes 131072 | tf_op jit(solution)/shard_map/all_to_all | solution.py:276
  51.8 0.0 copy-done
  51.8 1.2 %shard_map.101 = f32[1,32,1024]{2,1,0:T(8,128)} custom-call(bf16[16,16,128]{2,1,0:T(8,128)(2,1)S(1)} %all_to_all.23.got_ref, bf16[1024,1024]{1,0:T(8,128)(2,1)S(1)} %copy-done), custom_call_target="tpu_custom_call" | custom-call | tf_op jit(solution)/shard_map/pallas_call | solution.py:254
  (1 shorter events, 0.0 us)
Async XLA Ops:
  15.2 1.4 %collective-permute-start = (bf16[16,48,128]{2,1,0:T(8,128)(2,1)S(1)}, bf16[16,48,128]{2,1,0:T(8,128)(2,1)S(1)}, u32[]{:S(2)}, u32[]{:S(2)}) collective-permute-start(bf16[16,48,128]{2,1,0:T(8,128)(2,1)S(1)} %all_to_all.20.mine_ref), channel_id=1, source_target_pairs={{0,1},{1,0},{2,3},{3,2},{4,5},{5,4},{6,7},{7,6},{8,9},{9,8},{10,11... | collective-permute-start | bytes 589832 | tf_op jit(solution)/shard_map/ppermute | solution.py:280
  16.6 11.0 %slice-start = ((s8[6291456]{0:T(1024)(128)(4,1)}), s8[4194304]{0:T(1024)(128)(4,1)S(1)}, s32[]{:S(2)}) async-start(s8[6291456]{0:T(1024)(128)(4,1)} %bitcast.1), calls=%async_computation.4 | async-start | bytes 8388608
  16.6 11.0 %slice-start.1 = ((s8[6291456]{0:T(1024)(128)(4,1)}), s8[2097152]{0:T(1024)(128)(4,1)S(1)}, s32[]{:S(2)}) async-start(s8[6291456]{0:T(1024)(128)(4,1)} %bitcast.1), calls=%async_computation.5 | async-start | bytes 4194304
  16.6 11.0 %copy-start.1 = (bf16[1024,1024]{1,0:T(8,128)(2,1)S(1)}, bf16[1024,1024]{1,0:T(8,128)(2,1)}, u32[]{:S(2)}) copy-start(bf16[1024,1024]{1,0:T(8,128)(2,1)} %wv_ref.1) | copy-start | bytes 6291460
  16.6 11.0 %copy-start.2 = (bf16[1,32,1024]{2,1,0:T(8,128)(2,1)S(1)}, bf16[1,32,1024]{2,1,0:T(8,128)(2,1)}, u32[]{:S(2)}) copy-start(bf16[1,32,1024]{2,1,0:T(8,128)(2,1)} %x2_ref.1) | copy-start | bytes 196612
  16.6 11.0 %copy-start.3 = (f32[1024]{0:T(1024)S(1)}, f32[1024]{0:T(1024)}, u32[]{:S(2)}) copy-start(f32[1024]{0:T(1024)} %param.14) | copy-start | bytes 12292
  39.7 1.8 %collective-permute-start.1 = (bf16[16,48,128]{2,1,0:T(8,128)(2,1)S(1)}, bf16[16,48,128]{2,1,0:T(8,128)(2,1)S(1)}, u32[]{:S(2)}, u32[]{:S(2)}) collective-permute-start(bf16[16,48,128]{2,1,0:T(8,128)(2,1)S(1)} %all_to_all.22.mine_ref), channel_id=1, source_target_pairs={{0,1},{1,0},{2,3},{3,2},{4,5},{5,4},{6,7},{7,6},{8,9},{9,8},{10,11... | collective-permute-start | bytes 589832 | tf_op jit(solution)/shard_map/ppermute | solution.py:280
  41.5 10.3 %copy-start = (bf16[1024,1024]{1,0:T(8,128)(2,1)S(1)}, bf16[1024,1024]{1,0:T(8,128)(2,1)}, u32[]{:S(2)}) copy-start(bf16[1024,1024]{1,0:T(8,128)(2,1)} %wout_ref.1) | copy-start | bytes 6291460

commit v26 on v24

--- a/solution.py
+++ b/solution.py
@@ -195,29 +195,24 @@
     lines = mine_ref.shape[1]
     packed = mine_ref[:, lines * 2 // 3 : lines, :].reshape(-1, 2 * HD)
     keys, vals = key_values(mine_ref)
-    n = packed.shape[0]
-    for i, part in enumerate((packed, turned(packed))):
-        at = slice(i * n, (i + 1) * n)
-        queries = jnp.where(lower_half(part.shape), part, jnp.zeros_like(part))
-        query_ref[at, :] = queries
-        scores = score(queries, keys)
-        peak = jnp.max(scores, axis=-1, keepdims=True)
-        peak_ref[at, :] = jnp.broadcast_to(peak, (n, 2 * HD))
-        sum_ref[at, :] = weigh(scores, peak, vals)
+    both = jnp.concatenate([packed, turned(packed)], axis=0)
+    queries = jnp.where(lower_half(both.shape), both, jnp.zeros_like(both))
+    query_ref[...] = queries
+    scores = score(queries, keys)
+    peak = jnp.max(scores, axis=-1, keepdims=True)
+    peak_ref[...] = jnp.broadcast_to(peak, peak_ref.shape)
+    sum_ref[...] = weigh(scores, peak, vals)
 
 
 def finish_kernel(other_ref, query_ref, peak_ref, sum_ref, out_ref):
     keys, vals = key_values(other_ref)
     n = query_ref.shape[0] // 2
-    sums = []
-    for i in range(2):
-        at = slice(i * n, (i + 1) * n)
-        scores = score(query_ref[at, :], keys)
-        before = peak_ref[at, :]
-        peak = jnp.maximum(before, jnp.broadcast_to(jnp.max(scores, axis=-1, keepdims=True), before.shape))
-        wide_peak = jnp.concatenate([peak] * (scores.shape[1] // peak.shape[1]), axis=-1)
-        sums.append(sum_ref[at, :] * jnp.exp2((before - peak) * SHARP) + weigh(scores, wide_peak, vals))
-    top, low = sums
+    scores = score(query_ref[...], keys)
+    before = peak_ref[...]
+    peak = jnp.maximum(before, jnp.broadcast_to(jnp.max(scores, axis=-1, keepdims=True), before.shape))
+    wide_peak = jnp.concatenate([peak] * (scores.shape[1] // peak.shape[1]), axis=-1)
+    summed = sum_ref[...] * jnp.exp2((before - peak) * SHARP) + weigh(scores, wide_peak, vals)
+    top, low = summed[:n], summed[n:]
     left = lower_half(top.shape)
     attn = jnp.where(left, pltpu.roll(top, HD, 1), low) / jnp.where(left, top, pltpu.roll(low, HD, 1))
     out_ref[...] = attn.astype(jnp.bfloat16).reshape(out_ref.shape)

time: 53.3 us -> 52.9 us (level)
  no operation moved by 1% of the time
where the time goes in v26:
time: 52.9 us; the launch traced here: 52.6 us
  blocking collectives  43.8 us (83%)
  Pallas kernels  6.7 us (13%)
  waiting for transfers between devices  1.25 us (2%)
  between operations  0.72 us (1%)
    all_to_all x4, blocking collectives, trade(): lax.all_to_all(piece, ALL, split_axis=0, concat_axis=0, tiled=True, axis_...  43.8 us
    pallas_call x7, Pallas kernels, call(): pl.pallas_call(body, out_shape=[jax.ShapeDtypeStruct(shape, dtype) for sh...  6.7 us
    ppermute x2, waiting for transfers between devices, attention(): other = lax.ppermute(mine, ALL, [(i, i ^ 1) for i in range(devices)])  1.25 us
  transfers between devices with their start and end apart: 2, of which 2 were waited for; matrix products, arithmetic and copies ran while one was open for 0% of the time, Pallas kernels for 3%

profile of v26, /device:TPU:0, one launch (start us, length us, event | category | flops | bytes accessed | tf_op | source)
XLA Modules:
  0.0 52.6 jit_solution(2784779364519816663)
XLA Ops:
  0.6 1.0 %shard_map.95 = bf16[16,48,128]{2,1,0:T(8,128)(2,1)S(1)} custom-call(bf16[1,32,1024]{2,1,0:T(8,128)(2,1)} %q_hbm.1, bf16[1,32,1024]{2,1,0:T(8,128)(2,1)} %k_hbm.1, bf16[1,32,1024]{2,1,0:T(8,128)(2,1)} %v_hbm.1), custom_call_target="tpu_custom_call" | custom-call | tf_op jit(solution)/shard_map/pallas_call | solution.py:251
  1.7 14.1 %all_to_all.20.mine_ref = bf16[16,48,128]{2,1,0:T(8,128)(2,1)S(1)} all-to-all(bf16[16,48,128]{2,1,0:T(8,128)(2,1)S(1)} %shard_map.95), channel_id=1, replica_groups={{23,24,27,28,31,0,3,4,7,8,11,12,15,16,19,20},{21,22,25,26,29,30,1,2,5,6..., dimensions={0} | all-to-all | bytes 393216 | tf_op jit(solution)/shard_map/all_to_all | solution.py:273
  15.7 0.0 collective-permute-start
  15.7 0.8 %shard_map.96 = (bf16[512,128]{1,0:T(8,128)(2,1)S(1)}, f32[512,128]{1,0:T(8,128)S(1)}, f32[512,128]{1,0:T(8,128)S(1)}) custom-call(bf16[16,48,128]{2,1,0:T(8,128)(2,1)S(1)} %all_to_all.20.mine_ref), custom_call_target="tpu_custom_call" | custom-call | flops 1073741824 | bytes 1048576 | tf_op jit(solution)/shard_map/pallas_call | solution.py:251
  16.5 0.7 %collective-permute-done.other_ref = bf16[16,48,128]{2,1,0:T(8,128)(2,1)S(1)} collective-permute-done((bf16[16,48,128]{2,1,0:T(8,128)(2,1)S(1)}, bf16[16,48,128]{2,1,0:T(8,128)(2,1)S(1)}, u32[]{:S(2)}, u32[]{:S(2)}) %collective-permute-start) | collective-permute-done | bytes 196640 | tf_op jit(solution)/shard_map/ppermute | solution.py:277
  17.2 0.0 slice-start
  17.2 0.0 slice-start.1
  17.2 0.0 copy-start.1
  17.2 0.0 copy-start.2
  17.2 0.0 copy-start.3
  17.2 0.6 %shard_map.97 = bf16[16,16,128]{2,1,0:T(8,128)(2,1)S(1)} custom-call(bf16[16,48,128]{2,1,0:T(8,128)(2,1)S(1)} %collective-permute-done.other_ref, bf16[512,128]{1,0:T(8,128)(2,1)S(1)} %get-tuple-element.10.query_ref, f32[512,128]{1,0:T(8,128)S(1)} %get-tuple-element.11.peak_ref, f32[512,128]{1,0:T(8,128)S(1)} %get-tuple-element.12.sum_ref), custom_call_target="tpu_custom_call" | custom-call | flops 17179869184 | bytes 41943040 | tf_op jit(solution)/shard_map/pallas_call | solution.py:251
  17.9 9.5 %all_to_all.21.got_ref = bf16[16,16,128]{2,1,0:T(8,128)(2,1)S(1)} all-to-all(bf16[16,16,128]{2,1,0:T(8,128)(2,1)S(1)} %shard_map.97), channel_id=1, replica_groups={{23,24,27,28,31,0,3,4,7,8,11,12,15,16,19,20},{21,22,25,26,29,30,1,2,5,6..., dimensions={0} | all-to-all | bytes 131072 | tf_op jit(solution)/shard_map/all_to_all | solution.py:273
  27.4 0.0 slice-done
  27.4 0.0 slice-done.1
  27.4 0.0 copy-done.1
  27.4 0.0 copy-done.2
  27.4 0.0 copy-done.3
  27.4 1.7 %shard_map.98 = (f32[1,32,1024]{2,1,0:T(8,128)}, bf16[16,48,128]{2,1,0:T(8,128)(2,1)S(1)}) custom-call(bf16[16,16,128]{2,1,0:T(8,128)(2,1)S(1)} %all_to_all.21.got_ref, bf16[1,32,1024]{2,1,0:T(8,128)(2,1)S(1)} %copy-done.2, bf16[1024,1024]{1,0:T(8,128)(2,1)S(1)} %copy-done.1, f32[1,1024]{1,0:T(1,128)S(1)} %bitcast.3, bf16[1024,3072]{1,0:T(8,128)(2,1)S(1)} %bitcast.2), custom_call_target="tpu_custom_call" | custom-call | tf_op jit(solution)/shard_map/pallas_call | solution.py:251
  29.1 10.9 %all_to_all.22.mine_ref = bf16[16,48,128]{2,1,0:T(8,128)(2,1)S(1)} all-to-all(bf16[16,48,128]{2,1,0:T(8,128)(2,1)S(1)} %get-tuple-element.14), channel_id=1, replica_groups={{23,24,27,28,31,0,3,4,7,8,11,12,15,16,19,20},{21,22,25,26,29,30,1,2,5,6..., dimensions={0} | all-to-all | bytes 393216 | tf_op jit(solution)/shard_map/all_to_all | solution.py:273
  40.1 0.1 collective-permute-start.1
  40.2 0.7 %shard_map.99 = (bf16[512,128]{1,0:T(8,128)(2,1)S(1)}, f32[512,128]{1,0:T(8,128)S(1)}, f32[512,128]{1,0:T(8,128)S(1)}) custom-call(bf16[16,48,128]{2,1,0:T(8,128)(2,1)S(1)} %all_to_all.22.mine_ref), custom_call_target="tpu_custom_call" | custom-call | flops 1073741824 | bytes 1048576 | tf_op jit(solution)/shard_map/pallas_call | solution.py:251
  40.9 0.6 %collective-permute-done.1.other_ref = bf16[16,48,128]{2,1,0:T(8,128)(2,1)S(1)} collective-permute-done((bf16[16,48,128]{2,1,0:T(8,128)(2,1)S(1)}, bf16[16,48,128]{2,1,0:T(8,128)(2,1)S(1)}, u32[]{:S(2)}, u32[]{:S(2)}) %collective-permute-start.1) | collective-permute-done | bytes 196640 | tf_op jit(solution)/shard_map/ppermute | solution.py:277
  41.5 0.0 copy-start
  41.5 0.6 %shard_map.100 = bf16[16,16,128]{2,1,0:T(8,128)(2,1)S(1)} custom-call(bf16[16,48,128]{2,1,0:T(8,128)(2,1)S(1)} %collective-permute-done.1.other_ref, bf16[512,128]{1,0:T(8,128)(2,1)S(1)} %get-tuple-element.15.query_ref, f32[512,128]{1,0:T(8,128)S(1)} %get-tuple-element.16.peak_ref, f32[512,128]{1,0:T(8,128)S(1)} %get-tuple-element.17.sum_ref), custom_call_target="tpu_custom_call" | custom-call | flops 17179869184 | bytes 41943040 | tf_op jit(solution)/shard_map/pallas_call | solution.py:251
  42.2 9.3 %all_to_all.23.got_ref = bf16[16,16,128]{2,1,0:T(8,128)(2,1)S(1)} all-to-all(bf16[16,16,128]{2,1,0:T(8,128)(2,1)S(1)} %shard_map.100), channel_id=1, replica_groups={{23,24,27,28,31,0,3,4,7,8,11,12,15,16,19,20},{21,22,25,26,29,30,1,2,5,6..., dimensions={0} | all-to-all | bytes 131072 | tf_op jit(solution)/shard_map/all_to_all | solution.py:273
  51.4 0.0 copy-done
  51.4 1.2 %shard_map.101 = f32[1,32,1024]{2,1,0:T(8,128)} custom-call(bf16[16,16,128]{2,1,0:T(8,128)(2,1)S(1)} %all_to_all.23.got_ref, bf16[1024,1024]{1,0:T(8,128)(2,1)S(1)} %copy-done), custom_call_target="tpu_custom_call" | custom-call | tf_op jit(solution)/shard_map/pallas_call | solution.py:251
  (1 shorter events, 0.0 us)
Async XLA Ops:
  15.7 1.4 %collective-permute-start = (bf16[16,48,128]{2,1,0:T(8,128)(2,1)S(1)}, bf16[16,48,128]{2,1,0:T(8,128)(2,1)S(1)}, u32[]{:S(2)}, u32[]{:S(2)}) collective-permute-start(bf16[16,48,128]{2,1,0:T(8,128)(2,1)S(1)} %all_to_all.20.mine_ref), channel_id=1, source_target_pairs={{0,1},{1,0},{2,3},{3,2},{4,5},{5,4},{6,7},{7,6},{8,9},{9,8},{10,11... | collective-permute-start | bytes 589832 | tf_op jit(solution)/shard_map/ppermute | solution.py:277
  17.2 10.2 %slice-start = ((s8[6291456]{0:T(1024)(128)(4,1)}), s8[4194304]{0:T(1024)(128)(4,1)S(1)}, s32[]{:S(2)}) async-start(s8[6291456]{0:T(1024)(128)(4,1)} %bitcast.1), calls=%async_computation.4 | async-start | bytes 8388608
  17.2 10.2 %slice-start.1 = ((s8[6291456]{0:T(1024)(128)(4,1)}), s8[2097152]{0:T(1024)(128)(4,1)S(1)}, s32[]{:S(2)}) async-start(s8[6291456]{0:T(1024)(128)(4,1)} %bitcast.1), calls=%async_computation.5 | async-start | bytes 4194304
  17.2 10.2 %copy-start.1 = (bf16[1024,1024]{1,0:T(8,128)(2,1)S(1)}, bf16[1024,1024]{1,0:T(8,128)(2,1)}, u32[]{:S(2)}) copy-start(bf16[1024,1024]{1,0:T(8,128)(2,1)} %wv_ref.1) | copy-start | bytes 6291460
  17.2 10.2 %copy-start.2 = (bf16[1,32,1024]{2,1,0:T(8,128)(2,1)S(1)}, bf16[1,32,1024]{2,1,0:T(8,128)(2,1)}, u32[]{:S(2)}) copy-start(bf16[1,32,1024]{2,1,0:T(8,128)(2,1)} %x2_ref.1) | copy-start | bytes 196612
  17.2 10.2 %copy-start.3 = (f32[1024]{0:T(1024)S(1)}, f32[1024]{0:T(1024)}, u32[]{:S(2)}) copy-start(f32[1024]{0:T(1024)} %param.14) | copy-start | bytes 12292
  40.1 1.4 %collective-permute-start.1 = (bf16[16,48,128]{2,1,0:T(8,128)(2,1)S(1)}, bf16[16,48,128]{2,1,0:T(8,128)(2,1)S(1)}, u32[]{:S(2)}, u32[]{:S(2)}) collective-permute-start(bf16[16,48,128]{2,1,0:T(8,128)(2,1)S(1)} %all_to_all.22.mine_ref), channel_id=1, source_target_pairs={{0,1},{1,0},{2,3},{3,2},{4,5},{5,4},{6,7},{7,6},{8,9},{9,8},{10,11... | collective-permute-start | bytes 589832 | tf_op jit(solution)/shard_map/ppermute | solution.py:277
  41.5 9.9 %copy-start = (bf16[1024,1024]{1,0:T(8,128)(2,1)S(1)}, bf16[1024,1024]{1,0:T(8,128)(2,1)}, u32[]{:S(2)}) copy-start(bf16[1024,1024]{1,0:T(8,128)(2,1)} %wout_ref.1) | copy-start | bytes 6291460

commit v27 on v26

--- a/solution.py
+++ b/solution.py
@@ -177,8 +177,12 @@
     return jnp.concatenate([x[:, HD:], x[:, :HD]], axis=-1)
 
 
-def key_values(piece_ref):
-    kv = piece_ref[:, 0 : piece_ref.shape[1] * 2 // 3, :].reshape(-1, 2 * HD)
+def collect_kernel(piece_ref, kv_ref):
+    kv_ref[...] = piece_ref[:, 0 : piece_ref.shape[1] * 2 // 3, :].reshape(kv_ref.shape)
+
+
+def key_values(kv_ref):
+    kv = kv_ref[...]
     return kv, jnp.where(lower_half(kv.shape), jnp.ones_like(kv), kv)
 
 
@@ -191,10 +195,10 @@
     return jnp.dot(weights, vals, preferred_element_type=jnp.float32)
 
 
-def begin_kernel(mine_ref, query_ref, peak_ref, sum_ref):
+def begin_kernel(mine_ref, kv_ref, query_ref, peak_ref, sum_ref):
     lines = mine_ref.shape[1]
     packed = mine_ref[:, lines * 2 // 3 : lines, :].reshape(-1, 2 * HD)
-    keys, vals = key_values(mine_ref)
+    keys, vals = key_values(kv_ref)
     both = jnp.concatenate([packed, turned(packed)], axis=0)
     queries = jnp.where(lower_half(both.shape), both, jnp.zeros_like(both))
     query_ref[...] = queries
@@ -274,8 +278,9 @@
 
     def attention(packed):
         mine = trade(packed)
-        other = lax.ppermute(mine, ALL, [(i, i ^ 1) for i in range(devices)])
-        begun = call(begin_kernel, [queries, lines, lines], (mine,), cost=pl.CostEstimate(1 << 30, 0, 1 << 20))
+        (own,) = call(collect_kernel, [queries], (mine,))
+        other = lax.ppermute(own, ALL, [(i, i ^ 1) for i in range(devices)])
+        begun = call(begin_kernel, [queries, lines, lines], (mine, own), cost=pl.CostEstimate(1 << 30, 0, 1 << 20))
         cost = pl.CostEstimate(flops=16 << 30, bytes_accessed=40 << 20, transcendentals=0)
         (half,) = call(finish_kernel, [halves], (other, *begun), cost=cost)
         return trade(half)

time: 52.9 us -> 52.9 us (level)
    pallas_call x7 -> x9, Pallas kernels: 6.7 us -> 6.73 us  [call(): pl.pallas_call(body, out_shape=[jax.ShapeDtypeStruct(shape, dtype) for sh...]
where the time goes in v27:
time: 52.9 us; the launch traced here: 52.6 us
  blocking collectives  43.8 us (83%)
  Pallas kernels  6.73 us (13%)
  waiting for transfers between devices  1.05 us (2%)
  between operations  0.74 us (1%)
    all_to_all x4, blocking collectives, trade(): lax.all_to_all(piece, ALL, split_axis=0, concat_axis=0, tiled=True, axis_...  43.8 us
    pallas_call x9, Pallas kernels, call(): pl.pallas_call(body, out_shape=[jax.ShapeDtypeStruct(shape, dtype) for sh...  6.73 us
  transfers between devices with their start and end apart: 2, of which 2 were waited for; matrix products, arithmetic and copies ran while one was open for 0% of the time, Pallas kernels for 3%

profile of v27, /device:TPU:0, one launch (start us, length us, event | category | flops | bytes accessed | tf_op | source)
XLA Modules:
  0.0 52.6 jit_solution(4557349877029395956)
XLA Ops:
  0.6 1.0 %shard_map.95 = bf16[16,48,128]{2,1,0:T(8,128)(2,1)S(1)} custom-call(bf16[1,32,1024]{2,1,0:T(8,128)(2,1)} %q_hbm.1, bf16[1,32,1024]{2,1,0:T(8,128)(2,1)} %k_hbm.1, bf16[1,32,1024]{2,1,0:T(8,128)(2,1)} %v_hbm.1), custom_call_target="tpu_custom_call" | custom-call | tf_op jit(solution)/shard_map/pallas_call | solution.py:255
  1.7 14.1 %all_to_all.20.piece_ref.mine_ref = bf16[16,48,128]{2,1,0:T(8,128)(2,1)S(1)} all-to-all(bf16[16,48,128]{2,1,0:T(8,128)(2,1)S(1)} %shard_map.95), channel_id=1, replica_groups={{23,24,27,28,31,0,3,4,7,8,11,12,15,16,19,20},{21,22,25,26,29,30,1,2,5,6..., dimensions={0} | all-to-all | bytes 393216 | tf_op jit(solution)/shard_map/all_to_all | solution.py:277
  15.8 0.1 collective-permute-start
  15.8 0.8 %shard_map.97 = (bf16[512,128]{1,0:T(8,128)(2,1)S(1)}, f32[512,128]{1,0:T(8,128)S(1)}, f32[512,128]{1,0:T(8,128)S(1)}) custom-call(bf16[16,48,128]{2,1,0:T(8,128)(2,1)S(1)} %all_to_all.20.piece_ref.mine_ref, bf16[512,128]{1,0:T(8,128)(2,1)S(1)} %shard_map.96.kv_ref), custom_call_target="tpu_custom_call" | custom-call | flops 1073741824 | bytes 1048576 | tf_op jit(solution)/shard_map/pallas_call | solution.py:255
  16.6 0.6 %collective-permute-done.other_ref = bf16[512,128]{1,0:T(8,128)(2,1)S(1)} collective-permute-done((bf16[512,128]{1,0:T(8,128)(2,1)S(1)}, bf16[512,128]{1,0:T(8,128)(2,1)S(1)}, u32[]{:S(2)}, u32[]{:S(2)}) %collective-permute-start) | collective-permute-done | bytes 131104 | tf_op jit(solution)/shard_map/ppermute | solution.py:282
  17.2 0.0 slice-start
  17.2 0.0 slice-start.1
  17.2 0.0 copy-start.1
  17.2 0.0 copy-start.2
  17.2 0.0 copy-start.3
  17.2 0.6 %shard_map.98 = bf16[16,16,128]{2,1,0:T(8,128)(2,1)S(1)} custom-call(bf16[512,128]{1,0:T(8,128)(2,1)S(1)} %collective-permute-done.other_ref, bf16[512,128]{1,0:T(8,128)(2,1)S(1)} %get-tuple-element.10.query_ref, f32[512,128]{1,0:T(8,128)S(1)} %get-tuple-element.11.peak_ref, f32[512,128]{1,0:T(8,128)S(1)} %get-tuple-element.12.sum_ref), custom_call_target="tpu_custom_call" | custom-call | flops 17179869184 | bytes 41943040 | tf_op jit(solution)/shard_map/pallas_call | solution.py:255
  17.8 9.5 %all_to_all.21.got_ref = bf16[16,16,128]{2,1,0:T(8,128)(2,1)S(1)} all-to-all(bf16[16,16,128]{2,1,0:T(8,128)(2,1)S(1)} %shard_map.98), channel_id=1, replica_groups={{23,24,27,28,31,0,3,4,7,8,11,12,15,16,19,20},{21,22,25,26,29,30,1,2,5,6..., dimensions={0} | all-to-all | bytes 131072 | tf_op jit(solution)/shard_map/all_to_all | solution.py:277
  27.4 0.0 slice-done
  27.4 0.0 slice-done.1
  27.4 0.0 copy-done.1
  27.4 0.0 copy-done.2
  27.4 0.0 copy-done.3
  27.4 1.7 %shard_map.99 = (f32[1,32,1024]{2,1,0:T(8,128)}, bf16[16,48,128]{2,1,0:T(8,128)(2,1)S(1)}) custom-call(bf16[16,16,128]{2,1,0:T(8,128)(2,1)S(1)} %all_to_all.21.got_ref, bf16[1,32,1024]{2,1,0:T(8,128)(2,1)S(1)} %copy-done.2, bf16[1024,1024]{1,0:T(8,128)(2,1)S(1)} %copy-done.1, f32[1,1024]{1,0:T(1,128)S(1)} %bitcast.3, bf16[1024,3072]{1,0:T(8,128)(2,1)S(1)} %bitcast.2), custom_call_target="tpu_custom_call" | custom-call | tf_op jit(solution)/shard_map/pallas_call | solution.py:255
  29.1 10.9 %all_to_all.22.piece_ref.mine_ref = bf16[16,48,128]{2,1,0:T(8,128)(2,1)S(1)} all-to-all(bf16[16,48,128]{2,1,0:T(8,128)(2,1)S(1)} %get-tuple-element.14), channel_id=1, replica_groups={{23,24,27,28,31,0,3,4,7,8,11,12,15,16,19,20},{21,22,25,26,29,30,1,2,5,6..., dimensions={0} | all-to-all | bytes 393216 | tf_op jit(solution)/shard_map/all_to_all | solution.py:277
  40.1 0.2 collective-permute-start.1
  40.2 0.8 %shard_map.101 = (bf16[512,128]{1,0:T(8,128)(2,1)S(1)}, f32[512,128]{1,0:T(8,128)S(1)}, f32[512,128]{1,0:T(8,128)S(1)}) custom-call(bf16[16,48,128]{2,1,0:T(8,128)(2,1)S(1)} %all_to_all.22.piece_ref.mine_ref, bf16[512,128]{1,0:T(8,128)(2,1)S(1)} %shard_map.100.kv_ref), custom_call_target="tpu_custom_call" | custom-call | flops 1073741824 | bytes 1048576 | tf_op jit(solution)/shard_map/pallas_call | solution.py:255
  41.0 0.5 collective-permute-done.1.other_ref
  41.5 0.0 copy-start
  41.5 0.6 %shard_map.102 = bf16[16,16,128]{2,1,0:T(8,128)(2,1)S(1)} custom-call(bf16[512,128]{1,0:T(8,128)(2,1)S(1)} %collective-permute-done.1.other_ref, bf16[512,128]{1,0:T(8,128)(2,1)S(1)} %get-tuple-element.15.query_ref, f32[512,128]{1,0:T(8,128)S(1)} %get-tuple-element.16.peak_ref, f32[512,128]{1,0:T(8,128)S(1)} %get-tuple-element.17.sum_ref), custom_call_target="tpu_custom_call" | custom-call | flops 17179869184 | bytes 41943040 | tf_op jit(solution)/shard_map/pallas_call | solution.py:255
  42.1 9.3 %all_to_all.23.got_ref = bf16[16,16,128]{2,1,0:T(8,128)(2,1)S(1)} all-to-all(bf16[16,16,128]{2,1,0:T(8,128)(2,1)S(1)} %shard_map.102), channel_id=1, replica_groups={{23,24,27,28,31,0,3,4,7,8,11,12,15,16,19,20},{21,22,25,26,29,30,1,2,5,6..., dimensions={0} | all-to-all | bytes 131072 | tf_op jit(solution)/shard_map/all_to_all | solution.py:277
  51.4 0.0 copy-done
  51.4 1.2 %shard_map.103 = f32[1,32,1024]{2,1,0:T(8,128)} custom-call(bf16[16,16,128]{2,1,0:T(8,128)(2,1)S(1)} %all_to_all.23.got_ref, bf16[1024,1024]{1,0:T(8,128)(2,1)S(1)} %copy-done), custom_call_target="tpu_custom_call" | custom-call | tf_op jit(solution)/shard_map/pallas_call | solution.py:255
  (3 shorter events, 0.0 us)
Async XLA Ops:
  15.8 1.4 %collective-permute-start = (bf16[512,128]{1,0:T(8,128)(2,1)S(1)}, bf16[512,128]{1,0:T(8,128)(2,1)S(1)}, u32[]{:S(2)}, u32[]{:S(2)}) collective-permute-start(bf16[512,128]{1,0:T(8,128)(2,1)S(1)} %shard_map.96.kv_ref), channel_id=1, source_target_pairs={{0,1},{1,0},{2,3},{3,2},{4,5},{5,4},{6,7},{7,6},{8,9},{9,8},{10,11... | collective-permute-start | bytes 393224 | tf_op jit(solution)/shard_map/ppermute | solution.py:282
  17.2 10.2 %slice-start = ((s8[6291456]{0:T(1024)(128)(4,1)}), s8[4194304]{0:T(1024)(128)(4,1)S(1)}, s32[]{:S(2)}) async-start(s8[6291456]{0:T(1024)(128)(4,1)} %bitcast.1), calls=%async_computation.4 | async-start | bytes 8388608
  17.2 10.2 %slice-start.1 = ((s8[6291456]{0:T(1024)(128)(4,1)}), s8[2097152]{0:T(1024)(128)(4,1)S(1)}, s32[]{:S(2)}) async-start(s8[6291456]{0:T(1024)(128)(4,1)} %bitcast.1), calls=%async_computation.5 | async-start | bytes 4194304
  17.2 10.2 %copy-start.1 = (bf16[1024,1024]{1,0:T(8,128)(2,1)S(1)}, bf16[1024,1024]{1,0:T(8,128)(2,1)}, u32[]{:S(2)}) copy-start(bf16[1024,1024]{1,0:T(8,128)(2,1)} %wv_ref.1) | copy-start | bytes 6291460
  17.2 10.2 %copy-start.2 = (bf16[1,32,1024]{2,1,0:T(8,128)(2,1)S(1)}, bf16[1,32,1024]{2,1,0:T(8,128)(2,1)}, u32[]{:S(2)}) copy-start(bf16[1,32,1024]{2,1,0:T(8,128)(2,1)} %x2_ref.1) | copy-start | bytes 196612
  17.2 10.2 %copy-start.3 = (f32[1024]{0:T(1024)S(1)}, f32[1024]{0:T(1024)}, u32[]{:S(2)}) copy-start(f32[1024]{0:T(1024)} %param.14) | copy-start | bytes 12292
  40.1 1.4 %collective-permute-start.1 = (bf16[512,128]{1,0:T(8,128)(2,1)S(1)}, bf16[512,128]{1,0:T(8,128)(2,1)S(1)}, u32[]{:S(2)}, u32[]{:S(2)}) collective-permute-start(bf16[512,128]{1,0:T(8,128)(2,1)S(1)} %shard_map.100.kv_ref), channel_id=1, source_target_pairs={{0,1},{1,0},{2,3},{3,2},{4,5},{5,4},{6,7},{7,6},{8,9},{9,8},{10,11... | collective-permute-start | bytes 393224 | tf_op jit(solution)/shard_map/ppermute | solution.py:282
  41.5 9.9 %copy-start = (bf16[1024,1024]{1,0:T(8,128)(2,1)S(1)}, bf16[1024,1024]{1,0:T(8,128)(2,1)}, u32[]{:S(2)}) copy-start(bf16[1024,1024]{1,0:T(8,128)(2,1)} %wout_ref.1) | copy-start | bytes 6291460

commit v28 on v27

--- a/solution.py
+++ b/solution.py
@@ -239,14 +239,14 @@
 
 def last_kernel(got_ref, wout_ref, out_hbm, out_ref, sems):
     rows = unpack_rows(got_ref)
-    scale = factor(rows.astype(jnp.float32))
-    copies = []
-    width = wout_ref.shape[1] // 4
-    for i in range(4):
-        cols = slice(i * width, (i + 1) * width)
-        out_ref[0, :, cols] = times(rows, wout_ref[:, cols]) * scale
-        copies.append(pltpu.make_async_copy(out_ref.at[:, :, cols], out_hbm.at[:, :, cols], sems.at[i]))
-        copies[i].start()
+    out_ref[0] = times(rows, wout_ref[...]) * factor(rows.astype(jnp.float32))
+    half = rows.shape[0] // 2
+    copies = [
+        pltpu.make_async_copy(out_ref.at[:, at : at + half], out_hbm.at[:, at : at + half], sems.at[at // half])
+        for at in (0, half)
+    ]
+    for copy in copies:
+        copy.start()
     for copy in copies:
         copy.wait()
 
@@ -298,7 +298,7 @@
         last_kernel,
         [(wide, jnp.float32, pltpu.HBM)],
         (attention(piece), w_out),
-        [pltpu.VMEM(wide, jnp.float32), pltpu.SemaphoreType.DMA((4,))],
+        [pltpu.VMEM(wide, jnp.float32), pltpu.SemaphoreType.DMA((2,))],
     )
     return feats, result
 

time: 52.9 us -> 52.9 us (level)
  no operation moved by 1% of the time
where the time goes in v28:
time: 52.9 us; the launch traced here: 52.6 us
  blocking collectives  43.8 us (83%)
  Pallas kernels  6.74 us (13%)
  waiting for transfers between devices  1.05 us (2%)
  between operations  0.74 us (1%)
    all_to_all x4, blocking collectives, trade(): lax.all_to_all(piece, ALL, split_axis=0, concat_axis=0, tiled=True, axis_...  43.8 us
    pallas_call x9, Pallas kernels, call(): pl.pallas_call(body, out_shape=[jax.ShapeDtypeStruct(shape, dtype) for sh...  6.74 us
  transfers between devices with their start and end apart: 2, of which 2 were waited for; matrix products, arithmetic and copies ran while one was open for 0% of the time, Pallas kernels for 3%

profile of v28, /device:TPU:0, one launch (start us, length us, event | category | flops | bytes accessed | tf_op | source)
XLA Modules:
  0.0 52.6 jit_solution(8044943216984981285)
XLA Ops:
  0.6 1.0 %shard_map.95 = bf16[16,48,128]{2,1,0:T(8,128)(2,1)S(1)} custom-call(bf16[1,32,1024]{2,1,0:T(8,128)(2,1)} %q_hbm.1, bf16[1,32,1024]{2,1,0:T(8,128)(2,1)} %k_hbm.1, bf16[1,32,1024]{2,1,0:T(8,128)(2,1)} %v_hbm.1), custom_call_target="tpu_custom_call" | custom-call | tf_op jit(solution)/shard_map/pallas_call | solution.py:255
  1.7 14.1 %all_to_all.20.piece_ref.mine_ref = bf16[16,48,128]{2,1,0:T(8,128)(2,1)S(1)} all-to-all(bf16[16,48,128]{2,1,0:T(8,128)(2,1)S(1)} %shard_map.95), channel_id=1, replica_groups={{23,24,27,28,31,0,3,4,7,8,11,12,15,16,19,20},{21,22,25,26,29,30,1,2,5,6..., dimensions={0} | all-to-all | bytes 393216 | tf_op jit(solution)/shard_map/all_to_all | solution.py:277
  15.8 0.1 collective-permute-start
  15.8 0.8 %shard_map.97 = (bf16[512,128]{1,0:T(8,128)(2,1)S(1)}, f32[512,128]{1,0:T(8,128)S(1)}, f32[512,128]{1,0:T(8,128)S(1)}) custom-call(bf16[16,48,128]{2,1,0:T(8,128)(2,1)S(1)} %all_to_all.20.piece_ref.mine_ref, bf16[512,128]{1,0:T(8,128)(2,1)S(1)} %shard_map.96.kv_ref), custom_call_target="tpu_custom_call" | custom-call | flops 1073741824 | bytes 1048576 | tf_op jit(solution)/shard_map/pallas_call | solution.py:255
  16.6 0.6 %collective-permute-done.other_ref = bf16[512,128]{1,0:T(8,128)(2,1)S(1)} collective-permute-done((bf16[512,128]{1,0:T(8,128)(2,1)S(1)}, bf16[512,128]{1,0:T(8,128)(2,1)S(1)}, u32[]{:S(2)}, u32[]{:S(2)}) %collective-permute-start) | collective-permute-done | bytes 131104 | tf_op jit(solution)/shard_map/ppermute | solution.py:282
  17.2 0.0 slice-start
  17.2 0.0 slice-start.1
  17.2 0.0 copy-start.1
  17.2 0.0 copy-start.2
  17.2 0.0 copy-start.3
  17.2 0.6 %shard_map.98 = bf16[16,16,128]{2,1,0:T(8,128)(2,1)S(1)} custom-call(bf16[512,128]{1,0:T(8,128)(2,1)S(1)} %collective-permute-done.other_ref, bf16[512,128]{1,0:T(8,128)(2,1)S(1)} %get-tuple-element.10.query_ref, f32[512,128]{1,0:T(8,128)S(1)} %get-tuple-element.11.peak_ref, f32[512,128]{1,0:T(8,128)S(1)} %get-tuple-element.12.sum_ref), custom_call_target="tpu_custom_call" | custom-call | flops 17179869184 | bytes 41943040 | tf_op jit(solution)/shard_map/pallas_call | solution.py:255
  17.8 9.5 %all_to_all.21.got_ref = bf16[16,16,128]{2,1,0:T(8,128)(2,1)S(1)} all-to-all(bf16[16,16,128]{2,1,0:T(8,128)(2,1)S(1)} %shard_map.98), channel_id=1, replica_groups={{23,24,27,28,31,0,3,4,7,8,11,12,15,16,19,20},{21,22,25,26,29,30,1,2,5,6..., dimensions={0} | all-to-all | bytes 131072 | tf_op jit(solution)/shard_map/all_to_all | solution.py:277
  27.4 0.0 slice-done
  27.4 0.0 slice-done.1
  27.4 0.0 copy-done.1
  27.4 0.0 copy-done.2
  27.4 0.0 copy-done.3
  27.4 1.7 %shard_map.99 = (f32[1,32,1024]{2,1,0:T(8,128)}, bf16[16,48,128]{2,1,0:T(8,128)(2,1)S(1)}) custom-call(bf16[16,16,128]{2,1,0:T(8,128)(2,1)S(1)} %all_to_all.21.got_ref, bf16[1,32,1024]{2,1,0:T(8,128)(2,1)S(1)} %copy-done.2, bf16[1024,1024]{1,0:T(8,128)(2,1)S(1)} %copy-done.1, f32[1,1024]{1,0:T(1,128)S(1)} %bitcast.3, bf16[1024,3072]{1,0:T(8,128)(2,1)S(1)} %bitcast.2), custom_call_target="tpu_custom_call" | custom-call | tf_op jit(solution)/shard_map/pallas_call | solution.py:255
  29.1 10.9 %all_to_all.22.piece_ref.mine_ref = bf16[16,48,128]{2,1,0:T(8,128)(2,1)S(1)} all-to-all(bf16[16,48,128]{2,1,0:T(8,128)(2,1)S(1)} %get-tuple-element.14), channel_id=1, replica_groups={{23,24,27,28,31,0,3,4,7,8,11,12,15,16,19,20},{21,22,25,26,29,30,1,2,5,6..., dimensions={0} | all-to-all | bytes 393216 | tf_op jit(solution)/shard_map/all_to_all | solution.py:277
  40.1 0.2 collective-permute-start.1
  40.2 0.8 %shard_map.101 = (bf16[512,128]{1,0:T(8,128)(2,1)S(1)}, f32[512,128]{1,0:T(8,128)S(1)}, f32[512,128]{1,0:T(8,128)S(1)}) custom-call(bf16[16,48,128]{2,1,0:T(8,128)(2,1)S(1)} %all_to_all.22.piece_ref.mine_ref, bf16[512,128]{1,0:T(8,128)(2,1)S(1)} %shard_map.100.kv_ref), custom_call_target="tpu_custom_call" | custom-call | flops 1073741824 | bytes 1048576 | tf_op jit(solution)/shard_map/pallas_call | solution.py:255
  41.0 0.5 collective-permute-done.1.other_ref
  41.5 0.0 copy-start
  41.5 0.6 %shard_map.102 = bf16[16,16,128]{2,1,0:T(8,128)(2,1)S(1)} custom-call(bf16[512,128]{1,0:T(8,128)(2,1)S(1)} %collective-permute-done.1.other_ref, bf16[512,128]{1,0:T(8,128)(2,1)S(1)} %get-tuple-element.15.query_ref, f32[512,128]{1,0:T(8,128)S(1)} %get-tuple-element.16.peak_ref, f32[512,128]{1,0:T(8,128)S(1)} %get-tuple-element.17.sum_ref), custom_call_target="tpu_custom_call" | custom-call | flops 17179869184 | bytes 41943040 | tf_op jit(solution)/shard_map/pallas_call | solution.py:255
  42.1 9.3 %all_to_all.23.got_ref = bf16[16,16,128]{2,1,0:T(8,128)(2,1)S(1)} all-to-all(bf16[16,16,128]{2,1,0:T(8,128)(2,1)S(1)} %shard_map.102), channel_id=1, replica_groups={{23,24,27,28,31,0,3,4,7,8,11,12,15,16,19,20},{21,22,25,26,29,30,1,2,5,6..., dimensions={0} | all-to-all | bytes 131072 | tf_op jit(solution)/shard_map/all_to_all | solution.py:277
  51.4 0.0 copy-done
  51.4 1.2 %shard_map.103 = f32[1,32,1024]{2,1,0:T(8,128)} custom-call(bf16[16,16,128]{2,1,0:T(8,128)(2,1)S(1)} %all_to_all.23.got_ref, bf16[1024,1024]{1,0:T(8,128)(2,1)S(1)} %copy-done), custom_call_target="tpu_custom_call" | custom-call | tf_op jit(solution)/shard_map/pallas_call | solution.py:255
  (3 shorter events, 0.0 us)
Async XLA Ops:
  15.8 1.4 %collective-permute-start = (bf16[512,128]{1,0:T(8,128)(2,1)S(1)}, bf16[512,128]{1,0:T(8,128)(2,1)S(1)}, u32[]{:S(2)}, u32[]{:S(2)}) collective-permute-start(bf16[512,128]{1,0:T(8,128)(2,1)S(1)} %shard_map.96.kv_ref), channel_id=1, source_target_pairs={{0,1},{1,0},{2,3},{3,2},{4,5},{5,4},{6,7},{7,6},{8,9},{9,8},{10,11... | collective-permute-start | bytes 393224 | tf_op jit(solution)/shard_map/ppermute | solution.py:282
  17.2 10.2 %slice-start = ((s8[6291456]{0:T(1024)(128)(4,1)}), s8[4194304]{0:T(1024)(128)(4,1)S(1)}, s32[]{:S(2)}) async-start(s8[6291456]{0:T(1024)(128)(4,1)} %bitcast.1), calls=%async_computation.4 | async-start | bytes 8388608
  17.2 10.2 %slice-start.1 = ((s8[6291456]{0:T(1024)(128)(4,1)}), s8[2097152]{0:T(1024)(128)(4,1)S(1)}, s32[]{:S(2)}) async-start(s8[6291456]{0:T(1024)(128)(4,1)} %bitcast.1), calls=%async_computation.5 | async-start | bytes 4194304
  17.2 10.2 %copy-start.1 = (bf16[1024,1024]{1,0:T(8,128)(2,1)S(1)}, bf16[1024,1024]{1,0:T(8,128)(2,1)}, u32[]{:S(2)}) copy-start(bf16[1024,1024]{1,0:T(8,128)(2,1)} %wv_ref.1) | copy-start | bytes 6291460
  17.2 10.2 %copy-start.2 = (bf16[1,32,1024]{2,1,0:T(8,128)(2,1)S(1)}, bf16[1,32,1024]{2,1,0:T(8,128)(2,1)}, u32[]{:S(2)}) copy-start(bf16[1,32,1024]{2,1,0:T(8,128)(2,1)} %x2_ref.1) | copy-start | bytes 196612
  17.2 10.2 %copy-start.3 = (f32[1024]{0:T(1024)S(1)}, f32[1024]{0:T(1024)}, u32[]{:S(2)}) copy-start(f32[1024]{0:T(1024)} %param.14) | copy-start | bytes 12292
  40.1 1.4 %collective-permute-start.1 = (bf16[512,128]{1,0:T(8,128)(2,1)S(1)}, bf16[512,128]{1,0:T(8,128)(2,1)S(1)}, u32[]{:S(2)}, u32[]{:S(2)}) collective-permute-start(bf16[512,128]{1,0:T(8,128)(2,1)S(1)} %shard_map.100.kv_ref), channel_id=1, source_target_pairs={{0,1},{1,0},{2,3},{3,2},{4,5},{5,4},{6,7},{7,6},{8,9},{9,8},{10,11... | collective-permute-start | bytes 393224 | tf_op jit(solution)/shard_map/ppermute | solution.py:282
  41.5 9.9 %copy-start = (bf16[1024,1024]{1,0:T(8,128)(2,1)S(1)}, bf16[1024,1024]{1,0:T(8,128)(2,1)}, u32[]{:S(2)}) copy-start(bf16[1024,1024]{1,0:T(8,128)(2,1)} %wout_ref.1) | copy-start | bytes 6291460

commit v29 on v28

--- a/solution.py
+++ b/solution.py
@@ -125,17 +125,21 @@
     return ((device ^ (device >> 1)) & 1) == 0
 
 
-def pack_heads(out_ref, q, k, v):
+def pack_keys(out_ref, k, v):
+    first = first_group()
+    cuts = [slice(h * HD, (h + 1) * HD) for h in range(HEADS)]
+    kv = [jnp.concatenate([k[:, cols], v[:, cols]], axis=-1) for cols in cuts]
+    for at in range(HEADS):
+        out_ref[at, 0 : k.shape[0], :] = jnp.where(first, kv[at], kv[at - 1])
+
+
+def pack_queries(out_ref, q):
     rows = q.shape[0]
     half = rows // 2
     first = first_group()
-    kv, lines = [], []
-    for h in range(HEADS):
-        cols = slice(h * HD, (h + 1) * HD)
-        kv.append(jnp.concatenate([k[:, cols], v[:, cols]], axis=-1))
-        lines.append(jnp.concatenate([q[:half, cols], q[half:, cols]], axis=-1))
+    cuts = [slice(h * HD, (h + 1) * HD) for h in range(HEADS)]
+    lines = [jnp.concatenate([q[:half, cols], q[half:, cols]], axis=-1) for cols in cuts]
     for at in range(HEADS):
-        out_ref[at, 0:rows, :] = jnp.where(first, kv[at], kv[at - 1])
         out_ref[at, rows : rows + half, :] = jnp.where(first, lines[at], lines[at - 1])
 
 
@@ -159,14 +163,17 @@
     half = q_ref.shape[1] // 2
     copies = [
         pltpu.make_async_copy(src.at[:, at : at + half], dst.at[:, at : at + half], sems.at[i, at // half])
-        for i, (src, dst) in enumerate(((q_hbm, q_ref), (k_hbm, k_ref), (v_hbm, v_ref)))
+        for i, (src, dst) in enumerate(((k_hbm, k_ref), (v_hbm, v_ref), (q_hbm, q_ref)))
         for at in (0, half)
     ]
     for copy in copies:
         copy.start()
-    for copy in copies:
+    for copy in copies[:4]:
         copy.wait()
-    pack_heads(out_ref, q_ref[0], k_ref[0], v_ref[0])
+    pack_keys(out_ref, k_ref[0], v_ref[0])
+    for copy in copies[4:]:
+        copy.wait()
+    pack_queries(out_ref, q_ref[0])
 
 
 def lower_half(shape):
@@ -233,7 +240,8 @@
     gained = (hidden * gain_ref[...]).astype(jnp.bfloat16)
     projected = (times(gained, wqkv_ref[...]) * factor(hidden)).astype(jnp.bfloat16)
     width = HEADS * HD
-    pack_heads(out_ref, projected[:, :width], projected[:, width : 2 * width], projected[:, 2 * width :])
+    pack_keys(out_ref, projected[:, width : 2 * width], projected[:, 2 * width :])
+    pack_queries(out_ref, projected[:, :width])
     copy.wait()
 
 

time: 52.9 us -> 53 us (level)
  no operation moved by 1% of the time
where the time goes in v29:
time: 53 us; the launch traced here: 52.7 us
  blocking collectives  43.8 us (83%)
  Pallas kernels  6.78 us (13%)
  waiting for transfers between devices  1.05 us (2%)
  between operations  0.74 us (1%)
    all_to_all x4, blocking collectives, trade(): lax.all_to_all(piece, ALL, split_axis=0, concat_axis=0, tiled=True, axis_...  43.8 us
    pallas_call x9, Pallas kernels, call(): pl.pallas_call(body, out_shape=[jax.ShapeDtypeStruct(shape, dtype) for sh...  6.78 us
  transfers between devices with their start and end apart: 2, of which 2 were waited for; matrix products, arithmetic and copies ran while one was open for 0% of the time, Pallas kernels for 3%

profile of v29, /device:TPU:0, one launch (start us, length us, event | category | flops | bytes accessed | tf_op | source)
XLA Modules:
  0.0 52.7 jit_solution(12178941824212293844)
XLA Ops:
  0.6 1.1 %shard_map.95 = bf16[16,48,128]{2,1,0:T(8,128)(2,1)S(1)} custom-call(bf16[1,32,1024]{2,1,0:T(8,128)(2,1)} %q_hbm.1, bf16[1,32,1024]{2,1,0:T(8,128)(2,1)} %k_hbm.1, bf16[1,32,1024]{2,1,0:T(8,128)(2,1)} %v_hbm.1), custom_call_target="tpu_custom_call" | custom-call | tf_op jit(solution)/shard_map/pallas_call | solution.py:263
  1.7 14.1 %all_to_all.20.piece_ref.mine_ref = bf16[16,48,128]{2,1,0:T(8,128)(2,1)S(1)} all-to-all(bf16[16,48,128]{2,1,0:T(8,128)(2,1)S(1)} %shard_map.95), channel_id=1, replica_groups={{23,24,27,28,31,0,3,4,7,8,11,12,15,16,19,20},{21,22,25,26,29,30,1,2,5,6..., dimensions={0} | all-to-all | bytes 393216 | tf_op jit(solution)/shard_map/all_to_all | solution.py:285
  15.8 0.1 collective-permute-start
  15.9 0.8 %shard_map.97 = (bf16[512,128]{1,0:T(8,128)(2,1)S(1)}, f32[512,128]{1,0:T(8,128)S(1)}, f32[512,128]{1,0:T(8,128)S(1)}) custom-call(bf16[16,48,128]{2,1,0:T(8,128)(2,1)S(1)} %all_to_all.20.piece_ref.mine_ref, bf16[512,128]{1,0:T(8,128)(2,1)S(1)} %shard_map.96.kv_ref), custom_call_target="tpu_custom_call" | custom-call | flops 1073741824 | bytes 1048576 | tf_op jit(solution)/shard_map/pallas_call | solution.py:263
  16.6 0.6 %collective-permute-done.other_ref = bf16[512,128]{1,0:T(8,128)(2,1)S(1)} collective-permute-done((bf16[512,128]{1,0:T(8,128)(2,1)S(1)}, bf16[512,128]{1,0:T(8,128)(2,1)S(1)}, u32[]{:S(2)}, u32[]{:S(2)}) %collective-permute-start) | collective-permute-done | bytes 131104 | tf_op jit(solution)/shard_map/ppermute | solution.py:290
  17.2 0.0 slice-start
  17.2 0.0 slice-start.1
  17.2 0.0 copy-start.1
  17.2 0.0 copy-start.2
  17.2 0.0 copy-start.3
  17.2 0.6 %shard_map.98 = bf16[16,16,128]{2,1,0:T(8,128)(2,1)S(1)} custom-call(bf16[512,128]{1,0:T(8,128)(2,1)S(1)} %collective-permute-done.other_ref, bf16[512,128]{1,0:T(8,128)(2,1)S(1)} %get-tuple-element.10.query_ref, f32[512,128]{1,0:T(8,128)S(1)} %get-tuple-element.11.peak_ref, f32[512,128]{1,0:T(8,128)S(1)} %get-tuple-element.12.sum_ref), custom_call_target="tpu_custom_call" | custom-call | flops 17179869184 | bytes 41943040 | tf_op jit(solution)/shard_map/pallas_call | solution.py:263
  17.9 9.5 %all_to_all.21.got_ref = bf16[16,16,128]{2,1,0:T(8,128)(2,1)S(1)} all-to-all(bf16[16,16,128]{2,1,0:T(8,128)(2,1)S(1)} %shard_map.98), channel_id=1, replica_groups={{23,24,27,28,31,0,3,4,7,8,11,12,15,16,19,20},{21,22,25,26,29,30,1,2,5,6..., dimensions={0} | all-to-all | bytes 131072 | tf_op jit(solution)/shard_map/all_to_all | solution.py:285
  27.4 0.0 slice-done
  27.4 0.0 slice-done.1
  27.4 0.0 copy-done.1
  27.4 0.0 copy-done.2
  27.4 0.0 copy-done.3
  27.4 1.7 %shard_map.99 = (f32[1,32,1024]{2,1,0:T(8,128)}, bf16[16,48,128]{2,1,0:T(8,128)(2,1)S(1)}) custom-call(bf16[16,16,128]{2,1,0:T(8,128)(2,1)S(1)} %all_to_all.21.got_ref, bf16[1,32,1024]{2,1,0:T(8,128)(2,1)S(1)} %copy-done.2, bf16[1024,1024]{1,0:T(8,128)(2,1)S(1)} %copy-done.1, f32[1,1024]{1,0:T(1,128)S(1)} %bitcast.3, bf16[1024,3072]{1,0:T(8,128)(2,1)S(1)} %bitcast.2), custom_call_target="tpu_custom_call" | custom-call | tf_op jit(solution)/shard_map/pallas_call | solution.py:263
  29.2 10.9 %all_to_all.22.piece_ref.mine_ref = bf16[16,48,128]{2,1,0:T(8,128)(2,1)S(1)} all-to-all(bf16[16,48,128]{2,1,0:T(8,128)(2,1)S(1)} %get-tuple-element.14), channel_id=1, replica_groups={{23,24,27,28,31,0,3,4,7,8,11,12,15,16,19,20},{21,22,25,26,29,30,1,2,5,6..., dimensions={0} | all-to-all | bytes 393216 | tf_op jit(solution)/shard_map/all_to_all | solution.py:285
  40.1 0.2 collective-permute-start.1
  40.3 0.8 %shard_map.101 = (bf16[512,128]{1,0:T(8,128)(2,1)S(1)}, f32[512,128]{1,0:T(8,128)S(1)}, f32[512,128]{1,0:T(8,128)S(1)}) custom-call(bf16[16,48,128]{2,1,0:T(8,128)(2,1)S(1)} %all_to_all.22.piece_ref.mine_ref, bf16[512,128]{1,0:T(8,128)(2,1)S(1)} %shard_map.100.kv_ref), custom_call_target="tpu_custom_call" | custom-call | flops 1073741824 | bytes 1048576 | tf_op jit(solution)/shard_map/pallas_call | solution.py:263
  41.0 0.5 collective-permute-done.1.other_ref
  41.5 0.0 copy-start
  41.5 0.6 %shard_map.102 = bf16[16,16,128]{2,1,0:T(8,128)(2,1)S(1)} custom-call(bf16[512,128]{1,0:T(8,128)(2,1)S(1)} %collective-permute-done.1.other_ref, bf16[512,128]{1,0:T(8,128)(2,1)S(1)} %get-tuple-element.15.query_ref, f32[512,128]{1,0:T(8,128)S(1)} %get-tuple-element.16.peak_ref, f32[512,128]{1,0:T(8,128)S(1)} %get-tuple-element.17.sum_ref), custom_call_target="tpu_custom_call" | custom-call | flops 17179869184 | bytes 41943040 | tf_op jit(solution)/shard_map/pallas_call | solution.py:263
  42.2 9.3 %all_to_all.23.got_ref = bf16[16,16,128]{2,1,0:T(8,128)(2,1)S(1)} all-to-all(bf16[16,16,128]{2,1,0:T(8,128)(2,1)S(1)} %shard_map.102), channel_id=1, replica_groups={{23,24,27,28,31,0,3,4,7,8,11,12,15,16,19,20},{21,22,25,26,29,30,1,2,5,6..., dimensions={0} | all-to-all | bytes 131072 | tf_op jit(solution)/shard_map/all_to_all | solution.py:285
  51.5 0.0 copy-done
  51.5 1.2 %shard_map.103 = f32[1,32,1024]{2,1,0:T(8,128)} custom-call(bf16[16,16,128]{2,1,0:T(8,128)(2,1)S(1)} %all_to_all.23.got_ref, bf16[1024,1024]{1,0:T(8,128)(2,1)S(1)} %copy-done), custom_call_target="tpu_custom_call" | custom-call | tf_op jit(solution)/shard_map/pallas_call | solution.py:263
  (3 shorter events, 0.0 us)
Async XLA Ops:
  15.8 1.4 %collective-permute-start = (bf16[512,128]{1,0:T(8,128)(2,1)S(1)}, bf16[512,128]{1,0:T(8,128)(2,1)S(1)}, u32[]{:S(2)}, u32[]{:S(2)}) collective-permute-start(bf16[512,128]{1,0:T(8,128)(2,1)S(1)} %shard_map.96.kv_ref), channel_id=1, source_target_pairs={{0,1},{1,0},{2,3},{3,2},{4,5},{5,4},{6,7},{7,6},{8,9},{9,8},{10,11... | collective-permute-start | bytes 393224 | tf_op jit(solution)/shard_map/ppermute | solution.py:290
  17.2 10.2 %slice-start = ((s8[6291456]{0:T(1024)(128)(4,1)}), s8[4194304]{0:T(1024)(128)(4,1)S(1)}, s32[]{:S(2)}) async-start(s8[6291456]{0:T(1024)(128)(4,1)} %bitcast.1), calls=%async_computation.4 | async-start | bytes 8388608
  17.2 10.2 %slice-start.1 = ((s8[6291456]{0:T(1024)(128)(4,1)}), s8[2097152]{0:T(1024)(128)(4,1)S(1)}, s32[]{:S(2)}) async-start(s8[6291456]{0:T(1024)(128)(4,1)} %bitcast.1), calls=%async_computation.5 | async-start | bytes 4194304
  17.2 10.2 %copy-start.1 = (bf16[1024,1024]{1,0:T(8,128)(2,1)S(1)}, bf16[1024,1024]{1,0:T(8,128)(2,1)}, u32[]{:S(2)}) copy-start(bf16[1024,1024]{1,0:T(8,128)(2,1)} %wv_ref.1) | copy-start | bytes 6291460
  17.2 10.2 %copy-start.2 = (bf16[1,32,1024]{2,1,0:T(8,128)(2,1)S(1)}, bf16[1,32,1024]{2,1,0:T(8,128)(2,1)}, u32[]{:S(2)}) copy-start(bf16[1,32,1024]{2,1,0:T(8,128)(2,1)} %x2_ref.1) | copy-start | bytes 196612
  17.2 10.2 %copy-start.3 = (f32[1024]{0:T(1024)S(1)}, f32[1024]{0:T(1024)}, u32[]{:S(2)}) copy-start(f32[1024]{0:T(1024)} %param.14) | copy-start | bytes 12292
  40.1 1.4 %collective-permute-start.1 = (bf16[512,128]{1,0:T(8,128)(2,1)S(1)}, bf16[512,128]{1,0:T(8,128)(2,1)S(1)}, u32[]{:S(2)}, u32[]{:S(2)}) collective-permute-start(bf16[512,128]{1,0:T(8,128)(2,1)S(1)} %shard_map.100.kv_ref), channel_id=1, source_target_pairs={{0,1},{1,0},{2,3},{3,2},{4,5},{5,4},{6,7},{7,6},{8,9},{9,8},{10,11... | collective-permute-start | bytes 393224 | tf_op jit(solution)/shard_map/ppermute | solution.py:290
  41.5 9.9 %copy-start = (bf16[1024,1024]{1,0:T(8,128)(2,1)S(1)}, bf16[1024,1024]{1,0:T(8,128)(2,1)}, u32[]{:S(2)}) copy-start(bf16[1024,1024]{1,0:T(8,128)(2,1)} %wout_ref.1) | copy-start | bytes 6291460

commit v30 on v28

--- a/solution.py
+++ b/solution.py
@@ -218,7 +218,7 @@
     summed = sum_ref[...] * jnp.exp2((before - peak) * SHARP) + weigh(scores, wide_peak, vals)
     top, low = summed[:n], summed[n:]
     left = lower_half(top.shape)
-    attn = jnp.where(left, pltpu.roll(top, HD, 1), low) / jnp.where(left, top, pltpu.roll(low, HD, 1))
+    attn = jnp.where(left, pltpu.roll(top, HD, 1), low) * pltpu.reciprocal(jnp.where(left, top, pltpu.roll(low, HD, 1)))
     out_ref[...] = attn.astype(jnp.bfloat16).reshape(out_ref.shape)
 
 

time: 52.9 us -> 52.9 us (level)
  no operation moved by 1% of the time
where the time goes in v30:
time: 52.9 us; the launch traced here: 52.6 us
  blocking collectives  43.8 us (83%)
  Pallas kernels  6.74 us (13%)
  waiting for transfers between devices  1.05 us (2%)
  between operations  0.74 us (1%)
    all_to_all x4, blocking collectives, trade(): lax.all_to_all(piece, ALL, split_axis=0, concat_axis=0, tiled=True, axis_...  43.8 us
    pallas_call x9, Pallas kernels, call(): pl.pallas_call(body, out_shape=[jax.ShapeDtypeStruct(shape, dtype) for sh...  6.74 us
  transfers between devices with their start and end apart: 2, of which 2 were waited for; matrix products, arithmetic and copies ran while one was open for 0% of the time, Pallas kernels for 3%

profile of v30, /device:TPU:0, one launch (start us, length us, event | category | flops | bytes accessed | tf_op | source)
XLA Modules:
  0.0 52.6 jit_solution(8044943216984981285)
XLA Ops:
  0.6 1.0 %shard_map.95 = bf16[16,48,128]{2,1,0:T(8,128)(2,1)S(1)} custom-call(bf16[1,32,1024]{2,1,0:T(8,128)(2,1)} %q_hbm.1, bf16[1,32,1024]{2,1,0:T(8,128)(2,1)} %k_hbm.1, bf16[1,32,1024]{2,1,0:T(8,128)(2,1)} %v_hbm.1), custom_call_target="tpu_custom_call" | custom-call | tf_op jit(solution)/shard_map/pallas_call | solution.py:255
  1.7 14.1 %all_to_all.20.piece_ref.mine_ref = bf16[16,48,128]{2,1,0:T(8,128)(2,1)S(1)} all-to-all(bf16[16,48,128]{2,1,0:T(8,128)(2,1)S(1)} %shard_map.95), channel_id=1, replica_groups={{23,24,27,28,31,0,3,4,7,8,11,12,15,16,19,20},{21,22,25,26,29,30,1,2,5,6..., dimensions={0} | all-to-all | bytes 393216 | tf_op jit(solution)/shard_map/all_to_all | solution.py:277
  15.8 0.1 collective-permute-start
  15.8 0.8 %shard_map.97 = (bf16[512,128]{1,0:T(8,128)(2,1)S(1)}, f32[512,128]{1,0:T(8,128)S(1)}, f32[512,128]{1,0:T(8,128)S(1)}) custom-call(bf16[16,48,128]{2,1,0:T(8,128)(2,1)S(1)} %all_to_all.20.piece_ref.mine_ref, bf16[512,128]{1,0:T(8,128)(2,1)S(1)} %shard_map.96.kv_ref), custom_call_target="tpu_custom_call" | custom-call | flops 1073741824 | bytes 1048576 | tf_op jit(solution)/shard_map/pallas_call | solution.py:255
  16.6 0.6 %collective-permute-done.other_ref = bf16[512,128]{1,0:T(8,128)(2,1)S(1)} collective-permute-done((bf16[512,128]{1,0:T(8,128)(2,1)S(1)}, bf16[512,128]{1,0:T(8,128)(2,1)S(1)}, u32[]{:S(2)}, u32[]{:S(2)}) %collective-permute-start) | collective-permute-done | bytes 131104 | tf_op jit(solution)/shard_map/ppermute | solution.py:282
  17.2 0.0 slice-start
  17.2 0.0 slice-start.1
  17.2 0.0 copy-start.1
  17.2 0.0 copy-start.2
  17.2 0.0 copy-start.3
  17.2 0.6 %shard_map.98 = bf16[16,16,128]{2,1,0:T(8,128)(2,1)S(1)} custom-call(bf16[512,128]{1,0:T(8,128)(2,1)S(1)} %collective-permute-done.other_ref, bf16[512,128]{1,0:T(8,128)(2,1)S(1)} %get-tuple-element.10.query_ref, f32[512,128]{1,0:T(8,128)S(1)} %get-tuple-element.11.peak_ref, f32[512,128]{1,0:T(8,128)S(1)} %get-tuple-element.12.sum_ref), custom_call_target="tpu_custom_call" | custom-call | flops 17179869184 | bytes 41943040 | tf_op jit(solution)/shard_map/pallas_call | solution.py:255
  17.8 9.5 %all_to_all.21.got_ref = bf16[16,16,128]{2,1,0:T(8,128)(2,1)S(1)} all-to-all(bf16[16,16,128]{2,1,0:T(8,128)(2,1)S(1)} %shard_map.98), channel_id=1, replica_groups={{23,24,27,28,31,0,3,4,7,8,11,12,15,16,19,20},{21,22,25,26,29,30,1,2,5,6..., dimensions={0} | all-to-all | bytes 131072 | tf_op jit(solution)/shard_map/all_to_all | solution.py:277
  27.4 0.0 slice-done
  27.4 0.0 slice-done.1
  27.4 0.0 copy-done.1
  27.4 0.0 copy-done.2
  27.4 0.0 copy-done.3
  27.4 1.7 %shard_map.99 = (f32[1,32,1024]{2,1,0:T(8,128)}, bf16[16,48,128]{2,1,0:T(8,128)(2,1)S(1)}) custom-call(bf16[16,16,128]{2,1,0:T(8,128)(2,1)S(1)} %all_to_all.21.got_ref, bf16[1,32,1024]{2,1,0:T(8,128)(2,1)S(1)} %copy-done.2, bf16[1024,1024]{1,0:T(8,128)(2,1)S(1)} %copy-done.1, f32[1,1024]{1,0:T(1,128)S(1)} %bitcast.3, bf16[1024,3072]{1,0:T(8,128)(2,1)S(1)} %bitcast.2), custom_call_target="tpu_custom_call" | custom-call | tf_op jit(solution)/shard_map/pallas_call | solution.py:255
  29.1 10.9 %all_to_all.22.piece_ref.mine_ref = bf16[16,48,128]{2,1,0:T(8,128)(2,1)S(1)} all-to-all(bf16[16,48,128]{2,1,0:T(8,128)(2,1)S(1)} %get-tuple-element.14), channel_id=1, replica_groups={{23,24,27,28,31,0,3,4,7,8,11,12,15,16,19,20},{21,22,25,26,29,30,1,2,5,6..., dimensions={0} | all-to-all | bytes 393216 | tf_op jit(solution)/shard_map/all_to_all | solution.py:277
  40.1 0.2 collective-permute-start.1
  40.2 0.8 %shard_map.101 = (bf16[512,128]{1,0:T(8,128)(2,1)S(1)}, f32[512,128]{1,0:T(8,128)S(1)}, f32[512,128]{1,0:T(8,128)S(1)}) custom-call(bf16[16,48,128]{2,1,0:T(8,128)(2,1)S(1)} %all_to_all.22.piece_ref.mine_ref, bf16[512,128]{1,0:T(8,128)(2,1)S(1)} %shard_map.100.kv_ref), custom_call_target="tpu_custom_call" | custom-call | flops 1073741824 | bytes 1048576 | tf_op jit(solution)/shard_map/pallas_call | solution.py:255
  41.0 0.5 collective-permute-done.1.other_ref
  41.5 0.0 copy-start
  41.5 0.6 %shard_map.102 = bf16[16,16,128]{2,1,0:T(8,128)(2,1)S(1)} custom-call(bf16[512,128]{1,0:T(8,128)(2,1)S(1)} %collective-permute-done.1.other_ref, bf16[512,128]{1,0:T(8,128)(2,1)S(1)} %get-tuple-element.15.query_ref, f32[512,128]{1,0:T(8,128)S(1)} %get-tuple-element.16.peak_ref, f32[512,128]{1,0:T(8,128)S(1)} %get-tuple-element.17.sum_ref), custom_call_target="tpu_custom_call" | custom-call | flops 17179869184 | bytes 41943040 | tf_op jit(solution)/shard_map/pallas_call | solution.py:255
  42.1 9.3 %all_to_all.23.got_ref = bf16[16,16,128]{2,1,0:T(8,128)(2,1)S(1)} all-to-all(bf16[16,16,128]{2,1,0:T(8,128)(2,1)S(1)} %shard_map.102), channel_id=1, replica_groups={{23,24,27,28,31,0,3,4,7,8,11,12,15,16,19,20},{21,22,25,26,29,30,1,2,5,6..., dimensions={0} | all-to-all | bytes 131072 | tf_op jit(solution)/shard_map/all_to_all | solution.py:277
  51.4 0.0 copy-done
  51.4 1.2 %shard_map.103 = f32[1,32,1024]{2,1,0:T(8,128)} custom-call(bf16[16,16,128]{2,1,0:T(8,128)(2,1)S(1)} %all_to_all.23.got_ref, bf16[1024,1024]{1,0:T(8,128)(2,1)S(1)} %copy-done), custom_call_target="tpu_custom_call" | custom-call | tf_op jit(solution)/shard_map/pallas_call | solution.py:255
  (3 shorter events, 0.0 us)
Async XLA Ops:
  15.8 1.4 %collective-permute-start = (bf16[512,128]{1,0:T(8,128)(2,1)S(1)}, bf16[512,128]{1,0:T(8,128)(2,1)S(1)}, u32[]{:S(2)}, u32[]{:S(2)}) collective-permute-start(bf16[512,128]{1,0:T(8,128)(2,1)S(1)} %shard_map.96.kv_ref), channel_id=1, source_target_pairs={{0,1},{1,0},{2,3},{3,2},{4,5},{5,4},{6,7},{7,6},{8,9},{9,8},{10,11... | collective-permute-start | bytes 393224 | tf_op jit(solution)/shard_map/ppermute | solution.py:282
  17.2 10.2 %slice-start = ((s8[6291456]{0:T(1024)(128)(4,1)}), s8[4194304]{0:T(1024)(128)(4,1)S(1)}, s32[]{:S(2)}) async-start(s8[6291456]{0:T(1024)(128)(4,1)} %bitcast.1), calls=%async_computation.4 | async-start | bytes 8388608
  17.2 10.2 %slice-start.1 = ((s8[6291456]{0:T(1024)(128)(4,1)}), s8[2097152]{0:T(1024)(128)(4,1)S(1)}, s32[]{:S(2)}) async-start(s8[6291456]{0:T(1024)(128)(4,1)} %bitcast.1), calls=%async_computation.5 | async-start | bytes 4194304
  17.2 10.2 %copy-start.1 = (bf16[1024,1024]{1,0:T(8,128)(2,1)S(1)}, bf16[1024,1024]{1,0:T(8,128)(2,1)}, u32[]{:S(2)}) copy-start(bf16[1024,1024]{1,0:T(8,128)(2,1)} %wv_ref.1) | copy-start | bytes 6291460
  17.2 10.2 %copy-start.2 = (bf16[1,32,1024]{2,1,0:T(8,128)(2,1)S(1)}, bf16[1,32,1024]{2,1,0:T(8,128)(2,1)}, u32[]{:S(2)}) copy-start(bf16[1,32,1024]{2,1,0:T(8,128)(2,1)} %x2_ref.1) | copy-start | bytes 196612
  17.2 10.2 %copy-start.3 = (f32[1024]{0:T(1024)S(1)}, f32[1024]{0:T(1024)}, u32[]{:S(2)}) copy-start(f32[1024]{0:T(1024)} %param.14) | copy-start | bytes 12292
  40.1 1.4 %collective-permute-start.1 = (bf16[512,128]{1,0:T(8,128)(2,1)S(1)}, bf16[512,128]{1,0:T(8,128)(2,1)S(1)}, u32[]{:S(2)}, u32[]{:S(2)}) collective-permute-start(bf16[512,128]{1,0:T(8,128)(2,1)S(1)} %shard_map.100.kv_ref), channel_id=1, source_target_pairs={{0,1},{1,0},{2,3},{3,2},{4,5},{5,4},{6,7},{7,6},{8,9},{9,8},{10,11... | collective-permute-start | bytes 393224 | tf_op jit(solution)/shard_map/ppermute | solution.py:282
  41.5 9.9 %copy-start = (bf16[1024,1024]{1,0:T(8,128)(2,1)S(1)}, bf16[1024,1024]{1,0:T(8,128)(2,1)}, u32[]{:S(2)}) copy-start(bf16[1024,1024]{1,0:T(8,128)(2,1)} %wout_ref.1) | copy-start | bytes 6291460
